TPU v7x, 32 devices: a whole 2x2x4 slice. The times are simulated.
32 devices in a mesh: ens: 2 (over x), mode: 16 (over z, y, core).
Axes of the slice: x: 2, y: 2, z: 4, core: 2. Of those that a mesh axis runs over, the one named last changes fastest.
Arguments:
- velocity: float32 [6, 512, 2048], P('ens', 'mode'), parts along dimension 0, may hold values from -4 to 4
- log_conf: float32 [12, 512, 2048], P('ens', 'mode'), parts along dimension 0, may hold values from -3 to 3
- orientation: int32 [32], replicated, may hold values from 0 to 7
- wall_speed: float32 [2], P('ens'), parts along dimension 0, may hold values from 0.5 to 2
Outputs:
- vel_next: float32 [6, 512, 2048], P('ens', 'mode'), parts along dimension 0
- logc_next: float32 [12, 512, 2048], P('ens', 'mode'), parts along dimension 0
There are 2 independent parts, one for each index of `ens`. A program takes and returns all parts, laid end to end along the dimension named above; an argument that names none is the same for every part. Nothing has to cross between parts.
All inputs are finite; a program needn't handle non-finite values.
Results may differ from a plain program's by a relative error of at most 0.0003.
Values sent between devices are 32-bit elements; how exact they have to be, the bound alone decides.
No kernel may reach another device: no remote copies, remote signals or barrier semaphores. Data moves between devices by JAX's collectives and lax.ppermute only.
A program may use at most 512 MiB of HBM per device.

v0:
```python
import functools

import jax
import jax.numpy as jnp
import ml_dtypes
import numpy as np
from jax import lax
from jax.experimental import pallas as pl
from jax.experimental.pallas import tpu as pltpu
from jax.sharding import PartitionSpec as P

SIDE = 8
CYCLES = 2
RADIAL = SIDE * CYCLES
BLOCK = SIDE * RADIAL
STEP_DT = 0.002
RELAX_TIME = 0.02
MOBILITY = 0.3
LAYER_HEIGHT = 0.25
R_INNER = 1.0
MIB = 1 << 20
F32 = jnp.float32
BF16 = jnp.bfloat16


def split_table(table):
    high = np.asarray(table, np.float32).astype(ml_dtypes.bfloat16)
    low = (np.asarray(table, np.float64) - high.astype(np.float64)).astype(ml_dtypes.bfloat16)
    return high, low


def cheb_table(points):
    nodes_xi = -np.cos(np.pi * np.arange(points) / (points - 1))
    weights = np.ones(points)
    weights[0] = 2.0
    weights[-1] = 2.0
    weights = weights * (-1.0) ** np.arange(points)
    identity = np.eye(points)
    spacing = nodes_xi[:, None] - nodes_xi[None, :] + identity
    matrix = weights[:, None] / weights[None, :] / spacing
    matrix = matrix * (1.0 - identity)
    matrix = matrix - identity * matrix.sum(axis=1)[:, None]
    return nodes_xi, matrix


def fourier_tables(planes):
    phase = np.arange(planes)[:, None] * np.arange(planes // 2)[None, :] % planes
    angles = phase * (2.0 * np.pi / planes)
    cosine = np.cos(angles) * np.sqrt(2.0 / planes)
    sine = np.sin(angles) * np.sqrt(2.0 / planes)
    cosine[:, 0] = planes**-0.5
    sine[:, 0] = (-1.0) ** np.arange(planes) * planes**-0.5
    wavenums = np.arange(planes // 2)
    basis = np.stack([cosine, sine], axis=2).reshape(planes, planes)
    turned = np.stack([-wavenums * sine, wavenums * cosine], axis=2).reshape(planes, planes)
    return np.concatenate([basis, turned], axis=0)


def node_tables():
    nodes_xi, matrix = cheb_table(SIDE)
    radius = R_INNER + (np.arange(CYCLES)[:, None] + (nodes_xi[None, :] + 1.0) / 2.0) / CYCLES
    inv_r = 1.0 / radius.reshape(-1)
    radial_row = np.kron(np.eye(CYCLES), matrix.T * (2.0 * CYCLES))
    radial_mean = np.eye(RADIAL)
    for cycle in range(1, CYCLES):
        low, high = cycle * SIDE - 1, cycle * SIDE
        radial_mean[low : high + 1, low : high + 1] = 0.5
    d_radial = np.kron(np.eye(SIDE), radial_row)
    d_axial = np.kron(matrix.T * (2.0 / LAYER_HEIGHT), np.eye(RADIAL))
    own_weight = np.ones(SIDE)
    own_weight[[0, -1]] = 0.5
    average = np.kron(np.diag(own_weight), radial_mean)
    inv_r_nodes = np.tile(inv_r, SIDE)
    both = np.stack(
        [d_radial, d_axial, d_radial @ average, d_axial @ average, average * inv_r_nodes[None, :]]
    )
    faces = np.zeros((3, BLOCK, 2 * BLOCK))
    halos = np.zeros((9, 2 * BLOCK, BLOCK))
    for field in range(3):
        for side, row in ((0, SIDE - 1), (1, 0)):
            at_u = side * BLOCK + field * RADIAL
            at_dz = at_u + 3 * RADIAL
            face_nodes = slice(row * RADIAL, (row + 1) * RADIAL)
            faces[field, face_nodes, at_u : at_u + RADIAL] = np.eye(RADIAL)
            faces[field, :, at_dz : at_dz + RADIAL] = d_axial[:, face_nodes]
            here = SIDE - 1 - row
            out = slice(here * RADIAL, (here + 1) * RADIAL)
            halos[field, at_u : at_u + RADIAL, out] = 0.5 * radial_row @ radial_mean
            halos[3 + field, at_dz : at_dz + RADIAL, out] = 0.5 * radial_mean
            halos[6 + field, at_u : at_u + RADIAL, out] = 0.5 * radial_mean * inv_r[None, :]
    return both, faces, halos, inv_r_nodes


def split(values):
    high = values.astype(BF16)
    return high, (values - high.astype(F32)).astype(BF16)


def dot(left, right):
    return jnp.dot(left, right, preferred_element_type=F32)


def dot3(left, right):
    return dot(left[0], right[0]) + (dot(left[0], right[1]) + dot(left[1], right[0]))


def whole_spec():
    return pl.BlockSpec(memory_space=pltpu.VMEM)


def kernel_call(body, outs, count, scratch=(), vmem=40, flops=0, bytes_accessed=0, name=None):
    return pl.pallas_call(
        body,
        out_shape=outs,
        in_specs=[whole_spec()] * count,
        out_specs=jax.tree.map(lambda _: whole_spec(), outs),
        scratch_shapes=list(scratch),
        compiler_params=pltpu.CompilerParams(vmem_limit_bytes=vmem * MIB),
        cost_estimate=pl.CostEstimate(
            flops=flops, bytes_accessed=bytes_accessed, transcendentals=0
        ),
        name=name,
    )


def pack_body(in_ref, out_ref):
    for layer in range(out_ref.shape[0]):
        out_ref[layer] = in_ref[:, :, layer * BLOCK : (layer + 1) * BLOCK]


def pack(values):
    fields, local_modes, nodes = values.shape
    layers = nodes // BLOCK
    step = 4
    return pl.pallas_call(
        pack_body,
        grid=(layers // step,),
        in_specs=[pl.BlockSpec((fields, local_modes, step * BLOCK), lambda i: (0, 0, i))],
        out_specs=pl.BlockSpec((step, fields, local_modes, BLOCK), lambda i: (i, 0, 0, 0)),
        out_shape=jax.ShapeDtypeStruct((layers, fields, local_modes, BLOCK), F32),
        cost_estimate=pl.CostEstimate(
            flops=0, bytes_accessed=8 * values.size, transcendentals=0
        ),
        name="pack",
    )(values)


def exchange(blocks):
    return lax.all_to_all(blocks, "mode", split_axis=0, concat_axis=0, tiled=True)


def gathered(blocks):
    devices, fields, local_modes, nodes = blocks.shape
    if local_modes % 8 == 0:
        return blocks
    return blocks.transpose(1, 0, 2, 3).reshape(1, fields, devices * local_modes, nodes)


def field_of(ref, field):
    return ref[:, field].reshape(-1, BLOCK)


def order_body(to_grid, from_grid, both_ref, faces_ref, halos_ref, both_out, faces_out, halos_out):
    for at in range(both_ref.shape[0]):
        moved = dot(both_ref[at], from_grid[...]).astype(BF16)
        both_out[at] = dot(to_grid[...], moved).astype(BF16)
    for at in range(faces_ref.shape[0]):
        faces_out[at] = dot(to_grid[...], faces_ref[at]).astype(BF16)
    for at in range(halos_ref.shape[0]):
        halos_out[at] = dot(halos_ref[at], from_grid[...]).astype(BF16)


def face_body(vel_ref, faces_ref, up_ref, down_ref):
    total = None
    for field in range(3):
        own = split(field_of(vel_ref, field))
        part = dot3(own, (faces_ref[2 * field], faces_ref[2 * field + 1]))
        total = part if total is None else total + part
    up_ref[...] = total[:, :BLOCK]
    down_ref[...] = total[:, BLOCK:]


def velocity_body(
    vel_ref, below_ref, above_ref, high_ref, low_ref, both_ref, halos_ref, inv_r_ref,
    flow_ref, values,
):
    planes = high_ref.shape[1]
    table = (high_ref[...], low_ref[...])
    values[:, 0:256] = dot3(
        table, split(jnp.concatenate([field_of(vel_ref, 0), field_of(vel_ref, 1)], axis=1))
    )
    values[:, 256:384] = dot3(table, split(field_of(vel_ref, 2)))
    values[:, 384:640] = dot3(
        table, split(jnp.concatenate([below_ref[...], above_ref[...]], axis=1))
    )
    rows_step = 128

    def matrix(at):
        return both_ref[2 * at], both_ref[2 * at + 1]

    def halo(at):
        return halos_ref[2 * at], halos_ref[2 * at + 1]

    def chunk(step, carry):
        rows = pl.ds(pl.multiple_of(step * rows_step, rows_step), rows_step)
        turned = pl.ds(pl.multiple_of(planes + step * rows_step, rows_step), rows_step)
        u = [values[rows, f * BLOCK : (f + 1) * BLOCK] for f in range(3)]
        u_s = [split(v) for v in u]
        dth_s = [split(values[turned, f * BLOCK : (f + 1) * BLOCK]) for f in range(3)]
        edge = split(values[rows, 384:640])
        edge_dth = split(values[turned, 384:640])
        g_r = [dot3(u_s[f], matrix(2)) + dot3(edge, halo(f)) for f in range(3)]
        g_z = [dot3(u_s[f], matrix(3)) + dot3(edge, halo(3 + f)) for f in range(3)]
        g_t = [dot3(dth_s[f], matrix(4)) + dot3(edge_dth, halo(6 + f)) for f in range(3)]
        mean_r = dot3(u_s[0], matrix(4)) + dot3(edge, halo(6))
        mean_t = dot3(u_s[1], matrix(4)) + dot3(edge, halo(7))
        g_t[0] = g_t[0] - mean_t
        g_t[1] = g_t[1] + mean_r
        hoop_rate = u[1] * inv_r_ref[0:1, :]
        flow_ref[0, rows, :] = u[0]
        flow_ref[1, rows, :] = hoop_rate
        flow_ref[2, rows, :] = u[2]
        flow_ref[3, rows, :] = 0.5 * (g_t[0] - g_r[1]) + hoop_rate
        flow_ref[4, rows, :] = 0.5 * (g_z[0] - g_r[2])
        flow_ref[5, rows, :] = 0.5 * (g_z[1] - g_t[2])
        rest = (1.0 - 2.0 * MOBILITY) / RELAX_TIME
        flow_ref[6, rows, :] = 2.0 * g_r[0] - rest
        flow_ref[7, rows, :] = g_t[0] + g_r[1]
        flow_ref[8, rows, :] = g_z[0] + g_r[2]
        flow_ref[9, rows, :] = 2.0 * g_t[1] - rest
        flow_ref[10, rows, :] = g_z[1] + g_t[2]
        flow_ref[11, rows, :] = 2.0 * g_z[2] - rest
        for f in range(3):
            flow_ref[12 + f, rows, :] = -(g_r[f] * u[0] + g_t[f] * u[1] + g_z[f] * u[2])
        return carry

    lax.fori_loop(0, planes // rows_step, chunk, 0)


def square(m):
    a, b, c, d, e, f = m
    bb, cc, ee = b * b, c * c, e * e
    return (
        a * a + (bb + cc),
        b * (a + d) + c * e,
        c * (a + f) + b * e,
        d * d + (bb + ee),
        e * (d + f) + b * c,
        f * f + (cc + ee),
    )


def commuting_product(m, n):
    a, b, c, d, e, f = m
    p, q, r, s, t, u = n
    return (
        a * p + b * q + c * r,
        a * q + b * s + c * t,
        a * r + b * t + c * u,
        b * q + d * s + e * t,
        b * r + d * t + e * u,
        c * r + e * t + f * u,
    )


DIAGONAL = (0, 3, 5)


def plus_identity(m):
    return tuple(v + 1.0 if at in DIAGONAL else v for at, v in enumerate(m))


def exponentials(psi):
    x = tuple(v * 0.125 for v in psi)
    x2 = square(x)
    x4 = square(x2)
    even = plus_identity(tuple(v * 0.5 + w * (1.0 / 24.0) for v, w in zip(x2, x4)))
    odd = commuting_product(x, plus_identity(tuple(v * (1.0 / 6.0) for v in x2)))
    conform = tuple(v + w for v, w in zip(even, odd))
    inverse = tuple(v - w for v, w in zip(even, odd))
    for _ in range(3):
        conform = square(conform)
        inverse = square(inverse)
    return conform, inverse


def stress_body(
    psi_ref, flow_ref, high_ref, low_ref, back_high_ref, back_low_ref, both_ref, inv_r_ref,
    out_ref, psi_s, dth_s, grad_s, stress_h, stress_l, rate_h, rate_l, vel_h, vel_l, mom_s,
):
    planes = high_ref.shape[1]
    for pair in range(3):
        members = jnp.concatenate(
            [field_of(psi_ref, 2 * pair), field_of(psi_ref, 2 * pair + 1)], axis=1
        )
        values = dot3((high_ref[...], low_ref[...]), split(members))
        for at in range(2):
            psi_s[2 * pair + at] = values[:planes, at * BLOCK : (at + 1) * BLOCK]
            dth_s[2 * pair + at] = values[planes:, at * BLOCK : (at + 1) * BLOCK]
    gradient = tuple(
        jnp.concatenate([both_ref[at], both_ref[2 + at]], axis=1) for at in range(2)
    )
    for member in range(6):
        grad_s[member] = dot3(split(psi_s[member]), gradient)

    rows_step = 16
    inv_relax = 1.0 / RELAX_TIME

    def put(high, low, rows, lanes, value):
        value_h, value_l = split(value)
        high[rows, lanes] = value_h
        low[rows, lanes] = value_l

    def lanes_of(at):
        return slice(at * BLOCK, (at + 1) * BLOCK)

    def chunk(step, carry):
        rows = pl.ds(pl.multiple_of(step * rows_step, rows_step), rows_step)
        inv_r = inv_r_ref[0:1, :]
        psi = tuple(psi_s[member, rows, :] for member in range(6))
        conform, inverse = exponentials(psi)
        u_r, hoop_rate, u_z, p, q, s = (flow_ref[at, rows, :] for at in range(6))
        a, b, c, d, e, f = psi
        pb, qc, se = p * b, q * c, s * e
        turning = (
            2.0 * (pb + qc),
            p * (d - a) + (q * e + s * c),
            q * (f - a) + (p * e - s * b),
            2.0 * (se - pb),
            s * (f - d) - (p * c + q * b),
            -2.0 * (qc + se),
        )
        for member in range(6):
            advect = (
                u_r * grad_s[member, rows, 0:BLOCK]
                + hoop_rate * dth_s[member, rows, :]
                + u_z * grad_s[member, rows, BLOCK : 2 * BLOCK]
            )
            relaxing = ((1.0 - MOBILITY) * inv_relax) * inverse[member] - (
                MOBILITY * inv_relax
            ) * conform[member]
            rate = (turning[member] - advect) + (flow_ref[6 + member, rows, :] + relaxing)
            put(rate_h, rate_l, rows, lanes_of(member), rate)
        stress = tuple(v - 1.0 if at in DIAGONAL else v for at, v in enumerate(conform))
        for member in range(6):
            put(stress_h, stress_l, rows, lanes_of(member), stress[member])
        hoop = tuple(stress[at] * inv_r for at in (1, 3, 4))
        turned = pl.ds(pl.multiple_of(planes + step * rows_step, rows_step), rows_step)
        for at in range(3):
            put(vel_h, vel_l, turned, lanes_of(at), -hoop[at])
        mom_s[0, rows, :] = flow_ref[12, rows, :] + (stress[0] * inv_r - hoop[1])
        mom_s[1, rows, :] = flow_ref[13, rows, :] + 2.0 * hoop[0]
        mom_s[2, rows, :] = flow_ref[14, rows, :] + stress[2] * inv_r
        return carry

    lax.fori_loop(0, planes // rows_step, chunk, 0)

    divergence = tuple(
        jnp.concatenate([both_ref[at], both_ref[2 + at]], axis=0) for at in range(2)
    )
    for at, (radial, axial) in enumerate(((0, 2), (1, 4), (2, 5))):
        pair_s = tuple(
            jnp.concatenate([ref[:, lanes_of(radial)], ref[:, lanes_of(axial)]], axis=1)
            for ref in (stress_h, stress_l)
        )
        put(vel_h, vel_l, slice(0, planes), lanes_of(at), mom_s[at] + dot3(pair_s, divergence))
    blocks, local_modes = out_ref.shape[0], out_ref.shape[2]
    back = (back_high_ref[...], back_low_ref[...])
    for start, stop in ((0, 2), (2, 3)):
        lanes = slice(start * BLOCK, stop * BLOCK)
        coeffs = dot3(back, (vel_h[:, lanes], vel_l[:, lanes]))
        for at in range(start, stop):
            out_ref[:, at] = coeffs[:, lanes_of(at - start)].reshape(blocks, local_modes, BLOCK)
    back = (back_high_ref[:, :planes], back_low_ref[:, :planes])
    for pair in range(3):
        lanes = slice(2 * pair * BLOCK, (2 * pair + 2) * BLOCK)
        coeffs = dot3(back, (rate_h[:, lanes], rate_l[:, lanes]))
        for at in range(2):
            out_ref[:, 3 + 2 * pair + at] = coeffs[:, lanes_of(at)].reshape(
                blocks, local_modes, BLOCK
            )


def step_body(
    layers, step, rates_ref, mean_ref, place_ref, vel_ref, logc_ref, wall_ref, vel_out, logc_out
):
    fields, local_modes = rates_ref.shape[1], rates_ref.shape[2]
    merged = local_modes % 8 == 0
    first = pl.program_id(0) * step

    def averaged(index, at, field):
        below = lax.rem(index + (layers - 1), layers)
        above = lax.rem(index + 1, layers)
        total = None
        for number, layer in enumerate((below, index, above)):
            block = rates_ref[layer] if field is None else rates_ref[layer, field]
            high, low = split(block.reshape(-1, BLOCK))
            weights = mean_ref[at, number * BLOCK : (number + 1) * BLOCK, :]
            part = dot(high, weights) + dot(low, weights)
            total = part if total is None else total + part
        return total

    for at in range(step):
        index = first + at
        lanes = slice(at * BLOCK, (at + 1) * BLOCK)
        place = place_ref[at]
        inner = place % RADIAL == 0
        on_wall = jnp.logical_or(inner, place % RADIAL == RADIAL - 1)
        if merged:
            every = averaged(index, at, None)
            rates = [every[f * local_modes : (f + 1) * local_modes] for f in range(fields)]
        else:
            rates = [averaged(index, at, f) for f in range(fields)]
        shape = (local_modes, BLOCK)
        wall = jnp.broadcast_to(on_wall, shape)
        row_ids = lax.broadcasted_iota(jnp.int32, shape, 0)
        mean_row = jnp.logical_and(row_ids == 0, jnp.broadcast_to(inner, shape))
        driven = jnp.where(mean_row, wall_ref[0], 0.0)
        for field in range(3):
            stepped = vel_ref[field, :, lanes] + STEP_DT * rates[field]
            held = driven if field == 1 else 0.0
            vel_out[field, :, lanes] = jnp.where(wall, held, stepped)
        for field in range(6):
            logc_out[field, :, lanes] = logc_ref[field, :, lanes] + STEP_DT * rates[3 + field]


def advance(rates, means, place, velocity, log_conf, wall):
    layers, fields, local_modes, _ = rates.shape
    step = 4
    nodes = step * BLOCK
    return pl.pallas_call(
        functools.partial(step_body, layers, step),
        grid=(layers // step,),
        in_specs=[
            pl.BlockSpec(rates.shape, lambda i: (0, 0, 0, 0)),
            pl.BlockSpec((step, 3 * BLOCK, BLOCK), lambda i: (i, 0, 0)),
            pl.BlockSpec((step, 1, BLOCK), lambda i: (i, 0, 0)),
            pl.BlockSpec((3, local_modes, nodes), lambda i: (0, 0, i)),
            pl.BlockSpec((6, local_modes, nodes), lambda i: (0, 0, i)),
            pl.BlockSpec(memory_space=pltpu.SMEM),
        ],
        out_specs=[
            pl.BlockSpec((3, local_modes, nodes), lambda i: (0, 0, i)),
            pl.BlockSpec((6, local_modes, nodes), lambda i: (0, 0, i)),
        ],
        out_shape=[
            jax.ShapeDtypeStruct(velocity.shape, F32),
            jax.ShapeDtypeStruct(log_conf.shape, F32),
        ],
        compiler_params=pltpu.CompilerParams(vmem_limit_bytes=32 * MIB),
        name="advance",
    )(rates, means, place, velocity, log_conf, wall)


def grid_places(orientation):
    orient = orientation.reshape(-1, CYCLES, 1, 1)
    cycle = jnp.arange(CYCLES, dtype=jnp.int32).reshape(1, CYCLES, 1, 1)
    lead = jnp.arange(SIDE, dtype=jnp.int32).reshape(1, 1, SIDE, 1)
    trail = jnp.arange(SIDE, dtype=jnp.int32).reshape(1, 1, 1, SIDE)
    lead = jnp.where(orient % 2 == 1, SIDE - 1 - lead, lead)
    trail = jnp.where(orient // 2 % 2 == 1, SIDE - 1 - trail, trail)
    swapped = orient // 4 % 2 == 1
    row = jnp.where(swapped, trail, lead)
    col = jnp.where(swapped, lead, trail)
    return (row * RADIAL + cycle * SIDE + col).reshape(-1, BLOCK)


def mean_weights(place):
    below = jnp.roll(place, 1, axis=0)
    above = jnp.roll(place, -1, axis=0)
    source = jnp.stack([below, place, above], axis=1)[..., None]
    target = place[:, None, None, :]
    kind = jnp.arange(3, dtype=jnp.int32).reshape(1, 3, 1, 1)
    src_x, dst_x = source % RADIAL, target % RADIAL
    src_y, dst_y = source // RADIAL, target // RADIAL

    def near(x):
        inside = jnp.logical_and(x >= SIDE // 2, x < RADIAL - SIDE // 2)
        return jnp.logical_and(inside, jnp.logical_or(x % SIDE == 0, x % SIDE == SIDE - 1))

    both_near = jnp.logical_and(near(src_x), near(dst_x))
    joined = jnp.logical_and(both_near, (src_x + 1) // SIDE == (dst_x + 1) // SIDE)
    radial = jnp.where(joined, 0.5, jnp.where(src_x == dst_x, 1.0, 0.0))
    on_face = jnp.logical_or(dst_y == 0, dst_y == SIDE - 1)
    own = jnp.where(src_y == dst_y, jnp.where(on_face, 0.5, 1.0), 0.0)
    from_below = jnp.logical_and(dst_y == 0, src_y == SIDE - 1)
    from_above = jnp.logical_and(dst_y == SIDE - 1, src_y == 0)
    axial = jnp.where(
        kind == 1, own, jnp.where(jnp.where(kind == 0, from_below, from_above), 0.5, 0.0)
    )
    return (radial * axial).astype(BF16).reshape(-1, 3 * BLOCK, BLOCK)


def body(velocity, log_conf, orientation, wall_speed):
    devices = lax.axis_size("mode")
    device = lax.axis_index("mode")
    local_modes = velocity.shape[1]
    planes = local_modes * devices
    both, faces, halos, inv_r_nodes = node_tables()

    def parts(tables):
        return jnp.asarray(np.stack([half for table in tables for half in split_table(table)]))

    fourier = fourier_tables(planes)
    high, low = (jnp.asarray(half) for half in split_table(fourier))
    back_high, back_low = (jnp.asarray(half) for half in split_table(fourier.T))

    place = grid_places(orientation)
    own_place = lax.dynamic_slice_in_dim(place, device, 1)
    grid_ids = jnp.arange(BLOCK, dtype=jnp.int32)
    from_grid = (grid_ids[:, None] == own_place).astype(BF16)
    to_grid = (own_place.reshape(BLOCK, 1) == grid_ids[None, :]).astype(BF16)
    table_r = jnp.asarray(inv_r_nodes, F32)
    inv_r = jnp.sum(jnp.where(grid_ids[:, None] == own_place, table_r[:, None], 0.0), axis=0)
    inv_r = jnp.broadcast_to(inv_r[None, :], (8, BLOCK))

    vel_nodes = gathered(exchange(pack(velocity)))
    psi_nodes = gathered(exchange(pack(log_conf)))

    both_s, faces_s, halos_s = kernel_call(
        order_body,
        (
            jax.ShapeDtypeStruct((10, BLOCK, BLOCK), BF16),
            jax.ShapeDtypeStruct((6, BLOCK, 2 * BLOCK), BF16),
            jax.ShapeDtypeStruct((18, 2 * BLOCK, BLOCK), BF16),
        ),
        5,
        vmem=16,
        flops=2 * BLOCK**3 * 68,
        bytes_accessed=5 * MIB,
        name="order",
    )(to_grid, from_grid, parts(both), parts(faces), parts(halos))

    edge = jax.ShapeDtypeStruct((planes, BLOCK), F32)
    to_up, to_down = kernel_call(
        face_body, (edge, edge), 2, vmem=16, flops=2 * 3 * planes * 384 * 256,
        bytes_accessed=2 * MIB, name="faces",
    )(vel_nodes, faces_s)
    up = [(i, (i + 1) % devices) for i in range(devices)]
    below = lax.ppermute(to_up, "mode", up)
    above = lax.ppermute(to_down, "mode", [(j, i) for i, j in up])

    flow = kernel_call(
        velocity_body,
        jax.ShapeDtypeStruct((15, planes, BLOCK), F32),
        8,
        scratch=[pltpu.VMEM((2 * planes, 5 * BLOCK), F32)],
        vmem=32,
        flops=12 * 10**9,
        bytes_accessed=8 * MIB,
        name="velocity",
    )(vel_nodes, below, above, high, low, both_s, halos_s, inv_r)

    rates = kernel_call(
        stress_body,
        jax.ShapeDtypeStruct(psi_nodes.shape[:1] + (9,) + psi_nodes.shape[2:], F32),
        8,
        scratch=[
            pltpu.VMEM((6, planes, BLOCK), F32),
            pltpu.VMEM((6, planes, BLOCK), F32),
            pltpu.VMEM((6, planes, 2 * BLOCK), F32),
            pltpu.VMEM((planes, 6 * BLOCK), BF16),
            pltpu.VMEM((planes, 6 * BLOCK), BF16),
            pltpu.VMEM((planes, 6 * BLOCK), BF16),
            pltpu.VMEM((planes, 6 * BLOCK), BF16),
            pltpu.VMEM((2 * planes, 3 * BLOCK), BF16),
            pltpu.VMEM((2 * planes, 3 * BLOCK), BF16),
            pltpu.VMEM((3, planes, BLOCK), F32),
        ],
        vmem=50,
        flops=12 * 10**9,
        bytes_accessed=12 * MIB,
        name="stress",
    )(psi_nodes, flow, high, low, back_high, back_low, both_s, inv_r)

    if local_modes % 8:
        rates = rates.reshape(9, devices, local_modes, BLOCK).transpose(1, 0, 2, 3)
    mode_rates = exchange(rates)
    wall = jnp.where(device == 0, wall_speed, 0.0)
    return tuple(
        advance(mode_rates, mean_weights(place), place[:, None, :], velocity, log_conf, wall)
    )


def solution(mesh):
    in_specs = (P("ens", "mode", None), P("ens", "mode", None), P(), P("ens"))
    out_specs = (P("ens", "mode", None), P("ens", "mode", None))
    return jax.shard_map(body, mesh=mesh, in_specs=in_specs, out_specs=out_specs, check_vma=False)
```

profile of v0, /device:TPU:13, one launch (start us, length us, event | category | flops | bytes accessed | tf_op | source)
XLA Modules:
  0.0 165.1 jit_solution(9647741641723364518)
XLA Ops:
  0.6 3.3 %pack.3 = f32[16,3,32,128]{3,2,1,0:T(8,128)} custom-call(f32[3,32,2048]{2,1,0:T(8,128)} %vel_ref.1), custom_call_target="tpu_custom_call" | custom-call | bytes 1572864 | tf_op jit(solution)/shard_map/pack/pallas_call | solution.py:135
  3.9 6.6 %all-to-all-start.1 = ((f32[16,3,32,128]{3,2,1,0:T(8,128)}), f32[16,3,32,128]{3,2,1,0:T(8,128)S(1)}, u32[]{:S(2)}, u32[]{:S(2)}) async-start(f32[16,3,32,128]{3,2,1,0:T(8,128)} %pack.3), calls=%async_computation.1 | async-start | bytes 1572864 | tf_op jit(solution)/shard_map/all_to_all | solution.py:149
  10.5 3.7 %pack.2 = f32[16,6,32,128]{3,2,1,0:T(8,128)} custom-call(f32[6,32,2048]{2,1,0:T(8,128)} %logc_ref.1), custom_call_target="tpu_custom_call" | custom-call | bytes 3145728 | tf_op jit(solution)/shard_map/pack/pallas_call | solution.py:135
  14.2 15.5 %all-to-all-done.1.vel_ref = f32[16,3,32,128]{3,2,1,0:T(8,128)S(1)} async-done(((f32[16,3,32,128]{3,2,1,0:T(8,128)}), f32[16,3,32,128]{3,2,1,0:T(8,128)S(1)}, u32[]{:S(2)}, u32[]{:S(2)}) %all-to-all-start.1) | async-done | bytes 786464 | tf_op jit(solution)/shard_map/all_to_all | solution.py:149
  29.7 5.0 %all-to-all-start = ((f32[16,6,32,128]{3,2,1,0:T(8,128)}), f32[16,6,32,128]{3,2,1,0:T(8,128)}, u32[]{:S(2)}, u32[]{:S(2)}) async-start(f32[16,6,32,128]{3,2,1,0:T(8,128)} %pack.2), calls=%async_computation | async-start | bytes 3145728 | tf_op jit(solution)/shard_map/all_to_all | solution.py:149
  34.6 0.1 reshape.1522
  34.7 0.1 copy.93
  34.8 0.1 add.351
  34.9 0.1 add.352
  35.1 0.1 iota_select_fusion.1
  35.1 0.1 add_add_fusion
  35.2 0.7 or_and_fusion
  36.0 0.2 dynamic-slice_reduce_fusion
  36.1 0.1 fusion.2
  36.3 0.8 order.1
  37.1 0.8 faces.1
  37.9 1.5 collective-permute-start
  39.4 0.1 select_reduce_fusion
  39.5 32.5 %collective-permute-done.below_ref = f32[512,128]{1,0:T(8,128)S(1)} collective-permute-done((f32[512,128]{1,0:T(8,128)S(1)}, f32[512,128]{1,0:T(8,128)S(1)}, u32[]{:S(2)}, u32[]{:S(2)}) %collective-permute-start) | collective-permute-done | bytes 262176 | tf_op jit(solution)/shard_map/ppermute | solution.py:540
  72.0 1.6 collective-permute-done.1.above_ref
  73.6 6.7 %velocity.1.flow_ref = f32[15,512,128]{2,1,0:T(8,128)S(1)} custom-call(f32[16,3,32,128]{3,2,1,0:T(8,128)S(1)} %all-to-all-done.1.vel_ref, f32[512,128]{1,0:T(8,128)S(1)} %collective-permute-done.below_ref, f32[512,128]{1,0:T(8,128)S(1)} %collective-permute-done.1.above_ref, bf16[1024,512]{1,0:T(8,128)(2,1)S(1)} %copy-done.6, ...), custom_call_target="tpu_custom_call" | custom-call | flops 12000000000 | bytes 8388608 | tf_op jit(solution)/shard_map/velocity/pallas_call | solution.py:543
  80.2 1.9 %copy-done.11 = f32[15,512,128]{2,1,0:T(8,128)} copy-done((f32[15,512,128]{2,1,0:T(8,128)}, f32[15,512,128]{2,1,0:T(8,128)S(1)}, u32[]{:S(2)}) %copy-start.11) | copy-done | bytes 3932184
  82.1 1.2 copy-done.9
  83.3 1.2 copy-done.10
  84.6 16.5 %stress.1 = f32[16,9,32,128]{3,2,1,0:T(8,128)} custom-call(f32[16,6,32,128]{3,2,1,0:T(8,128)} %all-to-all-done.psi_ref, f32[15,512,128]{2,1,0:T(8,128)} %copy-done.11, bf16[1024,512]{1,0:T(8,128)(2,1)S(1)} %copy-done.7, bf16[1024,512]{1,0:T(8,128)(2,1)S(1)} %copy-done.9, bf16[512,1024]{1,0:T(8,128)(2,1)S(1)} %copy-done.10, ...), custom_call_target="tpu_custom_call" | custom-call | flops 12000000000 | bytes 12582912 | tf_op jit(solution)/shard_map/stress/pallas_call | solution.py:554
  101.1 4.6 %all-to-all-start.2 = ((f32[16,9,32,128]{3,2,1,0:T(8,128)}), f32[16,9,32,128]{3,2,1,0:T(8,128)S(1)}, u32[]{:S(2)}, u32[]{:S(2)}) async-start(f32[16,9,32,128]{3,2,1,0:T(8,128)} %stress.1), calls=%async_computation.2 | async-start | bytes 4718592 | tf_op jit(solution)/shard_map/all_to_all | solution.py:149
  105.7 0.7 or_select_fusion
  106.4 1.5 copy.104
  107.9 0.7 copy.103
  108.6 0.1 fusion.18
  108.7 0.1 fusion.17
  108.7 0.1 add_bitcast_fusion
  108.9 0.7 bitcast_add_fusion
  109.6 0.7 copy.110
  110.3 0.1 add_select_fusion.1
  110.4 0.8 copy.106
  111.2 0.1 copy.105
  111.3 0.8 copy.100
  112.1 0.1 copy.109
  112.2 0.1 copy.107
  113.0 0.1 broadcast_bitcast_fusion
  113.0 0.8 or_and_fusion.1
  113.8 0.6 add.371
  114.5 6.8 %multiply_convert_fusion.mean_ref = bf16[16,384,128]{2,1,0:T(8,128)(2,1)} fusion(f32[16,128]{1,0:T(8,128)} %copy.104, s32[16,128]{1,0:T(8,128)} %copy.103, s32[16,384]{1,0:T(8,128)S(1)} %get-tuple-element.28, s32[16,128]{1,0:T(8,128)S(1)} %copy.102, s32[16,384]{1,0:T(8,128)S(1)} %get-tuple-element.13, s32[16,128]{1,0:T(8,128)S(1)} %copy.101, ...), kind=kLoop, calls=%fused_computation | loop fusion | flops 11796480 | bytes 1704704 | tf_op jit(solution)/shard_map/convert_element_type | solution.py:491
  121.2 37.5 %all-to-all-done.2.rates_ref = f32[16,9,32,128]{3,2,1,0:T(8,128)S(1)} async-done(((f32[16,9,32,128]{3,2,1,0:T(8,128)}), f32[16,9,32,128]{3,2,1,0:T(8,128)S(1)}, u32[]{:S(2)}, u32[]{:S(2)}) %all-to-all-start.2) | async-done | bytes 2359328 | tf_op jit(solution)/shard_map/all_to_all | solution.py:149
  158.7 1.4 copy-done
  160.2 1.4 copy-done.1
  161.6 3.6 %advance.1 = (f32[3,32,2048]{2,1,0:T(8,128)}, f32[6,32,2048]{2,1,0:T(8,128)}) custom-call(f32[16,9,32,128]{3,2,1,0:T(8,128)S(1)} %all-to-all-done.2.rates_ref, bf16[16,384,128]{2,1,0:T(8,128)(2,1)S(1)} %copy-done.1, s32[16,1,128]{2,1,0:T(1,128)S(1)} %bitcast.35, f32[3,32,2048]{2,1,0:T(8,128)S(1)} %copy-done.2, f32[6,32,2048]{2,1,0:T(8,128)S(1)} %copy-done, ...), custom_call_target="tpu_custom_call" | custom-call | tf_op jit(solution)/shard_map/advance/pallas_call | solution.py:431
  (39 shorter events, 0.3 us)
Async XLA Ops:
  3.9 25.8 %all-to-all-start.1 = ((f32[16,3,32,128]{3,2,1,0:T(8,128)}), f32[16,3,32,128]{3,2,1,0:T(8,128)S(1)}, u32[]{:S(2)}, u32[]{:S(2)}) async-start(f32[16,3,32,128]{3,2,1,0:T(8,128)} %pack.3), calls=%async_computation.1 | async-start | bytes 1572864 | tf_op jit(solution)/shard_map/all_to_all | solution.py:149
  10.4 24.2 %copy-start.13 = (s32[32]{0:T(128)S(1)}, s32[32]{0:T(128)}, u32[]{:S(2)}) copy-start(s32[32]{0:T(128)} %param.14) | copy-start | bytes 388
  10.5 25.8 %copy-start.3 = (bf16[18,256,128]{2,1,0:T(8,128)(2,1)S(1)}, bf16[18,256,128]{2,1,0:T(8,128)(2,1)}, u32[]{:S(2)}) copy-start(bf16[18,256,128]{2,1,0:T(8,128)(2,1)} %constant.179.clone.halos_ref) | copy-start | bytes 3538948
  10.5 25.8 %copy-start.4 = (bf16[6,128,256]{2,1,0:T(8,128)(2,1)S(1)}, bf16[6,128,256]{2,1,0:T(8,128)(2,1)}, u32[]{:S(2)}) copy-start(bf16[6,128,256]{2,1,0:T(8,128)(2,1)} %constant.178.clone.faces_ref) | copy-start | bytes 1179652
  10.5 25.8 %copy-start.5 = (bf16[10,128,128]{2,1,0:T(8,128)(2,1)S(1)}, bf16[10,128,128]{2,1,0:T(8,128)(2,1)}, u32[]{:S(2)}) copy-start(bf16[10,128,128]{2,1,0:T(8,128)(2,1)} %constant.177.clone.both_ref) | copy-start | bytes 983044
  14.2 25.2 %copy-start.14 = (f32[128]{0:T(128)S(1)}, f32[128]{0:T(128)}, u32[]{:S(2)}) copy-start(f32[128]{0:T(128)} %constant.176.clone) | copy-start | bytes 1540
  29.7 52.4 %all-to-all-start = ((f32[16,6,32,128]{3,2,1,0:T(8,128)}), f32[16,6,32,128]{3,2,1,0:T(8,128)}, u32[]{:S(2)}, u32[]{:S(2)}) async-start(f32[16,6,32,128]{3,2,1,0:T(8,128)} %pack.2), calls=%async_computation | async-start | bytes 3145728 | tf_op jit(solution)/shard_map/all_to_all | solution.py:149
  35.0 45.2 %copy-start.12 = (s32[128]{0:T(128)}, s32[128]{0:T(128)S(1)}, u32[]{:S(2)}) copy-start(s32[128]{0:T(128)S(1)} %add.352) | copy-start | bytes 1540
  35.0 38.5 %copy-start.6 = (bf16[1024,512]{1,0:T(8,128)(2,1)S(1)}, bf16[1024,512]{1,0:T(8,128)(2,1)}, u32[]{:S(2)}) copy-start(bf16[1024,512]{1,0:T(8,128)(2,1)} %constant.172.clone.high_ref) | copy-start | bytes 3145732
  35.0 38.5 %copy-start.8 = (bf16[1024,512]{1,0:T(8,128)(2,1)S(1)}, bf16[1024,512]{1,0:T(8,128)(2,1)}, u32[]{:S(2)}) copy-start(bf16[1024,512]{1,0:T(8,128)(2,1)} %constant.173.clone.low_ref) | copy-start | bytes 3145732
  37.9 34.1 %collective-permute-start = (f32[512,128]{1,0:T(8,128)S(1)}, f32[512,128]{1,0:T(8,128)S(1)}, u32[]{:S(2)}, u32[]{:S(2)}) collective-permute-start(f32[512,128]{1,0:T(8,128)S(1)} %get-tuple-element.8), channel_id=1, source_target_pairs={{0,1},{1,2},{2,3},{3,4},{4,5},{5,6},{6,7},{7,8},{8,9},{9,10},{10,1... | collective-permute-start | bytes 786440 | tf_op jit(solution)/shard_map/ppermute | solution.py:540
  39.4 34.2 %collective-permute-start.1 = (f32[512,128]{1,0:T(8,128)S(1)}, f32[512,128]{1,0:T(8,128)S(1)}, u32[]{:S(2)}, u32[]{:S(2)}) collective-permute-start(f32[512,128]{1,0:T(8,128)S(1)} %get-tuple-element.9), channel_id=1, source_target_pairs={{1,0},{2,1},{3,2},{4,3},{5,4},{6,5},{7,6},{8,7},{9,8},{10,9},{11,1... | collective-permute-start | bytes 786440 | tf_op jit(solution)/shard_map/ppermute | solution.py:541
  73.5 8.6 %copy-start.7 = (bf16[1024,512]{1,0:T(8,128)(2,1)S(1)}, bf16[1024,512]{1,0:T(8,128)(2,1)}, u32[]{:S(2)}) copy-start(bf16[1024,512]{1,0:T(8,128)(2,1)} %constant.172.clone.high_ref) | copy-start | bytes 3145732
  80.2 1.9 %copy-start.11 = (f32[15,512,128]{2,1,0:T(8,128)}, f32[15,512,128]{2,1,0:T(8,128)S(1)}, u32[]{:S(2)}) copy-start(f32[15,512,128]{2,1,0:T(8,128)S(1)} %velocity.1.flow_ref) | copy-start | bytes 11796484
  82.1 1.2 copy-start.9
  83.3 1.2 copy-start.10
  101.1 57.6 %all-to-all-start.2 = ((f32[16,9,32,128]{3,2,1,0:T(8,128)}), f32[16,9,32,128]{3,2,1,0:T(8,128)S(1)}, u32[]{:S(2)}, u32[]{:S(2)}) async-start(f32[16,9,32,128]{3,2,1,0:T(8,128)} %stress.1), calls=%async_computation.2 | async-start | bytes 4718592 | tf_op jit(solution)/shard_map/all_to_all | solution.py:149
  105.7 53.0 %copy-start.2 = (f32[3,32,2048]{2,1,0:T(8,128)S(1)}, f32[3,32,2048]{2,1,0:T(8,128)}, u32[]{:S(2)}) copy-start(f32[3,32,2048]{2,1,0:T(8,128)} %vel_ref.1) | copy-start | bytes 2359300
  158.7 1.4 copy-start
  160.2 1.4 copy-start.1
where the time goes:
time: 166 us; the launch traced here: 165 us
  waiting for transfers between devices  87.1 us (52%)
  Pallas kernels  35.4 us (21%)
  starting transfers between devices  17.6 us (11%)
  local copies, waits for them, and re-layouts  13.3 us (8%)
  other arithmetic  10.3 us (6%)
    all_to_all x3, waiting for transfers between devices, exchange(): lax.all_to_all(blocks, 'mode', split_axis=0, concat_axis=0, tiled=True)  53 us
    ppermute x1, waiting for transfers between devices, body(): below = lax.ppermute(to_up, 'mode', up)  32.5 us
    pallas_call x1, Pallas kernels, body(): kernel_call(stress_body, jax.ShapeDtypeStruct(psi_nodes.shape[:1] + (9,)...  16.5 us
    all_to_all x3, starting transfers between devices, exchange(): lax.all_to_all(blocks, 'mode', split_axis=0, concat_axis=0, tiled=True)  16.1 us
    unnamed x30, local copies, waits for them, and re-layouts  7.18 us
    pallas_call x2, Pallas kernels, pack(): pl.pallas_call(pack_body, grid=(layers // step,), in_specs=[pl.BlockSpec(...  6.96 us
    convert_element_type x1, other arithmetic, mean_weights(): return (radial * axial).astype(BF16).reshape(-1, 3 * BLOCK, BLOCK)  6.78 us
    pallas_call x1, Pallas kernels, body(): kernel_call(velocity_body, jax.ShapeDtypeStruct((15, planes, BLOCK), F32)...  6.66 us
  transfers between devices with their start and end apart: 5, of which 4 were waited for; matrix products, arithmetic and copies ran while one was open for 10% of the time, Pallas kernels for 7%

commit v1 on v0

v1 whole, which is shorter than its diff:
```python
import functools

import jax
import jax.numpy as jnp
import ml_dtypes
import numpy as np
from jax import lax
from jax.experimental import pallas as pl
from jax.experimental.pallas import tpu as pltpu
from jax.sharding import PartitionSpec as P

SIDE = 8
CYCLES = 2
RADIAL = SIDE * CYCLES
BLOCK = SIDE * RADIAL
STEP_DT = 0.002
RELAX_TIME = 0.02
MOBILITY = 0.3
LAYER_HEIGHT = 0.25
R_INNER = 1.0
MIB = 1 << 20
F32 = jnp.float32
BF16 = jnp.bfloat16


def split_table(table):
    high = np.asarray(table, np.float32).astype(ml_dtypes.bfloat16)
    low = (np.asarray(table, np.float64) - high.astype(np.float64)).astype(ml_dtypes.bfloat16)
    return high, low


def cheb_table(points):
    nodes_xi = -np.cos(np.pi * np.arange(points) / (points - 1))
    weights = np.ones(points)
    weights[0] = 2.0
    weights[-1] = 2.0
    weights = weights * (-1.0) ** np.arange(points)
    identity = np.eye(points)
    spacing = nodes_xi[:, None] - nodes_xi[None, :] + identity
    matrix = weights[:, None] / weights[None, :] / spacing
    matrix = matrix * (1.0 - identity)
    matrix = matrix - identity * matrix.sum(axis=1)[:, None]
    return nodes_xi, matrix


def fourier_tables(planes):
    phase = np.arange(planes)[:, None] * np.arange(planes // 2)[None, :] % planes
    angles = phase * (2.0 * np.pi / planes)
    cosine = np.cos(angles) * np.sqrt(2.0 / planes)
    sine = np.sin(angles) * np.sqrt(2.0 / planes)
    cosine[:, 0] = planes**-0.5
    sine[:, 0] = (-1.0) ** np.arange(planes) * planes**-0.5
    wavenums = np.arange(planes // 2)
    basis = np.stack([cosine, sine], axis=2).reshape(planes, planes)
    turned = np.stack([-wavenums * sine, wavenums * cosine], axis=2).reshape(planes, planes)
    return np.concatenate([basis, turned], axis=0)


def node_tables():
    nodes_xi, matrix = cheb_table(SIDE)
    radius = R_INNER + (np.arange(CYCLES)[:, None] + (nodes_xi[None, :] + 1.0) / 2.0) / CYCLES
    inv_r = 1.0 / radius.reshape(-1)
    radial_row = np.kron(np.eye(CYCLES), matrix.T * (2.0 * CYCLES))
    radial_mean = np.eye(RADIAL)
    for cycle in range(1, CYCLES):
        low, high = cycle * SIDE - 1, cycle * SIDE
        radial_mean[low : high + 1, low : high + 1] = 0.5
    d_radial = np.kron(np.eye(SIDE), radial_row)
    d_axial = np.kron(matrix.T * (2.0 / LAYER_HEIGHT), np.eye(RADIAL))
    own_weight = np.ones(SIDE)
    own_weight[[0, -1]] = 0.5
    average = np.kron(np.diag(own_weight), radial_mean)
    inv_r_nodes = np.tile(inv_r, SIDE)
    both = np.stack(
        [d_radial, d_axial, d_radial @ average, d_axial @ average, average * inv_r_nodes[None, :]]
    )
    below = np.zeros((SIDE, SIDE))
    below[SIDE - 1, 0] = 0.5
    means = np.stack([np.kron(below, radial_mean), average, np.kron(below.T, radial_mean)])
    faces = np.zeros((3, BLOCK, 2 * BLOCK))
    halos = np.zeros((9, 2 * BLOCK, BLOCK))
    for field in range(3):
        for side, row in ((0, SIDE - 1), (1, 0)):
            at_u = side * BLOCK + field * RADIAL
            at_dz = at_u + 3 * RADIAL
            face_nodes = slice(row * RADIAL, (row + 1) * RADIAL)
            faces[field, face_nodes, at_u : at_u + RADIAL] = np.eye(RADIAL)
            faces[field, :, at_dz : at_dz + RADIAL] = d_axial[:, face_nodes]
            here = SIDE - 1 - row
            out = slice(here * RADIAL, (here + 1) * RADIAL)
            halos[field, at_u : at_u + RADIAL, out] = 0.5 * radial_row @ radial_mean
            halos[3 + field, at_dz : at_dz + RADIAL, out] = 0.5 * radial_mean
            halos[6 + field, at_u : at_u + RADIAL, out] = 0.5 * radial_mean * inv_r[None, :]
    return both, faces, halos, means, inv_r_nodes


def split(values):
    high = values.astype(BF16)
    return high, (values - high.astype(F32)).astype(BF16)


def dot(left, right):
    return jnp.dot(left, right, preferred_element_type=F32)


def dot3(left, right):
    return dot(left[0], right[0]) + (dot(left[0], right[1]) + dot(left[1], right[0]))


def whole_spec():
    return pl.BlockSpec(memory_space=pltpu.VMEM)


def kernel_call(
    body, outs, count, scalars=1, scratch=(), vmem=40, name=None
):
    return pl.pallas_call(
        body,
        out_shape=outs,
        in_specs=[pl.BlockSpec(memory_space=pltpu.SMEM)] * scalars + [whole_spec()] * count,
        out_specs=jax.tree.map(lambda _: whole_spec(), outs),
        scratch_shapes=list(scratch),
        compiler_params=pltpu.CompilerParams(vmem_limit_bytes=vmem * MIB),
        name=name,
    )


def lanes_of(at):
    return slice(at * BLOCK, (at + 1) * BLOCK)


def put(high, low, rows, lanes, value):
    value_h, value_l = split(value)
    high[rows, lanes] = value_h
    low[rows, lanes] = value_l


NEAR = 4


def swap(block, bits):
    devices = lax.axis_size("mode")
    return lax.ppermute(block, "mode", [(i, i ^ bits) for i in range(devices)])


def far_swaps(groups):
    return [groups[0]] + [swap(groups[s], NEAR * s) for s in (1, 2, 3)]


def near_swaps(groups):
    return [groups[0]] + [swap(groups[t], t) for t in (1, 2, 3)]


def regroup(groups):
    return [jnp.stack([group[at] for group in groups]) for at in range(NEAR)]


class Route:
    def __init__(self, devices, local_modes, far_first):
        self.staged = devices == NEAR * NEAR and local_modes % 16 == 0
        self.aligned = self.staged or local_modes % 16 == 0
        self.devices, self.local_modes, self.far_first = devices, local_modes, far_first
        self.modes = local_modes if self.aligned else local_modes * devices
        if not self.staged:
            self.pack = self.land = [(0, at, at) for at in range(devices)]
            self.leave = self.arrive = self.pack if self.aligned else [(0, 0, 0)]
            return
        far = [(s, t, NEAR * s + t) for s in range(NEAR) for t in range(NEAR)]
        near = [(t, s, NEAR * s + t) for s in range(NEAR) for t in range(NEAR)]
        self.pack = self.leave = far if far_first else near
        self.land = self.arrive = near if far_first else far

    def outs(self, blocks, *block):
        arrays, places = (1 + max(entry[at] for entry in blocks) for at in range(2))
        return [jax.ShapeDtypeStruct((places,) + block, F32)] * arrays

    def index(self, me_ref, rel):
        return (me_ref[0] ^ rel) if self.staged else rel

    def rows(self, me_ref, rel):
        start = self.index(me_ref, rel) * self.modes
        return pl.ds(pl.multiple_of(start, self.modes), self.modes)

    def load(self, me_ref, refs, high, low):
        for array, place, rel in self.arrive:
            rows = self.rows(me_ref, rel)
            for field in range(refs[array].shape[1]):
                put(high, low, rows, lanes_of(field), refs[array][place, field])

    def store(self, me_ref, refs, field, coeffs):
        for array, place, rel in self.leave:
            refs[array][place, field] = coeffs[self.rows(me_ref, rel), :]

    def packed(self, arrays):
        if self.aligned:
            return arrays
        _, fields, planes, nodes = arrays[0].shape
        blocks = arrays[0].reshape(fields, planes // self.local_modes, self.local_modes, nodes)
        return [blocks.transpose(1, 0, 2, 3)]

    def unpacked(self, arrays):
        if self.aligned:
            return arrays
        devices, fields, modes, nodes = arrays[0].shape
        return [arrays[0].transpose(1, 0, 2, 3).reshape(1, fields, devices * modes, nodes)]


def in_one(arrays):
    return [lax.all_to_all(arrays[0], "mode", split_axis=0, concat_axis=0, tiled=True)]


def pack(me, values, routes):
    outs, copies = [], []
    for at, (array, route) in enumerate(zip(values, routes)):
        fields, local_modes, _ = array.shape
        copies += [(at, len(outs) + out, place, rel) for out, place, rel in route.pack]
        outs += route.outs(route.pack, fields, local_modes, BLOCK)
    count = len(values)

    def body(me_ref, *refs):
        in_refs, out_refs, sems = refs[:count], refs[count:-1], refs[-1]
        started = []
        for number, (at, out, place, rel) in enumerate(copies):
            layer = routes[at].index(me_ref, rel)
            lanes = pl.ds(pl.multiple_of(layer * BLOCK, BLOCK), BLOCK)
            copy = pltpu.make_async_copy(
                in_refs[at].at[:, :, lanes], out_refs[out].at[place], sems.at[number]
            )
            copy.start()
            started.append(copy)
        for copy in started:
            copy.wait()

    packed = pl.pallas_call(
        body,
        in_specs=[pl.BlockSpec(memory_space=pltpu.SMEM)]
        + [pl.BlockSpec(memory_space=pl.ANY)] * count,
        out_specs=[whole_spec()] * len(outs),
        out_shape=outs,
        scratch_shapes=[pltpu.SemaphoreType.DMA((len(copies),))],
        name="pack",
    )(me, *values)
    first = len(routes[0].outs(routes[0].pack, 1))
    return packed[:first], packed[first:]


def places(orient_ref, layer, shape):
    lane = lax.broadcasted_iota(jnp.int32, shape, 1)
    cycle = lane // (SIDE * SIDE)
    orient = jnp.where(
        cycle == 0, orient_ref[CYCLES * layer], orient_ref[CYCLES * layer + 1]
    )
    lead, trail = lane // SIDE % SIDE, lane % SIDE
    lead = jnp.where(orient % 2 == 1, SIDE - 1 - lead, lead)
    trail = jnp.where(orient // 2 % 2 == 1, SIDE - 1 - trail, trail)
    swapped = orient // 4 % 2 == 1
    row = jnp.where(swapped, trail, lead)
    col = jnp.where(swapped, lead, trail)
    return row * RADIAL + cycle * SIDE + col


def from_grid(orient_ref, layer):
    shape = (BLOCK, BLOCK)
    grid_ids = lax.broadcasted_iota(jnp.int32, shape, 0)
    return (grid_ids == places(orient_ref, layer, shape)).astype(F32)


def order_body(
    me_ref, orient_ref, both_ref, faces_ref, halos_ref, inv_r_ref,
    both_out, faces_out, halos_out, inv_r_out,
):
    onto = from_grid(orient_ref, me_ref[0])
    inv_r_out[...] = jnp.broadcast_to(
        jnp.sum(onto * inv_r_ref[...], axis=0, keepdims=True), inv_r_out.shape
    )
    back = onto.T.astype(BF16)
    onto = onto.astype(BF16)
    for at in range(both_ref.shape[0]):
        moved = dot(both_ref[at], onto).astype(BF16)
        both_out[at] = dot(back, moved).astype(BF16)
    for at in range(faces_ref.shape[0]):
        faces_out[at] = dot(back, faces_ref[at]).astype(BF16)
    for at in range(halos_ref.shape[0]):
        halos_out[at] = dot(halos_ref[at], onto).astype(BF16)


def weights_body(layers, step, orient_ref, means_ref, out_ref):
    first = pl.program_id(0) * step
    for at in range(step):
        index = first + at
        onto = from_grid(orient_ref, index).astype(BF16)
        below = lax.rem(index + (layers - 1), layers)
        above = lax.rem(index + 1, layers)
        for number, layer in enumerate((below, index, above)):
            back = from_grid(orient_ref, layer).T.astype(BF16)
            moved = dot(means_ref[number], onto).astype(BF16)
            rows = slice(number * BLOCK, (number + 1) * BLOCK)
            out_ref[at, rows, :] = dot(back, moved).astype(BF16)


def mean_weights(orientation, means, layers):
    step = 4
    return pl.pallas_call(
        functools.partial(weights_body, layers, step),
        grid=(layers // step,),
        in_specs=[
            pl.BlockSpec(memory_space=pltpu.SMEM),
            pl.BlockSpec(means.shape, lambda i: (0, 0, 0)),
        ],
        out_specs=pl.BlockSpec((step, 3 * BLOCK, BLOCK), lambda i: (i, 0, 0)),
        out_shape=jax.ShapeDtypeStruct((layers, 3 * BLOCK, BLOCK), BF16),
        name="weights",
    )(orientation, means)


def face_body(route, count, me_ref, *refs):
    vel_refs, (faces_ref, up_ref, down_ref, high, low) = refs[:count], refs[count:]
    route.load(me_ref, vel_refs, high, low)
    total = None
    for field in range(3):
        lanes = lanes_of(field)
        own = (high[:, lanes], low[:, lanes])
        part = dot3(own, (faces_ref[2 * field], faces_ref[2 * field + 1]))
        total = part if total is None else total + part
    up_ref[...] = total[:, :BLOCK]
    down_ref[...] = total[:, BLOCK:]


def velocity_body(
    vel_h, vel_l, below_ref, above_ref, high_ref, low_ref, both_ref, halos_ref, inv_r_ref,
    flow_ref, values,
):
    planes = high_ref.shape[1]
    table = (high_ref[...], low_ref[...])
    values[:, 0:256] = dot3(table, (vel_h[:, 0:256], vel_l[:, 0:256]))
    values[:, 256:384] = dot3(table, (vel_h[:, 256:384], vel_l[:, 256:384]))
    values[:, 384:640] = dot3(
        table, split(jnp.concatenate([below_ref[...], above_ref[...]], axis=1))
    )
    rows_step = 128

    def matrix(at):
        return both_ref[2 * at], both_ref[2 * at + 1]

    def halo(at):
        return halos_ref[2 * at], halos_ref[2 * at + 1]

    def chunk(step, carry):
        rows = pl.ds(pl.multiple_of(step * rows_step, rows_step), rows_step)
        turned = pl.ds(pl.multiple_of(planes + step * rows_step, rows_step), rows_step)
        u = [values[rows, lanes_of(f)] for f in range(3)]
        u_s = [split(v) for v in u]
        dth_s = [split(values[turned, lanes_of(f)]) for f in range(3)]
        edge = split(values[rows, 384:640])
        edge_dth = split(values[turned, 384:640])
        g_r = [dot3(u_s[f], matrix(2)) + dot3(edge, halo(f)) for f in range(3)]
        g_z = [dot3(u_s[f], matrix(3)) + dot3(edge, halo(3 + f)) for f in range(3)]
        g_t = [dot3(dth_s[f], matrix(4)) + dot3(edge_dth, halo(6 + f)) for f in range(3)]
        mean_r = dot3(u_s[0], matrix(4)) + dot3(edge, halo(6))
        mean_t = dot3(u_s[1], matrix(4)) + dot3(edge, halo(7))
        g_t[0] = g_t[0] - mean_t
        g_t[1] = g_t[1] + mean_r
        hoop_rate = u[1] * inv_r_ref[0:1, :]
        flow_ref[0, rows, :] = u[0]
        flow_ref[1, rows, :] = hoop_rate
        flow_ref[2, rows, :] = u[2]
        flow_ref[3, rows, :] = 0.5 * (g_t[0] - g_r[1]) + hoop_rate
        flow_ref[4, rows, :] = 0.5 * (g_z[0] - g_r[2])
        flow_ref[5, rows, :] = 0.5 * (g_z[1] - g_t[2])
        rest = (1.0 - 2.0 * MOBILITY) / RELAX_TIME
        flow_ref[6, rows, :] = 2.0 * g_r[0] - rest
        flow_ref[7, rows, :] = g_t[0] + g_r[1]
        flow_ref[8, rows, :] = g_z[0] + g_r[2]
        flow_ref[9, rows, :] = 2.0 * g_t[1] - rest
        flow_ref[10, rows, :] = g_z[1] + g_t[2]
        flow_ref[11, rows, :] = 2.0 * g_z[2] - rest
        for f in range(3):
            flow_ref[12 + f, rows, :] = -(g_r[f] * u[0] + g_t[f] * u[1] + g_z[f] * u[2])
        return carry

    lax.fori_loop(0, planes // rows_step, chunk, 0)


def square(m):
    a, b, c, d, e, f = m
    bb, cc, ee = b * b, c * c, e * e
    return (
        a * a + (bb + cc),
        b * (a + d) + c * e,
        c * (a + f) + b * e,
        d * d + (bb + ee),
        e * (d + f) + b * c,
        f * f + (cc + ee),
    )


def commuting_product(m, n):
    a, b, c, d, e, f = m
    p, q, r, s, t, u = n
    return (
        a * p + b * q + c * r,
        a * q + b * s + c * t,
        a * r + b * t + c * u,
        b * q + d * s + e * t,
        b * r + d * t + e * u,
        c * r + e * t + f * u,
    )


DIAGONAL = (0, 3, 5)


def plus_identity(m):
    return tuple(v + 1.0 if at in DIAGONAL else v for at, v in enumerate(m))


def exponential(psi, sign):
    x = tuple(v * (sign * 0.125) for v in psi)
    x2 = square(x)
    x4 = square(x2)
    even = plus_identity(tuple(v * 0.5 + w * (1.0 / 24.0) for v, w in zip(x2, x4)))
    odd = commuting_product(x, plus_identity(tuple(v * (1.0 / 6.0) for v in x2)))
    total = tuple(v + w for v, w in zip(even, odd))
    for _ in range(3):
        total = square(total)
    return total


def row_chunks(planes, rows_step, body):
    def chunk(step, carry):
        body(pl.multiple_of(step * rows_step, rows_step))
        return carry

    lax.fori_loop(0, planes // rows_step, chunk, 0)


def momentum_body(route, count, out_route, out_count, me_ref, *refs):
    psi_refs, refs = refs[:count], refs[count:]
    flow_ref, high_ref, low_ref, back_high_ref, back_low_ref, both_ref, inv_r_ref = refs[:7]
    out_refs, refs = refs[7 : 7 + out_count], refs[7 + out_count :]
    coef_h, coef_l, psi_out, conform_out, stress_h, stress_l, vel_h, vel_l, mom_s, coeffs = refs
    planes = high_ref.shape[1]
    route.load(me_ref, psi_refs, coef_h, coef_l)
    table = (high_ref[:planes, :], low_ref[:planes, :])
    for pair in range(3):
        lanes = slice(2 * pair * BLOCK, (2 * pair + 2) * BLOCK)
        values = dot3(table, (coef_h[:, lanes], coef_l[:, lanes]))
        for at in range(2):
            psi_out[2 * pair + at] = values[:, lanes_of(at)]
    rows_step = 16

    def chunk(start):
        rows = pl.ds(start, rows_step)
        inv_r = inv_r_ref[0:1, :]
        conform = exponential(tuple(psi_out[member, rows, :] for member in range(6)), 1.0)
        for member in range(6):
            conform_out[member, rows, :] = conform[member]
        stress = tuple(v - 1.0 if at in DIAGONAL else v for at, v in enumerate(conform))
        for lane, member in enumerate((0, 2, 1, 4, 2, 5)):
            put(stress_h, stress_l, rows, lanes_of(lane), stress[member])
        hoop = tuple(stress[at] * inv_r for at in (1, 3, 4))
        turned = pl.ds(pl.multiple_of(planes + start, rows_step), rows_step)
        for at in range(3):
            put(vel_h, vel_l, turned, lanes_of(at), -hoop[at])
        mom_s[0, rows, :] = flow_ref[12, rows, :] + (stress[0] * inv_r - hoop[1])
        mom_s[1, rows, :] = flow_ref[13, rows, :] + 2.0 * hoop[0]
        mom_s[2, rows, :] = flow_ref[14, rows, :] + stress[2] * inv_r

    row_chunks(planes, rows_step, chunk)
    divergence = tuple(
        jnp.concatenate([both_ref[at], both_ref[2 + at]], axis=0) for at in range(2)
    )
    for at in range(3):
        lanes = slice(2 * at * BLOCK, (2 * at + 2) * BLOCK)
        force = dot3((stress_h[:, lanes], stress_l[:, lanes]), divergence)
        put(vel_h, vel_l, slice(0, planes), lanes_of(at), mom_s[at] + force)
    back = (back_high_ref[...], back_low_ref[...])
    for start, stop in ((0, 2), (2, 3)):
        lanes = slice(start * BLOCK, stop * BLOCK)
        coeffs[:, lanes] = dot3(back, (vel_h[:, lanes], vel_l[:, lanes]))
    for field in range(3):
        out_route.store(me_ref, out_refs, field, coeffs.at[:, lanes_of(field)])


def elastic_body(first_route, first_count, second_route, second_count, me_ref, *refs):
    (
        coef_h, coef_l, psi_ref, conform_ref, flow_ref, high_ref, low_ref,
        back_high_ref, back_low_ref, both_ref,
    ) = refs[:10]
    first_refs, refs = refs[10 : 10 + first_count], refs[10 + first_count :]
    second_refs, refs = refs[:second_count], refs[second_count:]
    dth_s, grad_s, rate_h, rate_l, coeffs = refs
    planes = high_ref.shape[1]
    table = (high_ref[planes:, :], low_ref[planes:, :])
    for pair in range(3):
        lanes = slice(2 * pair * BLOCK, (2 * pair + 2) * BLOCK)
        values = dot3(table, (coef_h[:, lanes], coef_l[:, lanes]))
        for at in range(2):
            dth_s[2 * pair + at] = values[:, lanes_of(at)]
    gradient = tuple(
        jnp.concatenate([both_ref[at], both_ref[2 + at]], axis=1) for at in range(2)
    )
    for member in range(6):
        grad_s[member] = dot3(split(psi_ref[member]), gradient)
    rows_step = 16
    inv_relax = 1.0 / RELAX_TIME

    def chunk(start):
        rows = pl.ds(start, rows_step)
        psi = tuple(psi_ref[member, rows, :] for member in range(6))
        inverse = exponential(psi, -1.0)
        u_r, hoop_rate, u_z, p, q, s = (flow_ref[at, rows, :] for at in range(6))
        a, b, c, d, e, f = psi
        pb, qc, se = p * b, q * c, s * e
        turning = (
            2.0 * (pb + qc),
            p * (d - a) + (q * e + s * c),
            q * (f - a) + (p * e - s * b),
            2.0 * (se - pb),
            s * (f - d) - (p * c + q * b),
            -2.0 * (qc + se),
        )
        for member in range(6):
            advect = (
                u_r * grad_s[member, rows, 0:BLOCK]
                + hoop_rate * dth_s[member, rows, :]
                + u_z * grad_s[member, rows, BLOCK : 2 * BLOCK]
            )
            relaxing = ((1.0 - MOBILITY) * inv_relax) * inverse[member] - (
                MOBILITY * inv_relax
            ) * conform_ref[member, rows, :]
            rate = (turning[member] - advect) + (flow_ref[6 + member, rows, :] + relaxing)
            put(rate_h, rate_l, rows, lanes_of(member), rate)

    row_chunks(planes, rows_step, chunk)
    back = (back_high_ref[:, :planes], back_low_ref[:, :planes])
    for pair in range(3):
        lanes = slice(2 * pair * BLOCK, (2 * pair + 2) * BLOCK)
        coeffs[:, lanes] = dot3(back, (rate_h[:, lanes], rate_l[:, lanes]))
    for field in range(3):
        first_route.store(me_ref, first_refs, field, coeffs.at[:, lanes_of(field)])
        second_route.store(me_ref, second_refs, field, coeffs.at[:, lanes_of(3 + field)])


def advance_body(layers, step, route, count, start, is_velocity, aliased, *refs):
    me_ref, orient_ref, wall_ref = refs[:3]
    rate_refs, refs = refs[3 : 3 + count], refs[3 + count :]
    mean_ref, old_ref = refs[:2]
    out_ref, rates = refs[2 + aliased :]
    fields, local_modes = old_ref.shape[0], old_ref.shape[1]

    @pl.when(pl.program_id(0) == 0)
    def _():
        for array, place, rel in route.land:
            rates[route.index(me_ref, rel)] = rate_refs[array][place, start : start + fields]

    first = pl.program_id(0) * step
    merged = local_modes % 8 == 0

    def averaged(index, at, field):
        below = lax.rem(index + (layers - 1), layers)
        above = lax.rem(index + 1, layers)
        total = None
        for number, layer in enumerate((below, index, above)):
            block = rates[layer] if field is None else rates[layer, field]
            high, low = split(block.reshape(-1, BLOCK))
            weights = mean_ref[at, number * BLOCK : (number + 1) * BLOCK, :]
            part = dot(high, weights) + dot(low, weights)
            total = part if total is None else total + part
        return total

    for at in range(step):
        index = first + at
        lanes = lanes_of(at)
        if merged:
            every = averaged(index, at, None)
            change = [every[f * local_modes : (f + 1) * local_modes] for f in range(fields)]
        else:
            change = [averaged(index, at, f) for f in range(fields)]
        shape = (local_modes, BLOCK)
        column = places(orient_ref, index, shape) % RADIAL
        inner = column == 0
        on_wall = jnp.logical_or(inner, column == RADIAL - 1)
        mean_row = jnp.logical_and(lax.broadcasted_iota(jnp.int32, shape, 0) == 0, inner)
        driven = jnp.where(mean_row, wall_ref[0], 0.0)
        for field in range(fields):
            stepped = old_ref[field, :, lanes] + STEP_DT * change[field]
            if is_velocity:
                stepped = jnp.where(on_wall, driven if field == 1 else 0.0, stepped)
            out_ref[field, :, lanes] = stepped


def whole_block(array):
    return pl.BlockSpec(array.shape, lambda i: (0,) * array.ndim)


def advance(rates, start, route, weights, old, half, into, me, orientation, wall):
    _, local_modes, nodes = old.shape
    layers = nodes // BLOCK
    step = 4
    fields = 3
    aliased = 0 if into is None else 1
    block = pl.BlockSpec((fields, local_modes, step * BLOCK), lambda i: (half, 0, i))
    scalar = pl.BlockSpec(memory_space=pltpu.SMEM)
    is_velocity = old.shape[0] == fields
    operands = [me, orientation, wall, *rates, weights, old] + ([into] if aliased else [])
    return pl.pallas_call(
        functools.partial(
            advance_body, layers, step, route, len(rates), start, is_velocity, aliased
        ),
        grid=(layers // step,),
        in_specs=[scalar] * 3
        + [whole_block(part) for part in rates]
        + [pl.BlockSpec((step, 3 * BLOCK, BLOCK), lambda i: (i, 0, 0)), block]
        + [pl.BlockSpec(memory_space=pl.ANY)] * aliased,
        out_specs=block,
        out_shape=jax.ShapeDtypeStruct(old.shape, F32),
        scratch_shapes=[pltpu.VMEM((layers, fields, local_modes, BLOCK), F32)],
        input_output_aliases={len(operands) - 1: 0} if aliased else {},
        compiler_params=pltpu.CompilerParams(vmem_limit_bytes=24 * MIB),
        name="advance",
    )(*operands)


def body(velocity, log_conf, orientation, wall_speed):
    devices = lax.axis_size("mode")
    device = lax.axis_index("mode").astype(jnp.int32)
    me = device.reshape(1)
    local_modes = velocity.shape[1]
    layers = velocity.shape[2] // BLOCK
    planes = local_modes * devices
    far_first = Route(devices, local_modes, True)
    near_first = Route(devices, local_modes, False)
    barrier = lax.optimization_barrier
    staged = far_first.staged
    both, faces, halos, means, inv_r_nodes = node_tables()

    def parts(tables):
        return jnp.asarray(np.stack([half for table in tables for half in split_table(table)]))

    fourier = fourier_tables(planes)
    high, low = (jnp.asarray(half) for half in split_table(fourier))
    back_high, back_low = (jnp.asarray(half) for half in split_table(fourier.T))
    inv_r_table = jnp.asarray(np.tile(inv_r_nodes[:, None], (1, BLOCK)), F32)

    both_s, faces_s, halos_s, inv_r = kernel_call(
        order_body,
        (
            jax.ShapeDtypeStruct((10, BLOCK, BLOCK), BF16),
            jax.ShapeDtypeStruct((6, BLOCK, 2 * BLOCK), BF16),
            jax.ShapeDtypeStruct((18, 2 * BLOCK, BLOCK), BF16),
            jax.ShapeDtypeStruct((8, BLOCK), F32),
        ),
        4,
        scalars=2,
        vmem=16,
        name="order",
    )(me, orientation, parts(both), parts(faces), parts(halos), inv_r_table)
    weights = mean_weights(orientation, jnp.asarray(means, BF16), layers)

    vel_nodes, psi_nodes = pack(me, (velocity, log_conf), (far_first, near_first))
    if staged:
        vel_nodes, psi_nodes, (both_s, faces_s, halos_s, inv_r) = barrier(
            (far_swaps(vel_nodes), near_swaps(psi_nodes), (both_s, faces_s, halos_s, inv_r))
        )
        psi_nodes = far_swaps(regroup(psi_nodes))
        vel_nodes = near_swaps(regroup(vel_nodes))
    else:
        vel_nodes = far_first.unpacked(in_one(vel_nodes))
        psi_nodes = near_first.unpacked(in_one(psi_nodes))

    edge = jax.ShapeDtypeStruct((planes, BLOCK), F32)
    vel_half = jax.ShapeDtypeStruct((planes, 3 * BLOCK), BF16)
    to_up, to_down, vel_h, vel_l = kernel_call(
        functools.partial(face_body, far_first, len(vel_nodes)),
        (edge, edge, vel_half, vel_half),
        len(vel_nodes) + 1,
        vmem=16,
        name="faces",
    )(me, *vel_nodes, faces_s)
    up = [(i, (i + 1) % devices) for i in range(devices)]
    below = lax.ppermute(to_up, "mode", up)
    above = lax.ppermute(to_down, "mode", [(j, i) for i, j in up])

    flow = kernel_call(
        velocity_body,
        jax.ShapeDtypeStruct((15, planes, BLOCK), F32),
        9,
        scalars=0,
        scratch=[pltpu.VMEM((2 * planes, 5 * BLOCK), F32)],
        vmem=20,
        name="velocity",
    )(vel_h, vel_l, below, above, high, low, both_s, halos_s, inv_r)

    def leaves(route):
        return route.outs(route.leave, 3, route.modes, BLOCK)

    far_outs, near_outs = leaves(far_first), leaves(near_first)
    psi_half = jax.ShapeDtypeStruct((planes, 6 * BLOCK), BF16)
    field6 = jax.ShapeDtypeStruct((6, planes, BLOCK), F32)
    *vel_rates, psi_h, psi_l, psi, conform = kernel_call(
        functools.partial(
            momentum_body, near_first, len(psi_nodes), far_first, len(far_outs)
        ),
        (*far_outs, psi_half, psi_half, field6, field6),
        len(psi_nodes) + 7,
        scratch=[
            pltpu.VMEM((planes, 6 * BLOCK), BF16),
            pltpu.VMEM((planes, 6 * BLOCK), BF16),
            pltpu.VMEM((2 * planes, 3 * BLOCK), BF16),
            pltpu.VMEM((2 * planes, 3 * BLOCK), BF16),
            pltpu.VMEM((3, planes, BLOCK), F32),
            pltpu.VMEM((planes, 3 * BLOCK), F32),
        ],
        vmem=24,
        name="momentum",
    )(me, *psi_nodes, flow, high, low, back_high, back_low, both_s, inv_r)
    vel_rates = far_first.packed(vel_rates)
    psi_rates = kernel_call(
        functools.partial(
            elastic_body, far_first, len(far_outs), near_first, len(near_outs)
        ),
        (*far_outs, *near_outs),
        10,
        scratch=[
            pltpu.VMEM((6, planes, BLOCK), F32),
            pltpu.VMEM((6, planes, 2 * BLOCK), F32),
            pltpu.VMEM((planes, 6 * BLOCK), BF16),
            pltpu.VMEM((planes, 6 * BLOCK), BF16),
            pltpu.VMEM((planes, 6 * BLOCK), F32),
        ],
        vmem=24,
        name="elastic",
    )(me, psi_h, psi_l, psi, conform, flow, high, low, back_high, back_low, both_s)

    first_rates = far_first.packed(psi_rates[: len(far_outs)])
    second_rates = near_first.packed(psi_rates[len(far_outs) :])
    if staged:
        vel_rates, first_rates, second_rates = barrier(
            (far_swaps(vel_rates), first_rates, second_rates)
        )
        joined = [
            jnp.concatenate(pair, axis=1) for pair in zip(regroup(vel_rates), second_rates)
        ]
        first_rates, vel_rates, weights = barrier(
            (far_swaps(first_rates), near_swaps(joined), weights)
        )
        second_rates = far_swaps(regroup([group[:, 3:] for group in vel_rates]))
        first_rates = near_swaps(regroup(first_rates))
    else:
        vel_rates, first_rates, second_rates = (
            in_one(rates) for rates in (vel_rates, first_rates, second_rates)
        )
    wall = jnp.where(device == 0, wall_speed, 0.0)
    fixed = (me, orientation, wall)
    vel_next = advance(vel_rates, 0, far_first, weights, velocity, 0, None, *fixed)
    logc_next = advance(first_rates, 0, far_first, weights, log_conf, 0, None, *fixed)
    logc_next = advance(second_rates, 0, near_first, weights, log_conf, 1, logc_next, *fixed)
    return vel_next, logc_next


def solution(mesh):
    in_specs = (P("ens", "mode", None), P("ens", "mode", None), P(), P("ens"))
    out_specs = (P("ens", "mode", None), P("ens", "mode", None))
    return jax.shard_map(body, mesh=mesh, in_specs=in_specs, out_specs=out_specs, check_vma=False)
```

time: 166 us -> 148 us (0.89)
  the two profiles are of different devices: /device:TPU:13 before, /device:TPU:0 now
where the time goes in v1:
time: 148 us
  starting transfers between devices  52.7 us (36%)
  waiting for transfers between devices  49.8 us (34%)
  Pallas kernels  41.1 us (28%)
  local copies, waits for them, and re-layouts  2.17 us (1%)
  between operations  1.8 us (1%)
    ppermute x27, starting transfers between devices, swap(): return lax.ppermute(block, 'mode', [(i, i ^ bits) for i in range(devices)])  48.2 us
    ppermute x27, waiting for transfers between devices, swap(): return lax.ppermute(block, 'mode', [(i, i ^ bits) for i in range(devices)])  30.3 us
    ppermute x1, waiting for transfers between devices, body(): below = lax.ppermute(to_up, 'mode', up)  19.5 us
    pallas_call x3, Pallas kernels, advance(): pl.pallas_call(functools.partial(advance_body, layers, step, route, len(r...  9.37 us
    pallas_call x1, Pallas kernels, body(): kernel_call(functools.partial(elastic_body, far_first, len(far_outs), nea...  7.92 us
    pallas_call x1, Pallas kernels, body(): kernel_call(functools.partial(momentum_body, near_first, len(psi_nodes),...  7.1 us
    pallas_call x1, Pallas kernels, body(): kernel_call(velocity_body, jax.ShapeDtypeStruct((15, planes, BLOCK), F32)...  6.92 us
    ppermute x1, starting transfers between devices, body(): above = lax.ppermute(to_down, 'mode', [(j, i) for i, j in up])  4.43 us
  transfers between devices with their start and end apart: 29, of which 8 were waited for; matrix products, arithmetic and copies ran while one was open for 0% of the time, Pallas kernels for 18%

profile of v1, /device:TPU:0, one launch (start us, length us, event | category | flops | bytes accessed | tf_op | source)
XLA Modules:
  0.0 147.9 jit_solution(7234865447855557122)
XLA Ops:
  0.7 3.5 %pack.1 = (f32[4,3,32,128]{3,2,1,0:T(8,128)}, f32[4,3,32,128]{3,2,1,0:T(8,128)}, f32[4,3,32,128]{3,2,1,0:T(8,128)}, f32[4,3,32,128]{3,2,1,0:T(8,128)}, f32[4,6,3...) custom-call(s32[1]{0:T(128)} %bitcast.me_ref.refs_0_, ...), custom_call_target="tpu_custom_call" | custom-call | tf_op jit(solution)/shard_map/pack/pallas_call | solution.py:234
  4.3 3.1 %collective-permute-start = (f32[4,3,32,128]{3,2,1,0:T(8,128)}, f32[4,3,32,128]{3,2,1,0:T(8,128)S(1)}, u32[]{:S(2)}, u32[]{:S(2)}) collective-permute-start(f32[4,3,32,128]{3,2,1,0:T(8,128)} %get-tuple-element.68), channel_id=1, source_target_pairs={{0,4},{1,5},{2,6},{3,7},{4,0},{5,1},{6,2},{7,3},{8,12},{9,13},{10,... | collective-permute-start | bytes 589832 | tf_op jit(solution)/shard_map/ppermute | solution.py:143
  7.3 1.5 %collective-permute-start.4 = (f32[4,6,32,128]{3,2,1,0:T(8,128)}, f32[4,6,32,128]{3,2,1,0:T(8,128)S(1)}, u32[]{:S(2)}, u32[]{:S(2)}) collective-permute-start(f32[4,6,32,128]{3,2,1,0:T(8,128)} %get-tuple-element.73), channel_id=1, source_target_pairs={{0,2},{1,3},{2,0},{3,1},{4,6},{5,7},{6,4},{7,5},{8,10},{9,11},{10,... | collective-permute-start | bytes 1179656 | tf_op jit(solution)/shard_map/ppermute | solution.py:143
  8.9 0.3 collective-permute-start.5
  9.2 2.6 %collective-permute-start.1 = (f32[4,3,32,128]{3,2,1,0:T(8,128)}, f32[4,3,32,128]{3,2,1,0:T(8,128)S(1)}, u32[]{:S(2)}, u32[]{:S(2)}) collective-permute-start(f32[4,3,32,128]{3,2,1,0:T(8,128)} %get-tuple-element.69), channel_id=1, source_target_pairs={{0,8},{1,9},{2,10},{3,11},{4,12},{5,13},{6,14},{7,15},{8,0},{9,1},... | collective-permute-start | bytes 589832 | tf_op jit(solution)/shard_map/ppermute | solution.py:143
  11.8 0.7 collective-permute-done
  12.5 4.8 %collective-permute-start.2 = (f32[4,3,32,128]{3,2,1,0:T(8,128)}, f32[4,3,32,128]{3,2,1,0:T(8,128)S(1)}, u32[]{:S(2)}, u32[]{:S(2)}) collective-permute-start(f32[4,3,32,128]{3,2,1,0:T(8,128)} %get-tuple-element.70), channel_id=1, source_target_pairs={{0,12},{1,13},{2,14},{3,15},{4,8},{5,9},{6,10},{7,11},{8,4},{9,5},... | collective-permute-start | bytes 589832 | tf_op jit(solution)/shard_map/ppermute | solution.py:143
  17.3 1.4 order.1
  18.7 7.5 %collective-permute-done.1 = f32[4,3,32,128]{3,2,1,0:T(8,128)S(1)} collective-permute-done((f32[4,3,32,128]{3,2,1,0:T(8,128)}, f32[4,3,32,128]{3,2,1,0:T(8,128)S(1)}, u32[]{:S(2)}, u32[]{:S(2)}) %collective-permute-start.1) | collective-permute-done | bytes 196640 | tf_op jit(solution)/shard_map/ppermute | solution.py:143
  26.3 0.8 collective-permute-done.5
  27.2 1.4 collective-permute-start.11
  28.6 0.6 collective-permute-start.10
  29.2 0.1 collective-permute-start.9
  29.5 2.5 %collective-permute-start.8 = (f32[4,6,32,128]{3,2,1,0:T(8,128)S(1)}, f32[4,6,32,128]{3,2,1,0:T(8,128)S(1)}, u32[]{:S(2)}, u32[]{:S(2)}) collective-permute-start(f32[4,6,32,128]{3,2,1,0:T(8,128)S(1)} %pad_maximum_fusion.3), channel_id=1, source_target_pairs={{0,12},{1,13},{2,14},{3,15},{4,8},{5,9},{6,10},{7,11},{8,4},{9,5},... | collective-permute-start | bytes 1179656 | tf_op jit(solution)/shard_map/ppermute | solution.py:143
  32.0 2.6 %collective-permute-start.7 = (f32[4,6,32,128]{3,2,1,0:T(8,128)S(1)}, f32[4,6,32,128]{3,2,1,0:T(8,128)S(1)}, u32[]{:S(2)}, u32[]{:S(2)}) collective-permute-start(f32[4,6,32,128]{3,2,1,0:T(8,128)S(1)} %pad_maximum_fusion.2), channel_id=1, source_target_pairs={{0,8},{1,9},{2,10},{3,11},{4,12},{5,13},{6,14},{7,15},{8,0},{9,1},... | collective-permute-start | bytes 1179656 | tf_op jit(solution)/shard_map/ppermute | solution.py:143
  34.6 3.3 %collective-permute-start.6 = (f32[4,6,32,128]{3,2,1,0:T(8,128)S(1)}, f32[4,6,32,128]{3,2,1,0:T(8,128)S(1)}, u32[]{:S(2)}, u32[]{:S(2)}) collective-permute-start(f32[4,6,32,128]{3,2,1,0:T(8,128)S(1)} %pad_maximum_fusion.1), channel_id=1, source_target_pairs={{0,4},{1,5},{2,6},{3,7},{4,0},{5,1},{6,2},{7,3},{8,12},{9,13},{10,... | collective-permute-start | bytes 1179656 | tf_op jit(solution)/shard_map/ppermute | solution.py:143
  37.9 0.8 collective-permute-done.10.refs_2_
  38.7 0.9 faces.1
  39.6 0.1 collective-permute-start.12
  39.7 4.4 %collective-permute-start.13 = (f32[512,128]{1,0:T(8,128)S(1)}, f32[512,128]{1,0:T(8,128)S(1)}, u32[]{:S(2)}, u32[]{:S(2)}) collective-permute-start(f32[512,128]{1,0:T(8,128)S(1)} %get-tuple-element.91), channel_id=1, source_target_pairs={{1,0},{2,1},{3,2},{4,3},{5,4},{6,5},{7,6},{8,7},{9,8},{10,9},{11,1... | collective-permute-start | bytes 786440 | tf_op jit(solution)/shard_map/ppermute | solution.py:683
  44.1 19.5 %collective-permute-done.12.below_ref = f32[512,128]{1,0:T(8,128)S(1)} collective-permute-done((f32[512,128]{1,0:T(8,128)S(1)}, f32[512,128]{1,0:T(8,128)S(1)}, u32[]{:S(2)}, u32[]{:S(2)}) %collective-permute-start.12) | collective-permute-done | bytes 262176 | tf_op jit(solution)/shard_map/ppermute | solution.py:682
  63.7 6.9 %velocity.1.refs_4_ = f32[15,512,128]{2,1,0:T(8,128)S(1)} custom-call(bf16[512,384]{1,0:T(8,128)(2,1)S(1)} %get-tuple-element.88.vel_h, bf16[512,384]{1,0:T(8,128)(2,1)S(1)} %get-tuple-element.89.vel_l, f32[512,128]{1,0:T(8,128)S(1)} %collective-permute-done.12.below_ref, f32[512,128]{1,0:T(8,128)S(1)} %collective-permute-done.13.above_ref, ...), custom_call_target="tpu_custom_call" | custom-call | tf_op jit(solution)/shard_map/velocity/pallas_call | solution.py:685
  70.7 7.1 %momentum.1 = (f32[4,3,32,128]{3,2,1,0:T(8,128)S(1)}, f32[4,3,32,128]{3,2,1,0:T(8,128)S(1)}, f32[4,3,32,128]{3,2,1,0:T(8,128)S(1)}, f32[4,3,32,128]{3,2,1,0:T(8,...) custom-call(s32[1]{0:T(128)} %bitcast.me_ref.refs_0_, ...), custom_call_target="tpu_custom_call" | custom-call | tf_op jit(solution)/shard_map/momentum/pallas_call | solution.py:701
  77.8 0.6 collective-permute-start.14
  78.4 9.3 %collective-permute-start.15 = (f32[4,3,32,128]{3,2,1,0:T(8,128)S(1)}, f32[4,3,32,128]{3,2,1,0:T(8,128)S(1)}, u32[]{:S(2)}, u32[]{:S(2)}) collective-permute-start(f32[4,3,32,128]{3,2,1,0:T(8,128)S(1)} %get-tuple-element.97), channel_id=1, source_target_pairs={{0,8},{1,9},{2,10},{3,11},{4,12},{5,13},{6,14},{7,15},{8,0},{9,1},... | collective-permute-start | bytes 589832 | tf_op jit(solution)/shard_map/ppermute | solution.py:143
  87.7 1.4 collective-permute-start.16
  89.1 7.9 %elastic.1 = (f32[4,3,32,128]{3,2,1,0:T(8,128)S(1)}, f32[4,3,32,128]{3,2,1,0:T(8,128)S(1)}, f32[4,3,32,128]{3,2,1,0:T(8,128)S(1)}, f32[4,3,32,128]{3,2,1,0:T(8,1...) custom-call(s32[1]{0:T(128)} %bitcast.me_ref.refs_0_, ...), custom_call_target="tpu_custom_call" | custom-call | tf_op jit(solution)/shard_map/elastic/pallas_call | solution.py:719
  97.2 0.9 collective-permute-start.22
  98.2 0.1 collective-permute-start.21
  98.3 3.2 %collective-permute-start.17 = (f32[4,3,32,128]{3,2,1,0:T(8,128)S(1)}, f32[4,3,32,128]{3,2,1,0:T(8,128)S(1)}, u32[]{:S(2)}, u32[]{:S(2)}) collective-permute-start(f32[4,3,32,128]{3,2,1,0:T(8,128)S(1)} %get-tuple-element.112), channel_id=1, source_target_pairs={{0,4},{1,5},{2,6},{3,7},{4,0},{5,1},{6,2},{7,3},{8,12},{9,13},{10,... | collective-permute-start | bytes 589832 | tf_op jit(solution)/shard_map/ppermute | solution.py:143
  101.5 0.1 collective-permute-start.20
  101.6 1.3 collective-permute-start.18
  102.9 6.9 %collective-permute-done.17 = f32[4,3,32,128]{3,2,1,0:T(8,128)S(1)} collective-permute-done((f32[4,3,32,128]{3,2,1,0:T(8,128)S(1)}, f32[4,3,32,128]{3,2,1,0:T(8,128)S(1)}, u32[]{:S(2)}, u32[]{:S(2)}) %collective-permute-start.17) | collective-permute-done | bytes 196640 | tf_op jit(solution)/shard_map/ppermute | solution.py:143
  109.8 0.2 collective-permute-start.19
  110.0 3.9 %weights.1.refs_7_ = bf16[16,384,128]{2,1,0:T(8,128)(2,1)} custom-call(s32[32]{0:T(128)} %refs_1_.7, bf16[3,128,128]{2,1,0:T(8,128)(2,1)} %constant.35.clone.means_ref), custom_call_target="tpu_custom_call" | custom-call | tf_op jit(solution)/shard_map/weights/pallas_call | solution.py:303
  114.6 4.2 %collective-permute-done.18 = f32[4,3,32,128]{3,2,1,0:T(8,128)} collective-permute-done((f32[4,3,32,128]{3,2,1,0:T(8,128)S(1)}, f32[4,3,32,128]{3,2,1,0:T(8,128)}, u32[]{:S(2)}, u32[]{:S(2)}) %collective-permute-start.18) | collective-permute-done | bytes 196640 | tf_op jit(solution)/shard_map/ppermute | solution.py:143
  118.9 0.9 fusion.10
  119.8 0.9 fusion.11
  120.7 0.8 collective-permute-start.28
  121.5 1.3 collective-permute-start.27
  122.8 0.2 collective-permute-start.26
  123.1 2.3 %collective-permute-start.25 = (f32[4,3,32,128]{3,2,1,0:T(8,128)S(1)}, f32[4,3,32,128]{3,2,1,0:T(8,128)S(1)}, u32[]{:S(2)}, u32[]{:S(2)}) collective-permute-start(f32[4,3,32,128]{3,2,1,0:T(8,128)S(1)} %pad_maximum_fusion.15), channel_id=1, source_target_pairs={{0,12},{1,13},{2,14},{3,15},{4,8},{5,9},{6,10},{7,11},{8,4},{9,5},... | collective-permute-start | bytes 589832 | tf_op jit(solution)/shard_map/ppermute | solution.py:143
  125.4 3.6 %collective-permute-start.24 = (f32[4,3,32,128]{3,2,1,0:T(8,128)S(1)}, f32[4,3,32,128]{3,2,1,0:T(8,128)S(1)}, u32[]{:S(2)}, u32[]{:S(2)}) collective-permute-start(f32[4,3,32,128]{3,2,1,0:T(8,128)S(1)} %pad_maximum_fusion.14), channel_id=1, source_target_pairs={{0,8},{1,9},{2,10},{3,11},{4,12},{5,13},{6,14},{7,15},{8,0},{9,1},... | collective-permute-start | bytes 589832 | tf_op jit(solution)/shard_map/ppermute | solution.py:143
  129.0 3.1 %advance.3 = f32[3,32,2048]{2,1,0:T(8,128)} custom-call(s32[1]{0:T(128)} %bitcast.me_ref.refs_0_, s32[32]{0:T(128)S(1)} %copy-done.12, f32[1]{0:T(128)S(6)} %select_n.9.refs_2_, f32[4,6,32,128]{3,2,1,0:T(8,128)S(1)} %pad_maximum_fusion.4.refs_3_, f32[4,6,32,128]{3,2,1,0:T(8,128)S(1)} %collective-permute-done.20.refs_4_, ...), custom_call_target="tpu_custom_call" | custom-call | tf_op jit(solution)/shard_map/advance/pallas_call | solution.py:607
  132.2 0.1 collective-permute-start.23
  132.3 3.1 %advance.4.refs_9_ = f32[6,32,2048]{2,1,0:T(8,128)} custom-call(s32[1]{0:T(128)} %bitcast.me_ref.refs_0_, s32[32]{0:T(128)S(1)} %copy-done.12, f32[1]{0:T(128)S(6)} %select_n.9.refs_2_, f32[4,3,32,128]{3,2,1,0:T(8,128)S(1)} %pad_maximum_fusion.16.refs_3_, f32[4,3,32,128]{3,2,1,0:T(8,128)S(1)} %collective-permute-done.26.refs_4_, ...), custom_call_target="tpu_custom_call" | custom-call | tf_op jit(solution)/shard_map/advance/pallas_call | solution.py:607
  135.5 9.4 %collective-permute-done.24.refs_5_ = f32[4,3,32,128]{3,2,1,0:T(8,128)S(1)} collective-permute-done((f32[4,3,32,128]{3,2,1,0:T(8,128)S(1)}, f32[4,3,32,128]{3,2,1,0:T(8,128)S(1)}, u32[]{:S(2)}, u32[]{:S(2)}) %collective-permute-start.24) | collective-permute-done | bytes 196640 | tf_op jit(solution)/shard_map/ppermute | solution.py:143
  144.8 3.1 %advance.5 = f32[6,32,2048]{2,1,0:T(8,128)} custom-call(s32[1]{0:T(128)} %bitcast.me_ref.refs_0_, s32[32]{0:T(128)S(1)} %copy-done.12, f32[1]{0:T(128)S(6)} %select_n.9.refs_2_, f32[4,3,32,128]{3,2,1,0:T(8,128)S(1)} %pad_maximum_fusion.12.refs_3_, f32[4,3,32,128]{3,2,1,0:T(8,128)S(1)} %collective-permute-done.23.refs_4_, ...), custom_call_target="tpu_custom_call", output_to_operand_aliasing={{}: (9, {})} | custom-call | tf_op jit(solution)/shard_map/advance/pallas_call | solution.py:607
  (86 shorter events, 0.9 us)
Async XLA Ops:
  0.6 16.7 %copy-start.10 = (f32[128,128]{1,0:T(8,128)S(1)}, f32[128,128]{1,0:T(8,128)}, u32[]{:S(2)}) copy-start(f32[128,128]{1,0:T(8,128)} %constant.31.clone.inv_r_ref) | copy-start | bytes 196612
  0.6 16.6 %copy-start.9 = (bf16[10,128,128]{2,1,0:T(8,128)(2,1)S(1)}, bf16[10,128,128]{2,1,0:T(8,128)(2,1)}, u32[]{:S(2)}) copy-start(bf16[10,128,128]{2,1,0:T(8,128)(2,1)} %constant.32.clone.both_ref) | copy-start | bytes 983044
  0.7 16.6 %copy-start.8 = (bf16[6,128,256]{2,1,0:T(8,128)(2,1)S(1)}, bf16[6,128,256]{2,1,0:T(8,128)(2,1)}, u32[]{:S(2)}) copy-start(bf16[6,128,256]{2,1,0:T(8,128)(2,1)} %constant.33.clone.faces_ref) | copy-start | bytes 1179652
  0.7 16.6 %copy-start.7 = (bf16[18,256,128]{2,1,0:T(8,128)(2,1)S(1)}, bf16[18,256,128]{2,1,0:T(8,128)(2,1)}, u32[]{:S(2)}) copy-start(bf16[18,256,128]{2,1,0:T(8,128)(2,1)} %constant.34.clone.halos_ref) | copy-start | bytes 3538948
  0.7 16.6 %copy-start.11 = (s32[32]{0:T(128)S(1)}, s32[32]{0:T(128)}, u32[]{:S(2)}) copy-start(s32[32]{0:T(128)} %refs_1_.7) | copy-start | bytes 388
  4.2 22.9 %copy-start.14 = (f32[4,3,32,128]{3,2,1,0:T(8,128)S(1)}, f32[4,3,32,128]{3,2,1,0:T(8,128)}, u32[]{:S(2)}) copy-start(f32[4,3,32,128]{3,2,1,0:T(8,128)} %get-tuple-element.83) | copy-start | bytes 589828
  4.3 8.2 %collective-permute-start = (f32[4,3,32,128]{3,2,1,0:T(8,128)}, f32[4,3,32,128]{3,2,1,0:T(8,128)S(1)}, u32[]{:S(2)}, u32[]{:S(2)}) collective-permute-start(f32[4,3,32,128]{3,2,1,0:T(8,128)} %get-tuple-element.68), channel_id=1, source_target_pairs={{0,4},{1,5},{2,6},{3,7},{4,0},{5,1},{6,2},{7,3},{8,12},{9,13},{10,... | collective-permute-start | bytes 589832 | tf_op jit(solution)/shard_map/ppermute | solution.py:143
  7.3 18.9 %collective-permute-start.3 = (f32[4,6,32,128]{3,2,1,0:T(8,128)}, f32[4,6,32,128]{3,2,1,0:T(8,128)S(1)}, u32[]{:S(2)}, u32[]{:S(2)}) collective-permute-start(f32[4,6,32,128]{3,2,1,0:T(8,128)} %get-tuple-element.72), channel_id=1, source_target_pairs={{0,1},{1,0},{2,3},{3,2},{4,5},{5,4},{6,7},{7,6},{8,9},{9,8},{10,11... | collective-permute-start | bytes 1179656 | tf_op jit(solution)/shard_map/ppermute | solution.py:143
  7.3 18.9 %collective-permute-start.4 = (f32[4,6,32,128]{3,2,1,0:T(8,128)}, f32[4,6,32,128]{3,2,1,0:T(8,128)S(1)}, u32[]{:S(2)}, u32[]{:S(2)}) collective-permute-start(f32[4,6,32,128]{3,2,1,0:T(8,128)} %get-tuple-element.73), channel_id=1, source_target_pairs={{0,2},{1,3},{2,0},{3,1},{4,6},{5,7},{6,4},{7,5},{8,10},{9,11},{10,... | collective-permute-start | bytes 1179656 | tf_op jit(solution)/shard_map/ppermute | solution.py:143
  8.9 18.3 %collective-permute-start.5 = (f32[4,6,32,128]{3,2,1,0:T(8,128)}, f32[4,6,32,128]{3,2,1,0:T(8,128)S(1)}, u32[]{:S(2)}, u32[]{:S(2)}) collective-permute-start(f32[4,6,32,128]{3,2,1,0:T(8,128)} %get-tuple-element.74), channel_id=1, source_target_pairs={{0,3},{1,2},{2,1},{3,0},{4,7},{5,6},{6,5},{7,4},{8,11},{9,10},{10,... | collective-permute-start | bytes 1179656 | tf_op jit(solution)/shard_map/ppermute | solution.py:143
  9.2 17.1 %collective-permute-start.1 = (f32[4,3,32,128]{3,2,1,0:T(8,128)}, f32[4,3,32,128]{3,2,1,0:T(8,128)S(1)}, u32[]{:S(2)}, u32[]{:S(2)}) collective-permute-start(f32[4,3,32,128]{3,2,1,0:T(8,128)} %get-tuple-element.69), channel_id=1, source_target_pairs={{0,8},{1,9},{2,10},{3,11},{4,12},{5,13},{6,14},{7,15},{8,0},{9,1},... | collective-permute-start | bytes 589832 | tf_op jit(solution)/shard_map/ppermute | solution.py:143
  12.5 13.8 %collective-permute-start.2 = (f32[4,3,32,128]{3,2,1,0:T(8,128)}, f32[4,3,32,128]{3,2,1,0:T(8,128)S(1)}, u32[]{:S(2)}, u32[]{:S(2)}) collective-permute-start(f32[4,3,32,128]{3,2,1,0:T(8,128)} %get-tuple-element.70), channel_id=1, source_target_pairs={{0,12},{1,13},{2,14},{3,15},{4,8},{5,9},{6,10},{7,11},{8,4},{9,5},... | collective-permute-start | bytes 589832 | tf_op jit(solution)/shard_map/ppermute | solution.py:143
  18.7 10.6 %copy-start.13 = (f32[4,6,32,128]{3,2,1,0:T(8,128)S(1)}, f32[4,6,32,128]{3,2,1,0:T(8,128)}, u32[]{:S(2)}) copy-start(f32[4,6,32,128]{3,2,1,0:T(8,128)} %get-tuple-element.79) | copy-start | bytes 1179652
  27.2 7.4 %collective-permute-start.11 = (f32[4,3,32,128]{3,2,1,0:T(8,128)S(1)}, f32[4,3,32,128]{3,2,1,0:T(8,128)S(1)}, u32[]{:S(2)}, u32[]{:S(2)}) collective-permute-start(f32[4,3,32,128]{3,2,1,0:T(8,128)S(1)} %pad_maximum_fusion.11), channel_id=1, source_target_pairs={{0,3},{1,2},{2,1},{3,0},{4,7},{5,6},{6,5},{7,4},{8,11},{9,10},{10,... | collective-permute-start | bytes 589832 | tf_op jit(solution)/shard_map/ppermute | solution.py:143
  28.6 10.1 %collective-permute-start.10 = (f32[4,3,32,128]{3,2,1,0:T(8,128)S(1)}, f32[4,3,32,128]{3,2,1,0:T(8,128)S(1)}, u32[]{:S(2)}, u32[]{:S(2)}) collective-permute-start(f32[4,3,32,128]{3,2,1,0:T(8,128)S(1)} %pad_maximum_fusion.10), channel_id=1, source_target_pairs={{0,2},{1,3},{2,0},{3,1},{4,6},{5,7},{6,4},{7,5},{8,10},{9,11},{10,... | collective-permute-start | bytes 589832 | tf_op jit(solution)/shard_map/ppermute | solution.py:143
  29.2 9.5 %collective-permute-start.9 = (f32[4,3,32,128]{3,2,1,0:T(8,128)S(1)}, f32[4,3,32,128]{3,2,1,0:T(8,128)S(1)}, u32[]{:S(2)}, u32[]{:S(2)}) collective-permute-start(f32[4,3,32,128]{3,2,1,0:T(8,128)S(1)} %pad_maximum_fusion.9), channel_id=1, source_target_pairs={{0,1},{1,0},{2,3},{3,2},{4,5},{5,4},{6,7},{7,6},{8,9},{9,8},{10,11... | collective-permute-start | bytes 589832 | tf_op jit(solution)/shard_map/ppermute | solution.py:143
  29.5 41.1 %collective-permute-start.8 = (f32[4,6,32,128]{3,2,1,0:T(8,128)S(1)}, f32[4,6,32,128]{3,2,1,0:T(8,128)S(1)}, u32[]{:S(2)}, u32[]{:S(2)}) collective-permute-start(f32[4,6,32,128]{3,2,1,0:T(8,128)S(1)} %pad_maximum_fusion.3), channel_id=1, source_target_pairs={{0,12},{1,13},{2,14},{3,15},{4,8},{5,9},{6,10},{7,11},{8,4},{9,5},... | collective-permute-start | bytes 1179656 | tf_op jit(solution)/shard_map/ppermute | solution.py:143
  32.0 38.6 %collective-permute-start.7 = (f32[4,6,32,128]{3,2,1,0:T(8,128)S(1)}, f32[4,6,32,128]{3,2,1,0:T(8,128)S(1)}, u32[]{:S(2)}, u32[]{:S(2)}) collective-permute-start(f32[4,6,32,128]{3,2,1,0:T(8,128)S(1)} %pad_maximum_fusion.2), channel_id=1, source_target_pairs={{0,8},{1,9},{2,10},{3,11},{4,12},{5,13},{6,14},{7,15},{8,0},{9,1},... | collective-permute-start | bytes 1179656 | tf_op jit(solution)/shard_map/ppermute | solution.py:143
  34.6 29.0 %copy-start.2 = (bf16[1024,512]{1,0:T(8,128)(2,1)S(1)}, bf16[1024,512]{1,0:T(8,128)(2,1)}, u32[]{:S(2)}) copy-start(bf16[1024,512]{1,0:T(8,128)(2,1)} %constant.27.clone.high_ref.refs_5_) | copy-start | bytes 3145732
  34.6 29.0 %copy-start.3 = (bf16[1024,512]{1,0:T(8,128)(2,1)S(1)}, bf16[1024,512]{1,0:T(8,128)(2,1)}, u32[]{:S(2)}) copy-start(bf16[1024,512]{1,0:T(8,128)(2,1)} %constant.28.clone.low_ref.refs_6_) | copy-start | bytes 3145732
  34.6 36.0 %collective-permute-start.6 = (f32[4,6,32,128]{3,2,1,0:T(8,128)S(1)}, f32[4,6,32,128]{3,2,1,0:T(8,128)S(1)}, u32[]{:S(2)}, u32[]{:S(2)}) collective-permute-start(f32[4,6,32,128]{3,2,1,0:T(8,128)S(1)} %pad_maximum_fusion.1), channel_id=1, source_target_pairs={{0,4},{1,5},{2,6},{3,7},{4,0},{5,1},{6,2},{7,3},{8,12},{9,13},{10,... | collective-permute-start | bytes 1179656 | tf_op jit(solution)/shard_map/ppermute | solution.py:143
  39.6 24.0 %collective-permute-start.12 = (f32[512,128]{1,0:T(8,128)S(1)}, f32[512,128]{1,0:T(8,128)S(1)}, u32[]{:S(2)}, u32[]{:S(2)}) collective-permute-start(f32[512,128]{1,0:T(8,128)S(1)} %get-tuple-element.90), channel_id=1, source_target_pairs={{0,1},{1,2},{2,3},{3,4},{4,5},{5,6},{6,7},{7,8},{8,9},{9,10},{10,1... | collective-permute-start | bytes 786440 | tf_op jit(solution)/shard_map/ppermute | solution.py:682
  39.7 24.0 %collective-permute-start.13 = (f32[512,128]{1,0:T(8,128)S(1)}, f32[512,128]{1,0:T(8,128)S(1)}, u32[]{:S(2)}, u32[]{:S(2)}) collective-permute-start(f32[512,128]{1,0:T(8,128)S(1)} %get-tuple-element.91), channel_id=1, source_target_pairs={{1,0},{2,1},{3,2},{4,3},{5,4},{6,5},{7,6},{8,7},{9,8},{10,9},{11,1... | collective-permute-start | bytes 786440 | tf_op jit(solution)/shard_map/ppermute | solution.py:683
  63.7 7.0 %copy-start.4 = (bf16[512,1024]{1,0:T(8,128)(2,1)S(1)}, bf16[512,1024]{1,0:T(8,128)(2,1)}, u32[]{:S(2)}) copy-start(bf16[512,1024]{1,0:T(8,128)(2,1)} %constant.29.clone.refs_7_) | copy-start | bytes 3145732
  63.7 7.0 %copy-start.5 = (bf16[512,1024]{1,0:T(8,128)(2,1)S(1)}, bf16[512,1024]{1,0:T(8,128)(2,1)}, u32[]{:S(2)}) copy-start(bf16[512,1024]{1,0:T(8,128)(2,1)} %constant.30.clone.refs_8_) | copy-start | bytes 3145732
  77.8 19.3 %collective-permute-start.14 = (f32[4,3,32,128]{3,2,1,0:T(8,128)S(1)}, f32[4,3,32,128]{3,2,1,0:T(8,128)S(1)}, u32[]{:S(2)}, u32[]{:S(2)}) collective-permute-start(f32[4,3,32,128]{3,2,1,0:T(8,128)S(1)} %get-tuple-element.96), channel_id=1, source_target_pairs={{0,4},{1,5},{2,6},{3,7},{4,0},{5,1},{6,2},{7,3},{8,12},{9,13},{10,... | collective-permute-start | bytes 589832 | tf_op jit(solution)/shard_map/ppermute | solution.py:143
  78.4 18.6 %collective-permute-start.15 = (f32[4,3,32,128]{3,2,1,0:T(8,128)S(1)}, f32[4,3,32,128]{3,2,1,0:T(8,128)S(1)}, u32[]{:S(2)}, u32[]{:S(2)}) collective-permute-start(f32[4,3,32,128]{3,2,1,0:T(8,128)S(1)} %get-tuple-element.97), channel_id=1, source_target_pairs={{0,8},{1,9},{2,10},{3,11},{4,12},{5,13},{6,14},{7,15},{8,0},{9,1},... | collective-permute-start | bytes 589832 | tf_op jit(solution)/shard_map/ppermute | solution.py:143
  87.7 9.3 %collective-permute-start.16 = (f32[4,3,32,128]{3,2,1,0:T(8,128)S(1)}, f32[4,3,32,128]{3,2,1,0:T(8,128)S(1)}, u32[]{:S(2)}, u32[]{:S(2)}) collective-permute-start(f32[4,3,32,128]{3,2,1,0:T(8,128)S(1)} %get-tuple-element.98), channel_id=1, source_target_pairs={{0,12},{1,13},{2,14},{3,15},{4,8},{5,9},{6,10},{7,11},{8,4},{9,5},... | collective-permute-start | bytes 589832 | tf_op jit(solution)/shard_map/ppermute | solution.py:143
  97.2 21.6 %collective-permute-start.22 = (f32[4,6,32,128]{3,2,1,0:T(8,128)S(1)}, f32[4,6,32,128]{3,2,1,0:T(8,128)S(1)}, u32[]{:S(2)}, u32[]{:S(2)}) collective-permute-start(f32[4,6,32,128]{3,2,1,0:T(8,128)S(1)} %pad_maximum_fusion.7), channel_id=1, source_target_pairs={{0,3},{1,2},{2,1},{3,0},{4,7},{5,6},{6,5},{7,4},{8,11},{9,10},{10,... | collective-permute-start | bytes 1179656 | tf_op jit(solution)/shard_map/ppermute | solution.py:143
  98.2 20.7 %collective-permute-start.21 = (f32[4,6,32,128]{3,2,1,0:T(8,128)S(1)}, f32[4,6,32,128]{3,2,1,0:T(8,128)S(1)}, u32[]{:S(2)}, u32[]{:S(2)}) collective-permute-start(f32[4,6,32,128]{3,2,1,0:T(8,128)S(1)} %pad_maximum_fusion.6), channel_id=1, source_target_pairs={{0,2},{1,3},{2,0},{3,1},{4,6},{5,7},{6,4},{7,5},{8,10},{9,11},{10,... | collective-permute-start | bytes 1179656 | tf_op jit(solution)/shard_map/ppermute | solution.py:143
  98.3 11.5 %collective-permute-start.17 = (f32[4,3,32,128]{3,2,1,0:T(8,128)S(1)}, f32[4,3,32,128]{3,2,1,0:T(8,128)S(1)}, u32[]{:S(2)}, u32[]{:S(2)}) collective-permute-start(f32[4,3,32,128]{3,2,1,0:T(8,128)S(1)} %get-tuple-element.112), channel_id=1, source_target_pairs={{0,4},{1,5},{2,6},{3,7},{4,0},{5,1},{6,2},{7,3},{8,12},{9,13},{10,... | collective-permute-start | bytes 589832 | tf_op jit(solution)/shard_map/ppermute | solution.py:143
  101.5 17.3 %collective-permute-start.20 = (f32[4,6,32,128]{3,2,1,0:T(8,128)S(1)}, f32[4,6,32,128]{3,2,1,0:T(8,128)S(1)}, u32[]{:S(2)}, u32[]{:S(2)}) collective-permute-start(f32[4,6,32,128]{3,2,1,0:T(8,128)S(1)} %pad_maximum_fusion.5), channel_id=1, source_target_pairs={{0,1},{1,0},{2,3},{3,2},{4,5},{5,4},{6,7},{7,6},{8,9},{9,8},{10,11... | collective-permute-start | bytes 1179656 | tf_op jit(solution)/shard_map/ppermute | solution.py:143
  101.6 17.2 %collective-permute-start.18 = (f32[4,3,32,128]{3,2,1,0:T(8,128)S(1)}, f32[4,3,32,128]{3,2,1,0:T(8,128)}, u32[]{:S(2)}, u32[]{:S(2)}) collective-permute-start(f32[4,3,32,128]{3,2,1,0:T(8,128)S(1)} %get-tuple-element.113), channel_id=1, source_target_pairs={{0,8},{1,9},{2,10},{3,11},{4,12},{5,13},{6,14},{7,15},{8,0},{9,1},... | collective-permute-start | bytes 589832 | tf_op jit(solution)/shard_map/ppermute | solution.py:143
  109.8 9.0 %collective-permute-start.19 = (f32[4,3,32,128]{3,2,1,0:T(8,128)S(1)}, f32[4,3,32,128]{3,2,1,0:T(8,128)}, u32[]{:S(2)}, u32[]{:S(2)}) collective-permute-start(f32[4,3,32,128]{3,2,1,0:T(8,128)S(1)} %get-tuple-element.114), channel_id=1, source_target_pairs={{0,12},{1,13},{2,14},{3,15},{4,8},{5,9},{6,10},{7,11},{8,4},{9,5},... | collective-permute-start | bytes 589832 | tf_op jit(solution)/shard_map/ppermute | solution.py:143
  120.7 11.5 %collective-permute-start.28 = (f32[4,3,32,128]{3,2,1,0:T(8,128)S(1)}, f32[4,3,32,128]{3,2,1,0:T(8,128)S(1)}, u32[]{:S(2)}, u32[]{:S(2)}) collective-permute-start(f32[4,3,32,128]{3,2,1,0:T(8,128)S(1)} %pad_maximum_fusion.19), channel_id=1, source_target_pairs={{0,3},{1,2},{2,1},{3,0},{4,7},{5,6},{6,5},{7,4},{8,11},{9,10},{10,... | collective-permute-start | bytes 589832 | tf_op jit(solution)/shard_map/ppermute | solution.py:143
  121.5 7.5 %copy-start = (bf16[16,384,128]{2,1,0:T(8,128)(2,1)S(1)}, bf16[16,384,128]{2,1,0:T(8,128)(2,1)}, u32[]{:S(2)}) copy-start(bf16[16,384,128]{2,1,0:T(8,128)(2,1)} %weights.1.refs_7_) | copy-start | bytes 4718596
  121.5 7.5 %copy-start.6 = (f32[3,32,2048]{2,1,0:T(8,128)S(1)}, f32[3,32,2048]{2,1,0:T(8,128)}, u32[]{:S(2)}) copy-start(f32[3,32,2048]{2,1,0:T(8,128)} %refs_8_.5) | copy-start | bytes 2359300
  121.5 7.5 %copy-start.12 = (s32[32]{0:T(128)S(1)}, s32[32]{0:T(128)}, u32[]{:S(2)}) copy-start(s32[32]{0:T(128)} %refs_1_.7) | copy-start | bytes 388
  121.5 10.8 %collective-permute-start.27 = (f32[4,3,32,128]{3,2,1,0:T(8,128)S(1)}, f32[4,3,32,128]{3,2,1,0:T(8,128)S(1)}, u32[]{:S(2)}, u32[]{:S(2)}) collective-permute-start(f32[4,3,32,128]{3,2,1,0:T(8,128)S(1)} %pad_maximum_fusion.18), channel_id=1, source_target_pairs={{0,2},{1,3},{2,0},{3,1},{4,6},{5,7},{6,4},{7,5},{8,10},{9,11},{10,... | collective-permute-start | bytes 589832 | tf_op jit(solution)/shard_map/ppermute | solution.py:143
  122.8 9.5 %collective-permute-start.26 = (f32[4,3,32,128]{3,2,1,0:T(8,128)S(1)}, f32[4,3,32,128]{3,2,1,0:T(8,128)S(1)}, u32[]{:S(2)}, u32[]{:S(2)}) collective-permute-start(f32[4,3,32,128]{3,2,1,0:T(8,128)S(1)} %pad_maximum_fusion.17), channel_id=1, source_target_pairs={{0,1},{1,0},{2,3},{3,2},{4,5},{5,4},{6,7},{7,6},{8,9},{9,8},{10,11... | collective-permute-start | bytes 589832 | tf_op jit(solution)/shard_map/ppermute | solution.py:143
  123.1 12.4 %collective-permute-start.25 = (f32[4,3,32,128]{3,2,1,0:T(8,128)S(1)}, f32[4,3,32,128]{3,2,1,0:T(8,128)S(1)}, u32[]{:S(2)}, u32[]{:S(2)}) collective-permute-start(f32[4,3,32,128]{3,2,1,0:T(8,128)S(1)} %pad_maximum_fusion.15), channel_id=1, source_target_pairs={{0,12},{1,13},{2,14},{3,15},{4,8},{5,9},{6,10},{7,11},{8,4},{9,5},... | collective-permute-start | bytes 589832 | tf_op jit(solution)/shard_map/ppermute | solution.py:143
  125.4 19.4 %collective-permute-start.24 = (f32[4,3,32,128]{3,2,1,0:T(8,128)S(1)}, f32[4,3,32,128]{3,2,1,0:T(8,128)S(1)}, u32[]{:S(2)}, u32[]{:S(2)}) collective-permute-start(f32[4,3,32,128]{3,2,1,0:T(8,128)S(1)} %pad_maximum_fusion.14), channel_id=1, source_target_pairs={{0,8},{1,9},{2,10},{3,11},{4,12},{5,13},{6,14},{7,15},{8,0},{9,1},... | collective-permute-start | bytes 589832 | tf_op jit(solution)/shard_map/ppermute | solution.py:143
  129.0 3.3 %copy-start.1 = (f32[6,32,2048]{2,1,0:T(8,128)S(1)}, f32[6,32,2048]{2,1,0:T(8,128)}, u32[]{:S(2)}) copy-start(f32[6,32,2048]{2,1,0:T(8,128)} %refs_8_.7) | copy-start | bytes 4718596
  132.2 12.6 %collective-permute-start.23 = (f32[4,3,32,128]{3,2,1,0:T(8,128)S(1)}, f32[4,3,32,128]{3,2,1,0:T(8,128)S(1)}, u32[]{:S(2)}, u32[]{:S(2)}) collective-permute-start(f32[4,3,32,128]{3,2,1,0:T(8,128)S(1)} %pad_maximum_fusion.13), channel_id=1, source_target_pairs={{0,4},{1,5},{2,6},{3,7},{4,0},{5,1},{6,2},{7,3},{8,12},{9,13},{10,... | collective-permute-start | bytes 589832 | tf_op jit(solution)/shard_map/ppermute | solution.py:143

commit v2 on v1

--- a/solution.py
+++ b/solution.py
@@ -91,7 +91,24 @@
             halos[field, at_u : at_u + RADIAL, out] = 0.5 * radial_row @ radial_mean
             halos[3 + field, at_dz : at_dz + RADIAL, out] = 0.5 * radial_mean
             halos[6 + field, at_u : at_u + RADIAL, out] = 0.5 * radial_mean * inv_r[None, :]
-    return both, faces, halos, means, inv_r_nodes
+    used = 6 * RADIAL
+    packed = [faces]
+    for number in range(3):
+        variant = np.zeros_like(faces)
+        for side in (0, BLOCK):
+            group = slice(side + number * (BLOCK - used), side + (number + 1) * (BLOCK - used))
+            variant[:, :, side + used : side + BLOCK] = faces[:, :, group]
+        packed.append(variant)
+    return both, np.concatenate(packed), halos, means, inv_r_nodes
+
+
+def free_places():
+    used = 6 * RADIAL
+    free = BLOCK - used
+    moves = np.zeros((3, BLOCK, BLOCK))
+    for number in range(3):
+        moves[number, used:, number * free : (number + 1) * free] = np.eye(free)
+    return moves
 
 
 def split(values):
@@ -143,21 +160,50 @@
     return lax.ppermute(block, "mode", [(i, i ^ bits) for i in range(devices)])
 
 
-def far_swaps(groups):
-    return [groups[0]] + [swap(groups[s], NEAR * s) for s in (1, 2, 3)]
+def after(block, token):
+    return lax.optimization_barrier((block, token))[0]
 
 
 def near_swaps(groups):
     return [groups[0]] + [swap(groups[t], t) for t in (1, 2, 3)]
 
 
+def far_swaps(groups, beside=None):
+    first = groups[1] if beside is None else after(groups[1], beside[1])
+    return [groups[0], swap(first, NEAR)] + [swap(groups[s], NEAR * s) for s in (2, 3)]
+
+
 def regroup(groups):
     return [jnp.stack([group[at] for group in groups]) for at in range(NEAR)]
 
 
+def turn(groups):
+    every = [(s, t) for s in range(NEAR) for t in range(NEAR)]
+
+    def body(*refs):
+        in_refs, out_refs, sems = refs[:NEAR], refs[NEAR : 2 * NEAR], refs[-1]
+        copies = []
+        for number, (s, t) in enumerate(every):
+            copy = pltpu.make_async_copy(in_refs[t].at[s], out_refs[s].at[t], sems.at[number])
+            copy.start()
+            copies.append(copy)
+        for copy in copies:
+            copy.wait()
+
+    return pl.pallas_call(
+        body,
+        in_specs=[pl.BlockSpec(memory_space=pl.ANY)] * NEAR,
+        out_specs=[pl.BlockSpec(memory_space=pl.ANY)] * NEAR,
+        out_shape=[jax.ShapeDtypeStruct(group.shape, F32) for group in groups],
+        scratch_shapes=[pltpu.SemaphoreType.DMA((len(every),))],
+        compiler_params=pltpu.CompilerParams(vmem_limit_bytes=4 * MIB),
+        name="turn",
+    )(*groups)
+
+
 class Route:
-    def __init__(self, devices, local_modes, far_first):
-        self.staged = devices == NEAR * NEAR and local_modes % 16 == 0
+    def __init__(self, devices, local_modes, far_first, staged=True):
+        self.staged = staged and devices == NEAR * NEAR and local_modes % 16 == 0
         self.aligned = self.staged or local_modes % 16 == 0
         self.devices, self.local_modes, self.far_first = devices, local_modes, far_first
         self.modes = local_modes if self.aligned else local_modes * devices
@@ -246,14 +292,14 @@
 
 def places(orient_ref, layer, shape):
     lane = lax.broadcasted_iota(jnp.int32, shape, 1)
-    cycle = lane // (SIDE * SIDE)
+    cycle = lane >> 6
     orient = jnp.where(
         cycle == 0, orient_ref[CYCLES * layer], orient_ref[CYCLES * layer + 1]
     )
-    lead, trail = lane // SIDE % SIDE, lane % SIDE
-    lead = jnp.where(orient % 2 == 1, SIDE - 1 - lead, lead)
-    trail = jnp.where(orient // 2 % 2 == 1, SIDE - 1 - trail, trail)
-    swapped = orient // 4 % 2 == 1
+    lead, trail = (lane >> 3) & 7, lane & 7
+    lead = jnp.where((orient & 1) == 1, SIDE - 1 - lead, lead)
+    trail = jnp.where((orient & 2) == 2, SIDE - 1 - trail, trail)
+    swapped = (orient & 4) == 4
     row = jnp.where(swapped, trail, lead)
     col = jnp.where(swapped, lead, trail)
     return row * RADIAL + cycle * SIDE + col
@@ -284,101 +330,131 @@
         halos_out[at] = dot(halos_ref[at], onto).astype(BF16)
 
 
-def weights_body(layers, step, orient_ref, means_ref, out_ref):
-    first = pl.program_id(0) * step
-    for at in range(step):
-        index = first + at
+def weights_body(layers, orient_ref, means_ref, out_ref):
+    def one(index, carry):
         onto = from_grid(orient_ref, index).astype(BF16)
         below = lax.rem(index + (layers - 1), layers)
         above = lax.rem(index + 1, layers)
         for number, layer in enumerate((below, index, above)):
             back = from_grid(orient_ref, layer).T.astype(BF16)
             moved = dot(means_ref[number], onto).astype(BF16)
-            rows = slice(number * BLOCK, (number + 1) * BLOCK)
-            out_ref[at, rows, :] = dot(back, moved).astype(BF16)
-
-
-def mean_weights(orientation, means, layers):
-    step = 4
-    return pl.pallas_call(
-        functools.partial(weights_body, layers, step),
-        grid=(layers // step,),
-        in_specs=[
-            pl.BlockSpec(memory_space=pltpu.SMEM),
-            pl.BlockSpec(means.shape, lambda i: (0, 0, 0)),
-        ],
-        out_specs=pl.BlockSpec((step, 3 * BLOCK, BLOCK), lambda i: (i, 0, 0)),
-        out_shape=jax.ShapeDtypeStruct((layers, 3 * BLOCK, BLOCK), BF16),
-        name="weights",
-    )(orientation, means)
+            out_ref[index, number * BLOCK : (number + 1) * BLOCK, :] = dot(back, moved).astype(BF16)
+        return carry
+
+    lax.fori_loop(0, layers, one, 0)
 
 
 def face_body(route, count, me_ref, *refs):
     vel_refs, (faces_ref, up_ref, down_ref, high, low) = refs[:count], refs[count:]
     route.load(me_ref, vel_refs, high, low)
-    total = None
-    for field in range(3):
-        lanes = lanes_of(field)
-        own = (high[:, lanes], low[:, lanes])
-        part = dot3(own, (faces_ref[2 * field], faces_ref[2 * field + 1]))
-        total = part if total is None else total + part
-    up_ref[...] = total[:, :BLOCK]
-    down_ref[...] = total[:, BLOCK:]
+    quarter = high.shape[0] // 4
+
+    def faces(rows, variant):
+        total = None
+        for field in range(3):
+            lanes, at = lanes_of(field), 6 * variant + 2 * field
+            part = dot3((high[rows, lanes], low[rows, lanes]), (faces_ref[at], faces_ref[at + 1]))
+            total = part if total is None else total + part
+        return total
+
+    for number in range(3):
+        rows = slice(number * quarter, (number + 1) * quarter)
+        total = faces(rows, 0) + faces(slice(3 * quarter, 4 * quarter), 1 + number)
+        up_ref[rows, :] = total[:, :BLOCK]
+        down_ref[rows, :] = total[:, BLOCK:]
+
+
+def flow_parts(g_r, g_t, g_z, u):
+    return (
+        0.5 * (g_t[0] - g_r[1]),
+        0.5 * (g_z[0] - g_r[2]),
+        0.5 * (g_z[1] - g_t[2]),
+        2.0 * g_r[0],
+        g_t[0] + g_r[1],
+        g_z[0] + g_r[2],
+        2.0 * g_t[1],
+        g_z[1] + g_t[2],
+        2.0 * g_z[2],
+        -(g_r[0] * u[0] + g_t[0] * u[1] + g_z[0] * u[2]),
+        -(g_r[1] * u[0] + g_t[1] * u[1] + g_z[1] * u[2]),
+        -(g_r[2] * u[0] + g_t[2] * u[1] + g_z[2] * u[2]),
+    )
+
+
+def matrix_of(ref, at):
+    return ref[2 * at], ref[2 * at + 1]
 
 
 def velocity_body(
-    vel_h, vel_l, below_ref, above_ref, high_ref, low_ref, both_ref, halos_ref, inv_r_ref,
-    flow_ref, values,
+    vel_h, vel_l, high_ref, low_ref, both_ref, inv_r_ref, vel_ref, flow_ref, values
 ):
     planes = high_ref.shape[1]
     table = (high_ref[...], low_ref[...])
     values[:, 0:256] = dot3(table, (vel_h[:, 0:256], vel_l[:, 0:256]))
     values[:, 256:384] = dot3(table, (vel_h[:, 256:384], vel_l[:, 256:384]))
-    values[:, 384:640] = dot3(
-        table, split(jnp.concatenate([below_ref[...], above_ref[...]], axis=1))
-    )
     rows_step = 128
 
-    def matrix(at):
-        return both_ref[2 * at], both_ref[2 * at + 1]
-
-    def halo(at):
-        return halos_ref[2 * at], halos_ref[2 * at + 1]
-
-    def chunk(step, carry):
-        rows = pl.ds(pl.multiple_of(step * rows_step, rows_step), rows_step)
-        turned = pl.ds(pl.multiple_of(planes + step * rows_step, rows_step), rows_step)
+    def chunk(start):
+        rows = pl.ds(start, rows_step)
+        turned = pl.ds(pl.multiple_of(planes + start, rows_step), rows_step)
         u = [values[rows, lanes_of(f)] for f in range(3)]
         u_s = [split(v) for v in u]
         dth_s = [split(values[turned, lanes_of(f)]) for f in range(3)]
-        edge = split(values[rows, 384:640])
-        edge_dth = split(values[turned, 384:640])
-        g_r = [dot3(u_s[f], matrix(2)) + dot3(edge, halo(f)) for f in range(3)]
-        g_z = [dot3(u_s[f], matrix(3)) + dot3(edge, halo(3 + f)) for f in range(3)]
-        g_t = [dot3(dth_s[f], matrix(4)) + dot3(edge_dth, halo(6 + f)) for f in range(3)]
-        mean_r = dot3(u_s[0], matrix(4)) + dot3(edge, halo(6))
-        mean_t = dot3(u_s[1], matrix(4)) + dot3(edge, halo(7))
-        g_t[0] = g_t[0] - mean_t
-        g_t[1] = g_t[1] + mean_r
+        g_r = [dot3(u_s[f], matrix_of(both_ref, 2)) for f in range(3)]
+        g_z = [dot3(u_s[f], matrix_of(both_ref, 3)) for f in range(3)]
+        g_t = [dot3(dth_s[f], matrix_of(both_ref, 4)) for f in range(3)]
+        g_t[0] = g_t[0] - dot3(u_s[1], matrix_of(both_ref, 4))
+        g_t[1] = g_t[1] + dot3(u_s[0], matrix_of(both_ref, 4))
         hoop_rate = u[1] * inv_r_ref[0:1, :]
-        flow_ref[0, rows, :] = u[0]
-        flow_ref[1, rows, :] = hoop_rate
-        flow_ref[2, rows, :] = u[2]
-        flow_ref[3, rows, :] = 0.5 * (g_t[0] - g_r[1]) + hoop_rate
-        flow_ref[4, rows, :] = 0.5 * (g_z[0] - g_r[2])
-        flow_ref[5, rows, :] = 0.5 * (g_z[1] - g_t[2])
+        parts = flow_parts(g_r, g_t, g_z, u)
         rest = (1.0 - 2.0 * MOBILITY) / RELAX_TIME
-        flow_ref[6, rows, :] = 2.0 * g_r[0] - rest
-        flow_ref[7, rows, :] = g_t[0] + g_r[1]
-        flow_ref[8, rows, :] = g_z[0] + g_r[2]
-        flow_ref[9, rows, :] = 2.0 * g_t[1] - rest
-        flow_ref[10, rows, :] = g_z[1] + g_t[2]
-        flow_ref[11, rows, :] = 2.0 * g_z[2] - rest
         for f in range(3):
-            flow_ref[12 + f, rows, :] = -(g_r[f] * u[0] + g_t[f] * u[1] + g_z[f] * u[2])
-        return carry
-
-    lax.fori_loop(0, planes // rows_step, chunk, 0)
+            vel_ref[f, rows, :] = u[f]
+        for at, part in enumerate((u[0], hoop_rate, u[2]) + parts):
+            if at == 3:
+                part = part + hoop_rate
+            if at - 6 in DIAGONAL:
+                part = part - rest
+            flow_ref[at, rows, :] = part
+
+    row_chunks(planes, rows_step, chunk)
+
+
+def halo_body(
+    below_ref, above_ref, vel_ref, own_ref, high_ref, low_ref, halos_ref, places_ref,
+    flow_ref, values,
+):
+    planes = high_ref.shape[1]
+    quarter = planes // 4
+    edges = []
+    for ref in (below_ref, above_ref):
+        last = None
+        for number in range(3):
+            part = split(ref[number * quarter : (number + 1) * quarter, :])
+            part = dot(part[0], places_ref[number]) + dot(part[1], places_ref[number])
+            last = part if last is None else last + part
+        edges.append(jnp.concatenate([ref[...], last], axis=0))
+    values[...] = dot3(
+        (high_ref[...], low_ref[...]), split(jnp.concatenate(edges, axis=1))
+    )
+    rows_step = 128
+
+    def chunk(start):
+        rows = pl.ds(start, rows_step)
+        turned = pl.ds(pl.multiple_of(planes + start, rows_step), rows_step)
+        edge, edge_dth = split(values[rows, :]), split(values[turned, :])
+        g_r = [dot3(edge, matrix_of(halos_ref, f)) for f in range(3)]
+        g_z = [dot3(edge, matrix_of(halos_ref, 3 + f)) for f in range(3)]
+        g_t = [dot3(edge_dth, matrix_of(halos_ref, 6 + f)) for f in range(3)]
+        g_t[0] = g_t[0] - dot3(edge, matrix_of(halos_ref, 7))
+        g_t[1] = g_t[1] + dot3(edge, matrix_of(halos_ref, 6))
+        u = [vel_ref[f, rows, :] for f in range(3)]
+        for at in range(3):
+            flow_ref[at, rows, :] = own_ref[at, rows, :]
+        for at, part in enumerate(flow_parts(g_r, g_t, g_z, u)):
+            flow_ref[3 + at, rows, :] = own_ref[3 + at, rows, :] + part
+
+    row_chunks(planes, rows_step, chunk)
 
 
 def square(m):
@@ -434,25 +510,38 @@
     lax.fori_loop(0, planes // rows_step, chunk, 0)
 
 
+def transform(high_ref, low_ref, rows, coef_h, coef_l, out_ref):
+    table = (high_ref[rows, :], low_ref[rows, :])
+    for start, stop in ((0, 2), (2, 3)):
+        lanes = slice(start * BLOCK, stop * BLOCK)
+        values = dot3(table, (coef_h[:, lanes], coef_l[:, lanes]))
+        for at in range(start, stop):
+            out_ref[at] = values[:, lanes_of(at - start)]
+
+
+def values_body(route, count, me_ref, *refs):
+    psi_refs, (high_ref, low_ref, coef_h, coef_l, psi_out) = refs[:count], refs[count:]
+    route.load(me_ref, psi_refs, coef_h, coef_l)
+    transform(high_ref, low_ref, slice(0, high_ref.shape[1]), coef_h, coef_l, psi_out)
+
+
 def momentum_body(route, count, out_route, out_count, me_ref, *refs):
     psi_refs, refs = refs[:count], refs[count:]
-    flow_ref, high_ref, low_ref, back_high_ref, back_low_ref, both_ref, inv_r_ref = refs[:7]
-    out_refs, refs = refs[7 : 7 + out_count], refs[7 + out_count :]
+    first_ref, flow_ref, high_ref, low_ref, back_high_ref, back_low_ref, both_ref, inv_r_ref = (
+        refs[:8]
+    )
+    out_refs, refs = refs[8 : 8 + out_count], refs[8 + out_count :]
     coef_h, coef_l, psi_out, conform_out, stress_h, stress_l, vel_h, vel_l, mom_s, coeffs = refs
     planes = high_ref.shape[1]
     route.load(me_ref, psi_refs, coef_h, coef_l)
-    table = (high_ref[:planes, :], low_ref[:planes, :])
-    for pair in range(3):
-        lanes = slice(2 * pair * BLOCK, (2 * pair + 2) * BLOCK)
-        values = dot3(table, (coef_h[:, lanes], coef_l[:, lanes]))
-        for at in range(2):
-            psi_out[2 * pair + at] = values[:, lanes_of(at)]
+    transform(high_ref, low_ref, slice(0, planes), coef_h, coef_l, psi_out)
     rows_step = 16
 
     def chunk(start):
         rows = pl.ds(start, rows_step)
         inv_r = inv_r_ref[0:1, :]
-        conform = exponential(tuple(psi_out[member, rows, :] for member in range(6)), 1.0)
+        psi = [ref[member, rows, :] for ref in (first_ref, psi_out) for member in range(3)]
+        conform = exponential(psi, 1.0)
         for member in range(6):
             conform_out[member, rows, :] = conform[member]
         stress = tuple(v - 1.0 if at in DIAGONAL else v for at, v in enumerate(conform))
@@ -482,32 +571,28 @@
         out_route.store(me_ref, out_refs, field, coeffs.at[:, lanes_of(field)])
 
 
-def elastic_body(first_route, first_count, second_route, second_count, me_ref, *refs):
+def elastic_body(route, me_ref, *refs):
     (
-        coef_h, coef_l, psi_ref, conform_ref, flow_ref, high_ref, low_ref,
-        back_high_ref, back_low_ref, both_ref,
-    ) = refs[:10]
-    first_refs, refs = refs[10 : 10 + first_count], refs[10 + first_count :]
-    second_refs, refs = refs[:second_count], refs[second_count:]
-    dth_s, grad_s, rate_h, rate_l, coeffs = refs
+        first_h, first_l, second_h, second_l, first_ref, second_ref, conform_ref, flow_ref,
+        high_ref, low_ref, back_high_ref, back_low_ref, both_ref,
+    ) = refs[:13]
+    out_ref, dth_s, grad_s, rate_h, rate_l, coeffs = refs[13:]
     planes = high_ref.shape[1]
-    table = (high_ref[planes:, :], low_ref[planes:, :])
-    for pair in range(3):
-        lanes = slice(2 * pair * BLOCK, (2 * pair + 2) * BLOCK)
-        values = dot3(table, (coef_h[:, lanes], coef_l[:, lanes]))
-        for at in range(2):
-            dth_s[2 * pair + at] = values[:, lanes_of(at)]
+    turned = slice(planes, 2 * planes)
+    transform(high_ref, low_ref, turned, first_h, first_l, dth_s.at[pl.ds(0, 3)])
+    transform(high_ref, low_ref, turned, second_h, second_l, dth_s.at[pl.ds(3, 3)])
     gradient = tuple(
         jnp.concatenate([both_ref[at], both_ref[2 + at]], axis=1) for at in range(2)
     )
     for member in range(6):
-        grad_s[member] = dot3(split(psi_ref[member]), gradient)
+        psi_ref = first_ref if member < 3 else second_ref
+        grad_s[member] = dot3(split(psi_ref[member % 3]), gradient)
     rows_step = 16
     inv_relax = 1.0 / RELAX_TIME
 
     def chunk(start):
         rows = pl.ds(start, rows_step)
-        psi = tuple(psi_ref[member, rows, :] for member in range(6))
+        psi = [ref[member, rows, :] for ref in (first_ref, second_ref) for member in range(3)]
         inverse = exponential(psi, -1.0)
         u_r, hoop_rate, u_z, p, q, s = (flow_ref[at, rows, :] for at in range(6))
         a, b, c, d, e, f = psi
@@ -537,22 +622,19 @@
     for pair in range(3):
         lanes = slice(2 * pair * BLOCK, (2 * pair + 2) * BLOCK)
         coeffs[:, lanes] = dot3(back, (rate_h[:, lanes], rate_l[:, lanes]))
-    for field in range(3):
-        first_route.store(me_ref, first_refs, field, coeffs.at[:, lanes_of(field)])
-        second_route.store(me_ref, second_refs, field, coeffs.at[:, lanes_of(3 + field)])
-
-
-def advance_body(layers, step, route, count, start, is_velocity, aliased, *refs):
+    for field in range(6):
+        route.store(me_ref, [out_ref], field, coeffs.at[:, lanes_of(field)])
+
+
+def advance_body(layers, step, route, count, *refs):
     me_ref, orient_ref, wall_ref = refs[:3]
-    rate_refs, refs = refs[3 : 3 + count], refs[3 + count :]
-    mean_ref, old_ref = refs[:2]
-    out_ref, rates = refs[2 + aliased :]
+    rate_refs, (mean_ref, old_ref, out_ref, rates) = refs[3 : 3 + count], refs[3 + count :]
     fields, local_modes = old_ref.shape[0], old_ref.shape[1]
 
     @pl.when(pl.program_id(0) == 0)
     def _():
         for array, place, rel in route.land:
-            rates[route.index(me_ref, rel)] = rate_refs[array][place, start : start + fields]
+            rates[route.index(me_ref, rel)] = rate_refs[array][place]
 
     first = pl.program_id(0) * step
     merged = local_modes % 8 == 0
@@ -578,48 +660,36 @@
         else:
             change = [averaged(index, at, f) for f in range(fields)]
         shape = (local_modes, BLOCK)
-        column = places(orient_ref, index, shape) % RADIAL
+        column = places(orient_ref, index, shape) & (RADIAL - 1)
         inner = column == 0
         on_wall = jnp.logical_or(inner, column == RADIAL - 1)
         mean_row = jnp.logical_and(lax.broadcasted_iota(jnp.int32, shape, 0) == 0, inner)
         driven = jnp.where(mean_row, wall_ref[0], 0.0)
         for field in range(fields):
             stepped = old_ref[field, :, lanes] + STEP_DT * change[field]
-            if is_velocity:
+            if fields == 3:
                 stepped = jnp.where(on_wall, driven if field == 1 else 0.0, stepped)
             out_ref[field, :, lanes] = stepped
 
 
-def whole_block(array):
-    return pl.BlockSpec(array.shape, lambda i: (0,) * array.ndim)
-
-
-def advance(rates, start, route, weights, old, half, into, me, orientation, wall):
-    _, local_modes, nodes = old.shape
+def advance(rates, route, weights, old, me, orientation, wall):
+    fields, local_modes, nodes = old.shape
     layers = nodes // BLOCK
     step = 4
-    fields = 3
-    aliased = 0 if into is None else 1
-    block = pl.BlockSpec((fields, local_modes, step * BLOCK), lambda i: (half, 0, i))
+    block = pl.BlockSpec((fields, local_modes, step * BLOCK), lambda i: (0, 0, i))
     scalar = pl.BlockSpec(memory_space=pltpu.SMEM)
-    is_velocity = old.shape[0] == fields
-    operands = [me, orientation, wall, *rates, weights, old] + ([into] if aliased else [])
     return pl.pallas_call(
-        functools.partial(
-            advance_body, layers, step, route, len(rates), start, is_velocity, aliased
-        ),
+        functools.partial(advance_body, layers, step, route, len(rates)),
         grid=(layers // step,),
         in_specs=[scalar] * 3
-        + [whole_block(part) for part in rates]
-        + [pl.BlockSpec((step, 3 * BLOCK, BLOCK), lambda i: (i, 0, 0)), block]
-        + [pl.BlockSpec(memory_space=pl.ANY)] * aliased,
+        + [pl.BlockSpec(part.shape, lambda i: (0, 0, 0, 0)) for part in rates]
+        + [pl.BlockSpec((step, 3 * BLOCK, BLOCK), lambda i: (i, 0, 0)), block],
         out_specs=block,
         out_shape=jax.ShapeDtypeStruct(old.shape, F32),
         scratch_shapes=[pltpu.VMEM((layers, fields, local_modes, BLOCK), F32)],
-        input_output_aliases={len(operands) - 1: 0} if aliased else {},
         compiler_params=pltpu.CompilerParams(vmem_limit_bytes=24 * MIB),
         name="advance",
-    )(*operands)
+    )(me, orientation, wall, *rates, weights, old)
 
 
 def body(velocity, log_conf, orientation, wall_speed):
@@ -631,6 +701,7 @@
     planes = local_modes * devices
     far_first = Route(devices, local_modes, True)
     near_first = Route(devices, local_modes, False)
+    whole = Route(devices, local_modes, False, False)
     barrier = lax.optimization_barrier
     staged = far_first.staged
     both, faces, halos, means, inv_r_nodes = node_tables()
@@ -647,7 +718,7 @@
         order_body,
         (
             jax.ShapeDtypeStruct((10, BLOCK, BLOCK), BF16),
-            jax.ShapeDtypeStruct((6, BLOCK, 2 * BLOCK), BF16),
+            jax.ShapeDtypeStruct((24, BLOCK, 2 * BLOCK), BF16),
             jax.ShapeDtypeStruct((18, 2 * BLOCK, BLOCK), BF16),
             jax.ShapeDtypeStruct((8, BLOCK), F32),
         ),
@@ -656,20 +727,31 @@
         vmem=16,
         name="order",
     )(me, orientation, parts(both), parts(faces), parts(halos), inv_r_table)
-    weights = mean_weights(orientation, jnp.asarray(means, BF16), layers)
+    weights = kernel_call(
+        functools.partial(weights_body, layers),
+        jax.ShapeDtypeStruct((layers, 3 * BLOCK, BLOCK), BF16),
+        1,
+        vmem=8 + layers // 8,
+        name="weights",
+    )(orientation, jnp.asarray(means, BF16))
 
     vel_nodes, psi_nodes = pack(me, (velocity, log_conf), (far_first, near_first))
+    fixed = (both_s, faces_s, halos_s, inv_r, weights)
     if staged:
-        vel_nodes, psi_nodes, (both_s, faces_s, halos_s, inv_r) = barrier(
-            (far_swaps(vel_nodes), near_swaps(psi_nodes), (both_s, faces_s, halos_s, inv_r))
-        )
-        psi_nodes = far_swaps(regroup(psi_nodes))
+        psi_nodes = near_swaps(psi_nodes)
+        vel_nodes = far_swaps(vel_nodes, psi_nodes)
+        vel_nodes, psi_nodes, fixed = barrier((vel_nodes, psi_nodes, fixed))
         vel_nodes = near_swaps(regroup(vel_nodes))
+        first_nodes = far_swaps(regroup([group[:, :3] for group in psi_nodes]), vel_nodes)
+        second_nodes = regroup([group[:, 3:] for group in psi_nodes])
     else:
         vel_nodes = far_first.unpacked(in_one(vel_nodes))
         psi_nodes = near_first.unpacked(in_one(psi_nodes))
-
-    edge = jax.ShapeDtypeStruct((planes, BLOCK), F32)
+        first_nodes = [group[:, :3] for group in psi_nodes]
+        second_nodes = [group[:, 3:] for group in psi_nodes]
+
+    both_s, faces_s, halos_s, inv_r, weights = fixed
+    edge = jax.ShapeDtypeStruct((planes // 4 * 3, BLOCK), F32)
     vel_half = jax.ShapeDtypeStruct((planes, 3 * BLOCK), BF16)
     to_up, to_down, vel_h, vel_l = kernel_call(
         functools.partial(face_body, far_first, len(vel_nodes)),
@@ -682,28 +764,50 @@
     below = lax.ppermute(to_up, "mode", up)
     above = lax.ppermute(to_down, "mode", [(j, i) for i, j in up])
 
-    flow = kernel_call(
+    if staged:
+        second_nodes, below, above = barrier((second_nodes, below, above))
+        second_nodes = far_swaps(second_nodes)
+
+    vel, own_flow = kernel_call(
         velocity_body,
-        jax.ShapeDtypeStruct((15, planes, BLOCK), F32),
-        9,
+        (
+            jax.ShapeDtypeStruct((3, planes, BLOCK), F32),
+            jax.ShapeDtypeStruct((15, planes, BLOCK), F32),
+        ),
+        6,
         scalars=0,
-        scratch=[pltpu.VMEM((2 * planes, 5 * BLOCK), F32)],
+        scratch=[pltpu.VMEM((2 * planes, 3 * BLOCK), F32)],
         vmem=20,
         name="velocity",
-    )(vel_h, vel_l, below, above, high, low, both_s, halos_s, inv_r)
-
-    def leaves(route):
-        return route.outs(route.leave, 3, route.modes, BLOCK)
-
-    far_outs, near_outs = leaves(far_first), leaves(near_first)
-    psi_half = jax.ShapeDtypeStruct((planes, 6 * BLOCK), BF16)
+    )(vel_h, vel_l, high, low, both_s, inv_r)
+    flow = kernel_call(
+        halo_body,
+        jax.ShapeDtypeStruct((15, planes, BLOCK), F32),
+        8,
+        scalars=0,
+        scratch=[pltpu.VMEM((2 * planes, 2 * BLOCK), F32)],
+        vmem=20,
+        name="halo",
+    )(below, above, vel, own_flow, high, low, halos_s, jnp.asarray(free_places(), BF16))
+
+    far_outs = far_first.outs(far_first.leave, 3, far_first.modes, BLOCK)
+    psi_outs = whole.outs(whole.leave, 6, whole.modes, BLOCK)
+    half = jax.ShapeDtypeStruct((planes, 3 * BLOCK), BF16)
+    field3 = jax.ShapeDtypeStruct((3, planes, BLOCK), F32)
     field6 = jax.ShapeDtypeStruct((6, planes, BLOCK), F32)
-    *vel_rates, psi_h, psi_l, psi, conform = kernel_call(
+    first_h, first_l, first = kernel_call(
+        functools.partial(values_body, near_first, len(first_nodes)),
+        (half, half, field3),
+        len(first_nodes) + 2,
+        vmem=10,
+        name="values",
+    )(me, *first_nodes, high, low)
+    *vel_rates, second_h, second_l, second, conform = kernel_call(
         functools.partial(
-            momentum_body, near_first, len(psi_nodes), far_first, len(far_outs)
+            momentum_body, near_first, len(second_nodes), far_first, len(far_outs)
         ),
-        (*far_outs, psi_half, psi_half, field6, field6),
-        len(psi_nodes) + 7,
+        (*far_outs, half, half, field3, field6),
+        len(second_nodes) + 8,
         scratch=[
             pltpu.VMEM((planes, 6 * BLOCK), BF16),
             pltpu.VMEM((planes, 6 * BLOCK), BF16),
@@ -714,14 +818,12 @@
         ],
         vmem=24,
         name="momentum",
-    )(me, *psi_nodes, flow, high, low, back_high, back_low, both_s, inv_r)
+    )(me, *second_nodes, first, flow, high, low, back_high, back_low, both_s, inv_r)
     vel_rates = far_first.packed(vel_rates)
     psi_rates = kernel_call(
-        functools.partial(
-            elastic_body, far_first, len(far_outs), near_first, len(near_outs)
-        ),
-        (*far_outs, *near_outs),
-        10,
+        functools.partial(elastic_body, whole),
+        (*psi_outs,),
+        13,
         scratch=[
             pltpu.VMEM((6, planes, BLOCK), F32),
             pltpu.VMEM((6, planes, 2 * BLOCK), F32),
@@ -731,31 +833,22 @@
         ],
         vmem=24,
         name="elastic",
-    )(me, psi_h, psi_l, psi, conform, flow, high, low, back_high, back_low, both_s)
-
-    first_rates = far_first.packed(psi_rates[: len(far_outs)])
-    second_rates = near_first.packed(psi_rates[len(far_outs) :])
+    )(
+        me, first_h, first_l, second_h, second_l, first, second, conform, flow, high, low,
+        back_high, back_low, both_s,
+    )
+
+    psi_rates = whole.packed(psi_rates)
     if staged:
-        vel_rates, first_rates, second_rates = barrier(
-            (far_swaps(vel_rates), first_rates, second_rates)
-        )
-        joined = [
-            jnp.concatenate(pair, axis=1) for pair in zip(regroup(vel_rates), second_rates)
-        ]
-        first_rates, vel_rates, weights = barrier(
-            (far_swaps(first_rates), near_swaps(joined), weights)
-        )
-        second_rates = far_swaps(regroup([group[:, 3:] for group in vel_rates]))
-        first_rates = near_swaps(regroup(first_rates))
+        vel_rates, psi_rates = barrier((far_swaps(vel_rates), psi_rates))
+        vel_rates = near_swaps(turn(vel_rates))
     else:
-        vel_rates, first_rates, second_rates = (
-            in_one(rates) for rates in (vel_rates, first_rates, second_rates)
-        )
+        vel_rates = in_one(vel_rates)
+    psi_rates = in_one(psi_rates)
     wall = jnp.where(device == 0, wall_speed, 0.0)
-    fixed = (me, orientation, wall)
-    vel_next = advance(vel_rates, 0, far_first, weights, velocity, 0, None, *fixed)
-    logc_next = advance(first_rates, 0, far_first, weights, log_conf, 0, None, *fixed)
-    logc_next = advance(second_rates, 0, near_first, weights, log_conf, 1, logc_next, *fixed)
+    at_walls = (me, orientation, wall)
+    vel_next = advance(vel_rates, far_first, weights, velocity, *at_walls)
+    logc_next = advance(psi_rates, whole, weights, log_conf, *at_walls)
     return vel_next, logc_next
 
 

time: 148 us -> 142 us (0.959)
  the two profiles are of different devices: /device:TPU:0 before, /device:TPU:13 now
where the time goes in v2:
time: 142 us; the launch traced here: 141 us
  waiting for transfers between devices  60 us (42%)
  Pallas kernels  45.4 us (32%)
  starting transfers between devices  28.6 us (20%)
  local copies, waits for them, and re-layouts  5.49 us (4%)
  between operations  1.69 us (1%)
    ppermute x21, waiting for transfers between devices, swap(): return lax.ppermute(block, 'mode', [(i, i ^ bits) for i in range(devices)])  43.4 us
    ppermute x21, starting transfers between devices, swap(): return lax.ppermute(block, 'mode', [(i, i ^ bits) for i in range(devices)])  19.8 us
    pallas_call x1, Pallas kernels, body(): kernel_call(functools.partial(elastic_body, whole), (*psi_outs,), 13, scr...  9.42 us
    all_to_all x1, waiting for transfers between devices, in_one(): lax.all_to_all(arrays[0], 'mode', split_axis=0, concat_axis=0, tiled=True)  8.82 us
    pallas_call x2, Pallas kernels, advance(): pl.pallas_call(functools.partial(advance_body, layers, step, route, len(r...  7.62 us
    ppermute x1, waiting for transfers between devices, body(): above = lax.ppermute(to_down, 'mode', [(j, i) for i, j in up])  7.24 us
    pallas_call x1, Pallas kernels, body(): kernel_call(functools.partial(momentum_body, near_first, len(second_nodes...  6.08 us
    all_to_all x1, starting transfers between devices, in_one(): lax.all_to_all(arrays[0], 'mode', split_axis=0, concat_axis=0, tiled=True)  5.95 us
  transfers between devices with their start and end apart: 24, of which 13 were waited for; matrix products, arithmetic and copies ran while one was open for 0% of the time, Pallas kernels for 22%

profile of v2, /device:TPU:13, one launch (start us, length us, event | category | flops | bytes accessed | tf_op | source)
XLA Modules:
  0.0 141.4 jit_solution(15712196147396921557)
XLA Ops:
  0.7 3.5 %pack.1 = (f32[4,3,32,128]{3,2,1,0:T(8,128)}, f32[4,3,32,128]{3,2,1,0:T(8,128)}, f32[4,3,32,128]{3,2,1,0:T(8,128)}, f32[4,3,32,128]{3,2,1,0:T(8,128)}, f32[4,6,3...) custom-call(s32[1]{0:T(128)} %bitcast.me_ref.refs_0_, ...), custom_call_target="tpu_custom_call" | custom-call | tf_op jit(solution)/shard_map/pack/pallas_call | solution.py:280
  4.2 0.7 collective-permute-start
  5.0 0.2 collective-permute-start.4
  5.2 1.5 %collective-permute-start.5 = (f32[4,6,32,128]{3,2,1,0:T(8,128)}, f32[4,6,32,128]{3,2,1,0:T(8,128)S(1)}, u32[]{:S(2)}, u32[]{:S(2)}) collective-permute-start(f32[4,6,32,128]{3,2,1,0:T(8,128)} %get-tuple-element.69), channel_id=1, source_target_pairs={{0,3},{1,2},{2,1},{3,0},{4,7},{5,6},{6,5},{7,4},{8,11},{9,10},{10,... | collective-permute-start | bytes 1179656 | tf_op jit(solution)/shard_map/ppermute | solution.py:160
  6.7 2.3 %collective-permute-start.2 = (f32[4,3,32,128]{3,2,1,0:T(8,128)}, f32[4,3,32,128]{3,2,1,0:T(8,128)S(1)}, u32[]{:S(2)}, u32[]{:S(2)}) collective-permute-start(f32[4,3,32,128]{3,2,1,0:T(8,128)} %get-tuple-element.65), channel_id=1, source_target_pairs={{0,8},{1,9},{2,10},{3,11},{4,12},{5,13},{6,14},{7,15},{8,0},{9,1},... | collective-permute-start | bytes 589832 | tf_op jit(solution)/shard_map/ppermute | solution.py:160
  9.0 1.2 collective-permute-start.1
  10.3 0.9 copy-done.14
  11.1 5.8 %weights.1.refs_7_.refs_4_ = bf16[16,384,128]{2,1,0:T(8,128)(2,1)S(1)} custom-call(s32[32]{0:T(128)S(1)} %copy-done.16, bf16[3,128,128]{2,1,0:T(8,128)(2,1)S(1)} %copy-done.14), custom_call_target="tpu_custom_call" | custom-call | tf_op jit(solution)/shard_map/weights/pallas_call | solution.py:730
  17.0 1.7 %order.1 = (bf16[10,128,128]{2,1,0:T(8,128)(2,1)S(1)}, bf16[24,128,256]{2,1,0:T(8,128)(2,1)S(1)}, bf16[18,256,128]{2,1,0:T(8,128)(2,1)S(1)}, f32[8,128]{1,0:T(8,128)S(1)}) custom-call(s32[1]{0:T(128)} %bitcast.me_ref.refs_0_, s32[32]{0:T(128)S(1)} %copy-done.16, bf16[10,128,128]{2,1,0:T(8,128)(2,1)S(1)} %copy-done.8, bf16[24,128,256]{2,1,0:T(8,128)(2,1)S(1)} %copy-done.6, ...), custom_call_target="tpu_custom_call" | custom-call | tf_op jit(solution)/shard_map/order/pallas_call | solution.py:717
  18.7 3.6 %collective-permute-done.2 = f32[4,3,32,128]{3,2,1,0:T(8,128)S(1)} collective-permute-done((f32[4,3,32,128]{3,2,1,0:T(8,128)}, f32[4,3,32,128]{3,2,1,0:T(8,128)S(1)}, u32[]{:S(2)}, u32[]{:S(2)}) %collective-permute-start.2) | collective-permute-done | bytes 196640 | tf_op jit(solution)/shard_map/ppermute | solution.py:160
  22.3 4.2 %collective-permute-done.3 = f32[4,3,32,128]{3,2,1,0:T(8,128)S(1)} collective-permute-done((f32[4,3,32,128]{3,2,1,0:T(8,128)}, f32[4,3,32,128]{3,2,1,0:T(8,128)S(1)}, u32[]{:S(2)}, u32[]{:S(2)}) %collective-permute-start.3) | collective-permute-done | bytes 196640 | tf_op jit(solution)/shard_map/ppermute | solution.py:160
  26.7 0.6 collective-permute-start.8
  27.3 1.3 collective-permute-start.7
  28.6 0.4 collective-permute-start.6
  29.2 2.2 %collective-permute-start.16 = (f32[4,3,32,128]{3,2,1,0:T(8,128)S(1)}, f32[4,3,32,128]{3,2,1,0:T(8,128)S(1)}, u32[]{:S(2)}, u32[]{:S(2)}) collective-permute-start(f32[4,3,32,128]{3,2,1,0:T(8,128)S(1)} %pad_maximum_fusion.11), channel_id=1, source_target_pairs={{0,12},{1,13},{2,14},{3,15},{4,8},{5,9},{6,10},{7,11},{8,4},{9,5},... | collective-permute-start | bytes 589832 | tf_op jit(solution)/shard_map/ppermute | solution.py:160
  31.6 2.6 %collective-permute-done.8.refs_3_ = f32[4,3,32,128]{3,2,1,0:T(8,128)S(1)} collective-permute-done((f32[4,3,32,128]{3,2,1,0:T(8,128)S(1)}, f32[4,3,32,128]{3,2,1,0:T(8,128)S(1)}, u32[]{:S(2)}, u32[]{:S(2)}) %collective-permute-start.8) | collective-permute-done | bytes 196640 | tf_op jit(solution)/shard_map/ppermute | solution.py:160
  34.2 3.7 %collective-permute-done.7.refs_2_ = f32[4,3,32,128]{3,2,1,0:T(8,128)S(1)} collective-permute-done((f32[4,3,32,128]{3,2,1,0:T(8,128)S(1)}, f32[4,3,32,128]{3,2,1,0:T(8,128)S(1)}, u32[]{:S(2)}, u32[]{:S(2)}) %collective-permute-start.7) | collective-permute-done | bytes 196640 | tf_op jit(solution)/shard_map/ppermute | solution.py:160
  38.0 1.2 faces.1
  39.2 0.7 collective-permute-start.10
  39.9 2.2 %collective-permute-start.9 = (f32[384,128]{1,0:T(8,128)S(1)}, f32[384,128]{1,0:T(8,128)S(1)}, u32[]{:S(2)}, u32[]{:S(2)}) collective-permute-start(f32[384,128]{1,0:T(8,128)S(1)} %get-tuple-element.83), channel_id=1, source_target_pairs={{0,1},{1,2},{2,3},{3,4},{4,5},{5,6},{6,7},{7,8},{8,9},{9,10},{10,1... | collective-permute-start | bytes 589832 | tf_op jit(solution)/shard_map/ppermute | solution.py:764
  42.2 7.2 %collective-permute-done.10.above_ref = f32[384,128]{1,0:T(8,128)S(1)} collective-permute-done((f32[384,128]{1,0:T(8,128)S(1)}, f32[384,128]{1,0:T(8,128)S(1)}, u32[]{:S(2)}, u32[]{:S(2)}) %collective-permute-start.10) | collective-permute-done | bytes 196640 | tf_op jit(solution)/shard_map/ppermute | solution.py:765
  49.4 0.5 collective-permute-done.9.below_ref
  49.9 4.2 %collective-permute-start.12 = (f32[4,3,32,128]{3,2,1,0:T(8,128)S(1)}, f32[4,3,32,128]{3,2,1,0:T(8,128)S(1)}, u32[]{:S(2)}, u32[]{:S(2)}) collective-permute-start(f32[4,3,32,128]{3,2,1,0:T(8,128)S(1)} %pad_maximum_fusion.2), channel_id=1, source_target_pairs={{0,8},{1,9},{2,10},{3,11},{4,12},{5,13},{6,14},{7,15},{8,0},{9,1},... | collective-permute-start | bytes 589832 | tf_op jit(solution)/shard_map/ppermute | solution.py:160
  54.2 3.6 %velocity.1 = (f32[3,512,128]{2,1,0:T(8,128)S(1)}, f32[15,512,128]{2,1,0:T(8,128)S(1)}) custom-call(bf16[512,384]{1,0:T(8,128)(2,1)S(1)} %get-tuple-element.93.vel_h, bf16[512,384]{1,0:T(8,128)(2,1)S(1)} %get-tuple-element.94.vel_l, bf16[1024,512]{1,0:T(8,128)(2,1)S(1)} %copy-done, bf16[1024,512]{1,0:T(8,128)(2,1)S(1)} %copy-done.1, ...), custom_call_target="tpu_custom_call" | custom-call | tf_op jit(solution)/shard_map/velocity/pallas_call | solution.py:771
  57.8 4.2 %halo.1.refs_5_.refs_7_ = f32[15,512,128]{2,1,0:T(8,128)S(1)} custom-call(f32[384,128]{1,0:T(8,128)S(1)} %collective-permute-done.9.below_ref, f32[384,128]{1,0:T(8,128)S(1)} %collective-permute-done.10.above_ref, f32[3,512,128]{2,1,0:T(8,128)S(1)} %get-tuple-element.97.vel_ref, f32[15,512,128]{2,1,0:T(8,128)S(1)} %get-tuple-element.98.own_ref, ...), custom_call_target="tpu_custom_call" | custom-call | tf_op jit(solution)/shard_map/halo/pallas_call | solution.py:783
  62.1 1.1 values.1
  63.2 2.2 %collective-permute-done.12.refs_2_ = f32[4,3,32,128]{3,2,1,0:T(8,128)S(1)} collective-permute-done((f32[4,3,32,128]{3,2,1,0:T(8,128)S(1)}, f32[4,3,32,128]{3,2,1,0:T(8,128)S(1)}, u32[]{:S(2)}, u32[]{:S(2)}) %collective-permute-start.12) | collective-permute-done | bytes 196640 | tf_op jit(solution)/shard_map/ppermute | solution.py:160
  65.3 3.2 %collective-permute-done.13.refs_3_ = f32[4,3,32,128]{3,2,1,0:T(8,128)S(1)} collective-permute-done((f32[4,3,32,128]{3,2,1,0:T(8,128)S(1)}, f32[4,3,32,128]{3,2,1,0:T(8,128)S(1)}, u32[]{:S(2)}, u32[]{:S(2)}) %collective-permute-start.13) | collective-permute-done | bytes 196640 | tf_op jit(solution)/shard_map/ppermute | solution.py:160
  68.6 6.1 %momentum.1 = (f32[4,3,32,128]{3,2,1,0:T(8,128)S(1)}, f32[4,3,32,128]{3,2,1,0:T(8,128)S(1)}, f32[4,3,32,128]{3,2,1,0:T(8,128)S(1)}, f32[4,3,32,128]{3,2,1,0:T(8,...) custom-call(s32[1]{0:T(128)} %bitcast.me_ref.refs_0_, ...), custom_call_target="tpu_custom_call" | custom-call | tf_op jit(solution)/shard_map/momentum/pallas_call | solution.py:805
  74.7 2.5 %collective-permute-start.18 = (f32[4,3,32,128]{3,2,1,0:T(8,128)S(1)}, f32[4,3,32,128]{3,2,1,0:T(8,128)S(1)}, u32[]{:S(2)}, u32[]{:S(2)}) collective-permute-start(f32[4,3,32,128]{3,2,1,0:T(8,128)S(1)} %get-tuple-element.102), channel_id=1, source_target_pairs={{0,8},{1,9},{2,10},{3,11},{4,12},{5,13},{6,14},{7,15},{8,0},{9,1},... | collective-permute-start | bytes 589832 | tf_op jit(solution)/shard_map/ppermute | solution.py:160
  77.4 9.4 %elastic.1 = f32[16,6,32,128]{3,2,1,0:T(8,128)} custom-call(s32[1]{0:T(128)} %bitcast.me_ref.refs_0_, bf16[512,384]{1,0:T(8,128)(2,1)S(1)} %get-tuple-element.104.refs_0_, bf16[512,384]{1,0:T(8,128)(2,1)S(1)} %get-tuple-element.105.refs_1_, bf16[512,384]{1,0:T(8,128)(2,1)S(1)} %get-tuple-element.106.refs_2_, ...), custom_call_target="tpu_custom_call" | custom-call | tf_op jit(solution)/shard_map/elastic/pallas_call | solution.py:823
  86.8 3.6 %collective-permute-done.18.refs_2_ = f32[4,3,32,128]{3,2,1,0:T(8,128)S(1)} collective-permute-done((f32[4,3,32,128]{3,2,1,0:T(8,128)S(1)}, f32[4,3,32,128]{3,2,1,0:T(8,128)S(1)}, u32[]{:S(2)}, u32[]{:S(2)}) %collective-permute-start.18) | collective-permute-done | bytes 196640 | tf_op jit(solution)/shard_map/ppermute | solution.py:160
  90.4 4.1 %collective-permute-done.19.refs_3_ = f32[4,3,32,128]{3,2,1,0:T(8,128)S(1)} collective-permute-done((f32[4,3,32,128]{3,2,1,0:T(8,128)S(1)}, f32[4,3,32,128]{3,2,1,0:T(8,128)S(1)}, u32[]{:S(2)}, u32[]{:S(2)}) %collective-permute-start.19) | collective-permute-done | bytes 196640 | tf_op jit(solution)/shard_map/ppermute | solution.py:160
  94.6 6.0 %all-to-all-start = ((f32[16,6,32,128]{3,2,1,0:T(8,128)}), f32[16,6,32,128]{3,2,1,0:T(8,128)}, u32[]{:S(2)}, u32[]{:S(2)}) async-start(f32[16,6,32,128]{3,2,1,0:T(8,128)} %elastic.1), calls=%async_computation | async-start | bytes 3145728 | tf_op jit(solution)/shard_map/all_to_all | solution.py:255
  100.5 1.2 turn.1
  101.7 0.4 collective-permute-start.20
  102.1 0.3 collective-permute-start.21
  102.4 1.5 %collective-permute-start.22 = (f32[4,3,32,128]{3,2,1,0:T(8,128)S(1)}, f32[4,3,32,128]{3,2,1,0:T(8,128)S(1)}, u32[]{:S(2)}, u32[]{:S(2)}) collective-permute-start(f32[4,3,32,128]{3,2,1,0:T(8,128)S(1)} %get-tuple-element.117), channel_id=1, source_target_pairs={{0,3},{1,2},{2,1},{3,0},{4,7},{5,6},{6,5},{7,4},{8,11},{9,10},{10,... | collective-permute-start | bytes 589832 | tf_op jit(solution)/shard_map/ppermute | solution.py:160
  104.6 9.8 %collective-permute-done.21.refs_5_ = f32[4,3,32,128]{3,2,1,0:T(8,128)S(1)} collective-permute-done((f32[4,3,32,128]{3,2,1,0:T(8,128)S(1)}, f32[4,3,32,128]{3,2,1,0:T(8,128)S(1)}, u32[]{:S(2)}, u32[]{:S(2)}) %collective-permute-start.21) | collective-permute-done | bytes 196640 | tf_op jit(solution)/shard_map/ppermute | solution.py:160
  114.4 0.7 copy-done.9
  115.1 6.2 %collective-permute-done.22.refs_6_ = f32[4,3,32,128]{3,2,1,0:T(8,128)S(1)} collective-permute-done((f32[4,3,32,128]{3,2,1,0:T(8,128)S(1)}, f32[4,3,32,128]{3,2,1,0:T(8,128)S(1)}, u32[]{:S(2)}, u32[]{:S(2)}) %collective-permute-start.22) | collective-permute-done | bytes 196640 | tf_op jit(solution)/shard_map/ppermute | solution.py:160
  121.3 0.7 copy-done.11
  122.0 1.1 copy-done.5
  123.1 0.9 copy-done.10
  124.0 0.9 copy-done.12
  125.0 3.1 %advance.2 = f32[3,32,2048]{2,1,0:T(8,128)} custom-call(s32[1]{0:T(128)} %bitcast.me_ref.refs_0_, s32[32]{0:T(128)S(1)} %copy-done.16, f32[1]{0:T(128)S(6)} %select_n.9.refs_2_, f32[4,3,32,128]{3,2,1,0:T(8,128)S(1)} %get-tuple-element.114.refs_3_, f32[4,3,32,128]{3,2,1,0:T(8,128)S(1)} %collective-permute-done.20.refs_4_, f32[4,3,32,128]{3,2,1,0:T(8,128)S(1)} %copy-done.10, ...), custom_call_target="tpu_custom_call" | custom-call | tf_op jit(solution)/shard_map/advance/pallas_call | solution.py:681
  128.1 8.8 %all-to-all-done.refs_3_ = f32[16,6,32,128]{3,2,1,0:T(8,128)} async-done(((f32[16,6,32,128]{3,2,1,0:T(8,128)}), f32[16,6,32,128]{3,2,1,0:T(8,128)}, u32[]{:S(2)}, u32[]{:S(2)}) %all-to-all-start) | async-done | bytes 1572896 | tf_op jit(solution)/shard_map/all_to_all | solution.py:255
  136.9 4.5 %advance.3 = f32[6,32,2048]{2,1,0:T(8,128)} custom-call(s32[1]{0:T(128)} %bitcast.me_ref.refs_0_, s32[32]{0:T(128)S(1)} %copy-done.16, f32[1]{0:T(128)S(6)} %select_n.9.refs_2_, f32[16,6,32,128]{3,2,1,0:T(8,128)} %all-to-all-done.refs_3_, bf16[16,384,128]{2,1,0:T(8,128)(2,1)S(1)} %weights.1.refs_7_.refs_4_, f32[6,32,2048]{2,1,0:T(8,128)S(1)} %copy-done.2), custom_call_target="tpu_custom_call" | custom-call | tf_op jit(solution)/shard_map/advance/pallas_call | solution.py:681
  (66 shorter events, 0.9 us)
Async XLA Ops:
  0.6 9.6 %copy-start.16 = (s32[32]{0:T(128)S(1)}, s32[32]{0:T(128)}, u32[]{:S(2)}) copy-start(s32[32]{0:T(128)} %refs_1_.5) | copy-start | bytes 388
  0.6 16.3 %copy-start.6 = (bf16[24,128,256]{2,1,0:T(8,128)(2,1)S(1)}, bf16[24,128,256]{2,1,0:T(8,128)(2,1)}, u32[]{:S(2)}) copy-start(bf16[24,128,256]{2,1,0:T(8,128)(2,1)} %constant.35.clone.faces_ref) | copy-start | bytes 4718596
  0.7 16.3 %copy-start.8 = (bf16[10,128,128]{2,1,0:T(8,128)(2,1)S(1)}, bf16[10,128,128]{2,1,0:T(8,128)(2,1)}, u32[]{:S(2)}) copy-start(bf16[10,128,128]{2,1,0:T(8,128)(2,1)} %constant.34.clone.both_ref) | copy-start | bytes 983044
  0.7 16.3 %copy-start.15 = (f32[128,128]{1,0:T(8,128)S(1)}, f32[128,128]{1,0:T(8,128)}, u32[]{:S(2)}) copy-start(f32[128,128]{1,0:T(8,128)} %constant.33.clone.inv_r_ref) | copy-start | bytes 196612
  4.2 12.7 %copy-start.7 = (bf16[18,256,128]{2,1,0:T(8,128)(2,1)S(1)}, bf16[18,256,128]{2,1,0:T(8,128)(2,1)}, u32[]{:S(2)}) copy-start(bf16[18,256,128]{2,1,0:T(8,128)(2,1)} %constant.36.clone.halos_ref) | copy-start | bytes 3538948
  4.2 4.8 %collective-permute-start = (f32[4,6,32,128]{3,2,1,0:T(8,128)}, f32[4,6,32,128]{3,2,1,0:T(8,128)S(1)}, u32[]{:S(2)}, u32[]{:S(2)}) collective-permute-start(f32[4,6,32,128]{3,2,1,0:T(8,128)} %get-tuple-element.63), channel_id=1, source_target_pairs={{0,1},{1,0},{2,3},{3,2},{4,5},{5,4},{6,7},{7,6},{8,9},{9,8},{10,11... | collective-permute-start | bytes 1179656 | tf_op jit(solution)/shard_map/ppermute | solution.py:160
  5.0 21.6 %collective-permute-start.4 = (f32[4,6,32,128]{3,2,1,0:T(8,128)}, f32[4,6,32,128]{3,2,1,0:T(8,128)S(1)}, u32[]{:S(2)}, u32[]{:S(2)}) collective-permute-start(f32[4,6,32,128]{3,2,1,0:T(8,128)} %get-tuple-element.68), channel_id=1, source_target_pairs={{0,2},{1,3},{2,0},{3,1},{4,6},{5,7},{6,4},{7,5},{8,10},{9,11},{10,... | collective-permute-start | bytes 1179656 | tf_op jit(solution)/shard_map/ppermute | solution.py:160
  5.2 21.3 %collective-permute-start.5 = (f32[4,6,32,128]{3,2,1,0:T(8,128)}, f32[4,6,32,128]{3,2,1,0:T(8,128)S(1)}, u32[]{:S(2)}, u32[]{:S(2)}) collective-permute-start(f32[4,6,32,128]{3,2,1,0:T(8,128)} %get-tuple-element.69), channel_id=1, source_target_pairs={{0,3},{1,2},{2,1},{3,0},{4,7},{5,6},{6,5},{7,4},{8,11},{9,10},{10,... | collective-permute-start | bytes 1179656 | tf_op jit(solution)/shard_map/ppermute | solution.py:160
  6.7 15.6 %collective-permute-start.2 = (f32[4,3,32,128]{3,2,1,0:T(8,128)}, f32[4,3,32,128]{3,2,1,0:T(8,128)S(1)}, u32[]{:S(2)}, u32[]{:S(2)}) collective-permute-start(f32[4,3,32,128]{3,2,1,0:T(8,128)} %get-tuple-element.65), channel_id=1, source_target_pairs={{0,8},{1,9},{2,10},{3,11},{4,12},{5,13},{6,14},{7,15},{8,0},{9,1},... | collective-permute-start | bytes 589832 | tf_op jit(solution)/shard_map/ppermute | solution.py:160
  9.0 17.5 %collective-permute-start.3 = (f32[4,3,32,128]{3,2,1,0:T(8,128)}, f32[4,3,32,128]{3,2,1,0:T(8,128)S(1)}, u32[]{:S(2)}, u32[]{:S(2)}) collective-permute-start(f32[4,3,32,128]{3,2,1,0:T(8,128)} %get-tuple-element.66), channel_id=1, source_target_pairs={{0,12},{1,13},{2,14},{3,15},{4,8},{5,9},{6,10},{7,11},{8,4},{9,5},... | collective-permute-start | bytes 589832 | tf_op jit(solution)/shard_map/ppermute | solution.py:160
  9.0 17.5 %collective-permute-start.1 = (f32[4,3,32,128]{3,2,1,0:T(8,128)}, f32[4,3,32,128]{3,2,1,0:T(8,128)S(1)}, u32[]{:S(2)}, u32[]{:S(2)}) collective-permute-start(f32[4,3,32,128]{3,2,1,0:T(8,128)} %get-tuple-element.64), channel_id=1, source_target_pairs={{0,4},{1,5},{2,6},{3,7},{4,0},{5,1},{6,2},{7,3},{8,12},{9,13},{10,... | collective-permute-start | bytes 589832 | tf_op jit(solution)/shard_map/ppermute | solution.py:160
  10.3 0.9 copy-start.14
  17.0 9.6 %copy-start.18 = (f32[4,3,32,128]{3,2,1,0:T(8,128)S(1)}, f32[4,3,32,128]{3,2,1,0:T(8,128)}, u32[]{:S(2)}) copy-start(f32[4,3,32,128]{3,2,1,0:T(8,128)} %get-tuple-element.78) | copy-start | bytes 589828
  18.7 10.3 %copy-start.17 = (f32[4,6,32,128]{3,2,1,0:T(8,128)S(1)}, f32[4,6,32,128]{3,2,1,0:T(8,128)}, u32[]{:S(2)}) copy-start(f32[4,6,32,128]{3,2,1,0:T(8,128)} %get-tuple-element.74) | copy-start | bytes 1179652
  26.7 7.6 %collective-permute-start.8 = (f32[4,3,32,128]{3,2,1,0:T(8,128)S(1)}, f32[4,3,32,128]{3,2,1,0:T(8,128)S(1)}, u32[]{:S(2)}, u32[]{:S(2)}) collective-permute-start(f32[4,3,32,128]{3,2,1,0:T(8,128)S(1)} %pad_maximum_fusion.7), channel_id=1, source_target_pairs={{0,3},{1,2},{2,1},{3,0},{4,7},{5,6},{6,5},{7,4},{8,11},{9,10},{10,... | collective-permute-start | bytes 589832 | tf_op jit(solution)/shard_map/ppermute | solution.py:160
  27.3 10.7 %collective-permute-start.7 = (f32[4,3,32,128]{3,2,1,0:T(8,128)S(1)}, f32[4,3,32,128]{3,2,1,0:T(8,128)S(1)}, u32[]{:S(2)}, u32[]{:S(2)}) collective-permute-start(f32[4,3,32,128]{3,2,1,0:T(8,128)S(1)} %pad_maximum_fusion.6), channel_id=1, source_target_pairs={{0,2},{1,3},{2,0},{3,1},{4,6},{5,7},{6,4},{7,5},{8,10},{9,11},{10,... | collective-permute-start | bytes 589832 | tf_op jit(solution)/shard_map/ppermute | solution.py:160
  28.6 9.3 %collective-permute-start.6 = (f32[4,3,32,128]{3,2,1,0:T(8,128)S(1)}, f32[4,3,32,128]{3,2,1,0:T(8,128)S(1)}, u32[]{:S(2)}, u32[]{:S(2)}) collective-permute-start(f32[4,3,32,128]{3,2,1,0:T(8,128)S(1)} %pad_maximum_fusion.5), channel_id=1, source_target_pairs={{0,1},{1,0},{2,3},{3,2},{4,5},{5,4},{6,7},{7,6},{8,9},{9,8},{10,11... | collective-permute-start | bytes 589832 | tf_op jit(solution)/shard_map/ppermute | solution.py:160
  29.2 24.9 %collective-permute-start.16 = (f32[4,3,32,128]{3,2,1,0:T(8,128)S(1)}, f32[4,3,32,128]{3,2,1,0:T(8,128)S(1)}, u32[]{:S(2)}, u32[]{:S(2)}) collective-permute-start(f32[4,3,32,128]{3,2,1,0:T(8,128)S(1)} %pad_maximum_fusion.11), channel_id=1, source_target_pairs={{0,12},{1,13},{2,14},{3,15},{4,8},{5,9},{6,10},{7,11},{8,4},{9,5},... | collective-permute-start | bytes 589832 | tf_op jit(solution)/shard_map/ppermute | solution.py:160
  31.4 30.7 %collective-permute-start.15 = (f32[4,3,32,128]{3,2,1,0:T(8,128)S(1)}, f32[4,3,32,128]{3,2,1,0:T(8,128)S(1)}, u32[]{:S(2)}, u32[]{:S(2)}) collective-permute-start(f32[4,3,32,128]{3,2,1,0:T(8,128)S(1)} %pad_maximum_fusion.10), channel_id=1, source_target_pairs={{0,8},{1,9},{2,10},{3,11},{4,12},{5,13},{6,14},{7,15},{8,0},{9,1},... | collective-permute-start | bytes 589832 | tf_op jit(solution)/shard_map/ppermute | solution.py:160
  31.6 22.6 %copy-start = (bf16[1024,512]{1,0:T(8,128)(2,1)S(1)}, bf16[1024,512]{1,0:T(8,128)(2,1)}, u32[]{:S(2)}) copy-start(bf16[1024,512]{1,0:T(8,128)(2,1)} %constant.29.clone.refs_4_.high_ref.refs_6_.refs_8_) | copy-start | bytes 3145732
  31.6 22.6 %copy-start.1 = (bf16[1024,512]{1,0:T(8,128)(2,1)S(1)}, bf16[1024,512]{1,0:T(8,128)(2,1)}, u32[]{:S(2)}) copy-start(bf16[1024,512]{1,0:T(8,128)(2,1)} %constant.30.clone.refs_5_.low_ref.refs_7_.refs_9_) | copy-start | bytes 3145732
  39.2 10.2 %collective-permute-start.10 = (f32[384,128]{1,0:T(8,128)S(1)}, f32[384,128]{1,0:T(8,128)S(1)}, u32[]{:S(2)}, u32[]{:S(2)}) collective-permute-start(f32[384,128]{1,0:T(8,128)S(1)} %get-tuple-element.84), channel_id=1, source_target_pairs={{1,0},{2,1},{3,2},{4,3},{5,4},{6,5},{7,6},{8,7},{9,8},{10,9},{11,1... | collective-permute-start | bytes 589832 | tf_op jit(solution)/shard_map/ppermute | solution.py:765
  39.9 10.0 %collective-permute-start.9 = (f32[384,128]{1,0:T(8,128)S(1)}, f32[384,128]{1,0:T(8,128)S(1)}, u32[]{:S(2)}, u32[]{:S(2)}) collective-permute-start(f32[384,128]{1,0:T(8,128)S(1)} %get-tuple-element.83), channel_id=1, source_target_pairs={{0,1},{1,2},{2,3},{3,4},{4,5},{5,6},{6,7},{7,8},{8,9},{9,10},{10,1... | collective-permute-start | bytes 589832 | tf_op jit(solution)/shard_map/ppermute | solution.py:764
  42.1 20.0 %collective-permute-start.14 = (f32[4,3,32,128]{3,2,1,0:T(8,128)S(1)}, f32[4,3,32,128]{3,2,1,0:T(8,128)S(1)}, u32[]{:S(2)}, u32[]{:S(2)}) collective-permute-start(f32[4,3,32,128]{3,2,1,0:T(8,128)S(1)} %pad_maximum_fusion.9), channel_id=1, source_target_pairs={{0,4},{1,5},{2,6},{3,7},{4,0},{5,1},{6,2},{7,3},{8,12},{9,13},{10,... | collective-permute-start | bytes 589832 | tf_op jit(solution)/shard_map/ppermute | solution.py:160
  49.9 13.3 %collective-permute-start.11 = (f32[4,3,32,128]{3,2,1,0:T(8,128)S(1)}, f32[4,3,32,128]{3,2,1,0:T(8,128)S(1)}, u32[]{:S(2)}, u32[]{:S(2)}) collective-permute-start(f32[4,3,32,128]{3,2,1,0:T(8,128)S(1)} %pad_maximum_fusion.1), channel_id=1, source_target_pairs={{0,4},{1,5},{2,6},{3,7},{4,0},{5,1},{6,2},{7,3},{8,12},{9,13},{10,... | collective-permute-start | bytes 589832 | tf_op jit(solution)/shard_map/ppermute | solution.py:160
  49.9 15.4 %collective-permute-start.12 = (f32[4,3,32,128]{3,2,1,0:T(8,128)S(1)}, f32[4,3,32,128]{3,2,1,0:T(8,128)S(1)}, u32[]{:S(2)}, u32[]{:S(2)}) collective-permute-start(f32[4,3,32,128]{3,2,1,0:T(8,128)S(1)} %pad_maximum_fusion.2), channel_id=1, source_target_pairs={{0,8},{1,9},{2,10},{3,11},{4,12},{5,13},{6,14},{7,15},{8,0},{9,1},... | collective-permute-start | bytes 589832 | tf_op jit(solution)/shard_map/ppermute | solution.py:160
  54.1 14.5 %collective-permute-start.13 = (f32[4,3,32,128]{3,2,1,0:T(8,128)S(1)}, f32[4,3,32,128]{3,2,1,0:T(8,128)S(1)}, u32[]{:S(2)}, u32[]{:S(2)}) collective-permute-start(f32[4,3,32,128]{3,2,1,0:T(8,128)S(1)} %pad_maximum_fusion.3), channel_id=1, source_target_pairs={{0,12},{1,13},{2,14},{3,15},{4,8},{5,9},{6,10},{7,11},{8,4},{9,5},... | collective-permute-start | bytes 589832 | tf_op jit(solution)/shard_map/ppermute | solution.py:160
  54.2 3.6 %copy-start.13 = (bf16[3,128,128]{2,1,0:T(8,128)(2,1)S(1)}, bf16[3,128,128]{2,1,0:T(8,128)(2,1)}, u32[]{:S(2)}) copy-start(bf16[3,128,128]{2,1,0:T(8,128)(2,1)} %constant.38.clone.places_ref) | copy-start | bytes 294916
  62.0 6.6 %copy-start.3 = (bf16[512,1024]{1,0:T(8,128)(2,1)S(1)}, bf16[512,1024]{1,0:T(8,128)(2,1)}, u32[]{:S(2)}) copy-start(bf16[512,1024]{1,0:T(8,128)(2,1)} %constant.31.clone.refs_8_.refs_10_) | copy-start | bytes 3145732
  62.0 6.6 %copy-start.4 = (bf16[512,1024]{1,0:T(8,128)(2,1)S(1)}, bf16[512,1024]{1,0:T(8,128)(2,1)}, u32[]{:S(2)}) copy-start(bf16[512,1024]{1,0:T(8,128)(2,1)} %constant.32.clone.refs_9_.refs_11_) | copy-start | bytes 3145732
  74.7 12.1 %collective-permute-start.17 = (f32[4,3,32,128]{3,2,1,0:T(8,128)S(1)}, f32[4,3,32,128]{3,2,1,0:T(8,128)S(1)}, u32[]{:S(2)}, u32[]{:S(2)}) collective-permute-start(f32[4,3,32,128]{3,2,1,0:T(8,128)S(1)} %get-tuple-element.101), channel_id=1, source_target_pairs={{0,4},{1,5},{2,6},{3,7},{4,0},{5,1},{6,2},{7,3},{8,12},{9,13},{10,... | collective-permute-start | bytes 589832 | tf_op jit(solution)/shard_map/ppermute | solution.py:160
  74.7 15.7 %collective-permute-start.18 = (f32[4,3,32,128]{3,2,1,0:T(8,128)S(1)}, f32[4,3,32,128]{3,2,1,0:T(8,128)S(1)}, u32[]{:S(2)}, u32[]{:S(2)}) collective-permute-start(f32[4,3,32,128]{3,2,1,0:T(8,128)S(1)} %get-tuple-element.102), channel_id=1, source_target_pairs={{0,8},{1,9},{2,10},{3,11},{4,12},{5,13},{6,14},{7,15},{8,0},{9,1},... | collective-permute-start | bytes 589832 | tf_op jit(solution)/shard_map/ppermute | solution.py:160
  77.2 17.3 %collective-permute-start.19 = (f32[4,3,32,128]{3,2,1,0:T(8,128)S(1)}, f32[4,3,32,128]{3,2,1,0:T(8,128)S(1)}, u32[]{:S(2)}, u32[]{:S(2)}) collective-permute-start(f32[4,3,32,128]{3,2,1,0:T(8,128)S(1)} %get-tuple-element.103), channel_id=1, source_target_pairs={{0,12},{1,13},{2,14},{3,15},{4,8},{5,9},{6,10},{7,11},{8,4},{9,5},... | collective-permute-start | bytes 589832 | tf_op jit(solution)/shard_map/ppermute | solution.py:160
  94.6 42.3 %all-to-all-start = ((f32[16,6,32,128]{3,2,1,0:T(8,128)}), f32[16,6,32,128]{3,2,1,0:T(8,128)}, u32[]{:S(2)}, u32[]{:S(2)}) async-start(f32[16,6,32,128]{3,2,1,0:T(8,128)} %elastic.1), calls=%async_computation | async-start | bytes 3145728 | tf_op jit(solution)/shard_map/all_to_all | solution.py:255
  101.7 2.9 %collective-permute-start.20 = (f32[4,3,32,128]{3,2,1,0:T(8,128)S(1)}, f32[4,3,32,128]{3,2,1,0:T(8,128)S(1)}, u32[]{:S(2)}, u32[]{:S(2)}) collective-permute-start(f32[4,3,32,128]{3,2,1,0:T(8,128)S(1)} %get-tuple-element.115), channel_id=1, source_target_pairs={{0,1},{1,0},{2,3},{3,2},{4,5},{5,4},{6,7},{7,6},{8,9},{9,8},{10,11... | collective-permute-start | bytes 589832 | tf_op jit(solution)/shard_map/ppermute | solution.py:160
  102.1 12.3 %collective-permute-start.21 = (f32[4,3,32,128]{3,2,1,0:T(8,128)S(1)}, f32[4,3,32,128]{3,2,1,0:T(8,128)S(1)}, u32[]{:S(2)}, u32[]{:S(2)}) collective-permute-start(f32[4,3,32,128]{3,2,1,0:T(8,128)S(1)} %get-tuple-element.116), channel_id=1, source_target_pairs={{0,2},{1,3},{2,0},{3,1},{4,6},{5,7},{6,4},{7,5},{8,10},{9,11},{10,... | collective-permute-start | bytes 589832 | tf_op jit(solution)/shard_map/ppermute | solution.py:160
  102.4 18.9 %collective-permute-start.22 = (f32[4,3,32,128]{3,2,1,0:T(8,128)S(1)}, f32[4,3,32,128]{3,2,1,0:T(8,128)S(1)}, u32[]{:S(2)}, u32[]{:S(2)}) collective-permute-start(f32[4,3,32,128]{3,2,1,0:T(8,128)S(1)} %get-tuple-element.117), channel_id=1, source_target_pairs={{0,3},{1,2},{2,1},{3,0},{4,7},{5,6},{6,5},{7,4},{8,11},{9,10},{10,... | collective-permute-start | bytes 589832 | tf_op jit(solution)/shard_map/ppermute | solution.py:160
  114.4 0.7 copy-start.9
  121.3 0.7 copy-start.11
  122.0 1.1 copy-start.5
  123.1 0.9 copy-start.10
  124.0 0.9 copy-start.12
  125.0 11.9 %copy-start.2 = (f32[6,32,2048]{2,1,0:T(8,128)S(1)}, f32[6,32,2048]{2,1,0:T(8,128)}, u32[]{:S(2)}) copy-start(f32[6,32,2048]{2,1,0:T(8,128)} %refs_5_.2) | copy-start | bytes 4718596

commit v3 on v2

--- a/solution.py
+++ b/solution.py
@@ -326,8 +326,12 @@
         both_out[at] = dot(back, moved).astype(BF16)
     for at in range(faces_ref.shape[0]):
         faces_out[at] = dot(back, faces_ref[at]).astype(BF16)
-    for at in range(halos_ref.shape[0]):
-        halos_out[at] = dot(halos_ref[at], onto).astype(BF16)
+    pairs = ((0, 3), (1, 4), (2, 5), (6, 7), (8, 8))
+    for at, pair in enumerate(pairs):
+        for half in range(2):
+            for side in range(2):
+                placed = dot(halos_ref[2 * pair[side] + half], onto).astype(BF16)
+                halos_out[2 * at + half, :, side * BLOCK : (side + 1) * BLOCK] = placed
 
 
 def weights_body(layers, orient_ref, means_ref, out_ref):
@@ -362,6 +366,24 @@
         total = faces(rows, 0) + faces(slice(3 * quarter, 4 * quarter), 1 + number)
         up_ref[rows, :] = total[:, :BLOCK]
         down_ref[rows, :] = total[:, BLOCK:]
+
+
+FIRST = 3
+
+
+def members_of(first_ref, second_ref, rows):
+    return [ref[at, rows, :] for ref in (first_ref, second_ref) for at in range(ref.shape[0])]
+
+
+def transform(high_ref, low_ref, rows, coef_h, coef_l, out_ref):
+    table = (high_ref[rows, :], low_ref[rows, :])
+    fields = out_ref.shape[0]
+    for start in range(0, fields, 2):
+        stop = min(start + 2, fields)
+        lanes = slice(start * BLOCK, stop * BLOCK)
+        values = dot3(table, (coef_h[:, lanes], coef_l[:, lanes]))
+        for at in range(start, stop):
+            out_ref[at] = values[:, lanes_of(at - start)]
 
 
 def flow_parts(g_r, g_t, g_z, u):
@@ -385,10 +407,13 @@
     return ref[2 * at], ref[2 * at + 1]
 
 
-def velocity_body(
-    vel_h, vel_l, high_ref, low_ref, both_ref, inv_r_ref, vel_ref, flow_ref, values
-):
+def velocity_body(route, count, me_ref, *refs):
+    psi_refs, refs = refs[:count], refs[count:]
+    vel_h, vel_l, high_ref, low_ref, both_ref, inv_r_ref, vel_ref, flow_ref = refs[:8]
+    coef_h, coef_l, psi_out, values = refs[8:]
     planes = high_ref.shape[1]
+    route.load(me_ref, psi_refs, coef_h, coef_l)
+    transform(high_ref, low_ref, slice(0, planes), coef_h, coef_l, psi_out)
     table = (high_ref[...], low_ref[...])
     values[:, 0:256] = dot3(table, (vel_h[:, 0:256], vel_l[:, 0:256]))
     values[:, 256:384] = dot3(table, (vel_h[:, 256:384], vel_l[:, 256:384]))
@@ -421,8 +446,7 @@
 
 
 def halo_body(
-    below_ref, above_ref, vel_ref, own_ref, high_ref, low_ref, halos_ref, places_ref,
-    flow_ref, values,
+    below_ref, above_ref, vel_ref, high_ref, low_ref, halos_ref, places_ref, part_ref, values
 ):
     planes = high_ref.shape[1]
     quarter = planes // 4
@@ -434,27 +458,30 @@
             part = dot(part[0], places_ref[number]) + dot(part[1], places_ref[number])
             last = part if last is None else last + part
         edges.append(jnp.concatenate([ref[...], last], axis=0))
-    values[...] = dot3(
-        (high_ref[...], low_ref[...]), split(jnp.concatenate(edges, axis=1))
-    )
-    rows_step = 128
+    values[...] = dot3((high_ref[...], low_ref[...]), split(jnp.concatenate(edges, axis=1)))
+    rows_step = planes // 2
 
     def chunk(start):
         rows = pl.ds(start, rows_step)
         turned = pl.ds(pl.multiple_of(planes + start, rows_step), rows_step)
         edge, edge_dth = split(values[rows, :]), split(values[turned, :])
-        g_r = [dot3(edge, matrix_of(halos_ref, f)) for f in range(3)]
-        g_z = [dot3(edge, matrix_of(halos_ref, 3 + f)) for f in range(3)]
-        g_t = [dot3(edge_dth, matrix_of(halos_ref, 6 + f)) for f in range(3)]
-        g_t[0] = g_t[0] - dot3(edge, matrix_of(halos_ref, 7))
-        g_t[1] = g_t[1] + dot3(edge, matrix_of(halos_ref, 6))
+        g_r, g_z = zip(*(halved(dot3(edge, matrix_of(halos_ref, f))) for f in range(3)))
+        g_t = [
+            *halved(dot3(edge_dth, matrix_of(halos_ref, 3))),
+            dot3(edge_dth, (halos_ref[8, :, :BLOCK], halos_ref[9, :, :BLOCK])),
+        ]
+        mean_r, mean_t = halved(dot3(edge, matrix_of(halos_ref, 3)))
+        g_t[0] = g_t[0] - mean_t
+        g_t[1] = g_t[1] + mean_r
         u = [vel_ref[f, rows, :] for f in range(3)]
-        for at in range(3):
-            flow_ref[at, rows, :] = own_ref[at, rows, :]
         for at, part in enumerate(flow_parts(g_r, g_t, g_z, u)):
-            flow_ref[3 + at, rows, :] = own_ref[3 + at, rows, :] + part
+            part_ref[at, rows, :] = part
 
     row_chunks(planes, rows_step, chunk)
+
+
+def halved(pair):
+    return pair[:, :BLOCK], pair[:, BLOCK:]
 
 
 def square(m):
@@ -510,27 +537,11 @@
     lax.fori_loop(0, planes // rows_step, chunk, 0)
 
 
-def transform(high_ref, low_ref, rows, coef_h, coef_l, out_ref):
-    table = (high_ref[rows, :], low_ref[rows, :])
-    for start, stop in ((0, 2), (2, 3)):
-        lanes = slice(start * BLOCK, stop * BLOCK)
-        values = dot3(table, (coef_h[:, lanes], coef_l[:, lanes]))
-        for at in range(start, stop):
-            out_ref[at] = values[:, lanes_of(at - start)]
-
-
-def values_body(route, count, me_ref, *refs):
-    psi_refs, (high_ref, low_ref, coef_h, coef_l, psi_out) = refs[:count], refs[count:]
-    route.load(me_ref, psi_refs, coef_h, coef_l)
-    transform(high_ref, low_ref, slice(0, high_ref.shape[1]), coef_h, coef_l, psi_out)
-
-
 def momentum_body(route, count, out_route, out_count, me_ref, *refs):
     psi_refs, refs = refs[:count], refs[count:]
-    first_ref, flow_ref, high_ref, low_ref, back_high_ref, back_low_ref, both_ref, inv_r_ref = (
-        refs[:8]
-    )
-    out_refs, refs = refs[8 : 8 + out_count], refs[8 + out_count :]
+    first_ref, flow_ref, halo_ref, high_ref, low_ref = refs[:5]
+    back_high_ref, back_low_ref, both_ref, inv_r_ref = refs[5:9]
+    out_refs, refs = refs[9 : 9 + out_count], refs[9 + out_count :]
     coef_h, coef_l, psi_out, conform_out, stress_h, stress_l, vel_h, vel_l, mom_s, coeffs = refs
     planes = high_ref.shape[1]
     route.load(me_ref, psi_refs, coef_h, coef_l)
@@ -540,7 +551,7 @@
     def chunk(start):
         rows = pl.ds(start, rows_step)
         inv_r = inv_r_ref[0:1, :]
-        psi = [ref[member, rows, :] for ref in (first_ref, psi_out) for member in range(3)]
+        psi = members_of(first_ref, psi_out, rows)
         conform = exponential(psi, 1.0)
         for member in range(6):
             conform_out[member, rows, :] = conform[member]
@@ -551,9 +562,10 @@
         turned = pl.ds(pl.multiple_of(planes + start, rows_step), rows_step)
         for at in range(3):
             put(vel_h, vel_l, turned, lanes_of(at), -hoop[at])
-        mom_s[0, rows, :] = flow_ref[12, rows, :] + (stress[0] * inv_r - hoop[1])
-        mom_s[1, rows, :] = flow_ref[13, rows, :] + 2.0 * hoop[0]
-        mom_s[2, rows, :] = flow_ref[14, rows, :] + stress[2] * inv_r
+        carried = [flow_ref[12 + at, rows, :] + halo_ref[9 + at, rows, :] for at in range(3)]
+        mom_s[0, rows, :] = carried[0] + (stress[0] * inv_r - hoop[1])
+        mom_s[1, rows, :] = carried[1] + 2.0 * hoop[0]
+        mom_s[2, rows, :] = carried[2] + stress[2] * inv_r
 
     row_chunks(planes, rows_step, chunk)
     divergence = tuple(
@@ -574,27 +586,30 @@
 def elastic_body(route, me_ref, *refs):
     (
         first_h, first_l, second_h, second_l, first_ref, second_ref, conform_ref, flow_ref,
-        high_ref, low_ref, back_high_ref, back_low_ref, both_ref,
-    ) = refs[:13]
-    out_ref, dth_s, grad_s, rate_h, rate_l, coeffs = refs[13:]
+        halo_ref, high_ref, low_ref, back_high_ref, back_low_ref, both_ref,
+    ) = refs[:14]
+    out_ref, dth_s, grad_s, rate_h, rate_l, coeffs = refs[14:]
     planes = high_ref.shape[1]
     turned = slice(planes, 2 * planes)
-    transform(high_ref, low_ref, turned, first_h, first_l, dth_s.at[pl.ds(0, 3)])
-    transform(high_ref, low_ref, turned, second_h, second_l, dth_s.at[pl.ds(3, 3)])
+    transform(high_ref, low_ref, turned, first_h, first_l, dth_s.at[pl.ds(0, FIRST)])
+    transform(high_ref, low_ref, turned, second_h, second_l, dth_s.at[pl.ds(FIRST, 6 - FIRST)])
     gradient = tuple(
         jnp.concatenate([both_ref[at], both_ref[2 + at]], axis=1) for at in range(2)
     )
     for member in range(6):
-        psi_ref = first_ref if member < 3 else second_ref
-        grad_s[member] = dot3(split(psi_ref[member % 3]), gradient)
+        psi_ref = first_ref if member < FIRST else second_ref
+        grad_s[member] = dot3(split(psi_ref[member % FIRST]), gradient)
     rows_step = 16
     inv_relax = 1.0 / RELAX_TIME
 
     def chunk(start):
         rows = pl.ds(start, rows_step)
-        psi = [ref[member, rows, :] for ref in (first_ref, second_ref) for member in range(3)]
+        psi = members_of(first_ref, second_ref, rows)
         inverse = exponential(psi, -1.0)
-        u_r, hoop_rate, u_z, p, q, s = (flow_ref[at, rows, :] for at in range(6))
+        u_r, hoop_rate, u_z = (flow_ref[at, rows, :] for at in range(3))
+        p, q, s, *strain = (
+            flow_ref[3 + at, rows, :] + halo_ref[at, rows, :] for at in range(9)
+        )
         a, b, c, d, e, f = psi
         pb, qc, se = p * b, q * c, s * e
         turning = (
@@ -614,7 +629,7 @@
             relaxing = ((1.0 - MOBILITY) * inv_relax) * inverse[member] - (
                 MOBILITY * inv_relax
             ) * conform_ref[member, rows, :]
-            rate = (turning[member] - advect) + (flow_ref[6 + member, rows, :] + relaxing)
+            rate = (turning[member] - advect) + (strain[member] + relaxing)
             put(rate_h, rate_l, rows, lanes_of(member), rate)
 
     row_chunks(planes, rows_step, chunk)
@@ -719,7 +734,7 @@
         (
             jax.ShapeDtypeStruct((10, BLOCK, BLOCK), BF16),
             jax.ShapeDtypeStruct((24, BLOCK, 2 * BLOCK), BF16),
-            jax.ShapeDtypeStruct((18, 2 * BLOCK, BLOCK), BF16),
+            jax.ShapeDtypeStruct((10, 2 * BLOCK, 2 * BLOCK), BF16),
             jax.ShapeDtypeStruct((8, BLOCK), F32),
         ),
         4,
@@ -742,13 +757,13 @@
         vel_nodes = far_swaps(vel_nodes, psi_nodes)
         vel_nodes, psi_nodes, fixed = barrier((vel_nodes, psi_nodes, fixed))
         vel_nodes = near_swaps(regroup(vel_nodes))
-        first_nodes = far_swaps(regroup([group[:, :3] for group in psi_nodes]), vel_nodes)
-        second_nodes = regroup([group[:, 3:] for group in psi_nodes])
+        first_nodes = far_swaps(regroup([group[:, :FIRST] for group in psi_nodes]), vel_nodes)
+        second_nodes = regroup([group[:, FIRST:] for group in psi_nodes])
     else:
         vel_nodes = far_first.unpacked(in_one(vel_nodes))
         psi_nodes = near_first.unpacked(in_one(psi_nodes))
-        first_nodes = [group[:, :3] for group in psi_nodes]
-        second_nodes = [group[:, 3:] for group in psi_nodes]
+        first_nodes = [group[:, :FIRST] for group in psi_nodes]
+        second_nodes = [group[:, FIRST:] for group in psi_nodes]
 
     both_s, faces_s, halos_s, inv_r, weights = fixed
     edge = jax.ShapeDtypeStruct((planes // 4 * 3, BLOCK), F32)
@@ -764,50 +779,48 @@
     below = lax.ppermute(to_up, "mode", up)
     above = lax.ppermute(to_down, "mode", [(j, i) for i, j in up])
 
-    if staged:
-        second_nodes, below, above = barrier((second_nodes, below, above))
-        second_nodes = far_swaps(second_nodes)
-
-    vel, own_flow = kernel_call(
-        velocity_body,
+    def halves(fields):
+        return (
+            jax.ShapeDtypeStruct((planes, fields * BLOCK), BF16),
+            jax.ShapeDtypeStruct((planes, fields * BLOCK), BF16),
+            jax.ShapeDtypeStruct((fields, planes, BLOCK), F32),
+        )
+
+    vel, own_flow, first_h, first_l, first = kernel_call(
+        functools.partial(velocity_body, near_first, len(first_nodes)),
         (
             jax.ShapeDtypeStruct((3, planes, BLOCK), F32),
             jax.ShapeDtypeStruct((15, planes, BLOCK), F32),
+            *halves(FIRST),
         ),
-        6,
-        scalars=0,
+        len(first_nodes) + 6,
         scratch=[pltpu.VMEM((2 * planes, 3 * BLOCK), F32)],
         vmem=20,
         name="velocity",
-    )(vel_h, vel_l, high, low, both_s, inv_r)
-    flow = kernel_call(
+    )(me, *first_nodes, vel_h, vel_l, high, low, both_s, inv_r)
+    if staged:
+        early = second_nodes
+        second_nodes, below, above, vel = barrier((second_nodes, below, above, vel))
+        second_nodes = far_swaps([early[0], second_nodes[1], early[2], early[3]])
+    halo_flow = kernel_call(
         halo_body,
-        jax.ShapeDtypeStruct((15, planes, BLOCK), F32),
-        8,
+        jax.ShapeDtypeStruct((12, planes, BLOCK), F32),
+        7,
         scalars=0,
         scratch=[pltpu.VMEM((2 * planes, 2 * BLOCK), F32)],
-        vmem=20,
+        vmem=24,
         name="halo",
-    )(below, above, vel, own_flow, high, low, halos_s, jnp.asarray(free_places(), BF16))
+    )(below, above, vel, high, low, halos_s, jnp.asarray(free_places(), BF16))
 
     far_outs = far_first.outs(far_first.leave, 3, far_first.modes, BLOCK)
     psi_outs = whole.outs(whole.leave, 6, whole.modes, BLOCK)
-    half = jax.ShapeDtypeStruct((planes, 3 * BLOCK), BF16)
-    field3 = jax.ShapeDtypeStruct((3, planes, BLOCK), F32)
     field6 = jax.ShapeDtypeStruct((6, planes, BLOCK), F32)
-    first_h, first_l, first = kernel_call(
-        functools.partial(values_body, near_first, len(first_nodes)),
-        (half, half, field3),
-        len(first_nodes) + 2,
-        vmem=10,
-        name="values",
-    )(me, *first_nodes, high, low)
     *vel_rates, second_h, second_l, second, conform = kernel_call(
         functools.partial(
             momentum_body, near_first, len(second_nodes), far_first, len(far_outs)
         ),
-        (*far_outs, half, half, field3, field6),
-        len(second_nodes) + 8,
+        (*far_outs, *halves(6 - FIRST), field6),
+        len(second_nodes) + 9,
         scratch=[
             pltpu.VMEM((planes, 6 * BLOCK), BF16),
             pltpu.VMEM((planes, 6 * BLOCK), BF16),
@@ -818,12 +831,12 @@
         ],
         vmem=24,
         name="momentum",
-    )(me, *second_nodes, first, flow, high, low, back_high, back_low, both_s, inv_r)
+    )(me, *second_nodes, first, own_flow, halo_flow, high, low, back_high, back_low, both_s, inv_r)
     vel_rates = far_first.packed(vel_rates)
     psi_rates = kernel_call(
         functools.partial(elastic_body, whole),
         (*psi_outs,),
-        13,
+        14,
         scratch=[
             pltpu.VMEM((6, planes, BLOCK), F32),
             pltpu.VMEM((6, planes, 2 * BLOCK), F32),
@@ -834,7 +847,7 @@
         vmem=24,
         name="elastic",
     )(
-        me, first_h, first_l, second_h, second_l, first, second, conform, flow, high, low,
+        me, first_h, first_l, second_h, second_l, first, second, conform, own_flow, halo_flow, high, low,
         back_high, back_low, both_s,
     )
 

time: 142 us -> 138 us (0.972)
  waiting for transfers between devices: 60 us -> 56.4 us
    ppermute x1, waiting for transfers between devices: 7.24 us -> 3 us  [body(): above = lax.ppermute(to_down, 'mode', [(j, i) for i, j in up])]
    ppermute x21, starting transfers between devices: 19.8 us -> 22.2 us  [swap(): return lax.ppermute(block, 'mode', [(i, i ^ bits) for i in range(devices)])]
    pallas_call x4 -> x3, Pallas kernels: 18.3 us -> 17 us  [the longest x1 9.5 us: body(): kernel_call(functools.partial(elastic_body, whole), (*psi_outs,), 14, scr...]
where the time goes in v3:
time: 138 us; the launch traced here: 137 us
  waiting for transfers between devices  56.4 us (41%)
  Pallas kernels  44.1 us (32%)
  starting transfers between devices  29.6 us (21%)
  local copies, waits for them, and re-layouts  5.5 us (4%)
  between operations  1.65 us (1%)
    ppermute x21, waiting for transfers between devices, swap(): return lax.ppermute(block, 'mode', [(i, i ^ bits) for i in range(devices)])  43.2 us
    ppermute x21, starting transfers between devices, swap(): return lax.ppermute(block, 'mode', [(i, i ^ bits) for i in range(devices)])  22.2 us
    pallas_call x1, Pallas kernels, body(): kernel_call(functools.partial(elastic_body, whole), (*psi_outs,), 14, scr...  9.5 us
    all_to_all x1, waiting for transfers between devices, in_one(): lax.all_to_all(arrays[0], 'mode', split_axis=0, concat_axis=0, tiled=True)  8.81 us
    pallas_call x2, Pallas kernels, advance(): pl.pallas_call(functools.partial(advance_body, layers, step, route, len(r...  7.62 us
    pallas_call x1, Pallas kernels, body(): kernel_call(functools.partial(momentum_body, near_first, len(second_nodes...  6.09 us
    pallas_call x1, Pallas kernels, body(): kernel_call(functools.partial(weights_body, layers), jax.ShapeDtypeStruct...  5.79 us
    unnamed x38, local copies, waits for them, and re-layouts  5.31 us
  transfers between devices with their start and end apart: 24, of which 13 were waited for; matrix products, arithmetic and copies ran while one was open for 0% of the time, Pallas kernels for 22%

profile of v3, /device:TPU:13, one launch (start us, length us, event | category | flops | bytes accessed | tf_op | source)
XLA Modules:
  0.0 137.5 jit_solution(5308040368587009172)
XLA Ops:
  0.7 3.5 %pack.1 = (f32[4,3,32,128]{3,2,1,0:T(8,128)}, f32[4,3,32,128]{3,2,1,0:T(8,128)}, f32[4,3,32,128]{3,2,1,0:T(8,128)}, f32[4,3,32,128]{3,2,1,0:T(8,128)}, f32[4,6,3...) custom-call(s32[1]{0:T(128)} %bitcast.me_ref.refs_0_, ...), custom_call_target="tpu_custom_call" | custom-call | tf_op jit(solution)/shard_map/pack/pallas_call | solution.py:280
  4.2 0.7 collective-permute-start
  5.2 1.5 %collective-permute-start.5 = (f32[4,6,32,128]{3,2,1,0:T(8,128)}, f32[4,6,32,128]{3,2,1,0:T(8,128)S(1)}, u32[]{:S(2)}, u32[]{:S(2)}) collective-permute-start(f32[4,6,32,128]{3,2,1,0:T(8,128)} %get-tuple-element.67), channel_id=1, source_target_pairs={{0,3},{1,2},{2,1},{3,0},{4,7},{5,6},{6,5},{7,4},{8,11},{9,10},{10,... | collective-permute-start | bytes 1179656 | tf_op jit(solution)/shard_map/ppermute | solution.py:160
  6.7 2.3 %collective-permute-start.2 = (f32[4,3,32,128]{3,2,1,0:T(8,128)}, f32[4,3,32,128]{3,2,1,0:T(8,128)S(1)}, u32[]{:S(2)}, u32[]{:S(2)}) collective-permute-start(f32[4,3,32,128]{3,2,1,0:T(8,128)} %get-tuple-element.63), channel_id=1, source_target_pairs={{0,8},{1,9},{2,10},{3,11},{4,12},{5,13},{6,14},{7,15},{8,0},{9,1},... | collective-permute-start | bytes 589832 | tf_op jit(solution)/shard_map/ppermute | solution.py:160
  9.0 1.2 collective-permute-start.1
  10.2 0.9 copy-done.14
  11.1 5.8 %weights.1.refs_7_.refs_4_ = bf16[16,384,128]{2,1,0:T(8,128)(2,1)S(1)} custom-call(s32[32]{0:T(128)S(1)} %copy-done.16, bf16[3,128,128]{2,1,0:T(8,128)(2,1)S(1)} %copy-done.14), custom_call_target="tpu_custom_call" | custom-call | tf_op jit(solution)/shard_map/weights/pallas_call | solution.py:745
  17.0 1.7 %order.1 = (bf16[10,128,128]{2,1,0:T(8,128)(2,1)S(1)}, bf16[24,128,256]{2,1,0:T(8,128)(2,1)S(1)}, bf16[10,256,256]{2,1,0:T(8,128)(2,1)S(1)}, f32[8,128]{1,0:T(8,128)S(1)}) custom-call(s32[1]{0:T(128)} %bitcast.me_ref.refs_0_, s32[32]{0:T(128)S(1)} %copy-done.16, bf16[10,128,128]{2,1,0:T(8,128)(2,1)S(1)} %copy-done.8, bf16[24,128,256]{2,1,0:T(8,128)(2,1)S(1)} %copy-done.6, ...), custom_call_target="tpu_custom_call" | custom-call | tf_op jit(solution)/shard_map/order/pallas_call | solution.py:732
  18.7 3.6 %collective-permute-done.2 = f32[4,3,32,128]{3,2,1,0:T(8,128)S(1)} collective-permute-done((f32[4,3,32,128]{3,2,1,0:T(8,128)}, f32[4,3,32,128]{3,2,1,0:T(8,128)S(1)}, u32[]{:S(2)}, u32[]{:S(2)}) %collective-permute-start.2) | collective-permute-done | bytes 196640 | tf_op jit(solution)/shard_map/ppermute | solution.py:160
  22.3 4.2 %collective-permute-done.3 = f32[4,3,32,128]{3,2,1,0:T(8,128)S(1)} collective-permute-done((f32[4,3,32,128]{3,2,1,0:T(8,128)}, f32[4,3,32,128]{3,2,1,0:T(8,128)S(1)}, u32[]{:S(2)}, u32[]{:S(2)}) %collective-permute-start.3) | collective-permute-done | bytes 196640 | tf_op jit(solution)/shard_map/ppermute | solution.py:160
  26.7 2.2 %collective-permute-start.13 = (f32[4,3,32,128]{3,2,1,0:T(8,128)S(1)}, f32[4,3,32,128]{3,2,1,0:T(8,128)S(1)}, u32[]{:S(2)}, u32[]{:S(2)}) collective-permute-start(f32[4,3,32,128]{3,2,1,0:T(8,128)S(1)} %pad_maximum_fusion.11), channel_id=1, source_target_pairs={{0,12},{1,13},{2,14},{3,15},{4,8},{5,9},{6,10},{7,11},{8,4},{9,5},... | collective-permute-start | bytes 589832 | tf_op jit(solution)/shard_map/ppermute | solution.py:160
  29.1 0.8 collective-permute-start.6
  30.1 1.3 collective-permute-start.7
  31.6 1.2 collective-permute-start.11
  32.8 4.6 %collective-permute-done.8.refs_3_ = f32[4,3,32,128]{3,2,1,0:T(8,128)S(1)} collective-permute-done((f32[4,3,32,128]{3,2,1,0:T(8,128)S(1)}, f32[4,3,32,128]{3,2,1,0:T(8,128)S(1)}, u32[]{:S(2)}, u32[]{:S(2)}) %collective-permute-start.8) | collective-permute-done | bytes 196640 | tf_op jit(solution)/shard_map/ppermute | solution.py:160
  37.4 3.0 %collective-permute-done.7.refs_2_ = f32[4,3,32,128]{3,2,1,0:T(8,128)S(1)} collective-permute-done((f32[4,3,32,128]{3,2,1,0:T(8,128)S(1)}, f32[4,3,32,128]{3,2,1,0:T(8,128)S(1)}, u32[]{:S(2)}, u32[]{:S(2)}) %collective-permute-start.7) | collective-permute-done | bytes 196640 | tf_op jit(solution)/shard_map/ppermute | solution.py:160
  40.4 1.2 faces.1
  41.6 1.1 collective-permute-start.10
  42.7 1.6 %collective-permute-start.9 = (f32[384,128]{1,0:T(8,128)S(1)}, f32[384,128]{1,0:T(8,128)S(1)}, u32[]{:S(2)}, u32[]{:S(2)}) collective-permute-start(f32[384,128]{1,0:T(8,128)S(1)} %get-tuple-element.81), channel_id=1, source_target_pairs={{0,1},{1,2},{2,3},{3,4},{4,5},{5,6},{6,7},{7,8},{8,9},{9,10},{10,1... | collective-permute-start | bytes 589832 | tf_op jit(solution)/shard_map/ppermute | solution.py:779
  44.3 1.4 %collective-permute-start.16 = (f32[4,3,32,128]{3,2,1,0:T(8,128)S(1)}, f32[4,3,32,128]{3,2,1,0:T(8,128)S(1)}, u32[]{:S(2)}, u32[]{:S(2)}) collective-permute-start(f32[4,3,32,128]{3,2,1,0:T(8,128)S(1)} %pad_maximum_fusion.3), channel_id=1, source_target_pairs={{0,12},{1,13},{2,14},{3,15},{4,8},{5,9},{6,10},{7,11},{8,4},{9,5},... | collective-permute-start | bytes 589832 | tf_op jit(solution)/shard_map/ppermute | solution.py:160
  45.8 3.2 %collective-permute-start.15 = (f32[4,3,32,128]{3,2,1,0:T(8,128)S(1)}, f32[4,3,32,128]{3,2,1,0:T(8,128)S(1)}, u32[]{:S(2)}, u32[]{:S(2)}) collective-permute-start(f32[4,3,32,128]{3,2,1,0:T(8,128)S(1)} %pad_maximum_fusion.2), channel_id=1, source_target_pairs={{0,8},{1,9},{2,10},{3,11},{4,12},{5,13},{6,14},{7,15},{8,0},{9,1},... | collective-permute-start | bytes 589832 | tf_op jit(solution)/shard_map/ppermute | solution.py:160
  48.9 4.5 %velocity.1 = (f32[3,512,128]{2,1,0:T(8,128)S(1)}, f32[15,512,128]{2,1,0:T(8,128)S(1)}, bf16[512,384]{1,0:T(8,128)(2,1)S(1)}, bf16[512,384]{1,0:T(8,128)(2,1)S(1)}, f32[3,512,128]{2,1,0:T(8,128)S(1)}) custom-call(s32[1]{0:T(128)} %bitcast.me_ref.refs_0_, f32[4,3,32,128]{3,2,1,0:T(8,128)S(1)} %pad_maximum_fusion.8.refs_0_, ...), custom_call_target="tpu_custom_call" | custom-call | tf_op jit(solution)/shard_map/velocity/pallas_call | solution.py:789
  53.5 3.0 %collective-permute-done.10.above_ref = f32[384,128]{1,0:T(8,128)S(1)} collective-permute-done((f32[384,128]{1,0:T(8,128)S(1)}, f32[384,128]{1,0:T(8,128)S(1)}, u32[]{:S(2)}, u32[]{:S(2)}) %collective-permute-start.10) | collective-permute-done | bytes 196640 | tf_op jit(solution)/shard_map/ppermute | solution.py:780
  56.5 1.4 collective-permute-done.9.below_ref
  57.8 2.9 %halo.1.refs_6_.refs_8_ = f32[12,512,128]{2,1,0:T(8,128)S(1)} custom-call(f32[384,128]{1,0:T(8,128)S(1)} %collective-permute-done.9.below_ref, f32[384,128]{1,0:T(8,128)S(1)} %collective-permute-done.10.above_ref, f32[3,512,128]{2,1,0:T(8,128)S(1)} %get-tuple-element.94.vel_ref, bf16[1024,512]{1,0:T(8,128)(2,1)S(1)} %copy-done, ...), custom_call_target="tpu_custom_call" | custom-call | tf_op jit(solution)/shard_map/halo/pallas_call | solution.py:805
  60.8 1.3 collective-permute-done.16.refs_3_
  62.0 2.2 %collective-permute-done.15.refs_2_ = f32[4,3,32,128]{3,2,1,0:T(8,128)S(1)} collective-permute-done((f32[4,3,32,128]{3,2,1,0:T(8,128)S(1)}, f32[4,3,32,128]{3,2,1,0:T(8,128)S(1)}, u32[]{:S(2)}, u32[]{:S(2)}) %collective-permute-start.15) | collective-permute-done | bytes 196640 | tf_op jit(solution)/shard_map/ppermute | solution.py:160
  64.2 6.1 %momentum.1 = (f32[4,3,32,128]{3,2,1,0:T(8,128)S(1)}, f32[4,3,32,128]{3,2,1,0:T(8,128)S(1)}, f32[4,3,32,128]{3,2,1,0:T(8,128)S(1)}, f32[4,3,32,128]{3,2,1,0:T(8,...) custom-call(s32[1]{0:T(128)} %bitcast.me_ref.refs_0_, ...), custom_call_target="tpu_custom_call" | custom-call | tf_op jit(solution)/shard_map/momentum/pallas_call | solution.py:818
  70.4 2.4 %collective-permute-start.17 = (f32[4,3,32,128]{3,2,1,0:T(8,128)S(1)}, f32[4,3,32,128]{3,2,1,0:T(8,128)S(1)}, u32[]{:S(2)}, u32[]{:S(2)}) collective-permute-start(f32[4,3,32,128]{3,2,1,0:T(8,128)S(1)} %get-tuple-element.97), channel_id=1, source_target_pairs={{0,4},{1,5},{2,6},{3,7},{4,0},{5,1},{6,2},{7,3},{8,12},{9,13},{10,... | collective-permute-start | bytes 589832 | tf_op jit(solution)/shard_map/ppermute | solution.py:160
  72.7 0.6 collective-permute-start.18
  73.3 0.7 collective-permute-start.19
  74.0 9.5 %elastic.1 = f32[16,6,32,128]{3,2,1,0:T(8,128)} custom-call(s32[1]{0:T(128)} %bitcast.me_ref.refs_0_, bf16[512,384]{1,0:T(8,128)(2,1)S(1)} %get-tuple-element.100.refs_0_, bf16[512,384]{1,0:T(8,128)(2,1)S(1)} %get-tuple-element.101.refs_1_, bf16[512,384]{1,0:T(8,128)(2,1)S(1)} %get-tuple-element.102.refs_2_, ...), custom_call_target="tpu_custom_call" | custom-call | tf_op jit(solution)/shard_map/elastic/pallas_call | solution.py:836
  83.5 3.0 %collective-permute-done.18.refs_2_ = f32[4,3,32,128]{3,2,1,0:T(8,128)S(1)} collective-permute-done((f32[4,3,32,128]{3,2,1,0:T(8,128)S(1)}, f32[4,3,32,128]{3,2,1,0:T(8,128)S(1)}, u32[]{:S(2)}, u32[]{:S(2)}) %collective-permute-start.18) | collective-permute-done | bytes 196640 | tf_op jit(solution)/shard_map/ppermute | solution.py:160
  86.5 5.3 %collective-permute-done.19.refs_3_ = f32[4,3,32,128]{3,2,1,0:T(8,128)S(1)} collective-permute-done((f32[4,3,32,128]{3,2,1,0:T(8,128)S(1)}, f32[4,3,32,128]{3,2,1,0:T(8,128)S(1)}, u32[]{:S(2)}, u32[]{:S(2)}) %collective-permute-start.19) | collective-permute-done | bytes 196640 | tf_op jit(solution)/shard_map/ppermute | solution.py:160
  91.8 4.7 %all-to-all-start = ((f32[16,6,32,128]{3,2,1,0:T(8,128)}), f32[16,6,32,128]{3,2,1,0:T(8,128)}, u32[]{:S(2)}, u32[]{:S(2)}) async-start(f32[16,6,32,128]{3,2,1,0:T(8,128)} %elastic.1), calls=%async_computation | async-start | bytes 3145728 | tf_op jit(solution)/shard_map/all_to_all | solution.py:255
  96.5 1.2 turn.1
  97.7 0.4 collective-permute-start.20
  98.4 1.5 %collective-permute-start.22 = (f32[4,3,32,128]{3,2,1,0:T(8,128)S(1)}, f32[4,3,32,128]{3,2,1,0:T(8,128)S(1)}, u32[]{:S(2)}, u32[]{:S(2)}) collective-permute-start(f32[4,3,32,128]{3,2,1,0:T(8,128)S(1)} %get-tuple-element.113), channel_id=1, source_target_pairs={{0,3},{1,2},{2,1},{3,0},{4,7},{5,6},{6,5},{7,4},{8,11},{9,10},{10,... | collective-permute-start | bytes 589832 | tf_op jit(solution)/shard_map/ppermute | solution.py:160
  100.6 9.8 %collective-permute-done.21.refs_5_ = f32[4,3,32,128]{3,2,1,0:T(8,128)S(1)} collective-permute-done((f32[4,3,32,128]{3,2,1,0:T(8,128)S(1)}, f32[4,3,32,128]{3,2,1,0:T(8,128)S(1)}, u32[]{:S(2)}, u32[]{:S(2)}) %collective-permute-start.21) | collective-permute-done | bytes 196640 | tf_op jit(solution)/shard_map/ppermute | solution.py:160
  110.4 0.7 copy-done.9
  111.1 6.2 %collective-permute-done.22.refs_6_ = f32[4,3,32,128]{3,2,1,0:T(8,128)S(1)} collective-permute-done((f32[4,3,32,128]{3,2,1,0:T(8,128)S(1)}, f32[4,3,32,128]{3,2,1,0:T(8,128)S(1)}, u32[]{:S(2)}, u32[]{:S(2)}) %collective-permute-start.22) | collective-permute-done | bytes 196640 | tf_op jit(solution)/shard_map/ppermute | solution.py:160
  117.3 0.7 copy-done.11
  118.0 1.1 copy-done.5
  119.2 0.9 copy-done.10
  120.1 0.9 copy-done.12
  121.0 3.1 %advance.2 = f32[3,32,2048]{2,1,0:T(8,128)} custom-call(s32[1]{0:T(128)} %bitcast.me_ref.refs_0_, s32[32]{0:T(128)S(1)} %copy-done.16, f32[1]{0:T(128)S(6)} %select_n.9.refs_2_, f32[4,3,32,128]{3,2,1,0:T(8,128)S(1)} %get-tuple-element.110.refs_3_, f32[4,3,32,128]{3,2,1,0:T(8,128)S(1)} %collective-permute-done.20.refs_4_, f32[4,3,32,128]{3,2,1,0:T(8,128)S(1)} %copy-done.10, ...), custom_call_target="tpu_custom_call" | custom-call | tf_op jit(solution)/shard_map/advance/pallas_call | solution.py:696
  124.1 8.8 %all-to-all-done.refs_3_ = f32[16,6,32,128]{3,2,1,0:T(8,128)} async-done(((f32[16,6,32,128]{3,2,1,0:T(8,128)}), f32[16,6,32,128]{3,2,1,0:T(8,128)}, u32[]{:S(2)}, u32[]{:S(2)}) %all-to-all-start) | async-done | bytes 1572896 | tf_op jit(solution)/shard_map/all_to_all | solution.py:255
  132.9 4.5 %advance.3 = f32[6,32,2048]{2,1,0:T(8,128)} custom-call(s32[1]{0:T(128)} %bitcast.me_ref.refs_0_, s32[32]{0:T(128)S(1)} %copy-done.16, f32[1]{0:T(128)S(6)} %select_n.9.refs_2_, f32[16,6,32,128]{3,2,1,0:T(8,128)} %all-to-all-done.refs_3_, bf16[16,384,128]{2,1,0:T(8,128)(2,1)S(1)} %weights.1.refs_7_.refs_4_, f32[6,32,2048]{2,1,0:T(8,128)S(1)} %copy-done.2), custom_call_target="tpu_custom_call" | custom-call | tf_op jit(solution)/shard_map/advance/pallas_call | solution.py:696
  (65 shorter events, 1.3 us)
Async XLA Ops:
  0.6 9.6 %copy-start.16 = (s32[32]{0:T(128)S(1)}, s32[32]{0:T(128)}, u32[]{:S(2)}) copy-start(s32[32]{0:T(128)} %refs_1_.5) | copy-start | bytes 388
  0.6 16.3 %copy-start.6 = (bf16[24,128,256]{2,1,0:T(8,128)(2,1)S(1)}, bf16[24,128,256]{2,1,0:T(8,128)(2,1)}, u32[]{:S(2)}) copy-start(bf16[24,128,256]{2,1,0:T(8,128)(2,1)} %constant.35.clone.faces_ref) | copy-start | bytes 4718596
  0.7 16.3 %copy-start.8 = (bf16[10,128,128]{2,1,0:T(8,128)(2,1)S(1)}, bf16[10,128,128]{2,1,0:T(8,128)(2,1)}, u32[]{:S(2)}) copy-start(bf16[10,128,128]{2,1,0:T(8,128)(2,1)} %constant.34.clone.both_ref) | copy-start | bytes 983044
  0.7 16.3 %copy-start.15 = (f32[128,128]{1,0:T(8,128)S(1)}, f32[128,128]{1,0:T(8,128)}, u32[]{:S(2)}) copy-start(f32[128,128]{1,0:T(8,128)} %constant.33.clone.inv_r_ref) | copy-start | bytes 196612
  4.2 12.7 %copy-start.7 = (bf16[18,256,128]{2,1,0:T(8,128)(2,1)S(1)}, bf16[18,256,128]{2,1,0:T(8,128)(2,1)}, u32[]{:S(2)}) copy-start(bf16[18,256,128]{2,1,0:T(8,128)(2,1)} %constant.36.clone.halos_ref) | copy-start | bytes 3538948
  4.2 4.8 %collective-permute-start = (f32[4,6,32,128]{3,2,1,0:T(8,128)}, f32[4,6,32,128]{3,2,1,0:T(8,128)S(1)}, u32[]{:S(2)}, u32[]{:S(2)}) collective-permute-start(f32[4,6,32,128]{3,2,1,0:T(8,128)} %get-tuple-element.61), channel_id=1, source_target_pairs={{0,1},{1,0},{2,3},{3,2},{4,5},{5,4},{6,7},{7,6},{8,9},{9,8},{10,11... | collective-permute-start | bytes 1179656 | tf_op jit(solution)/shard_map/ppermute | solution.py:160
  5.0 21.6 %collective-permute-start.4 = (f32[4,6,32,128]{3,2,1,0:T(8,128)}, f32[4,6,32,128]{3,2,1,0:T(8,128)S(1)}, u32[]{:S(2)}, u32[]{:S(2)}) collective-permute-start(f32[4,6,32,128]{3,2,1,0:T(8,128)} %get-tuple-element.66), channel_id=1, source_target_pairs={{0,2},{1,3},{2,0},{3,1},{4,6},{5,7},{6,4},{7,5},{8,10},{9,11},{10,... | collective-permute-start | bytes 1179656 | tf_op jit(solution)/shard_map/ppermute | solution.py:160
  5.2 21.3 %collective-permute-start.5 = (f32[4,6,32,128]{3,2,1,0:T(8,128)}, f32[4,6,32,128]{3,2,1,0:T(8,128)S(1)}, u32[]{:S(2)}, u32[]{:S(2)}) collective-permute-start(f32[4,6,32,128]{3,2,1,0:T(8,128)} %get-tuple-element.67), channel_id=1, source_target_pairs={{0,3},{1,2},{2,1},{3,0},{4,7},{5,6},{6,5},{7,4},{8,11},{9,10},{10,... | collective-permute-start | bytes 1179656 | tf_op jit(solution)/shard_map/ppermute | solution.py:160
  6.7 15.6 %collective-permute-start.2 = (f32[4,3,32,128]{3,2,1,0:T(8,128)}, f32[4,3,32,128]{3,2,1,0:T(8,128)S(1)}, u32[]{:S(2)}, u32[]{:S(2)}) collective-permute-start(f32[4,3,32,128]{3,2,1,0:T(8,128)} %get-tuple-element.63), channel_id=1, source_target_pairs={{0,8},{1,9},{2,10},{3,11},{4,12},{5,13},{6,14},{7,15},{8,0},{9,1},... | collective-permute-start | bytes 589832 | tf_op jit(solution)/shard_map/ppermute | solution.py:160
  9.0 17.5 %collective-permute-start.3 = (f32[4,3,32,128]{3,2,1,0:T(8,128)}, f32[4,3,32,128]{3,2,1,0:T(8,128)S(1)}, u32[]{:S(2)}, u32[]{:S(2)}) collective-permute-start(f32[4,3,32,128]{3,2,1,0:T(8,128)} %get-tuple-element.64), channel_id=1, source_target_pairs={{0,12},{1,13},{2,14},{3,15},{4,8},{5,9},{6,10},{7,11},{8,4},{9,5},... | collective-permute-start | bytes 589832 | tf_op jit(solution)/shard_map/ppermute | solution.py:160
  9.0 17.5 %collective-permute-start.1 = (f32[4,3,32,128]{3,2,1,0:T(8,128)}, f32[4,3,32,128]{3,2,1,0:T(8,128)S(1)}, u32[]{:S(2)}, u32[]{:S(2)}) collective-permute-start(f32[4,3,32,128]{3,2,1,0:T(8,128)} %get-tuple-element.62), channel_id=1, source_target_pairs={{0,4},{1,5},{2,6},{3,7},{4,0},{5,1},{6,2},{7,3},{8,12},{9,13},{10,... | collective-permute-start | bytes 589832 | tf_op jit(solution)/shard_map/ppermute | solution.py:160
  10.2 0.9 copy-start.14
  17.0 9.6 %copy-start.17 = (f32[4,6,32,128]{3,2,1,0:T(8,128)S(1)}, f32[4,6,32,128]{3,2,1,0:T(8,128)}, u32[]{:S(2)}) copy-start(f32[4,6,32,128]{3,2,1,0:T(8,128)} %get-tuple-element.72) | copy-start | bytes 1179652
  26.6 2.4 %copy-start.18 = (f32[4,3,32,128]{3,2,1,0:T(8,128)S(1)}, f32[4,3,32,128]{3,2,1,0:T(8,128)}, u32[]{:S(2)}) copy-start(f32[4,3,32,128]{3,2,1,0:T(8,128)} %get-tuple-element.76) | copy-start | bytes 589828
  26.7 17.6 %collective-permute-start.13 = (f32[4,3,32,128]{3,2,1,0:T(8,128)S(1)}, f32[4,3,32,128]{3,2,1,0:T(8,128)S(1)}, u32[]{:S(2)}, u32[]{:S(2)}) collective-permute-start(f32[4,3,32,128]{3,2,1,0:T(8,128)S(1)} %pad_maximum_fusion.11), channel_id=1, source_target_pairs={{0,12},{1,13},{2,14},{3,15},{4,8},{5,9},{6,10},{7,11},{8,4},{9,5},... | collective-permute-start | bytes 589832 | tf_op jit(solution)/shard_map/ppermute | solution.py:160
  28.9 16.9 %collective-permute-start.12 = (f32[4,3,32,128]{3,2,1,0:T(8,128)S(1)}, f32[4,3,32,128]{3,2,1,0:T(8,128)S(1)}, u32[]{:S(2)}, u32[]{:S(2)}) collective-permute-start(f32[4,3,32,128]{3,2,1,0:T(8,128)S(1)} %pad_maximum_fusion.10), channel_id=1, source_target_pairs={{0,8},{1,9},{2,10},{3,11},{4,12},{5,13},{6,14},{7,15},{8,0},{9,1},... | collective-permute-start | bytes 589832 | tf_op jit(solution)/shard_map/ppermute | solution.py:160
  29.1 2.5 %collective-permute-start.6 = (f32[4,3,32,128]{3,2,1,0:T(8,128)S(1)}, f32[4,3,32,128]{3,2,1,0:T(8,128)S(1)}, u32[]{:S(2)}, u32[]{:S(2)}) collective-permute-start(f32[4,3,32,128]{3,2,1,0:T(8,128)S(1)} %pad_maximum_fusion.5), channel_id=1, source_target_pairs={{0,1},{1,0},{2,3},{3,2},{4,5},{5,4},{6,7},{7,6},{8,9},{9,8},{10,11... | collective-permute-start | bytes 589832 | tf_op jit(solution)/shard_map/ppermute | solution.py:160
  29.9 7.5 %collective-permute-start.8 = (f32[4,3,32,128]{3,2,1,0:T(8,128)S(1)}, f32[4,3,32,128]{3,2,1,0:T(8,128)S(1)}, u32[]{:S(2)}, u32[]{:S(2)}) collective-permute-start(f32[4,3,32,128]{3,2,1,0:T(8,128)S(1)} %pad_maximum_fusion.7), channel_id=1, source_target_pairs={{0,3},{1,2},{2,1},{3,0},{4,7},{5,6},{6,5},{7,4},{8,11},{9,10},{10,... | collective-permute-start | bytes 589832 | tf_op jit(solution)/shard_map/ppermute | solution.py:160
  30.1 10.3 %collective-permute-start.7 = (f32[4,3,32,128]{3,2,1,0:T(8,128)S(1)}, f32[4,3,32,128]{3,2,1,0:T(8,128)S(1)}, u32[]{:S(2)}, u32[]{:S(2)}) collective-permute-start(f32[4,3,32,128]{3,2,1,0:T(8,128)S(1)} %pad_maximum_fusion.6), channel_id=1, source_target_pairs={{0,2},{1,3},{2,0},{3,1},{4,6},{5,7},{6,4},{7,5},{8,10},{9,11},{10,... | collective-permute-start | bytes 589832 | tf_op jit(solution)/shard_map/ppermute | solution.py:160
  31.6 17.4 %copy-start = (bf16[1024,512]{1,0:T(8,128)(2,1)S(1)}, bf16[1024,512]{1,0:T(8,128)(2,1)}, u32[]{:S(2)}) copy-start(bf16[1024,512]{1,0:T(8,128)(2,1)} %constant.29.clone.refs_6_.high_ref.refs_7_.refs_9_) | copy-start | bytes 3145732
  31.6 17.4 %copy-start.1 = (bf16[1024,512]{1,0:T(8,128)(2,1)S(1)}, bf16[1024,512]{1,0:T(8,128)(2,1)}, u32[]{:S(2)}) copy-start(bf16[1024,512]{1,0:T(8,128)(2,1)} %constant.30.clone.refs_7_.low_ref.refs_8_.refs_10_) | copy-start | bytes 3145732
  31.6 17.3 %collective-permute-start.11 = (f32[4,3,32,128]{3,2,1,0:T(8,128)S(1)}, f32[4,3,32,128]{3,2,1,0:T(8,128)S(1)}, u32[]{:S(2)}, u32[]{:S(2)}) collective-permute-start(f32[4,3,32,128]{3,2,1,0:T(8,128)S(1)} %pad_maximum_fusion.9), channel_id=1, source_target_pairs={{0,4},{1,5},{2,6},{3,7},{4,0},{5,1},{6,2},{7,3},{8,12},{9,13},{10,... | collective-permute-start | bytes 589832 | tf_op jit(solution)/shard_map/ppermute | solution.py:160
  41.6 14.9 %collective-permute-start.10 = (f32[384,128]{1,0:T(8,128)S(1)}, f32[384,128]{1,0:T(8,128)S(1)}, u32[]{:S(2)}, u32[]{:S(2)}) collective-permute-start(f32[384,128]{1,0:T(8,128)S(1)} %get-tuple-element.82), channel_id=1, source_target_pairs={{1,0},{2,1},{3,2},{4,3},{5,4},{6,5},{7,6},{8,7},{9,8},{10,9},{11,1... | collective-permute-start | bytes 589832 | tf_op jit(solution)/shard_map/ppermute | solution.py:780
  42.7 15.2 %collective-permute-start.9 = (f32[384,128]{1,0:T(8,128)S(1)}, f32[384,128]{1,0:T(8,128)S(1)}, u32[]{:S(2)}, u32[]{:S(2)}) collective-permute-start(f32[384,128]{1,0:T(8,128)S(1)} %get-tuple-element.81), channel_id=1, source_target_pairs={{0,1},{1,2},{2,3},{3,4},{4,5},{5,6},{6,7},{7,8},{8,9},{9,10},{10,1... | collective-permute-start | bytes 589832 | tf_op jit(solution)/shard_map/ppermute | solution.py:779
  44.3 17.7 %collective-permute-start.16 = (f32[4,3,32,128]{3,2,1,0:T(8,128)S(1)}, f32[4,3,32,128]{3,2,1,0:T(8,128)S(1)}, u32[]{:S(2)}, u32[]{:S(2)}) collective-permute-start(f32[4,3,32,128]{3,2,1,0:T(8,128)S(1)} %pad_maximum_fusion.3), channel_id=1, source_target_pairs={{0,12},{1,13},{2,14},{3,15},{4,8},{5,9},{6,10},{7,11},{8,4},{9,5},... | collective-permute-start | bytes 589832 | tf_op jit(solution)/shard_map/ppermute | solution.py:160
  45.8 18.5 %collective-permute-start.15 = (f32[4,3,32,128]{3,2,1,0:T(8,128)S(1)}, f32[4,3,32,128]{3,2,1,0:T(8,128)S(1)}, u32[]{:S(2)}, u32[]{:S(2)}) collective-permute-start(f32[4,3,32,128]{3,2,1,0:T(8,128)S(1)} %pad_maximum_fusion.2), channel_id=1, source_target_pairs={{0,8},{1,9},{2,10},{3,11},{4,12},{5,13},{6,14},{7,15},{8,0},{9,1},... | collective-permute-start | bytes 589832 | tf_op jit(solution)/shard_map/ppermute | solution.py:160
  48.9 8.9 %copy-start.13 = (bf16[3,128,128]{2,1,0:T(8,128)(2,1)S(1)}, bf16[3,128,128]{2,1,0:T(8,128)(2,1)}, u32[]{:S(2)}) copy-start(bf16[3,128,128]{2,1,0:T(8,128)(2,1)} %constant.38.clone.places_ref) | copy-start | bytes 294916
  57.8 6.4 %copy-start.3 = (bf16[512,1024]{1,0:T(8,128)(2,1)S(1)}, bf16[512,1024]{1,0:T(8,128)(2,1)}, u32[]{:S(2)}) copy-start(bf16[512,1024]{1,0:T(8,128)(2,1)} %constant.31.clone.refs_9_.refs_11_) | copy-start | bytes 3145732
  57.8 6.4 %copy-start.4 = (bf16[512,1024]{1,0:T(8,128)(2,1)S(1)}, bf16[512,1024]{1,0:T(8,128)(2,1)}, u32[]{:S(2)}) copy-start(bf16[512,1024]{1,0:T(8,128)(2,1)} %constant.32.clone.refs_10_.refs_12_) | copy-start | bytes 3145732
  57.8 6.4 %collective-permute-start.14 = (f32[4,3,32,128]{3,2,1,0:T(8,128)S(1)}, f32[4,3,32,128]{3,2,1,0:T(8,128)S(1)}, u32[]{:S(2)}, u32[]{:S(2)}) collective-permute-start(f32[4,3,32,128]{3,2,1,0:T(8,128)S(1)} %pad_maximum_fusion.1), channel_id=1, source_target_pairs={{0,4},{1,5},{2,6},{3,7},{4,0},{5,1},{6,2},{7,3},{8,12},{9,13},{10,... | collective-permute-start | bytes 589832 | tf_op jit(solution)/shard_map/ppermute | solution.py:160
  70.4 13.2 %collective-permute-start.17 = (f32[4,3,32,128]{3,2,1,0:T(8,128)S(1)}, f32[4,3,32,128]{3,2,1,0:T(8,128)S(1)}, u32[]{:S(2)}, u32[]{:S(2)}) collective-permute-start(f32[4,3,32,128]{3,2,1,0:T(8,128)S(1)} %get-tuple-element.97), channel_id=1, source_target_pairs={{0,4},{1,5},{2,6},{3,7},{4,0},{5,1},{6,2},{7,3},{8,12},{9,13},{10,... | collective-permute-start | bytes 589832 | tf_op jit(solution)/shard_map/ppermute | solution.py:160
  72.7 13.8 %collective-permute-start.18 = (f32[4,3,32,128]{3,2,1,0:T(8,128)S(1)}, f32[4,3,32,128]{3,2,1,0:T(8,128)S(1)}, u32[]{:S(2)}, u32[]{:S(2)}) collective-permute-start(f32[4,3,32,128]{3,2,1,0:T(8,128)S(1)} %get-tuple-element.98), channel_id=1, source_target_pairs={{0,8},{1,9},{2,10},{3,11},{4,12},{5,13},{6,14},{7,15},{8,0},{9,1},... | collective-permute-start | bytes 589832 | tf_op jit(solution)/shard_map/ppermute | solution.py:160
  73.3 18.5 %collective-permute-start.19 = (f32[4,3,32,128]{3,2,1,0:T(8,128)S(1)}, f32[4,3,32,128]{3,2,1,0:T(8,128)S(1)}, u32[]{:S(2)}, u32[]{:S(2)}) collective-permute-start(f32[4,3,32,128]{3,2,1,0:T(8,128)S(1)} %get-tuple-element.99), channel_id=1, source_target_pairs={{0,12},{1,13},{2,14},{3,15},{4,8},{5,9},{6,10},{7,11},{8,4},{9,5},... | collective-permute-start | bytes 589832 | tf_op jit(solution)/shard_map/ppermute | solution.py:160
  91.8 41.1 %all-to-all-start = ((f32[16,6,32,128]{3,2,1,0:T(8,128)}), f32[16,6,32,128]{3,2,1,0:T(8,128)}, u32[]{:S(2)}, u32[]{:S(2)}) async-start(f32[16,6,32,128]{3,2,1,0:T(8,128)} %elastic.1), calls=%async_computation | async-start | bytes 3145728 | tf_op jit(solution)/shard_map/all_to_all | solution.py:255
  97.7 2.9 %collective-permute-start.20 = (f32[4,3,32,128]{3,2,1,0:T(8,128)S(1)}, f32[4,3,32,128]{3,2,1,0:T(8,128)S(1)}, u32[]{:S(2)}, u32[]{:S(2)}) collective-permute-start(f32[4,3,32,128]{3,2,1,0:T(8,128)S(1)} %get-tuple-element.111), channel_id=1, source_target_pairs={{0,1},{1,0},{2,3},{3,2},{4,5},{5,4},{6,7},{7,6},{8,9},{9,8},{10,11... | collective-permute-start | bytes 589832 | tf_op jit(solution)/shard_map/ppermute | solution.py:160
  98.2 12.3 %collective-permute-start.21 = (f32[4,3,32,128]{3,2,1,0:T(8,128)S(1)}, f32[4,3,32,128]{3,2,1,0:T(8,128)S(1)}, u32[]{:S(2)}, u32[]{:S(2)}) collective-permute-start(f32[4,3,32,128]{3,2,1,0:T(8,128)S(1)} %get-tuple-element.112), channel_id=1, source_target_pairs={{0,2},{1,3},{2,0},{3,1},{4,6},{5,7},{6,4},{7,5},{8,10},{9,11},{10,... | collective-permute-start | bytes 589832 | tf_op jit(solution)/shard_map/ppermute | solution.py:160
  98.4 18.9 %collective-permute-start.22 = (f32[4,3,32,128]{3,2,1,0:T(8,128)S(1)}, f32[4,3,32,128]{3,2,1,0:T(8,128)S(1)}, u32[]{:S(2)}, u32[]{:S(2)}) collective-permute-start(f32[4,3,32,128]{3,2,1,0:T(8,128)S(1)} %get-tuple-element.113), channel_id=1, source_target_pairs={{0,3},{1,2},{2,1},{3,0},{4,7},{5,6},{6,5},{7,4},{8,11},{9,10},{10,... | collective-permute-start | bytes 589832 | tf_op jit(solution)/shard_map/ppermute | solution.py:160
  110.4 0.7 copy-start.9
  117.3 0.7 copy-start.11
  118.0 1.1 copy-start.5
  119.2 0.9 copy-start.10
  120.1 0.9 copy-start.12
  121.0 11.9 %copy-start.2 = (f32[6,32,2048]{2,1,0:T(8,128)S(1)}, f32[6,32,2048]{2,1,0:T(8,128)}, u32[]{:S(2)}) copy-start(f32[6,32,2048]{2,1,0:T(8,128)} %refs_5_.1) | copy-start | bytes 4718596

commit v4 on v3

--- a/solution.py
+++ b/solution.py
@@ -121,7 +121,11 @@
 
 
 def dot3(left, right):
-    return dot(left[0], right[0]) + (dot(left[0], right[1]) + dot(left[1], right[0]))
+    width = right[0].shape[1]
+    if width > BLOCK:
+        return dot(left[0], right[0]) + (dot(left[0], right[1]) + dot(left[1], right[0]))
+    both = dot(left[0], jnp.concatenate(right, axis=1))
+    return both[:, :width] + (both[:, width:] + dot(left[1], right[0]))
 
 
 def whole_spec():
@@ -757,7 +761,7 @@
         vel_nodes = far_swaps(vel_nodes, psi_nodes)
         vel_nodes, psi_nodes, fixed = barrier((vel_nodes, psi_nodes, fixed))
         vel_nodes = near_swaps(regroup(vel_nodes))
-        first_nodes = far_swaps(regroup([group[:, :FIRST] for group in psi_nodes]), vel_nodes)
+        first_nodes = far_swaps(regroup([group[:, :FIRST] for group in psi_nodes]))
         second_nodes = regroup([group[:, FIRST:] for group in psi_nodes])
     else:
         vel_nodes = far_first.unpacked(in_one(vel_nodes))

time: 138 us -> 136 us (0.986)
    ppermute x1, waiting for transfers between devices: 3 us -> 4.78 us  [body(): above = lax.ppermute(to_down, 'mode', [(j, i) for i, j in up])]
where the time goes in v4:
time: 136 us
  waiting for transfers between devices  57.1 us (42%)
  Pallas kernels  43.2 us (32%)
  starting transfers between devices  28.5 us (21%)
  local copies, waits for them, and re-layouts  5.5 us (4%)
  between operations  1.66 us (1%)
    ppermute x21, waiting for transfers between devices, swap(): return lax.ppermute(block, 'mode', [(i, i ^ bits) for i in range(devices)])  43.5 us
    ppermute x21, starting transfers between devices, swap(): return lax.ppermute(block, 'mode', [(i, i ^ bits) for i in range(devices)])  21.5 us
    pallas_call x1, Pallas kernels, body(): kernel_call(functools.partial(elastic_body, whole), (*psi_outs,), 14, scr...  9.26 us
    all_to_all x1, waiting for transfers between devices, in_one(): lax.all_to_all(arrays[0], 'mode', split_axis=0, concat_axis=0, tiled=True)  8.81 us
    pallas_call x2, Pallas kernels, advance(): pl.pallas_call(functools.partial(advance_body, layers, step, route, len(r...  7.62 us
    pallas_call x1, Pallas kernels, body(): kernel_call(functools.partial(weights_body, layers), jax.ShapeDtypeStruct...  5.79 us
    pallas_call x1, Pallas kernels, body(): kernel_call(functools.partial(momentum_body, near_first, len(second_nodes...  5.79 us
    unnamed x38, local copies, waits for them, and re-layouts  5.31 us
  transfers between devices with their start and end apart: 24, of which 13 were waited for; matrix products, arithmetic and copies ran while one was open for 0% of the time, Pallas kernels for 22%

profile of v4, /device:TPU:13, one launch (start us, length us, event | category | flops | bytes accessed | tf_op | source)
XLA Modules:
  0.0 136.1 jit_solution(1778355614223107209)
XLA Ops:
  0.7 3.5 %pack.1 = (f32[4,3,32,128]{3,2,1,0:T(8,128)}, f32[4,3,32,128]{3,2,1,0:T(8,128)}, f32[4,3,32,128]{3,2,1,0:T(8,128)}, f32[4,3,32,128]{3,2,1,0:T(8,128)}, f32[4,6,3...) custom-call(s32[1]{0:T(128)} %bitcast.me_ref.refs_0_, ...), custom_call_target="tpu_custom_call" | custom-call | tf_op jit(solution)/shard_map/pack/pallas_call | solution.py:284
  4.2 0.7 collective-permute-start
  5.2 1.5 %collective-permute-start.5 = (f32[4,6,32,128]{3,2,1,0:T(8,128)}, f32[4,6,32,128]{3,2,1,0:T(8,128)S(1)}, u32[]{:S(2)}, u32[]{:S(2)}) collective-permute-start(f32[4,6,32,128]{3,2,1,0:T(8,128)} %get-tuple-element.66), channel_id=1, source_target_pairs={{0,3},{1,2},{2,1},{3,0},{4,7},{5,6},{6,5},{7,4},{8,11},{9,10},{10,... | collective-permute-start | bytes 1179656 | tf_op jit(solution)/shard_map/ppermute | solution.py:164
  6.7 2.3 %collective-permute-start.2 = (f32[4,3,32,128]{3,2,1,0:T(8,128)}, f32[4,3,32,128]{3,2,1,0:T(8,128)S(1)}, u32[]{:S(2)}, u32[]{:S(2)}) collective-permute-start(f32[4,3,32,128]{3,2,1,0:T(8,128)} %get-tuple-element.62), channel_id=1, source_target_pairs={{0,8},{1,9},{2,10},{3,11},{4,12},{5,13},{6,14},{7,15},{8,0},{9,1},... | collective-permute-start | bytes 589832 | tf_op jit(solution)/shard_map/ppermute | solution.py:164
  9.0 1.2 collective-permute-start.1
  10.2 0.9 copy-done.14
  11.1 5.8 %weights.1.refs_7_.refs_4_ = bf16[16,384,128]{2,1,0:T(8,128)(2,1)S(1)} custom-call(s32[32]{0:T(128)S(1)} %copy-done.16, bf16[3,128,128]{2,1,0:T(8,128)(2,1)S(1)} %copy-done.14), custom_call_target="tpu_custom_call" | custom-call | tf_op jit(solution)/shard_map/weights/pallas_call | solution.py:749
  17.0 1.7 %order.1 = (bf16[10,128,128]{2,1,0:T(8,128)(2,1)S(1)}, bf16[24,128,256]{2,1,0:T(8,128)(2,1)S(1)}, bf16[10,256,256]{2,1,0:T(8,128)(2,1)S(1)}, f32[8,128]{1,0:T(8,128)S(1)}) custom-call(s32[1]{0:T(128)} %bitcast.me_ref.refs_0_, s32[32]{0:T(128)S(1)} %copy-done.16, bf16[10,128,128]{2,1,0:T(8,128)(2,1)S(1)} %copy-done.8, bf16[24,128,256]{2,1,0:T(8,128)(2,1)S(1)} %copy-done.6, ...), custom_call_target="tpu_custom_call" | custom-call | tf_op jit(solution)/shard_map/order/pallas_call | solution.py:736
  18.7 3.6 %collective-permute-done.2 = f32[4,3,32,128]{3,2,1,0:T(8,128)S(1)} collective-permute-done((f32[4,3,32,128]{3,2,1,0:T(8,128)}, f32[4,3,32,128]{3,2,1,0:T(8,128)S(1)}, u32[]{:S(2)}, u32[]{:S(2)}) %collective-permute-start.2) | collective-permute-done | bytes 196640 | tf_op jit(solution)/shard_map/ppermute | solution.py:164
  22.3 4.2 %collective-permute-done.3 = f32[4,3,32,128]{3,2,1,0:T(8,128)S(1)} collective-permute-done((f32[4,3,32,128]{3,2,1,0:T(8,128)}, f32[4,3,32,128]{3,2,1,0:T(8,128)S(1)}, u32[]{:S(2)}, u32[]{:S(2)}) %collective-permute-start.3) | collective-permute-done | bytes 196640 | tf_op jit(solution)/shard_map/ppermute | solution.py:164
  26.7 2.2 %collective-permute-start.13 = (f32[4,3,32,128]{3,2,1,0:T(8,128)S(1)}, f32[4,3,32,128]{3,2,1,0:T(8,128)S(1)}, u32[]{:S(2)}, u32[]{:S(2)}) collective-permute-start(f32[4,3,32,128]{3,2,1,0:T(8,128)S(1)} %pad_maximum_fusion.11), channel_id=1, source_target_pairs={{0,12},{1,13},{2,14},{3,15},{4,8},{5,9},{6,10},{7,11},{8,4},{9,5},... | collective-permute-start | bytes 589832 | tf_op jit(solution)/shard_map/ppermute | solution.py:164
  29.1 0.9 collective-permute-start.8
  30.0 1.3 collective-permute-start.7
  31.6 5.0 %collective-permute-done.8.refs_3_ = f32[4,3,32,128]{3,2,1,0:T(8,128)S(1)} collective-permute-done((f32[4,3,32,128]{3,2,1,0:T(8,128)S(1)}, f32[4,3,32,128]{3,2,1,0:T(8,128)S(1)}, u32[]{:S(2)}, u32[]{:S(2)}) %collective-permute-start.8) | collective-permute-done | bytes 196640 | tf_op jit(solution)/shard_map/ppermute | solution.py:164
  36.6 1.2 collective-permute-start.11
  37.8 3.1 %collective-permute-done.7.refs_2_ = f32[4,3,32,128]{3,2,1,0:T(8,128)S(1)} collective-permute-done((f32[4,3,32,128]{3,2,1,0:T(8,128)S(1)}, f32[4,3,32,128]{3,2,1,0:T(8,128)S(1)}, u32[]{:S(2)}, u32[]{:S(2)}) %collective-permute-start.7) | collective-permute-done | bytes 196640 | tf_op jit(solution)/shard_map/ppermute | solution.py:164
  40.9 1.2 faces.1
  42.1 0.4 collective-permute-start.10
  42.5 2.3 %collective-permute-start.9 = (f32[384,128]{1,0:T(8,128)S(1)}, f32[384,128]{1,0:T(8,128)S(1)}, u32[]{:S(2)}, u32[]{:S(2)}) collective-permute-start(f32[384,128]{1,0:T(8,128)S(1)} %get-tuple-element.80), channel_id=1, source_target_pairs={{0,1},{1,2},{2,3},{3,4},{4,5},{5,6},{6,7},{7,8},{8,9},{9,10},{10,1... | collective-permute-start | bytes 589832 | tf_op jit(solution)/shard_map/ppermute | solution.py:783
  44.8 0.8 collective-permute-start.16
  45.7 3.5 %collective-permute-start.15 = (f32[4,3,32,128]{3,2,1,0:T(8,128)S(1)}, f32[4,3,32,128]{3,2,1,0:T(8,128)S(1)}, u32[]{:S(2)}, u32[]{:S(2)}) collective-permute-start(f32[4,3,32,128]{3,2,1,0:T(8,128)S(1)} %pad_maximum_fusion.2), channel_id=1, source_target_pairs={{0,8},{1,9},{2,10},{3,11},{4,12},{5,13},{6,14},{7,15},{8,0},{9,1},... | collective-permute-start | bytes 589832 | tf_op jit(solution)/shard_map/ppermute | solution.py:164
  49.1 4.2 %velocity.1 = (f32[3,512,128]{2,1,0:T(8,128)S(1)}, f32[15,512,128]{2,1,0:T(8,128)S(1)}, bf16[512,384]{1,0:T(8,128)(2,1)S(1)}, bf16[512,384]{1,0:T(8,128)(2,1)S(1)}, f32[3,512,128]{2,1,0:T(8,128)S(1)}) custom-call(s32[1]{0:T(128)} %bitcast.me_ref.refs_0_, f32[4,3,32,128]{3,2,1,0:T(8,128)S(1)} %pad_maximum_fusion.8.refs_0_, ...), custom_call_target="tpu_custom_call" | custom-call | tf_op jit(solution)/shard_map/velocity/pallas_call | solution.py:793
  53.4 4.8 %collective-permute-done.10.above_ref = f32[384,128]{1,0:T(8,128)S(1)} collective-permute-done((f32[384,128]{1,0:T(8,128)S(1)}, f32[384,128]{1,0:T(8,128)S(1)}, u32[]{:S(2)}, u32[]{:S(2)}) %collective-permute-start.10) | collective-permute-done | bytes 196640 | tf_op jit(solution)/shard_map/ppermute | solution.py:784
  58.3 2.9 %halo.1.refs_6_.refs_8_ = f32[12,512,128]{2,1,0:T(8,128)S(1)} custom-call(f32[384,128]{1,0:T(8,128)S(1)} %collective-permute-done.9.below_ref, f32[384,128]{1,0:T(8,128)S(1)} %collective-permute-done.10.above_ref, f32[3,512,128]{2,1,0:T(8,128)S(1)} %get-tuple-element.92.vel_ref, bf16[1024,512]{1,0:T(8,128)(2,1)S(1)} %copy-done, ...), custom_call_target="tpu_custom_call" | custom-call | tf_op jit(solution)/shard_map/halo/pallas_call | solution.py:809
  61.1 1.1 collective-permute-done.16.refs_3_
  62.2 2.1 %collective-permute-done.15.refs_2_ = f32[4,3,32,128]{3,2,1,0:T(8,128)S(1)} collective-permute-done((f32[4,3,32,128]{3,2,1,0:T(8,128)S(1)}, f32[4,3,32,128]{3,2,1,0:T(8,128)S(1)}, u32[]{:S(2)}, u32[]{:S(2)}) %collective-permute-start.15) | collective-permute-done | bytes 196640 | tf_op jit(solution)/shard_map/ppermute | solution.py:164
  64.3 0.7 collective-permute-done.14.refs_1_
  65.0 5.8 %momentum.1 = (f32[4,3,32,128]{3,2,1,0:T(8,128)S(1)}, f32[4,3,32,128]{3,2,1,0:T(8,128)S(1)}, f32[4,3,32,128]{3,2,1,0:T(8,128)S(1)}, f32[4,3,32,128]{3,2,1,0:T(8,...) custom-call(s32[1]{0:T(128)} %bitcast.me_ref.refs_0_, ...), custom_call_target="tpu_custom_call" | custom-call | tf_op jit(solution)/shard_map/momentum/pallas_call | solution.py:822
  70.8 2.0 %collective-permute-start.17 = (f32[4,3,32,128]{3,2,1,0:T(8,128)S(1)}, f32[4,3,32,128]{3,2,1,0:T(8,128)S(1)}, u32[]{:S(2)}, u32[]{:S(2)}) collective-permute-start(f32[4,3,32,128]{3,2,1,0:T(8,128)S(1)} %get-tuple-element.95), channel_id=1, source_target_pairs={{0,4},{1,5},{2,6},{3,7},{4,0},{5,1},{6,2},{7,3},{8,12},{9,13},{10,... | collective-permute-start | bytes 589832 | tf_op jit(solution)/shard_map/ppermute | solution.py:164
  73.1 1.0 collective-permute-start.19
  74.0 9.3 %elastic.1 = f32[16,6,32,128]{3,2,1,0:T(8,128)} custom-call(s32[1]{0:T(128)} %bitcast.me_ref.refs_0_, bf16[512,384]{1,0:T(8,128)(2,1)S(1)} %get-tuple-element.98.refs_0_, bf16[512,384]{1,0:T(8,128)(2,1)S(1)} %get-tuple-element.99.refs_1_, bf16[512,384]{1,0:T(8,128)(2,1)S(1)} %get-tuple-element.100.refs_2_, bf16[512,384]{1,0:T(8,128)(2,1)S(1)} %get-tuple-element.101.refs_3_, ...), custom_call_target="tpu_custom_call" | custom-call | tf_op jit(solution)/shard_map/elastic/pallas_call | solution.py:840
  83.3 2.9 %collective-permute-done.18.refs_2_ = f32[4,3,32,128]{3,2,1,0:T(8,128)S(1)} collective-permute-done((f32[4,3,32,128]{3,2,1,0:T(8,128)S(1)}, f32[4,3,32,128]{3,2,1,0:T(8,128)S(1)}, u32[]{:S(2)}, u32[]{:S(2)}) %collective-permute-start.18) | collective-permute-done | bytes 196640 | tf_op jit(solution)/shard_map/ppermute | solution.py:164
  86.2 4.8 %collective-permute-done.19.refs_3_ = f32[4,3,32,128]{3,2,1,0:T(8,128)S(1)} collective-permute-done((f32[4,3,32,128]{3,2,1,0:T(8,128)S(1)}, f32[4,3,32,128]{3,2,1,0:T(8,128)S(1)}, u32[]{:S(2)}, u32[]{:S(2)}) %collective-permute-start.19) | collective-permute-done | bytes 196640 | tf_op jit(solution)/shard_map/ppermute | solution.py:164
  91.0 4.3 %all-to-all-start = ((f32[16,6,32,128]{3,2,1,0:T(8,128)}), f32[16,6,32,128]{3,2,1,0:T(8,128)}, u32[]{:S(2)}, u32[]{:S(2)}) async-start(f32[16,6,32,128]{3,2,1,0:T(8,128)} %elastic.1), calls=%async_computation | async-start | bytes 3145728 | tf_op jit(solution)/shard_map/all_to_all | solution.py:259
  95.3 1.2 turn.1
  96.5 0.4 collective-permute-start.20
  96.8 0.3 collective-permute-start.21
  97.1 1.5 %collective-permute-start.22 = (f32[4,3,32,128]{3,2,1,0:T(8,128)S(1)}, f32[4,3,32,128]{3,2,1,0:T(8,128)S(1)}, u32[]{:S(2)}, u32[]{:S(2)}) collective-permute-start(f32[4,3,32,128]{3,2,1,0:T(8,128)S(1)} %get-tuple-element.111), channel_id=1, source_target_pairs={{0,3},{1,2},{2,1},{3,0},{4,7},{5,6},{6,5},{7,4},{8,11},{9,10},{10,... | collective-permute-start | bytes 589832 | tf_op jit(solution)/shard_map/ppermute | solution.py:164
  99.4 9.8 %collective-permute-done.21.refs_5_ = f32[4,3,32,128]{3,2,1,0:T(8,128)S(1)} collective-permute-done((f32[4,3,32,128]{3,2,1,0:T(8,128)S(1)}, f32[4,3,32,128]{3,2,1,0:T(8,128)S(1)}, u32[]{:S(2)}, u32[]{:S(2)}) %collective-permute-start.21) | collective-permute-done | bytes 196640 | tf_op jit(solution)/shard_map/ppermute | solution.py:164
  109.1 0.7 copy-done.9
  109.8 6.2 %collective-permute-done.22.refs_6_ = f32[4,3,32,128]{3,2,1,0:T(8,128)S(1)} collective-permute-done((f32[4,3,32,128]{3,2,1,0:T(8,128)S(1)}, f32[4,3,32,128]{3,2,1,0:T(8,128)S(1)}, u32[]{:S(2)}, u32[]{:S(2)}) %collective-permute-start.22) | collective-permute-done | bytes 196640 | tf_op jit(solution)/shard_map/ppermute | solution.py:164
  116.0 0.7 copy-done.11
  116.7 1.1 copy-done.5
  117.8 0.9 copy-done.10
  118.8 0.9 copy-done.12
  119.7 3.1 %advance.2 = f32[3,32,2048]{2,1,0:T(8,128)} custom-call(s32[1]{0:T(128)} %bitcast.me_ref.refs_0_, s32[32]{0:T(128)S(1)} %copy-done.16, f32[1]{0:T(128)S(6)} %select_n.9.refs_2_, f32[4,3,32,128]{3,2,1,0:T(8,128)S(1)} %get-tuple-element.108.refs_3_, f32[4,3,32,128]{3,2,1,0:T(8,128)S(1)} %collective-permute-done.20.refs_4_, f32[4,3,32,128]{3,2,1,0:T(8,128)S(1)} %copy-done.10, ...), custom_call_target="tpu_custom_call" | custom-call | tf_op jit(solution)/shard_map/advance/pallas_call | solution.py:700
  122.8 8.8 %all-to-all-done.refs_3_ = f32[16,6,32,128]{3,2,1,0:T(8,128)} async-done(((f32[16,6,32,128]{3,2,1,0:T(8,128)}), f32[16,6,32,128]{3,2,1,0:T(8,128)}, u32[]{:S(2)}, u32[]{:S(2)}) %all-to-all-start) | async-done | bytes 1572896 | tf_op jit(solution)/shard_map/all_to_all | solution.py:259
  131.6 4.5 %advance.3 = f32[6,32,2048]{2,1,0:T(8,128)} custom-call(s32[1]{0:T(128)} %bitcast.me_ref.refs_0_, s32[32]{0:T(128)S(1)} %copy-done.16, f32[1]{0:T(128)S(6)} %select_n.9.refs_2_, f32[16,6,32,128]{3,2,1,0:T(8,128)} %all-to-all-done.refs_3_, bf16[16,384,128]{2,1,0:T(8,128)(2,1)S(1)} %weights.1.refs_7_.refs_4_, f32[6,32,2048]{2,1,0:T(8,128)S(1)} %copy-done.2), custom_call_target="tpu_custom_call" | custom-call | tf_op jit(solution)/shard_map/advance/pallas_call | solution.py:700
  (65 shorter events, 1.3 us)
Async XLA Ops:
  0.6 9.6 %copy-start.16 = (s32[32]{0:T(128)S(1)}, s32[32]{0:T(128)}, u32[]{:S(2)}) copy-start(s32[32]{0:T(128)} %refs_1_.5) | copy-start | bytes 388
  0.6 16.3 %copy-start.6 = (bf16[24,128,256]{2,1,0:T(8,128)(2,1)S(1)}, bf16[24,128,256]{2,1,0:T(8,128)(2,1)}, u32[]{:S(2)}) copy-start(bf16[24,128,256]{2,1,0:T(8,128)(2,1)} %constant.35.clone.faces_ref) | copy-start | bytes 4718596
  0.7 16.3 %copy-start.8 = (bf16[10,128,128]{2,1,0:T(8,128)(2,1)S(1)}, bf16[10,128,128]{2,1,0:T(8,128)(2,1)}, u32[]{:S(2)}) copy-start(bf16[10,128,128]{2,1,0:T(8,128)(2,1)} %constant.34.clone.both_ref) | copy-start | bytes 983044
  0.7 16.3 %copy-start.15 = (f32[128,128]{1,0:T(8,128)S(1)}, f32[128,128]{1,0:T(8,128)}, u32[]{:S(2)}) copy-start(f32[128,128]{1,0:T(8,128)} %constant.33.clone.inv_r_ref) | copy-start | bytes 196612
  4.2 12.7 %copy-start.7 = (bf16[18,256,128]{2,1,0:T(8,128)(2,1)S(1)}, bf16[18,256,128]{2,1,0:T(8,128)(2,1)}, u32[]{:S(2)}) copy-start(bf16[18,256,128]{2,1,0:T(8,128)(2,1)} %constant.36.clone.halos_ref) | copy-start | bytes 3538948
  4.2 4.8 %collective-permute-start = (f32[4,6,32,128]{3,2,1,0:T(8,128)}, f32[4,6,32,128]{3,2,1,0:T(8,128)S(1)}, u32[]{:S(2)}, u32[]{:S(2)}) collective-permute-start(f32[4,6,32,128]{3,2,1,0:T(8,128)} %get-tuple-element.60), channel_id=1, source_target_pairs={{0,1},{1,0},{2,3},{3,2},{4,5},{5,4},{6,7},{7,6},{8,9},{9,8},{10,11... | collective-permute-start | bytes 1179656 | tf_op jit(solution)/shard_map/ppermute | solution.py:164
  5.0 21.6 %collective-permute-start.4 = (f32[4,6,32,128]{3,2,1,0:T(8,128)}, f32[4,6,32,128]{3,2,1,0:T(8,128)S(1)}, u32[]{:S(2)}, u32[]{:S(2)}) collective-permute-start(f32[4,6,32,128]{3,2,1,0:T(8,128)} %get-tuple-element.65), channel_id=1, source_target_pairs={{0,2},{1,3},{2,0},{3,1},{4,6},{5,7},{6,4},{7,5},{8,10},{9,11},{10,... | collective-permute-start | bytes 1179656 | tf_op jit(solution)/shard_map/ppermute | solution.py:164
  5.2 21.3 %collective-permute-start.5 = (f32[4,6,32,128]{3,2,1,0:T(8,128)}, f32[4,6,32,128]{3,2,1,0:T(8,128)S(1)}, u32[]{:S(2)}, u32[]{:S(2)}) collective-permute-start(f32[4,6,32,128]{3,2,1,0:T(8,128)} %get-tuple-element.66), channel_id=1, source_target_pairs={{0,3},{1,2},{2,1},{3,0},{4,7},{5,6},{6,5},{7,4},{8,11},{9,10},{10,... | collective-permute-start | bytes 1179656 | tf_op jit(solution)/shard_map/ppermute | solution.py:164
  6.7 15.6 %collective-permute-start.2 = (f32[4,3,32,128]{3,2,1,0:T(8,128)}, f32[4,3,32,128]{3,2,1,0:T(8,128)S(1)}, u32[]{:S(2)}, u32[]{:S(2)}) collective-permute-start(f32[4,3,32,128]{3,2,1,0:T(8,128)} %get-tuple-element.62), channel_id=1, source_target_pairs={{0,8},{1,9},{2,10},{3,11},{4,12},{5,13},{6,14},{7,15},{8,0},{9,1},... | collective-permute-start | bytes 589832 | tf_op jit(solution)/shard_map/ppermute | solution.py:164
  9.0 17.5 %collective-permute-start.3 = (f32[4,3,32,128]{3,2,1,0:T(8,128)}, f32[4,3,32,128]{3,2,1,0:T(8,128)S(1)}, u32[]{:S(2)}, u32[]{:S(2)}) collective-permute-start(f32[4,3,32,128]{3,2,1,0:T(8,128)} %get-tuple-element.63), channel_id=1, source_target_pairs={{0,12},{1,13},{2,14},{3,15},{4,8},{5,9},{6,10},{7,11},{8,4},{9,5},... | collective-permute-start | bytes 589832 | tf_op jit(solution)/shard_map/ppermute | solution.py:164
  9.0 17.5 %collective-permute-start.1 = (f32[4,3,32,128]{3,2,1,0:T(8,128)}, f32[4,3,32,128]{3,2,1,0:T(8,128)S(1)}, u32[]{:S(2)}, u32[]{:S(2)}) collective-permute-start(f32[4,3,32,128]{3,2,1,0:T(8,128)} %get-tuple-element.61), channel_id=1, source_target_pairs={{0,4},{1,5},{2,6},{3,7},{4,0},{5,1},{6,2},{7,3},{8,12},{9,13},{10,... | collective-permute-start | bytes 589832 | tf_op jit(solution)/shard_map/ppermute | solution.py:164
  10.2 0.9 copy-start.14
  17.0 9.6 %copy-start.17 = (f32[4,6,32,128]{3,2,1,0:T(8,128)S(1)}, f32[4,6,32,128]{3,2,1,0:T(8,128)}, u32[]{:S(2)}) copy-start(f32[4,6,32,128]{3,2,1,0:T(8,128)} %get-tuple-element.71) | copy-start | bytes 1179652
  26.6 2.4 %copy-start.18 = (f32[4,3,32,128]{3,2,1,0:T(8,128)S(1)}, f32[4,3,32,128]{3,2,1,0:T(8,128)}, u32[]{:S(2)}) copy-start(f32[4,3,32,128]{3,2,1,0:T(8,128)} %get-tuple-element.75) | copy-start | bytes 589828
  26.7 18.1 %collective-permute-start.13 = (f32[4,3,32,128]{3,2,1,0:T(8,128)S(1)}, f32[4,3,32,128]{3,2,1,0:T(8,128)S(1)}, u32[]{:S(2)}, u32[]{:S(2)}) collective-permute-start(f32[4,3,32,128]{3,2,1,0:T(8,128)S(1)} %pad_maximum_fusion.11), channel_id=1, source_target_pairs={{0,12},{1,13},{2,14},{3,15},{4,8},{5,9},{6,10},{7,11},{8,4},{9,5},... | collective-permute-start | bytes 589832 | tf_op jit(solution)/shard_map/ppermute | solution.py:164
  28.9 16.8 %collective-permute-start.12 = (f32[4,3,32,128]{3,2,1,0:T(8,128)S(1)}, f32[4,3,32,128]{3,2,1,0:T(8,128)S(1)}, u32[]{:S(2)}, u32[]{:S(2)}) collective-permute-start(f32[4,3,32,128]{3,2,1,0:T(8,128)S(1)} %pad_maximum_fusion.10), channel_id=1, source_target_pairs={{0,8},{1,9},{2,10},{3,11},{4,12},{5,13},{6,14},{7,15},{8,0},{9,1},... | collective-permute-start | bytes 589832 | tf_op jit(solution)/shard_map/ppermute | solution.py:164
  29.1 7.5 %collective-permute-start.8 = (f32[4,3,32,128]{3,2,1,0:T(8,128)S(1)}, f32[4,3,32,128]{3,2,1,0:T(8,128)S(1)}, u32[]{:S(2)}, u32[]{:S(2)}) collective-permute-start(f32[4,3,32,128]{3,2,1,0:T(8,128)S(1)} %pad_maximum_fusion.7), channel_id=1, source_target_pairs={{0,3},{1,2},{2,1},{3,0},{4,7},{5,6},{6,5},{7,4},{8,11},{9,10},{10,... | collective-permute-start | bytes 589832 | tf_op jit(solution)/shard_map/ppermute | solution.py:164
  30.0 10.8 %collective-permute-start.7 = (f32[4,3,32,128]{3,2,1,0:T(8,128)S(1)}, f32[4,3,32,128]{3,2,1,0:T(8,128)S(1)}, u32[]{:S(2)}, u32[]{:S(2)}) collective-permute-start(f32[4,3,32,128]{3,2,1,0:T(8,128)S(1)} %pad_maximum_fusion.6), channel_id=1, source_target_pairs={{0,2},{1,3},{2,0},{3,1},{4,6},{5,7},{6,4},{7,5},{8,10},{9,11},{10,... | collective-permute-start | bytes 589832 | tf_op jit(solution)/shard_map/ppermute | solution.py:164
  31.4 9.5 %collective-permute-start.6 = (f32[4,3,32,128]{3,2,1,0:T(8,128)S(1)}, f32[4,3,32,128]{3,2,1,0:T(8,128)S(1)}, u32[]{:S(2)}, u32[]{:S(2)}) collective-permute-start(f32[4,3,32,128]{3,2,1,0:T(8,128)S(1)} %pad_maximum_fusion.5), channel_id=1, source_target_pairs={{0,1},{1,0},{2,3},{3,2},{4,5},{5,4},{6,7},{7,6},{8,9},{9,8},{10,11... | collective-permute-start | bytes 589832 | tf_op jit(solution)/shard_map/ppermute | solution.py:164
  31.6 17.5 %copy-start = (bf16[1024,512]{1,0:T(8,128)(2,1)S(1)}, bf16[1024,512]{1,0:T(8,128)(2,1)}, u32[]{:S(2)}) copy-start(bf16[1024,512]{1,0:T(8,128)(2,1)} %constant.29.clone.refs_6_.high_ref.refs_7_.refs_9_) | copy-start | bytes 3145732
  31.6 17.5 %copy-start.1 = (bf16[1024,512]{1,0:T(8,128)(2,1)S(1)}, bf16[1024,512]{1,0:T(8,128)(2,1)}, u32[]{:S(2)}) copy-start(bf16[1024,512]{1,0:T(8,128)(2,1)} %constant.30.clone.refs_7_.low_ref.refs_8_.refs_10_) | copy-start | bytes 3145732
  36.6 12.5 %collective-permute-start.11 = (f32[4,3,32,128]{3,2,1,0:T(8,128)S(1)}, f32[4,3,32,128]{3,2,1,0:T(8,128)S(1)}, u32[]{:S(2)}, u32[]{:S(2)}) collective-permute-start(f32[4,3,32,128]{3,2,1,0:T(8,128)S(1)} %pad_maximum_fusion.9), channel_id=1, source_target_pairs={{0,4},{1,5},{2,6},{3,7},{4,0},{5,1},{6,2},{7,3},{8,12},{9,13},{10,... | collective-permute-start | bytes 589832 | tf_op jit(solution)/shard_map/ppermute | solution.py:164
  42.1 16.1 %collective-permute-start.10 = (f32[384,128]{1,0:T(8,128)S(1)}, f32[384,128]{1,0:T(8,128)S(1)}, u32[]{:S(2)}, u32[]{:S(2)}) collective-permute-start(f32[384,128]{1,0:T(8,128)S(1)} %get-tuple-element.81), channel_id=1, source_target_pairs={{1,0},{2,1},{3,2},{4,3},{5,4},{6,5},{7,6},{8,7},{9,8},{10,9},{11,1... | collective-permute-start | bytes 589832 | tf_op jit(solution)/shard_map/ppermute | solution.py:784
  42.5 15.7 %collective-permute-start.9 = (f32[384,128]{1,0:T(8,128)S(1)}, f32[384,128]{1,0:T(8,128)S(1)}, u32[]{:S(2)}, u32[]{:S(2)}) collective-permute-start(f32[384,128]{1,0:T(8,128)S(1)} %get-tuple-element.80), channel_id=1, source_target_pairs={{0,1},{1,2},{2,3},{3,4},{4,5},{5,6},{6,7},{7,8},{8,9},{9,10},{10,1... | collective-permute-start | bytes 589832 | tf_op jit(solution)/shard_map/ppermute | solution.py:783
  44.8 17.4 %collective-permute-start.16 = (f32[4,3,32,128]{3,2,1,0:T(8,128)S(1)}, f32[4,3,32,128]{3,2,1,0:T(8,128)S(1)}, u32[]{:S(2)}, u32[]{:S(2)}) collective-permute-start(f32[4,3,32,128]{3,2,1,0:T(8,128)S(1)} %pad_maximum_fusion.3), channel_id=1, source_target_pairs={{0,12},{1,13},{2,14},{3,15},{4,8},{5,9},{6,10},{7,11},{8,4},{9,5},... | collective-permute-start | bytes 589832 | tf_op jit(solution)/shard_map/ppermute | solution.py:164
  45.7 18.6 %collective-permute-start.15 = (f32[4,3,32,128]{3,2,1,0:T(8,128)S(1)}, f32[4,3,32,128]{3,2,1,0:T(8,128)S(1)}, u32[]{:S(2)}, u32[]{:S(2)}) collective-permute-start(f32[4,3,32,128]{3,2,1,0:T(8,128)S(1)} %pad_maximum_fusion.2), channel_id=1, source_target_pairs={{0,8},{1,9},{2,10},{3,11},{4,12},{5,13},{6,14},{7,15},{8,0},{9,1},... | collective-permute-start | bytes 589832 | tf_op jit(solution)/shard_map/ppermute | solution.py:164
  49.1 9.1 %copy-start.13 = (bf16[3,128,128]{2,1,0:T(8,128)(2,1)S(1)}, bf16[3,128,128]{2,1,0:T(8,128)(2,1)}, u32[]{:S(2)}) copy-start(bf16[3,128,128]{2,1,0:T(8,128)(2,1)} %constant.38.clone.places_ref) | copy-start | bytes 294916
  58.2 6.8 %copy-start.3 = (bf16[512,1024]{1,0:T(8,128)(2,1)S(1)}, bf16[512,1024]{1,0:T(8,128)(2,1)}, u32[]{:S(2)}) copy-start(bf16[512,1024]{1,0:T(8,128)(2,1)} %constant.31.clone.refs_9_.refs_11_) | copy-start | bytes 3145732
  58.2 6.8 %copy-start.4 = (bf16[512,1024]{1,0:T(8,128)(2,1)S(1)}, bf16[512,1024]{1,0:T(8,128)(2,1)}, u32[]{:S(2)}) copy-start(bf16[512,1024]{1,0:T(8,128)(2,1)} %constant.32.clone.refs_10_.refs_12_) | copy-start | bytes 3145732
  58.2 6.8 %collective-permute-start.14 = (f32[4,3,32,128]{3,2,1,0:T(8,128)S(1)}, f32[4,3,32,128]{3,2,1,0:T(8,128)S(1)}, u32[]{:S(2)}, u32[]{:S(2)}) collective-permute-start(f32[4,3,32,128]{3,2,1,0:T(8,128)S(1)} %pad_maximum_fusion.1), channel_id=1, source_target_pairs={{0,4},{1,5},{2,6},{3,7},{4,0},{5,1},{6,2},{7,3},{8,12},{9,13},{10,... | collective-permute-start | bytes 589832 | tf_op jit(solution)/shard_map/ppermute | solution.py:164
  70.8 12.5 %collective-permute-start.17 = (f32[4,3,32,128]{3,2,1,0:T(8,128)S(1)}, f32[4,3,32,128]{3,2,1,0:T(8,128)S(1)}, u32[]{:S(2)}, u32[]{:S(2)}) collective-permute-start(f32[4,3,32,128]{3,2,1,0:T(8,128)S(1)} %get-tuple-element.95), channel_id=1, source_target_pairs={{0,4},{1,5},{2,6},{3,7},{4,0},{5,1},{6,2},{7,3},{8,12},{9,13},{10,... | collective-permute-start | bytes 589832 | tf_op jit(solution)/shard_map/ppermute | solution.py:164
  72.8 13.4 %collective-permute-start.18 = (f32[4,3,32,128]{3,2,1,0:T(8,128)S(1)}, f32[4,3,32,128]{3,2,1,0:T(8,128)S(1)}, u32[]{:S(2)}, u32[]{:S(2)}) collective-permute-start(f32[4,3,32,128]{3,2,1,0:T(8,128)S(1)} %get-tuple-element.96), channel_id=1, source_target_pairs={{0,8},{1,9},{2,10},{3,11},{4,12},{5,13},{6,14},{7,15},{8,0},{9,1},... | collective-permute-start | bytes 589832 | tf_op jit(solution)/shard_map/ppermute | solution.py:164
  73.1 17.9 %collective-permute-start.19 = (f32[4,3,32,128]{3,2,1,0:T(8,128)S(1)}, f32[4,3,32,128]{3,2,1,0:T(8,128)S(1)}, u32[]{:S(2)}, u32[]{:S(2)}) collective-permute-start(f32[4,3,32,128]{3,2,1,0:T(8,128)S(1)} %get-tuple-element.97), channel_id=1, source_target_pairs={{0,12},{1,13},{2,14},{3,15},{4,8},{5,9},{6,10},{7,11},{8,4},{9,5},... | collective-permute-start | bytes 589832 | tf_op jit(solution)/shard_map/ppermute | solution.py:164
  91.0 40.6 %all-to-all-start = ((f32[16,6,32,128]{3,2,1,0:T(8,128)}), f32[16,6,32,128]{3,2,1,0:T(8,128)}, u32[]{:S(2)}, u32[]{:S(2)}) async-start(f32[16,6,32,128]{3,2,1,0:T(8,128)} %elastic.1), calls=%async_computation | async-start | bytes 3145728 | tf_op jit(solution)/shard_map/all_to_all | solution.py:259
  96.5 2.9 %collective-permute-start.20 = (f32[4,3,32,128]{3,2,1,0:T(8,128)S(1)}, f32[4,3,32,128]{3,2,1,0:T(8,128)S(1)}, u32[]{:S(2)}, u32[]{:S(2)}) collective-permute-start(f32[4,3,32,128]{3,2,1,0:T(8,128)S(1)} %get-tuple-element.109), channel_id=1, source_target_pairs={{0,1},{1,0},{2,3},{3,2},{4,5},{5,4},{6,7},{7,6},{8,9},{9,8},{10,11... | collective-permute-start | bytes 589832 | tf_op jit(solution)/shard_map/ppermute | solution.py:164
  96.8 12.3 %collective-permute-start.21 = (f32[4,3,32,128]{3,2,1,0:T(8,128)S(1)}, f32[4,3,32,128]{3,2,1,0:T(8,128)S(1)}, u32[]{:S(2)}, u32[]{:S(2)}) collective-permute-start(f32[4,3,32,128]{3,2,1,0:T(8,128)S(1)} %get-tuple-element.110), channel_id=1, source_target_pairs={{0,2},{1,3},{2,0},{3,1},{4,6},{5,7},{6,4},{7,5},{8,10},{9,11},{10,... | collective-permute-start | bytes 589832 | tf_op jit(solution)/shard_map/ppermute | solution.py:164
  97.1 18.9 %collective-permute-start.22 = (f32[4,3,32,128]{3,2,1,0:T(8,128)S(1)}, f32[4,3,32,128]{3,2,1,0:T(8,128)S(1)}, u32[]{:S(2)}, u32[]{:S(2)}) collective-permute-start(f32[4,3,32,128]{3,2,1,0:T(8,128)S(1)} %get-tuple-element.111), channel_id=1, source_target_pairs={{0,3},{1,2},{2,1},{3,0},{4,7},{5,6},{6,5},{7,4},{8,11},{9,10},{10,... | collective-permute-start | bytes 589832 | tf_op jit(solution)/shard_map/ppermute | solution.py:164
  109.1 0.7 copy-start.9
  116.0 0.7 copy-start.11
  116.7 1.1 copy-start.5
  117.8 0.9 copy-start.10
  118.8 0.9 copy-start.12
  119.7 11.9 %copy-start.2 = (f32[6,32,2048]{2,1,0:T(8,128)S(1)}, f32[6,32,2048]{2,1,0:T(8,128)}, u32[]{:S(2)}) copy-start(f32[6,32,2048]{2,1,0:T(8,128)} %refs_5_.1) | copy-start | bytes 4718596

commit v5 on v4

--- a/solution.py
+++ b/solution.py
@@ -522,11 +522,14 @@
 
 
 def exponential(psi, sign):
-    x = tuple(v * (sign * 0.125) for v in psi)
-    x2 = square(x)
-    x4 = square(x2)
-    even = plus_identity(tuple(v * 0.5 + w * (1.0 / 24.0) for v, w in zip(x2, x4)))
-    odd = commuting_product(x, plus_identity(tuple(v * (1.0 / 6.0) for v in x2)))
+    square_2 = square(psi)
+    square_4 = square(square_2)
+    even = plus_identity(
+        tuple(v * (0.5 / 64.0) + w * (1.0 / 24.0 / 4096.0) for v, w in zip(square_2, square_4))
+    )
+    factor = tuple(v * (sign / 6.0 / 512.0) for v in square_2)
+    factor = tuple(v + sign * 0.125 if at in DIAGONAL else v for at, v in enumerate(factor))
+    odd = commuting_product(psi, factor)
     total = tuple(v + w for v, w in zip(even, odd))
     for _ in range(3):
         total = square(total)
@@ -560,12 +563,15 @@
         for member in range(6):
             conform_out[member, rows, :] = conform[member]
         stress = tuple(v - 1.0 if at in DIAGONAL else v for at, v in enumerate(conform))
-        for lane, member in enumerate((0, 2, 1, 4, 2, 5)):
-            put(stress_h, stress_l, rows, lanes_of(lane), stress[member])
+        for member, at in ((0, (0,)), (2, (1, 4)), (1, (2,)), (4, (3,)), (5, (5,))):
+            high, low = split(stress[member])
+            for lane in at:
+                stress_h[rows, lanes_of(lane)] = high
+                stress_l[rows, lanes_of(lane)] = low
         hoop = tuple(stress[at] * inv_r for at in (1, 3, 4))
         turned = pl.ds(pl.multiple_of(planes + start, rows_step), rows_step)
         for at in range(3):
-            put(vel_h, vel_l, turned, lanes_of(at), -hoop[at])
+            put(vel_h, vel_l, turned, lanes_of(at), hoop[at])
         carried = [flow_ref[12 + at, rows, :] + halo_ref[9 + at, rows, :] for at in range(3)]
         mom_s[0, rows, :] = carried[0] + (stress[0] * inv_r - hoop[1])
         mom_s[1, rows, :] = carried[1] + 2.0 * hoop[0]
@@ -649,22 +655,28 @@
     me_ref, orient_ref, wall_ref = refs[:3]
     rate_refs, (mean_ref, old_ref, out_ref, rates) = refs[3 : 3 + count], refs[3 + count :]
     fields, local_modes = old_ref.shape[0], old_ref.shape[1]
+    aligned = rates.dtype == BF16
+    rows = fields * local_modes
 
     @pl.when(pl.program_id(0) == 0)
     def _():
         for array, place, rel in route.land:
-            rates[route.index(me_ref, rel)] = rate_refs[array][place]
+            layer = route.index(me_ref, rel)
+            if aligned:
+                high, low = split(rate_refs[array][place].reshape(rows, BLOCK))
+                rates[layer + 1, :rows, :] = high
+                rates[layer + 1, rows:, :] = low
+            else:
+                rates[layer + 1] = rate_refs[array][place]
+        rates[0] = rates[layers]
+        rates[layers + 1] = rates[1]
 
     first = pl.program_id(0) * step
-    merged = local_modes % 8 == 0
 
     def averaged(index, at, field):
-        below = lax.rem(index + (layers - 1), layers)
-        above = lax.rem(index + 1, layers)
         total = None
-        for number, layer in enumerate((below, index, above)):
-            block = rates[layer] if field is None else rates[layer, field]
-            high, low = split(block.reshape(-1, BLOCK))
+        for number in range(3):
+            high, low = split(rates[index + number, field])
             weights = mean_ref[at, number * BLOCK : (number + 1) * BLOCK, :]
             part = dot(high, weights) + dot(low, weights)
             total = part if total is None else total + part
@@ -673,8 +685,10 @@
     for at in range(step):
         index = first + at
         lanes = lanes_of(at)
-        if merged:
-            every = averaged(index, at, None)
+        if aligned:
+            near = jnp.concatenate([rates[index + number] for number in range(3)], axis=1)
+            every = dot(near, mean_ref[at])
+            every = every[:rows] + every[rows:]
             change = [every[f * local_modes : (f + 1) * local_modes] for f in range(fields)]
         else:
             change = [averaged(index, at, f) for f in range(fields)]
@@ -694,7 +708,7 @@
 def advance(rates, route, weights, old, me, orientation, wall):
     fields, local_modes, nodes = old.shape
     layers = nodes // BLOCK
-    step = 4
+    step = 16
     block = pl.BlockSpec((fields, local_modes, step * BLOCK), lambda i: (0, 0, i))
     scalar = pl.BlockSpec(memory_space=pltpu.SMEM)
     return pl.pallas_call(
@@ -705,7 +719,11 @@
         + [pl.BlockSpec((step, 3 * BLOCK, BLOCK), lambda i: (i, 0, 0)), block],
         out_specs=block,
         out_shape=jax.ShapeDtypeStruct(old.shape, F32),
-        scratch_shapes=[pltpu.VMEM((layers, fields, local_modes, BLOCK), F32)],
+        scratch_shapes=[
+            pltpu.VMEM((layers + 2, 2 * fields * local_modes, BLOCK), BF16)
+            if local_modes % 16 == 0
+            else pltpu.VMEM((layers + 2, fields, local_modes, BLOCK), F32)
+        ],
         compiler_params=pltpu.CompilerParams(vmem_limit_bytes=24 * MIB),
         name="advance",
     )(me, orientation, wall, *rates, weights, old)
@@ -730,7 +748,8 @@
 
     fourier = fourier_tables(planes)
     high, low = (jnp.asarray(half) for half in split_table(fourier))
-    back_high, back_low = (jnp.asarray(half) for half in split_table(fourier.T))
+    signed = np.concatenate([fourier[:planes].T, -fourier[planes:].T], axis=1)
+    back_high, back_low = (jnp.asarray(half) for half in split_table(signed))
     inv_r_table = jnp.asarray(np.tile(inv_r_nodes[:, None], (1, BLOCK)), F32)
 
     both_s, faces_s, halos_s, inv_r = kernel_call(

time: 136 us -> 136 us (level)
  Pallas kernels: 43.2 us -> 41.6 us
    pallas_call x2, Pallas kernels: 7.62 us -> 6.23 us  [advance(): pl.pallas_call(functools.partial(advance_body, layers, step, route, len(r...]
  transfers between devices with their start and end apart: 24 -> 24, of which waited for: 13 -> 13; matrix products, arithmetic and copies ran while one was open for 0% -> 0% of each run, Pallas kernels for 22% -> 21%
where the time goes in v5:
time: 136 us; the launch traced here: 135 us
  waiting for transfers between devices  57.8 us (42%)
  Pallas kernels  41.6 us (31%)
  starting transfers between devices  28.7 us (21%)
  local copies, waits for them, and re-layouts  5.5 us (4%)
  between operations  1.66 us (1%)
    ppermute x21, waiting for transfers between devices, swap(): return lax.ppermute(block, 'mode', [(i, i ^ bits) for i in range(devices)])  43.4 us
    ppermute x21, starting transfers between devices, swap(): return lax.ppermute(block, 'mode', [(i, i ^ bits) for i in range(devices)])  21.5 us
    all_to_all x1, waiting for transfers between devices, in_one(): lax.all_to_all(arrays[0], 'mode', split_axis=0, concat_axis=0, tiled=True)  9.62 us
    pallas_call x1, Pallas kernels, body(): kernel_call(functools.partial(elastic_body, whole), (*psi_outs,), 14, scr...  9.12 us
    pallas_call x2, Pallas kernels, advance(): pl.pallas_call(functools.partial(advance_body, layers, step, route, len(r...  6.23 us
    pallas_call x1, Pallas kernels, body(): kernel_call(functools.partial(weights_body, layers), jax.ShapeDtypeStruct...  5.79 us
    pallas_call x1, Pallas kernels, body(): kernel_call(functools.partial(momentum_body, near_first, len(second_nodes...  5.72 us
    unnamed x38, local copies, waits for them, and re-layouts  5.31 us
  transfers between devices with their start and end apart: 24, of which 13 were waited for; matrix products, arithmetic and copies ran while one was open for 0% of the time, Pallas kernels for 21%

profile of v5, /device:TPU:13, one launch (start us, length us, event | category | flops | bytes accessed | tf_op | source)
XLA Modules:
  0.0 135.5 jit_solution(2558092380217517983)
XLA Ops:
  0.7 3.5 %pack.1 = (f32[4,3,32,128]{3,2,1,0:T(8,128)}, f32[4,3,32,128]{3,2,1,0:T(8,128)}, f32[4,3,32,128]{3,2,1,0:T(8,128)}, f32[4,3,32,128]{3,2,1,0:T(8,128)}, f32[4,6,3...) custom-call(s32[1]{0:T(128)} %bitcast.me_ref.refs_0_, ...), custom_call_target="tpu_custom_call" | custom-call | tf_op jit(solution)/shard_map/pack/pallas_call | solution.py:284
  4.2 0.7 collective-permute-start
  5.2 1.5 %collective-permute-start.5 = (f32[4,6,32,128]{3,2,1,0:T(8,128)}, f32[4,6,32,128]{3,2,1,0:T(8,128)S(1)}, u32[]{:S(2)}, u32[]{:S(2)}) collective-permute-start(f32[4,6,32,128]{3,2,1,0:T(8,128)} %get-tuple-element.66), channel_id=1, source_target_pairs={{0,3},{1,2},{2,1},{3,0},{4,7},{5,6},{6,5},{7,4},{8,11},{9,10},{10,... | collective-permute-start | bytes 1179656 | tf_op jit(solution)/shard_map/ppermute | solution.py:164
  6.7 2.3 %collective-permute-start.2 = (f32[4,3,32,128]{3,2,1,0:T(8,128)}, f32[4,3,32,128]{3,2,1,0:T(8,128)S(1)}, u32[]{:S(2)}, u32[]{:S(2)}) collective-permute-start(f32[4,3,32,128]{3,2,1,0:T(8,128)} %get-tuple-element.62), channel_id=1, source_target_pairs={{0,8},{1,9},{2,10},{3,11},{4,12},{5,13},{6,14},{7,15},{8,0},{9,1},... | collective-permute-start | bytes 589832 | tf_op jit(solution)/shard_map/ppermute | solution.py:164
  9.0 1.2 collective-permute-start.1
  10.2 0.9 copy-done.14
  11.1 5.8 %weights.1.refs_7_.refs_4_ = bf16[16,384,128]{2,1,0:T(8,128)(2,1)S(1)} custom-call(s32[32]{0:T(128)S(1)} %copy-done.16, bf16[3,128,128]{2,1,0:T(8,128)(2,1)S(1)} %copy-done.14), custom_call_target="tpu_custom_call" | custom-call | tf_op jit(solution)/shard_map/weights/pallas_call | solution.py:768
  17.0 1.7 %order.1 = (bf16[10,128,128]{2,1,0:T(8,128)(2,1)S(1)}, bf16[24,128,256]{2,1,0:T(8,128)(2,1)S(1)}, bf16[10,256,256]{2,1,0:T(8,128)(2,1)S(1)}, f32[8,128]{1,0:T(8,128)S(1)}) custom-call(s32[1]{0:T(128)} %bitcast.me_ref.refs_0_, s32[32]{0:T(128)S(1)} %copy-done.16, bf16[10,128,128]{2,1,0:T(8,128)(2,1)S(1)} %copy-done.8, bf16[24,128,256]{2,1,0:T(8,128)(2,1)S(1)} %copy-done.6, ...), custom_call_target="tpu_custom_call" | custom-call | tf_op jit(solution)/shard_map/order/pallas_call | solution.py:755
  18.7 3.6 %collective-permute-done.2 = f32[4,3,32,128]{3,2,1,0:T(8,128)S(1)} collective-permute-done((f32[4,3,32,128]{3,2,1,0:T(8,128)}, f32[4,3,32,128]{3,2,1,0:T(8,128)S(1)}, u32[]{:S(2)}, u32[]{:S(2)}) %collective-permute-start.2) | collective-permute-done | bytes 196640 | tf_op jit(solution)/shard_map/ppermute | solution.py:164
  22.3 4.2 %collective-permute-done.3 = f32[4,3,32,128]{3,2,1,0:T(8,128)S(1)} collective-permute-done((f32[4,3,32,128]{3,2,1,0:T(8,128)}, f32[4,3,32,128]{3,2,1,0:T(8,128)S(1)}, u32[]{:S(2)}, u32[]{:S(2)}) %collective-permute-start.3) | collective-permute-done | bytes 196640 | tf_op jit(solution)/shard_map/ppermute | solution.py:164
  26.7 2.2 %collective-permute-start.13 = (f32[4,3,32,128]{3,2,1,0:T(8,128)S(1)}, f32[4,3,32,128]{3,2,1,0:T(8,128)S(1)}, u32[]{:S(2)}, u32[]{:S(2)}) collective-permute-start(f32[4,3,32,128]{3,2,1,0:T(8,128)S(1)} %pad_maximum_fusion.11), channel_id=1, source_target_pairs={{0,12},{1,13},{2,14},{3,15},{4,8},{5,9},{6,10},{7,11},{8,4},{9,5},... | collective-permute-start | bytes 589832 | tf_op jit(solution)/shard_map/ppermute | solution.py:164
  29.1 0.9 collective-permute-start.8
  30.0 1.3 collective-permute-start.7
  31.6 5.0 %collective-permute-done.8.refs_3_ = f32[4,3,32,128]{3,2,1,0:T(8,128)S(1)} collective-permute-done((f32[4,3,32,128]{3,2,1,0:T(8,128)S(1)}, f32[4,3,32,128]{3,2,1,0:T(8,128)S(1)}, u32[]{:S(2)}, u32[]{:S(2)}) %collective-permute-start.8) | collective-permute-done | bytes 196640 | tf_op jit(solution)/shard_map/ppermute | solution.py:164
  36.6 1.2 collective-permute-start.11
  37.8 3.1 %collective-permute-done.7.refs_2_ = f32[4,3,32,128]{3,2,1,0:T(8,128)S(1)} collective-permute-done((f32[4,3,32,128]{3,2,1,0:T(8,128)S(1)}, f32[4,3,32,128]{3,2,1,0:T(8,128)S(1)}, u32[]{:S(2)}, u32[]{:S(2)}) %collective-permute-start.7) | collective-permute-done | bytes 196640 | tf_op jit(solution)/shard_map/ppermute | solution.py:164
  40.9 1.2 faces.1
  42.1 0.4 collective-permute-start.10
  42.5 2.3 %collective-permute-start.9 = (f32[384,128]{1,0:T(8,128)S(1)}, f32[384,128]{1,0:T(8,128)S(1)}, u32[]{:S(2)}, u32[]{:S(2)}) collective-permute-start(f32[384,128]{1,0:T(8,128)S(1)} %get-tuple-element.80), channel_id=1, source_target_pairs={{0,1},{1,2},{2,3},{3,4},{4,5},{5,6},{6,7},{7,8},{8,9},{9,10},{10,1... | collective-permute-start | bytes 589832 | tf_op jit(solution)/shard_map/ppermute | solution.py:802
  44.8 0.8 collective-permute-start.16
  45.7 3.5 %collective-permute-start.15 = (f32[4,3,32,128]{3,2,1,0:T(8,128)S(1)}, f32[4,3,32,128]{3,2,1,0:T(8,128)S(1)}, u32[]{:S(2)}, u32[]{:S(2)}) collective-permute-start(f32[4,3,32,128]{3,2,1,0:T(8,128)S(1)} %pad_maximum_fusion.2), channel_id=1, source_target_pairs={{0,8},{1,9},{2,10},{3,11},{4,12},{5,13},{6,14},{7,15},{8,0},{9,1},... | collective-permute-start | bytes 589832 | tf_op jit(solution)/shard_map/ppermute | solution.py:164
  49.1 4.2 %velocity.1 = (f32[3,512,128]{2,1,0:T(8,128)S(1)}, f32[15,512,128]{2,1,0:T(8,128)S(1)}, bf16[512,384]{1,0:T(8,128)(2,1)S(1)}, bf16[512,384]{1,0:T(8,128)(2,1)S(1)}, f32[3,512,128]{2,1,0:T(8,128)S(1)}) custom-call(s32[1]{0:T(128)} %bitcast.me_ref.refs_0_, f32[4,3,32,128]{3,2,1,0:T(8,128)S(1)} %pad_maximum_fusion.8.refs_0_, ...), custom_call_target="tpu_custom_call" | custom-call | tf_op jit(solution)/shard_map/velocity/pallas_call | solution.py:812
  53.4 4.8 %collective-permute-done.10.above_ref = f32[384,128]{1,0:T(8,128)S(1)} collective-permute-done((f32[384,128]{1,0:T(8,128)S(1)}, f32[384,128]{1,0:T(8,128)S(1)}, u32[]{:S(2)}, u32[]{:S(2)}) %collective-permute-start.10) | collective-permute-done | bytes 196640 | tf_op jit(solution)/shard_map/ppermute | solution.py:803
  58.3 2.9 %halo.1.refs_6_.refs_8_ = f32[12,512,128]{2,1,0:T(8,128)S(1)} custom-call(f32[384,128]{1,0:T(8,128)S(1)} %collective-permute-done.9.below_ref, f32[384,128]{1,0:T(8,128)S(1)} %collective-permute-done.10.above_ref, f32[3,512,128]{2,1,0:T(8,128)S(1)} %get-tuple-element.92.vel_ref, bf16[1024,512]{1,0:T(8,128)(2,1)S(1)} %copy-done, ...), custom_call_target="tpu_custom_call" | custom-call | tf_op jit(solution)/shard_map/halo/pallas_call | solution.py:828
  61.1 1.1 collective-permute-done.16.refs_3_
  62.2 2.1 %collective-permute-done.15.refs_2_ = f32[4,3,32,128]{3,2,1,0:T(8,128)S(1)} collective-permute-done((f32[4,3,32,128]{3,2,1,0:T(8,128)S(1)}, f32[4,3,32,128]{3,2,1,0:T(8,128)S(1)}, u32[]{:S(2)}, u32[]{:S(2)}) %collective-permute-start.15) | collective-permute-done | bytes 196640 | tf_op jit(solution)/shard_map/ppermute | solution.py:164
  64.3 0.7 collective-permute-done.14.refs_1_
  65.0 5.7 %momentum.1 = (f32[4,3,32,128]{3,2,1,0:T(8,128)S(1)}, f32[4,3,32,128]{3,2,1,0:T(8,128)S(1)}, f32[4,3,32,128]{3,2,1,0:T(8,128)S(1)}, f32[4,3,32,128]{3,2,1,0:T(8,...) custom-call(s32[1]{0:T(128)} %bitcast.me_ref.refs_0_, ...), custom_call_target="tpu_custom_call" | custom-call | tf_op jit(solution)/shard_map/momentum/pallas_call | solution.py:841
  70.7 2.0 %collective-permute-start.17 = (f32[4,3,32,128]{3,2,1,0:T(8,128)S(1)}, f32[4,3,32,128]{3,2,1,0:T(8,128)S(1)}, u32[]{:S(2)}, u32[]{:S(2)}) collective-permute-start(f32[4,3,32,128]{3,2,1,0:T(8,128)S(1)} %get-tuple-element.95), channel_id=1, source_target_pairs={{0,4},{1,5},{2,6},{3,7},{4,0},{5,1},{6,2},{7,3},{8,12},{9,13},{10,... | collective-permute-start | bytes 589832 | tf_op jit(solution)/shard_map/ppermute | solution.py:164
  72.7 0.3 collective-permute-start.18
  73.0 1.0 collective-permute-start.19
  74.0 9.1 %elastic.1 = f32[16,6,32,128]{3,2,1,0:T(8,128)} custom-call(s32[1]{0:T(128)} %bitcast.me_ref.refs_0_, bf16[512,384]{1,0:T(8,128)(2,1)S(1)} %get-tuple-element.98.refs_0_, bf16[512,384]{1,0:T(8,128)(2,1)S(1)} %get-tuple-element.99.refs_1_, bf16[512,384]{1,0:T(8,128)(2,1)S(1)} %get-tuple-element.100.refs_2_, bf16[512,384]{1,0:T(8,128)(2,1)S(1)} %get-tuple-element.101.refs_3_, ...), custom_call_target="tpu_custom_call" | custom-call | tf_op jit(solution)/shard_map/elastic/pallas_call | solution.py:859
  83.1 3.1 %collective-permute-done.18.refs_2_ = f32[4,3,32,128]{3,2,1,0:T(8,128)S(1)} collective-permute-done((f32[4,3,32,128]{3,2,1,0:T(8,128)S(1)}, f32[4,3,32,128]{3,2,1,0:T(8,128)S(1)}, u32[]{:S(2)}, u32[]{:S(2)}) %collective-permute-start.18) | collective-permute-done | bytes 196640 | tf_op jit(solution)/shard_map/ppermute | solution.py:164
  86.2 4.8 %collective-permute-done.19.refs_3_ = f32[4,3,32,128]{3,2,1,0:T(8,128)S(1)} collective-permute-done((f32[4,3,32,128]{3,2,1,0:T(8,128)S(1)}, f32[4,3,32,128]{3,2,1,0:T(8,128)S(1)}, u32[]{:S(2)}, u32[]{:S(2)}) %collective-permute-start.19) | collective-permute-done | bytes 196640 | tf_op jit(solution)/shard_map/ppermute | solution.py:164
  90.9 4.5 %all-to-all-start = ((f32[16,6,32,128]{3,2,1,0:T(8,128)}), f32[16,6,32,128]{3,2,1,0:T(8,128)}, u32[]{:S(2)}, u32[]{:S(2)}) async-start(f32[16,6,32,128]{3,2,1,0:T(8,128)} %elastic.1), calls=%async_computation | async-start | bytes 3145728 | tf_op jit(solution)/shard_map/all_to_all | solution.py:259
  95.4 1.2 turn.1
  96.8 0.5 collective-permute-start.21
  97.3 1.5 %collective-permute-start.22 = (f32[4,3,32,128]{3,2,1,0:T(8,128)S(1)}, f32[4,3,32,128]{3,2,1,0:T(8,128)S(1)}, u32[]{:S(2)}, u32[]{:S(2)}) collective-permute-start(f32[4,3,32,128]{3,2,1,0:T(8,128)S(1)} %get-tuple-element.111), channel_id=1, source_target_pairs={{0,3},{1,2},{2,1},{3,0},{4,7},{5,6},{6,5},{7,4},{8,11},{9,10},{10,... | collective-permute-start | bytes 589832 | tf_op jit(solution)/shard_map/ppermute | solution.py:164
  99.5 9.4 %collective-permute-done.21.refs_5_ = f32[4,3,32,128]{3,2,1,0:T(8,128)S(1)} collective-permute-done((f32[4,3,32,128]{3,2,1,0:T(8,128)S(1)}, f32[4,3,32,128]{3,2,1,0:T(8,128)S(1)}, u32[]{:S(2)}, u32[]{:S(2)}) %collective-permute-start.21) | collective-permute-done | bytes 196640 | tf_op jit(solution)/shard_map/ppermute | solution.py:164
  108.9 0.7 copy-done.9
  109.6 6.4 %collective-permute-done.22.refs_6_ = f32[4,3,32,128]{3,2,1,0:T(8,128)S(1)} collective-permute-done((f32[4,3,32,128]{3,2,1,0:T(8,128)S(1)}, f32[4,3,32,128]{3,2,1,0:T(8,128)S(1)}, u32[]{:S(2)}, u32[]{:S(2)}) %collective-permute-start.22) | collective-permute-done | bytes 196640 | tf_op jit(solution)/shard_map/ppermute | solution.py:164
  116.0 0.7 copy-done.11
  116.6 1.1 copy-done.5
  117.8 0.9 copy-done.10
  118.7 0.9 copy-done.12
  119.6 2.3 %advance.2 = f32[3,32,2048]{2,1,0:T(8,128)} custom-call(s32[1]{0:T(128)} %bitcast.me_ref.refs_0_, s32[32]{0:T(128)S(1)} %copy-done.16, f32[1]{0:T(128)S(6)} %select_n.9.refs_2_, f32[4,3,32,128]{3,2,1,0:T(8,128)S(1)} %get-tuple-element.108.refs_3_, f32[4,3,32,128]{3,2,1,0:T(8,128)S(1)} %collective-permute-done.20.refs_4_, f32[4,3,32,128]{3,2,1,0:T(8,128)S(1)} %copy-done.10, ...), custom_call_target="tpu_custom_call" | custom-call | tf_op jit(solution)/shard_map/advance/pallas_call | solution.py:714
  121.9 9.6 %all-to-all-done.refs_3_ = f32[16,6,32,128]{3,2,1,0:T(8,128)} async-done(((f32[16,6,32,128]{3,2,1,0:T(8,128)}), f32[16,6,32,128]{3,2,1,0:T(8,128)}, u32[]{:S(2)}, u32[]{:S(2)}) %all-to-all-start) | async-done | bytes 1572896 | tf_op jit(solution)/shard_map/all_to_all | solution.py:259
  131.5 4.0 %advance.3 = f32[6,32,2048]{2,1,0:T(8,128)} custom-call(s32[1]{0:T(128)} %bitcast.me_ref.refs_0_, s32[32]{0:T(128)S(1)} %copy-done.16, f32[1]{0:T(128)S(6)} %select_n.9.refs_2_, f32[16,6,32,128]{3,2,1,0:T(8,128)} %all-to-all-done.refs_3_, bf16[16,384,128]{2,1,0:T(8,128)(2,1)S(1)} %weights.1.refs_7_.refs_4_, f32[6,32,2048]{2,1,0:T(8,128)S(1)} %copy-done.2), custom_call_target="tpu_custom_call" | custom-call | tf_op jit(solution)/shard_map/advance/pallas_call | solution.py:714
  (65 shorter events, 1.1 us)
Async XLA Ops:
  0.6 9.6 %copy-start.16 = (s32[32]{0:T(128)S(1)}, s32[32]{0:T(128)}, u32[]{:S(2)}) copy-start(s32[32]{0:T(128)} %refs_1_.5) | copy-start | bytes 388
  0.6 16.3 %copy-start.6 = (bf16[24,128,256]{2,1,0:T(8,128)(2,1)S(1)}, bf16[24,128,256]{2,1,0:T(8,128)(2,1)}, u32[]{:S(2)}) copy-start(bf16[24,128,256]{2,1,0:T(8,128)(2,1)} %constant.35.clone.faces_ref) | copy-start | bytes 4718596
  0.7 16.3 %copy-start.8 = (bf16[10,128,128]{2,1,0:T(8,128)(2,1)S(1)}, bf16[10,128,128]{2,1,0:T(8,128)(2,1)}, u32[]{:S(2)}) copy-start(bf16[10,128,128]{2,1,0:T(8,128)(2,1)} %constant.34.clone.both_ref) | copy-start | bytes 983044
  0.7 16.3 %copy-start.15 = (f32[128,128]{1,0:T(8,128)S(1)}, f32[128,128]{1,0:T(8,128)}, u32[]{:S(2)}) copy-start(f32[128,128]{1,0:T(8,128)} %constant.33.clone.inv_r_ref) | copy-start | bytes 196612
  4.2 12.7 %copy-start.7 = (bf16[18,256,128]{2,1,0:T(8,128)(2,1)S(1)}, bf16[18,256,128]{2,1,0:T(8,128)(2,1)}, u32[]{:S(2)}) copy-start(bf16[18,256,128]{2,1,0:T(8,128)(2,1)} %constant.36.clone.halos_ref) | copy-start | bytes 3538948
  4.2 4.8 %collective-permute-start = (f32[4,6,32,128]{3,2,1,0:T(8,128)}, f32[4,6,32,128]{3,2,1,0:T(8,128)S(1)}, u32[]{:S(2)}, u32[]{:S(2)}) collective-permute-start(f32[4,6,32,128]{3,2,1,0:T(8,128)} %get-tuple-element.60), channel_id=1, source_target_pairs={{0,1},{1,0},{2,3},{3,2},{4,5},{5,4},{6,7},{7,6},{8,9},{9,8},{10,11... | collective-permute-start | bytes 1179656 | tf_op jit(solution)/shard_map/ppermute | solution.py:164
  5.0 21.6 %collective-permute-start.4 = (f32[4,6,32,128]{3,2,1,0:T(8,128)}, f32[4,6,32,128]{3,2,1,0:T(8,128)S(1)}, u32[]{:S(2)}, u32[]{:S(2)}) collective-permute-start(f32[4,6,32,128]{3,2,1,0:T(8,128)} %get-tuple-element.65), channel_id=1, source_target_pairs={{0,2},{1,3},{2,0},{3,1},{4,6},{5,7},{6,4},{7,5},{8,10},{9,11},{10,... | collective-permute-start | bytes 1179656 | tf_op jit(solution)/shard_map/ppermute | solution.py:164
  5.2 21.3 %collective-permute-start.5 = (f32[4,6,32,128]{3,2,1,0:T(8,128)}, f32[4,6,32,128]{3,2,1,0:T(8,128)S(1)}, u32[]{:S(2)}, u32[]{:S(2)}) collective-permute-start(f32[4,6,32,128]{3,2,1,0:T(8,128)} %get-tuple-element.66), channel_id=1, source_target_pairs={{0,3},{1,2},{2,1},{3,0},{4,7},{5,6},{6,5},{7,4},{8,11},{9,10},{10,... | collective-permute-start | bytes 1179656 | tf_op jit(solution)/shard_map/ppermute | solution.py:164
  6.7 15.6 %collective-permute-start.2 = (f32[4,3,32,128]{3,2,1,0:T(8,128)}, f32[4,3,32,128]{3,2,1,0:T(8,128)S(1)}, u32[]{:S(2)}, u32[]{:S(2)}) collective-permute-start(f32[4,3,32,128]{3,2,1,0:T(8,128)} %get-tuple-element.62), channel_id=1, source_target_pairs={{0,8},{1,9},{2,10},{3,11},{4,12},{5,13},{6,14},{7,15},{8,0},{9,1},... | collective-permute-start | bytes 589832 | tf_op jit(solution)/shard_map/ppermute | solution.py:164
  9.0 17.5 %collective-permute-start.3 = (f32[4,3,32,128]{3,2,1,0:T(8,128)}, f32[4,3,32,128]{3,2,1,0:T(8,128)S(1)}, u32[]{:S(2)}, u32[]{:S(2)}) collective-permute-start(f32[4,3,32,128]{3,2,1,0:T(8,128)} %get-tuple-element.63), channel_id=1, source_target_pairs={{0,12},{1,13},{2,14},{3,15},{4,8},{5,9},{6,10},{7,11},{8,4},{9,5},... | collective-permute-start | bytes 589832 | tf_op jit(solution)/shard_map/ppermute | solution.py:164
  9.0 17.5 %collective-permute-start.1 = (f32[4,3,32,128]{3,2,1,0:T(8,128)}, f32[4,3,32,128]{3,2,1,0:T(8,128)S(1)}, u32[]{:S(2)}, u32[]{:S(2)}) collective-permute-start(f32[4,3,32,128]{3,2,1,0:T(8,128)} %get-tuple-element.61), channel_id=1, source_target_pairs={{0,4},{1,5},{2,6},{3,7},{4,0},{5,1},{6,2},{7,3},{8,12},{9,13},{10,... | collective-permute-start | bytes 589832 | tf_op jit(solution)/shard_map/ppermute | solution.py:164
  10.2 0.9 copy-start.14
  17.0 9.6 %copy-start.17 = (f32[4,6,32,128]{3,2,1,0:T(8,128)S(1)}, f32[4,6,32,128]{3,2,1,0:T(8,128)}, u32[]{:S(2)}) copy-start(f32[4,6,32,128]{3,2,1,0:T(8,128)} %get-tuple-element.71) | copy-start | bytes 1179652
  26.6 2.4 %copy-start.18 = (f32[4,3,32,128]{3,2,1,0:T(8,128)S(1)}, f32[4,3,32,128]{3,2,1,0:T(8,128)}, u32[]{:S(2)}) copy-start(f32[4,3,32,128]{3,2,1,0:T(8,128)} %get-tuple-element.75) | copy-start | bytes 589828
  26.7 18.1 %collective-permute-start.13 = (f32[4,3,32,128]{3,2,1,0:T(8,128)S(1)}, f32[4,3,32,128]{3,2,1,0:T(8,128)S(1)}, u32[]{:S(2)}, u32[]{:S(2)}) collective-permute-start(f32[4,3,32,128]{3,2,1,0:T(8,128)S(1)} %pad_maximum_fusion.11), channel_id=1, source_target_pairs={{0,12},{1,13},{2,14},{3,15},{4,8},{5,9},{6,10},{7,11},{8,4},{9,5},... | collective-permute-start | bytes 589832 | tf_op jit(solution)/shard_map/ppermute | solution.py:164
  28.9 16.8 %collective-permute-start.12 = (f32[4,3,32,128]{3,2,1,0:T(8,128)S(1)}, f32[4,3,32,128]{3,2,1,0:T(8,128)S(1)}, u32[]{:S(2)}, u32[]{:S(2)}) collective-permute-start(f32[4,3,32,128]{3,2,1,0:T(8,128)S(1)} %pad_maximum_fusion.10), channel_id=1, source_target_pairs={{0,8},{1,9},{2,10},{3,11},{4,12},{5,13},{6,14},{7,15},{8,0},{9,1},... | collective-permute-start | bytes 589832 | tf_op jit(solution)/shard_map/ppermute | solution.py:164
  29.1 7.5 %collective-permute-start.8 = (f32[4,3,32,128]{3,2,1,0:T(8,128)S(1)}, f32[4,3,32,128]{3,2,1,0:T(8,128)S(1)}, u32[]{:S(2)}, u32[]{:S(2)}) collective-permute-start(f32[4,3,32,128]{3,2,1,0:T(8,128)S(1)} %pad_maximum_fusion.7), channel_id=1, source_target_pairs={{0,3},{1,2},{2,1},{3,0},{4,7},{5,6},{6,5},{7,4},{8,11},{9,10},{10,... | collective-permute-start | bytes 589832 | tf_op jit(solution)/shard_map/ppermute | solution.py:164
  30.0 10.8 %collective-permute-start.7 = (f32[4,3,32,128]{3,2,1,0:T(8,128)S(1)}, f32[4,3,32,128]{3,2,1,0:T(8,128)S(1)}, u32[]{:S(2)}, u32[]{:S(2)}) collective-permute-start(f32[4,3,32,128]{3,2,1,0:T(8,128)S(1)} %pad_maximum_fusion.6), channel_id=1, source_target_pairs={{0,2},{1,3},{2,0},{3,1},{4,6},{5,7},{6,4},{7,5},{8,10},{9,11},{10,... | collective-permute-start | bytes 589832 | tf_op jit(solution)/shard_map/ppermute | solution.py:164
  31.4 9.5 %collective-permute-start.6 = (f32[4,3,32,128]{3,2,1,0:T(8,128)S(1)}, f32[4,3,32,128]{3,2,1,0:T(8,128)S(1)}, u32[]{:S(2)}, u32[]{:S(2)}) collective-permute-start(f32[4,3,32,128]{3,2,1,0:T(8,128)S(1)} %pad_maximum_fusion.5), channel_id=1, source_target_pairs={{0,1},{1,0},{2,3},{3,2},{4,5},{5,4},{6,7},{7,6},{8,9},{9,8},{10,11... | collective-permute-start | bytes 589832 | tf_op jit(solution)/shard_map/ppermute | solution.py:164
  31.6 17.5 %copy-start = (bf16[1024,512]{1,0:T(8,128)(2,1)S(1)}, bf16[1024,512]{1,0:T(8,128)(2,1)}, u32[]{:S(2)}) copy-start(bf16[1024,512]{1,0:T(8,128)(2,1)} %constant.29.clone.refs_6_.high_ref.refs_7_.refs_9_) | copy-start | bytes 3145732
  31.6 17.5 %copy-start.1 = (bf16[1024,512]{1,0:T(8,128)(2,1)S(1)}, bf16[1024,512]{1,0:T(8,128)(2,1)}, u32[]{:S(2)}) copy-start(bf16[1024,512]{1,0:T(8,128)(2,1)} %constant.30.clone.refs_7_.low_ref.refs_8_.refs_10_) | copy-start | bytes 3145732
  36.6 12.5 %collective-permute-start.11 = (f32[4,3,32,128]{3,2,1,0:T(8,128)S(1)}, f32[4,3,32,128]{3,2,1,0:T(8,128)S(1)}, u32[]{:S(2)}, u32[]{:S(2)}) collective-permute-start(f32[4,3,32,128]{3,2,1,0:T(8,128)S(1)} %pad_maximum_fusion.9), channel_id=1, source_target_pairs={{0,4},{1,5},{2,6},{3,7},{4,0},{5,1},{6,2},{7,3},{8,12},{9,13},{10,... | collective-permute-start | bytes 589832 | tf_op jit(solution)/shard_map/ppermute | solution.py:164
  42.1 16.1 %collective-permute-start.10 = (f32[384,128]{1,0:T(8,128)S(1)}, f32[384,128]{1,0:T(8,128)S(1)}, u32[]{:S(2)}, u32[]{:S(2)}) collective-permute-start(f32[384,128]{1,0:T(8,128)S(1)} %get-tuple-element.81), channel_id=1, source_target_pairs={{1,0},{2,1},{3,2},{4,3},{5,4},{6,5},{7,6},{8,7},{9,8},{10,9},{11,1... | collective-permute-start | bytes 589832 | tf_op jit(solution)/shard_map/ppermute | solution.py:803
  42.5 15.7 %collective-permute-start.9 = (f32[384,128]{1,0:T(8,128)S(1)}, f32[384,128]{1,0:T(8,128)S(1)}, u32[]{:S(2)}, u32[]{:S(2)}) collective-permute-start(f32[384,128]{1,0:T(8,128)S(1)} %get-tuple-element.80), channel_id=1, source_target_pairs={{0,1},{1,2},{2,3},{3,4},{4,5},{5,6},{6,7},{7,8},{8,9},{9,10},{10,1... | collective-permute-start | bytes 589832 | tf_op jit(solution)/shard_map/ppermute | solution.py:802
  44.8 17.4 %collective-permute-start.16 = (f32[4,3,32,128]{3,2,1,0:T(8,128)S(1)}, f32[4,3,32,128]{3,2,1,0:T(8,128)S(1)}, u32[]{:S(2)}, u32[]{:S(2)}) collective-permute-start(f32[4,3,32,128]{3,2,1,0:T(8,128)S(1)} %pad_maximum_fusion.3), channel_id=1, source_target_pairs={{0,12},{1,13},{2,14},{3,15},{4,8},{5,9},{6,10},{7,11},{8,4},{9,5},... | collective-permute-start | bytes 589832 | tf_op jit(solution)/shard_map/ppermute | solution.py:164
  45.7 18.6 %collective-permute-start.15 = (f32[4,3,32,128]{3,2,1,0:T(8,128)S(1)}, f32[4,3,32,128]{3,2,1,0:T(8,128)S(1)}, u32[]{:S(2)}, u32[]{:S(2)}) collective-permute-start(f32[4,3,32,128]{3,2,1,0:T(8,128)S(1)} %pad_maximum_fusion.2), channel_id=1, source_target_pairs={{0,8},{1,9},{2,10},{3,11},{4,12},{5,13},{6,14},{7,15},{8,0},{9,1},... | collective-permute-start | bytes 589832 | tf_op jit(solution)/shard_map/ppermute | solution.py:164
  49.1 9.1 %copy-start.13 = (bf16[3,128,128]{2,1,0:T(8,128)(2,1)S(1)}, bf16[3,128,128]{2,1,0:T(8,128)(2,1)}, u32[]{:S(2)}) copy-start(bf16[3,128,128]{2,1,0:T(8,128)(2,1)} %constant.38.clone.places_ref) | copy-start | bytes 294916
  58.2 6.8 %copy-start.3 = (bf16[512,1024]{1,0:T(8,128)(2,1)S(1)}, bf16[512,1024]{1,0:T(8,128)(2,1)}, u32[]{:S(2)}) copy-start(bf16[512,1024]{1,0:T(8,128)(2,1)} %constant.31.clone.refs_9_.refs_11_) | copy-start | bytes 3145732
  58.2 6.8 %copy-start.4 = (bf16[512,1024]{1,0:T(8,128)(2,1)S(1)}, bf16[512,1024]{1,0:T(8,128)(2,1)}, u32[]{:S(2)}) copy-start(bf16[512,1024]{1,0:T(8,128)(2,1)} %constant.32.clone.refs_10_.refs_12_) | copy-start | bytes 3145732
  58.2 6.8 %collective-permute-start.14 = (f32[4,3,32,128]{3,2,1,0:T(8,128)S(1)}, f32[4,3,32,128]{3,2,1,0:T(8,128)S(1)}, u32[]{:S(2)}, u32[]{:S(2)}) collective-permute-start(f32[4,3,32,128]{3,2,1,0:T(8,128)S(1)} %pad_maximum_fusion.1), channel_id=1, source_target_pairs={{0,4},{1,5},{2,6},{3,7},{4,0},{5,1},{6,2},{7,3},{8,12},{9,13},{10,... | collective-permute-start | bytes 589832 | tf_op jit(solution)/shard_map/ppermute | solution.py:164
  70.7 12.4 %collective-permute-start.17 = (f32[4,3,32,128]{3,2,1,0:T(8,128)S(1)}, f32[4,3,32,128]{3,2,1,0:T(8,128)S(1)}, u32[]{:S(2)}, u32[]{:S(2)}) collective-permute-start(f32[4,3,32,128]{3,2,1,0:T(8,128)S(1)} %get-tuple-element.95), channel_id=1, source_target_pairs={{0,4},{1,5},{2,6},{3,7},{4,0},{5,1},{6,2},{7,3},{8,12},{9,13},{10,... | collective-permute-start | bytes 589832 | tf_op jit(solution)/shard_map/ppermute | solution.py:164
  72.7 13.4 %collective-permute-start.18 = (f32[4,3,32,128]{3,2,1,0:T(8,128)S(1)}, f32[4,3,32,128]{3,2,1,0:T(8,128)S(1)}, u32[]{:S(2)}, u32[]{:S(2)}) collective-permute-start(f32[4,3,32,128]{3,2,1,0:T(8,128)S(1)} %get-tuple-element.96), channel_id=1, source_target_pairs={{0,8},{1,9},{2,10},{3,11},{4,12},{5,13},{6,14},{7,15},{8,0},{9,1},... | collective-permute-start | bytes 589832 | tf_op jit(solution)/shard_map/ppermute | solution.py:164
  73.0 17.9 %collective-permute-start.19 = (f32[4,3,32,128]{3,2,1,0:T(8,128)S(1)}, f32[4,3,32,128]{3,2,1,0:T(8,128)S(1)}, u32[]{:S(2)}, u32[]{:S(2)}) collective-permute-start(f32[4,3,32,128]{3,2,1,0:T(8,128)S(1)} %get-tuple-element.97), channel_id=1, source_target_pairs={{0,12},{1,13},{2,14},{3,15},{4,8},{5,9},{6,10},{7,11},{8,4},{9,5},... | collective-permute-start | bytes 589832 | tf_op jit(solution)/shard_map/ppermute | solution.py:164
  90.9 40.6 %all-to-all-start = ((f32[16,6,32,128]{3,2,1,0:T(8,128)}), f32[16,6,32,128]{3,2,1,0:T(8,128)}, u32[]{:S(2)}, u32[]{:S(2)}) async-start(f32[16,6,32,128]{3,2,1,0:T(8,128)} %elastic.1), calls=%async_computation | async-start | bytes 3145728 | tf_op jit(solution)/shard_map/all_to_all | solution.py:259
  96.6 2.9 %collective-permute-start.20 = (f32[4,3,32,128]{3,2,1,0:T(8,128)S(1)}, f32[4,3,32,128]{3,2,1,0:T(8,128)S(1)}, u32[]{:S(2)}, u32[]{:S(2)}) collective-permute-start(f32[4,3,32,128]{3,2,1,0:T(8,128)S(1)} %get-tuple-element.109), channel_id=1, source_target_pairs={{0,1},{1,0},{2,3},{3,2},{4,5},{5,4},{6,7},{7,6},{8,9},{9,8},{10,11... | collective-permute-start | bytes 589832 | tf_op jit(solution)/shard_map/ppermute | solution.py:164
  96.8 12.1 %collective-permute-start.21 = (f32[4,3,32,128]{3,2,1,0:T(8,128)S(1)}, f32[4,3,32,128]{3,2,1,0:T(8,128)S(1)}, u32[]{:S(2)}, u32[]{:S(2)}) collective-permute-start(f32[4,3,32,128]{3,2,1,0:T(8,128)S(1)} %get-tuple-element.110), channel_id=1, source_target_pairs={{0,2},{1,3},{2,0},{3,1},{4,6},{5,7},{6,4},{7,5},{8,10},{9,11},{10,... | collective-permute-start | bytes 589832 | tf_op jit(solution)/shard_map/ppermute | solution.py:164
  97.3 18.6 %collective-permute-start.22 = (f32[4,3,32,128]{3,2,1,0:T(8,128)S(1)}, f32[4,3,32,128]{3,2,1,0:T(8,128)S(1)}, u32[]{:S(2)}, u32[]{:S(2)}) collective-permute-start(f32[4,3,32,128]{3,2,1,0:T(8,128)S(1)} %get-tuple-element.111), channel_id=1, source_target_pairs={{0,3},{1,2},{2,1},{3,0},{4,7},{5,6},{6,5},{7,4},{8,11},{9,10},{10,... | collective-permute-start | bytes 589832 | tf_op jit(solution)/shard_map/ppermute | solution.py:164
  108.9 0.7 copy-start.9
  116.0 0.7 copy-start.11
  116.6 1.1 copy-start.5
  117.8 0.9 copy-start.10
  118.7 0.9 copy-start.12
  119.6 11.9 %copy-start.2 = (f32[6,32,2048]{2,1,0:T(8,128)S(1)}, f32[6,32,2048]{2,1,0:T(8,128)}, u32[]{:S(2)}) copy-start(f32[6,32,2048]{2,1,0:T(8,128)} %refs_5_.1) | copy-start | bytes 4718596

commit v6 on v5

--- a/solution.py
+++ b/solution.py
@@ -181,30 +181,6 @@
     return [jnp.stack([group[at] for group in groups]) for at in range(NEAR)]
 
 
-def turn(groups):
-    every = [(s, t) for s in range(NEAR) for t in range(NEAR)]
-
-    def body(*refs):
-        in_refs, out_refs, sems = refs[:NEAR], refs[NEAR : 2 * NEAR], refs[-1]
-        copies = []
-        for number, (s, t) in enumerate(every):
-            copy = pltpu.make_async_copy(in_refs[t].at[s], out_refs[s].at[t], sems.at[number])
-            copy.start()
-            copies.append(copy)
-        for copy in copies:
-            copy.wait()
-
-    return pl.pallas_call(
-        body,
-        in_specs=[pl.BlockSpec(memory_space=pl.ANY)] * NEAR,
-        out_specs=[pl.BlockSpec(memory_space=pl.ANY)] * NEAR,
-        out_shape=[jax.ShapeDtypeStruct(group.shape, F32) for group in groups],
-        scratch_shapes=[pltpu.SemaphoreType.DMA((len(every),))],
-        compiler_params=pltpu.CompilerParams(vmem_limit_bytes=4 * MIB),
-        name="turn",
-    )(*groups)
-
-
 class Route:
     def __init__(self, devices, local_modes, far_first, staged=True):
         self.staged = staged and devices == NEAR * NEAR and local_modes % 16 == 0
@@ -421,7 +397,7 @@
     table = (high_ref[...], low_ref[...])
     values[:, 0:256] = dot3(table, (vel_h[:, 0:256], vel_l[:, 0:256]))
     values[:, 256:384] = dot3(table, (vel_h[:, 256:384], vel_l[:, 256:384]))
-    rows_step = 128
+    rows_step = 256
 
     def chunk(start):
         rows = pl.ds(start, rows_step)
@@ -877,7 +853,7 @@
     psi_rates = whole.packed(psi_rates)
     if staged:
         vel_rates, psi_rates = barrier((far_swaps(vel_rates), psi_rates))
-        vel_rates = near_swaps(turn(vel_rates))
+        vel_rates = near_swaps(regroup(vel_rates))
     else:
         vel_rates = in_one(vel_rates)
     psi_rates = in_one(psi_rates)

time: 136 us -> 136 us (level)
  local copies, waits for them, and re-layouts: 5.5 us -> 2.35 us
  waiting for transfers between devices: 57.8 us -> 60 us
  other arithmetic: 0.19 us -> 2.28 us
    unnamed x38 -> x30, local copies, waits for them, and re-layouts: 5.31 us -> 2.1 us
    all_to_all x1, waiting for transfers between devices: 9.62 us -> 12 us  [in_one(): lax.all_to_all(arrays[0], 'mode', split_axis=0, concat_axis=0, tiled=True)]
    another operation x12 -> x16, other arithmetic: 0.19 us -> 2.28 us  [regroup(): return [jnp.stack([group[at] for group in groups]) for at in range(NEAR)]]
  transfers between devices with their start and end apart: 24 -> 24, of which waited for: 13 -> 13; matrix products, arithmetic and copies ran while one was open for 0% -> 2% of each run, Pallas kernels for 21% -> 20%
where the time goes in v6:
time: 136 us
  waiting for transfers between devices  60 us (44%)
  Pallas kernels  40.5 us (30%)
  starting transfers between devices  28.7 us (21%)
  local copies, waits for them, and re-layouts  2.35 us (2%)
  other arithmetic  2.28 us (2%)
  between operations  1.69 us (1%)
    ppermute x21, waiting for transfers between devices, swap(): return lax.ppermute(block, 'mode', [(i, i ^ bits) for i in range(devices)])  43.2 us
    ppermute x21, starting transfers between devices, swap(): return lax.ppermute(block, 'mode', [(i, i ^ bits) for i in range(devices)])  21.5 us
    all_to_all x1, waiting for transfers between devices, in_one(): lax.all_to_all(arrays[0], 'mode', split_axis=0, concat_axis=0, tiled=True)  12 us
    pallas_call x1, Pallas kernels, body(): kernel_call(functools.partial(elastic_body, whole), (*psi_outs,), 14, scr...  9.12 us
    pallas_call x2, Pallas kernels, advance(): pl.pallas_call(functools.partial(advance_body, layers, step, route, len(r...  6.63 us
    pallas_call x1, Pallas kernels, body(): kernel_call(functools.partial(weights_body, layers), jax.ShapeDtypeStruct...  5.79 us
    pallas_call x1, Pallas kernels, body(): kernel_call(functools.partial(momentum_body, near_first, len(second_nodes...  5.72 us
    ppermute x1, waiting for transfers between devices, body(): above = lax.ppermute(to_down, 'mode', [(j, i) for i, j in up])  4.78 us
  transfers between devices with their start and end apart: 24, of which 13 were waited for; matrix products, arithmetic and copies ran while one was open for 2% of the time, Pallas kernels for 20%

profile of v6, /device:TPU:13, one launch (start us, length us, event | category | flops | bytes accessed | tf_op | source)
XLA Modules:
  0.0 135.5 jit_solution(11383180153770052437)
XLA Ops:
  0.7 3.5 %pack.1 = (f32[4,3,32,128]{3,2,1,0:T(8,128)}, f32[4,3,32,128]{3,2,1,0:T(8,128)}, f32[4,3,32,128]{3,2,1,0:T(8,128)}, f32[4,3,32,128]{3,2,1,0:T(8,128)}, f32[4,6,3...) custom-call(s32[1]{0:T(128)} %bitcast.me_ref.refs_0_, ...), custom_call_target="tpu_custom_call" | custom-call | tf_op jit(solution)/shard_map/pack/pallas_call | solution.py:260
  4.2 0.7 collective-permute-start
  5.0 0.2 collective-permute-start.4
  5.2 1.5 %collective-permute-start.5 = (f32[4,6,32,128]{3,2,1,0:T(8,128)}, f32[4,6,32,128]{3,2,1,0:T(8,128)S(1)}, u32[]{:S(2)}, u32[]{:S(2)}) collective-permute-start(f32[4,6,32,128]{3,2,1,0:T(8,128)} %get-tuple-element.62), channel_id=1, source_target_pairs={{0,3},{1,2},{2,1},{3,0},{4,7},{5,6},{6,5},{7,4},{8,11},{9,10},{10,... | collective-permute-start | bytes 1179656 | tf_op jit(solution)/shard_map/ppermute | solution.py:164
  6.7 2.3 %collective-permute-start.2 = (f32[4,3,32,128]{3,2,1,0:T(8,128)}, f32[4,3,32,128]{3,2,1,0:T(8,128)S(1)}, u32[]{:S(2)}, u32[]{:S(2)}) collective-permute-start(f32[4,3,32,128]{3,2,1,0:T(8,128)} %get-tuple-element.58), channel_id=1, source_target_pairs={{0,8},{1,9},{2,10},{3,11},{4,12},{5,13},{6,14},{7,15},{8,0},{9,1},... | collective-permute-start | bytes 589832 | tf_op jit(solution)/shard_map/ppermute | solution.py:164
  9.0 1.2 collective-permute-start.1
  10.2 0.9 copy-done.10
  11.1 5.8 %weights.1.refs_7_.refs_4_ = bf16[16,384,128]{2,1,0:T(8,128)(2,1)S(1)} custom-call(s32[32]{0:T(128)S(1)} %copy-done.12, bf16[3,128,128]{2,1,0:T(8,128)(2,1)S(1)} %copy-done.10), custom_call_target="tpu_custom_call" | custom-call | tf_op jit(solution)/shard_map/weights/pallas_call | solution.py:744
  17.0 1.7 %order.1 = (bf16[10,128,128]{2,1,0:T(8,128)(2,1)S(1)}, bf16[24,128,256]{2,1,0:T(8,128)(2,1)S(1)}, bf16[10,256,256]{2,1,0:T(8,128)(2,1)S(1)}, f32[8,128]{1,0:T(8,128)S(1)}) custom-call(s32[1]{0:T(128)} %bitcast.me_ref.refs_0_, s32[32]{0:T(128)S(1)} %copy-done.12, bf16[10,128,128]{2,1,0:T(8,128)(2,1)S(1)} %copy-done.8, bf16[24,128,256]{2,1,0:T(8,128)(2,1)S(1)} %copy-done.6, ...), custom_call_target="tpu_custom_call" | custom-call | tf_op jit(solution)/shard_map/order/pallas_call | solution.py:731
  18.7 3.6 %collective-permute-done.2 = f32[4,3,32,128]{3,2,1,0:T(8,128)S(1)} collective-permute-done((f32[4,3,32,128]{3,2,1,0:T(8,128)}, f32[4,3,32,128]{3,2,1,0:T(8,128)S(1)}, u32[]{:S(2)}, u32[]{:S(2)}) %collective-permute-start.2) | collective-permute-done | bytes 196640 | tf_op jit(solution)/shard_map/ppermute | solution.py:164
  22.3 4.2 %collective-permute-done.3 = f32[4,3,32,128]{3,2,1,0:T(8,128)S(1)} collective-permute-done((f32[4,3,32,128]{3,2,1,0:T(8,128)}, f32[4,3,32,128]{3,2,1,0:T(8,128)S(1)}, u32[]{:S(2)}, u32[]{:S(2)}) %collective-permute-start.3) | collective-permute-done | bytes 196640 | tf_op jit(solution)/shard_map/ppermute | solution.py:164
  26.7 2.2 %collective-permute-start.13 = (f32[4,3,32,128]{3,2,1,0:T(8,128)S(1)}, f32[4,3,32,128]{3,2,1,0:T(8,128)S(1)}, u32[]{:S(2)}, u32[]{:S(2)}) collective-permute-start(f32[4,3,32,128]{3,2,1,0:T(8,128)S(1)} %pad_maximum_fusion.11), channel_id=1, source_target_pairs={{0,12},{1,13},{2,14},{3,15},{4,8},{5,9},{6,10},{7,11},{8,4},{9,5},... | collective-permute-start | bytes 589832 | tf_op jit(solution)/shard_map/ppermute | solution.py:164
  29.1 0.9 collective-permute-start.8
  30.0 1.3 collective-permute-start.7
  31.6 5.0 %collective-permute-done.8.refs_3_ = f32[4,3,32,128]{3,2,1,0:T(8,128)S(1)} collective-permute-done((f32[4,3,32,128]{3,2,1,0:T(8,128)S(1)}, f32[4,3,32,128]{3,2,1,0:T(8,128)S(1)}, u32[]{:S(2)}, u32[]{:S(2)}) %collective-permute-start.8) | collective-permute-done | bytes 196640 | tf_op jit(solution)/shard_map/ppermute | solution.py:164
  36.6 1.2 collective-permute-start.11
  37.8 3.1 %collective-permute-done.7.refs_2_ = f32[4,3,32,128]{3,2,1,0:T(8,128)S(1)} collective-permute-done((f32[4,3,32,128]{3,2,1,0:T(8,128)S(1)}, f32[4,3,32,128]{3,2,1,0:T(8,128)S(1)}, u32[]{:S(2)}, u32[]{:S(2)}) %collective-permute-start.7) | collective-permute-done | bytes 196640 | tf_op jit(solution)/shard_map/ppermute | solution.py:164
  40.9 1.2 faces.1
  42.1 0.4 collective-permute-start.10
  42.5 2.3 %collective-permute-start.9 = (f32[384,128]{1,0:T(8,128)S(1)}, f32[384,128]{1,0:T(8,128)S(1)}, u32[]{:S(2)}, u32[]{:S(2)}) collective-permute-start(f32[384,128]{1,0:T(8,128)S(1)} %get-tuple-element.76), channel_id=1, source_target_pairs={{0,1},{1,2},{2,3},{3,4},{4,5},{5,6},{6,7},{7,8},{8,9},{9,10},{10,1... | collective-permute-start | bytes 589832 | tf_op jit(solution)/shard_map/ppermute | solution.py:778
  44.8 0.8 collective-permute-start.16
  45.7 3.5 %collective-permute-start.15 = (f32[4,3,32,128]{3,2,1,0:T(8,128)S(1)}, f32[4,3,32,128]{3,2,1,0:T(8,128)S(1)}, u32[]{:S(2)}, u32[]{:S(2)}) collective-permute-start(f32[4,3,32,128]{3,2,1,0:T(8,128)S(1)} %pad_maximum_fusion.2), channel_id=1, source_target_pairs={{0,8},{1,9},{2,10},{3,11},{4,12},{5,13},{6,14},{7,15},{8,0},{9,1},... | collective-permute-start | bytes 589832 | tf_op jit(solution)/shard_map/ppermute | solution.py:164
  49.2 3.9 %velocity.1 = (f32[3,512,128]{2,1,0:T(8,128)S(1)}, f32[15,512,128]{2,1,0:T(8,128)S(1)}, bf16[512,384]{1,0:T(8,128)(2,1)S(1)}, bf16[512,384]{1,0:T(8,128)(2,1)S(1)}, f32[3,512,128]{2,1,0:T(8,128)S(1)}) custom-call(s32[1]{0:T(128)} %bitcast.me_ref.refs_0_, f32[4,3,32,128]{3,2,1,0:T(8,128)S(1)} %pad_maximum_fusion.8.refs_0_, ...), custom_call_target="tpu_custom_call" | custom-call | tf_op jit(solution)/shard_map/velocity/pallas_call | solution.py:788
  53.1 4.8 %collective-permute-done.10.above_ref = f32[384,128]{1,0:T(8,128)S(1)} collective-permute-done((f32[384,128]{1,0:T(8,128)S(1)}, f32[384,128]{1,0:T(8,128)S(1)}, u32[]{:S(2)}, u32[]{:S(2)}) %collective-permute-start.10) | collective-permute-done | bytes 196640 | tf_op jit(solution)/shard_map/ppermute | solution.py:779
  58.0 2.9 %halo.1.refs_6_.refs_8_ = f32[12,512,128]{2,1,0:T(8,128)S(1)} custom-call(f32[384,128]{1,0:T(8,128)S(1)} %collective-permute-done.9.below_ref, f32[384,128]{1,0:T(8,128)S(1)} %collective-permute-done.10.above_ref, f32[3,512,128]{2,1,0:T(8,128)S(1)} %get-tuple-element.88.vel_ref, bf16[1024,512]{1,0:T(8,128)(2,1)S(1)} %copy-done, ...), custom_call_target="tpu_custom_call" | custom-call | tf_op jit(solution)/shard_map/halo/pallas_call | solution.py:804
  60.9 1.4 %collective-permute-done.16.refs_3_ = f32[4,3,32,128]{3,2,1,0:T(8,128)S(1)} collective-permute-done((f32[4,3,32,128]{3,2,1,0:T(8,128)S(1)}, f32[4,3,32,128]{3,2,1,0:T(8,128)S(1)}, u32[]{:S(2)}, u32[]{:S(2)}) %collective-permute-start.16) | collective-permute-done | bytes 196640 | tf_op jit(solution)/shard_map/ppermute | solution.py:164
  62.2 2.1 %collective-permute-done.15.refs_2_ = f32[4,3,32,128]{3,2,1,0:T(8,128)S(1)} collective-permute-done((f32[4,3,32,128]{3,2,1,0:T(8,128)S(1)}, f32[4,3,32,128]{3,2,1,0:T(8,128)S(1)}, u32[]{:S(2)}, u32[]{:S(2)}) %collective-permute-start.15) | collective-permute-done | bytes 196640 | tf_op jit(solution)/shard_map/ppermute | solution.py:164
  64.3 0.5 collective-permute-done.14.refs_1_
  64.8 5.7 %momentum.1 = (f32[4,3,32,128]{3,2,1,0:T(8,128)S(1)}, f32[4,3,32,128]{3,2,1,0:T(8,128)S(1)}, f32[4,3,32,128]{3,2,1,0:T(8,128)S(1)}, f32[4,3,32,128]{3,2,1,0:T(8,...) custom-call(s32[1]{0:T(128)} %bitcast.me_ref.refs_0_, ...), custom_call_target="tpu_custom_call" | custom-call | tf_op jit(solution)/shard_map/momentum/pallas_call | solution.py:817
  70.5 2.0 %collective-permute-start.17 = (f32[4,3,32,128]{3,2,1,0:T(8,128)S(1)}, f32[4,3,32,128]{3,2,1,0:T(8,128)S(1)}, u32[]{:S(2)}, u32[]{:S(2)}) collective-permute-start(f32[4,3,32,128]{3,2,1,0:T(8,128)S(1)} %get-tuple-element.91), channel_id=1, source_target_pairs={{0,4},{1,5},{2,6},{3,7},{4,0},{5,1},{6,2},{7,3},{8,12},{9,13},{10,... | collective-permute-start | bytes 589832 | tf_op jit(solution)/shard_map/ppermute | solution.py:164
  72.5 0.5 collective-permute-start.18
  73.0 0.7 collective-permute-start.19
  73.8 9.1 %elastic.1 = f32[16,6,32,128]{3,2,1,0:T(8,128)} custom-call(s32[1]{0:T(128)} %bitcast.me_ref.refs_0_, bf16[512,384]{1,0:T(8,128)(2,1)S(1)} %get-tuple-element.94.refs_0_, bf16[512,384]{1,0:T(8,128)(2,1)S(1)} %get-tuple-element.95.refs_1_, bf16[512,384]{1,0:T(8,128)(2,1)S(1)} %get-tuple-element.96.refs_2_, bf16[512,384]{1,0:T(8,128)(2,1)S(1)} %get-tuple-element.97.refs_3_, ...), custom_call_target="tpu_custom_call" | custom-call | tf_op jit(solution)/shard_map/elastic/pallas_call | solution.py:835
  82.9 3.3 %collective-permute-done.18 = f32[4,3,32,128]{3,2,1,0:T(8,128)S(1)} collective-permute-done((f32[4,3,32,128]{3,2,1,0:T(8,128)S(1)}, f32[4,3,32,128]{3,2,1,0:T(8,128)S(1)}, u32[]{:S(2)}, u32[]{:S(2)}) %collective-permute-start.18) | collective-permute-done | bytes 196640 | tf_op jit(solution)/shard_map/ppermute | solution.py:164
  86.2 4.8 %collective-permute-done.19 = f32[4,3,32,128]{3,2,1,0:T(8,128)S(1)} collective-permute-done((f32[4,3,32,128]{3,2,1,0:T(8,128)S(1)}, f32[4,3,32,128]{3,2,1,0:T(8,128)S(1)}, u32[]{:S(2)}, u32[]{:S(2)}) %collective-permute-start.19) | collective-permute-done | bytes 196640 | tf_op jit(solution)/shard_map/ppermute | solution.py:164
  90.9 4.5 %all-to-all-start = ((f32[16,6,32,128]{3,2,1,0:T(8,128)}), f32[16,6,32,128]{3,2,1,0:T(8,128)}, u32[]{:S(2)}, u32[]{:S(2)}) async-start(f32[16,6,32,128]{3,2,1,0:T(8,128)} %elastic.1), calls=%async_computation | async-start | bytes 3145728 | tf_op jit(solution)/shard_map/all_to_all | solution.py:235
  95.6 0.7 pad_maximum_fusion.15
  96.3 0.5 collective-permute-start.22
  96.7 0.7 pad_maximum_fusion.14
  97.4 1.0 collective-permute-start.21
  98.4 0.7 pad_maximum_fusion.13
  99.1 0.7 collective-permute-start.20
  100.5 9.8 %collective-permute-done.22.refs_6_ = f32[4,3,32,128]{3,2,1,0:T(8,128)S(1)} collective-permute-done((f32[4,3,32,128]{3,2,1,0:T(8,128)}, f32[4,3,32,128]{3,2,1,0:T(8,128)S(1)}, u32[]{:S(2)}, u32[]{:S(2)}) %collective-permute-start.22) | collective-permute-done | bytes 196640 | tf_op jit(solution)/shard_map/ppermute | solution.py:164
  110.3 5.5 %collective-permute-done.21.refs_5_ = f32[4,3,32,128]{3,2,1,0:T(8,128)S(1)} collective-permute-done((f32[4,3,32,128]{3,2,1,0:T(8,128)}, f32[4,3,32,128]{3,2,1,0:T(8,128)S(1)}, u32[]{:S(2)}, u32[]{:S(2)}) %collective-permute-start.21) | collective-permute-done | bytes 196640 | tf_op jit(solution)/shard_map/ppermute | solution.py:164
  115.8 1.1 copy-done.5
  116.9 2.7 %advance.2 = f32[3,32,2048]{2,1,0:T(8,128)} custom-call(s32[1]{0:T(128)} %bitcast.me_ref.refs_0_, s32[32]{0:T(128)S(1)} %copy-done.12, f32[1]{0:T(128)S(6)} %select_n.9.refs_2_, f32[4,3,32,128]{3,2,1,0:T(8,128)S(1)} %pad_maximum_fusion.12.refs_3_, f32[4,3,32,128]{3,2,1,0:T(8,128)} %collective-permute-done.20.refs_4_, ...), custom_call_target="tpu_custom_call" | custom-call | tf_op jit(solution)/shard_map/advance/pallas_call | solution.py:690
  119.6 12.0 %all-to-all-done.refs_3_ = f32[16,6,32,128]{3,2,1,0:T(8,128)} async-done(((f32[16,6,32,128]{3,2,1,0:T(8,128)}), f32[16,6,32,128]{3,2,1,0:T(8,128)}, u32[]{:S(2)}, u32[]{:S(2)}) %all-to-all-start) | async-done | bytes 1572896 | tf_op jit(solution)/shard_map/all_to_all | solution.py:235
  131.6 4.0 %advance.3 = f32[6,32,2048]{2,1,0:T(8,128)} custom-call(s32[1]{0:T(128)} %bitcast.me_ref.refs_0_, s32[32]{0:T(128)S(1)} %copy-done.12, f32[1]{0:T(128)S(6)} %select_n.9.refs_2_, f32[16,6,32,128]{3,2,1,0:T(8,128)} %all-to-all-done.refs_3_, bf16[16,384,128]{2,1,0:T(8,128)(2,1)S(1)} %weights.1.refs_7_.refs_4_, f32[6,32,2048]{2,1,0:T(8,128)S(1)} %copy-done.2), custom_call_target="tpu_custom_call" | custom-call | tf_op jit(solution)/shard_map/advance/pallas_call | solution.py:690
  (64 shorter events, 0.8 us)
Async XLA Ops:
  0.6 9.6 %copy-start.12 = (s32[32]{0:T(128)S(1)}, s32[32]{0:T(128)}, u32[]{:S(2)}) copy-start(s32[32]{0:T(128)} %refs_1_.5) | copy-start | bytes 388
  0.6 16.3 %copy-start.6 = (bf16[24,128,256]{2,1,0:T(8,128)(2,1)S(1)}, bf16[24,128,256]{2,1,0:T(8,128)(2,1)}, u32[]{:S(2)}) copy-start(bf16[24,128,256]{2,1,0:T(8,128)(2,1)} %constant.35.clone.faces_ref) | copy-start | bytes 4718596
  0.7 16.3 %copy-start.8 = (bf16[10,128,128]{2,1,0:T(8,128)(2,1)S(1)}, bf16[10,128,128]{2,1,0:T(8,128)(2,1)}, u32[]{:S(2)}) copy-start(bf16[10,128,128]{2,1,0:T(8,128)(2,1)} %constant.34.clone.both_ref) | copy-start | bytes 983044
  0.7 16.3 %copy-start.11 = (f32[128,128]{1,0:T(8,128)S(1)}, f32[128,128]{1,0:T(8,128)}, u32[]{:S(2)}) copy-start(f32[128,128]{1,0:T(8,128)} %constant.33.clone.inv_r_ref) | copy-start | bytes 196612
  4.2 12.7 %copy-start.7 = (bf16[18,256,128]{2,1,0:T(8,128)(2,1)S(1)}, bf16[18,256,128]{2,1,0:T(8,128)(2,1)}, u32[]{:S(2)}) copy-start(bf16[18,256,128]{2,1,0:T(8,128)(2,1)} %constant.36.clone.halos_ref) | copy-start | bytes 3538948
  4.2 4.8 %collective-permute-start = (f32[4,6,32,128]{3,2,1,0:T(8,128)}, f32[4,6,32,128]{3,2,1,0:T(8,128)S(1)}, u32[]{:S(2)}, u32[]{:S(2)}) collective-permute-start(f32[4,6,32,128]{3,2,1,0:T(8,128)} %get-tuple-element.56), channel_id=1, source_target_pairs={{0,1},{1,0},{2,3},{3,2},{4,5},{5,4},{6,7},{7,6},{8,9},{9,8},{10,11... | collective-permute-start | bytes 1179656 | tf_op jit(solution)/shard_map/ppermute | solution.py:164
  5.0 21.6 %collective-permute-start.4 = (f32[4,6,32,128]{3,2,1,0:T(8,128)}, f32[4,6,32,128]{3,2,1,0:T(8,128)S(1)}, u32[]{:S(2)}, u32[]{:S(2)}) collective-permute-start(f32[4,6,32,128]{3,2,1,0:T(8,128)} %get-tuple-element.61), channel_id=1, source_target_pairs={{0,2},{1,3},{2,0},{3,1},{4,6},{5,7},{6,4},{7,5},{8,10},{9,11},{10,... | collective-permute-start | bytes 1179656 | tf_op jit(solution)/shard_map/ppermute | solution.py:164
  5.2 21.3 %collective-permute-start.5 = (f32[4,6,32,128]{3,2,1,0:T(8,128)}, f32[4,6,32,128]{3,2,1,0:T(8,128)S(1)}, u32[]{:S(2)}, u32[]{:S(2)}) collective-permute-start(f32[4,6,32,128]{3,2,1,0:T(8,128)} %get-tuple-element.62), channel_id=1, source_target_pairs={{0,3},{1,2},{2,1},{3,0},{4,7},{5,6},{6,5},{7,4},{8,11},{9,10},{10,... | collective-permute-start | bytes 1179656 | tf_op jit(solution)/shard_map/ppermute | solution.py:164
  6.7 15.6 %collective-permute-start.2 = (f32[4,3,32,128]{3,2,1,0:T(8,128)}, f32[4,3,32,128]{3,2,1,0:T(8,128)S(1)}, u32[]{:S(2)}, u32[]{:S(2)}) collective-permute-start(f32[4,3,32,128]{3,2,1,0:T(8,128)} %get-tuple-element.58), channel_id=1, source_target_pairs={{0,8},{1,9},{2,10},{3,11},{4,12},{5,13},{6,14},{7,15},{8,0},{9,1},... | collective-permute-start | bytes 589832 | tf_op jit(solution)/shard_map/ppermute | solution.py:164
  9.0 17.5 %collective-permute-start.3 = (f32[4,3,32,128]{3,2,1,0:T(8,128)}, f32[4,3,32,128]{3,2,1,0:T(8,128)S(1)}, u32[]{:S(2)}, u32[]{:S(2)}) collective-permute-start(f32[4,3,32,128]{3,2,1,0:T(8,128)} %get-tuple-element.59), channel_id=1, source_target_pairs={{0,12},{1,13},{2,14},{3,15},{4,8},{5,9},{6,10},{7,11},{8,4},{9,5},... | collective-permute-start | bytes 589832 | tf_op jit(solution)/shard_map/ppermute | solution.py:164
  9.0 17.5 %collective-permute-start.1 = (f32[4,3,32,128]{3,2,1,0:T(8,128)}, f32[4,3,32,128]{3,2,1,0:T(8,128)S(1)}, u32[]{:S(2)}, u32[]{:S(2)}) collective-permute-start(f32[4,3,32,128]{3,2,1,0:T(8,128)} %get-tuple-element.57), channel_id=1, source_target_pairs={{0,4},{1,5},{2,6},{3,7},{4,0},{5,1},{6,2},{7,3},{8,12},{9,13},{10,... | collective-permute-start | bytes 589832 | tf_op jit(solution)/shard_map/ppermute | solution.py:164
  10.2 0.9 copy-start.10
  17.0 9.6 %copy-start.13 = (f32[4,6,32,128]{3,2,1,0:T(8,128)S(1)}, f32[4,6,32,128]{3,2,1,0:T(8,128)}, u32[]{:S(2)}) copy-start(f32[4,6,32,128]{3,2,1,0:T(8,128)} %get-tuple-element.67) | copy-start | bytes 1179652
  26.6 2.4 %copy-start.14 = (f32[4,3,32,128]{3,2,1,0:T(8,128)S(1)}, f32[4,3,32,128]{3,2,1,0:T(8,128)}, u32[]{:S(2)}) copy-start(f32[4,3,32,128]{3,2,1,0:T(8,128)} %get-tuple-element.71) | copy-start | bytes 589828
  26.7 18.1 %collective-permute-start.13 = (f32[4,3,32,128]{3,2,1,0:T(8,128)S(1)}, f32[4,3,32,128]{3,2,1,0:T(8,128)S(1)}, u32[]{:S(2)}, u32[]{:S(2)}) collective-permute-start(f32[4,3,32,128]{3,2,1,0:T(8,128)S(1)} %pad_maximum_fusion.11), channel_id=1, source_target_pairs={{0,12},{1,13},{2,14},{3,15},{4,8},{5,9},{6,10},{7,11},{8,4},{9,5},... | collective-permute-start | bytes 589832 | tf_op jit(solution)/shard_map/ppermute | solution.py:164
  28.9 16.8 %collective-permute-start.12 = (f32[4,3,32,128]{3,2,1,0:T(8,128)S(1)}, f32[4,3,32,128]{3,2,1,0:T(8,128)S(1)}, u32[]{:S(2)}, u32[]{:S(2)}) collective-permute-start(f32[4,3,32,128]{3,2,1,0:T(8,128)S(1)} %pad_maximum_fusion.10), channel_id=1, source_target_pairs={{0,8},{1,9},{2,10},{3,11},{4,12},{5,13},{6,14},{7,15},{8,0},{9,1},... | collective-permute-start | bytes 589832 | tf_op jit(solution)/shard_map/ppermute | solution.py:164
  29.1 7.5 %collective-permute-start.8 = (f32[4,3,32,128]{3,2,1,0:T(8,128)S(1)}, f32[4,3,32,128]{3,2,1,0:T(8,128)S(1)}, u32[]{:S(2)}, u32[]{:S(2)}) collective-permute-start(f32[4,3,32,128]{3,2,1,0:T(8,128)S(1)} %pad_maximum_fusion.7), channel_id=1, source_target_pairs={{0,3},{1,2},{2,1},{3,0},{4,7},{5,6},{6,5},{7,4},{8,11},{9,10},{10,... | collective-permute-start | bytes 589832 | tf_op jit(solution)/shard_map/ppermute | solution.py:164
  30.0 10.8 %collective-permute-start.7 = (f32[4,3,32,128]{3,2,1,0:T(8,128)S(1)}, f32[4,3,32,128]{3,2,1,0:T(8,128)S(1)}, u32[]{:S(2)}, u32[]{:S(2)}) collective-permute-start(f32[4,3,32,128]{3,2,1,0:T(8,128)S(1)} %pad_maximum_fusion.6), channel_id=1, source_target_pairs={{0,2},{1,3},{2,0},{3,1},{4,6},{5,7},{6,4},{7,5},{8,10},{9,11},{10,... | collective-permute-start | bytes 589832 | tf_op jit(solution)/shard_map/ppermute | solution.py:164
  31.4 9.5 %collective-permute-start.6 = (f32[4,3,32,128]{3,2,1,0:T(8,128)S(1)}, f32[4,3,32,128]{3,2,1,0:T(8,128)S(1)}, u32[]{:S(2)}, u32[]{:S(2)}) collective-permute-start(f32[4,3,32,128]{3,2,1,0:T(8,128)S(1)} %pad_maximum_fusion.5), channel_id=1, source_target_pairs={{0,1},{1,0},{2,3},{3,2},{4,5},{5,4},{6,7},{7,6},{8,9},{9,8},{10,11... | collective-permute-start | bytes 589832 | tf_op jit(solution)/shard_map/ppermute | solution.py:164
  31.6 17.5 %copy-start = (bf16[1024,512]{1,0:T(8,128)(2,1)S(1)}, bf16[1024,512]{1,0:T(8,128)(2,1)}, u32[]{:S(2)}) copy-start(bf16[1024,512]{1,0:T(8,128)(2,1)} %constant.29.clone.refs_6_.high_ref.refs_7_.refs_9_) | copy-start | bytes 3145732
  31.6 17.5 %copy-start.1 = (bf16[1024,512]{1,0:T(8,128)(2,1)S(1)}, bf16[1024,512]{1,0:T(8,128)(2,1)}, u32[]{:S(2)}) copy-start(bf16[1024,512]{1,0:T(8,128)(2,1)} %constant.30.clone.refs_7_.low_ref.refs_8_.refs_10_) | copy-start | bytes 3145732
  36.6 12.5 %collective-permute-start.11 = (f32[4,3,32,128]{3,2,1,0:T(8,128)S(1)}, f32[4,3,32,128]{3,2,1,0:T(8,128)S(1)}, u32[]{:S(2)}, u32[]{:S(2)}) collective-permute-start(f32[4,3,32,128]{3,2,1,0:T(8,128)S(1)} %pad_maximum_fusion.9), channel_id=1, source_target_pairs={{0,4},{1,5},{2,6},{3,7},{4,0},{5,1},{6,2},{7,3},{8,12},{9,13},{10,... | collective-permute-start | bytes 589832 | tf_op jit(solution)/shard_map/ppermute | solution.py:164
  42.1 15.8 %collective-permute-start.10 = (f32[384,128]{1,0:T(8,128)S(1)}, f32[384,128]{1,0:T(8,128)S(1)}, u32[]{:S(2)}, u32[]{:S(2)}) collective-permute-start(f32[384,128]{1,0:T(8,128)S(1)} %get-tuple-element.77), channel_id=1, source_target_pairs={{1,0},{2,1},{3,2},{4,3},{5,4},{6,5},{7,6},{8,7},{9,8},{10,9},{11,1... | collective-permute-start | bytes 589832 | tf_op jit(solution)/shard_map/ppermute | solution.py:779
  42.5 15.4 %collective-permute-start.9 = (f32[384,128]{1,0:T(8,128)S(1)}, f32[384,128]{1,0:T(8,128)S(1)}, u32[]{:S(2)}, u32[]{:S(2)}) collective-permute-start(f32[384,128]{1,0:T(8,128)S(1)} %get-tuple-element.76), channel_id=1, source_target_pairs={{0,1},{1,2},{2,3},{3,4},{4,5},{5,6},{6,7},{7,8},{8,9},{9,10},{10,1... | collective-permute-start | bytes 589832 | tf_op jit(solution)/shard_map/ppermute | solution.py:778
  44.8 17.4 %collective-permute-start.16 = (f32[4,3,32,128]{3,2,1,0:T(8,128)S(1)}, f32[4,3,32,128]{3,2,1,0:T(8,128)S(1)}, u32[]{:S(2)}, u32[]{:S(2)}) collective-permute-start(f32[4,3,32,128]{3,2,1,0:T(8,128)S(1)} %pad_maximum_fusion.3), channel_id=1, source_target_pairs={{0,12},{1,13},{2,14},{3,15},{4,8},{5,9},{6,10},{7,11},{8,4},{9,5},... | collective-permute-start | bytes 589832 | tf_op jit(solution)/shard_map/ppermute | solution.py:164
  45.7 18.6 %collective-permute-start.15 = (f32[4,3,32,128]{3,2,1,0:T(8,128)S(1)}, f32[4,3,32,128]{3,2,1,0:T(8,128)S(1)}, u32[]{:S(2)}, u32[]{:S(2)}) collective-permute-start(f32[4,3,32,128]{3,2,1,0:T(8,128)S(1)} %pad_maximum_fusion.2), channel_id=1, source_target_pairs={{0,8},{1,9},{2,10},{3,11},{4,12},{5,13},{6,14},{7,15},{8,0},{9,1},... | collective-permute-start | bytes 589832 | tf_op jit(solution)/shard_map/ppermute | solution.py:164
  49.1 8.8 %copy-start.9 = (bf16[3,128,128]{2,1,0:T(8,128)(2,1)S(1)}, bf16[3,128,128]{2,1,0:T(8,128)(2,1)}, u32[]{:S(2)}) copy-start(bf16[3,128,128]{2,1,0:T(8,128)(2,1)} %constant.38.clone.places_ref) | copy-start | bytes 294916
  57.9 6.9 %copy-start.3 = (bf16[512,1024]{1,0:T(8,128)(2,1)S(1)}, bf16[512,1024]{1,0:T(8,128)(2,1)}, u32[]{:S(2)}) copy-start(bf16[512,1024]{1,0:T(8,128)(2,1)} %constant.31.clone.refs_9_.refs_11_) | copy-start | bytes 3145732
  57.9 6.9 %copy-start.4 = (bf16[512,1024]{1,0:T(8,128)(2,1)S(1)}, bf16[512,1024]{1,0:T(8,128)(2,1)}, u32[]{:S(2)}) copy-start(bf16[512,1024]{1,0:T(8,128)(2,1)} %constant.32.clone.refs_10_.refs_12_) | copy-start | bytes 3145732
  57.9 6.9 %collective-permute-start.14 = (f32[4,3,32,128]{3,2,1,0:T(8,128)S(1)}, f32[4,3,32,128]{3,2,1,0:T(8,128)S(1)}, u32[]{:S(2)}, u32[]{:S(2)}) collective-permute-start(f32[4,3,32,128]{3,2,1,0:T(8,128)S(1)} %pad_maximum_fusion.1), channel_id=1, source_target_pairs={{0,4},{1,5},{2,6},{3,7},{4,0},{5,1},{6,2},{7,3},{8,12},{9,13},{10,... | collective-permute-start | bytes 589832 | tf_op jit(solution)/shard_map/ppermute | solution.py:164
  70.5 12.4 %collective-permute-start.17 = (f32[4,3,32,128]{3,2,1,0:T(8,128)S(1)}, f32[4,3,32,128]{3,2,1,0:T(8,128)S(1)}, u32[]{:S(2)}, u32[]{:S(2)}) collective-permute-start(f32[4,3,32,128]{3,2,1,0:T(8,128)S(1)} %get-tuple-element.91), channel_id=1, source_target_pairs={{0,4},{1,5},{2,6},{3,7},{4,0},{5,1},{6,2},{7,3},{8,12},{9,13},{10,... | collective-permute-start | bytes 589832 | tf_op jit(solution)/shard_map/ppermute | solution.py:164
  72.5 13.7 %collective-permute-start.18 = (f32[4,3,32,128]{3,2,1,0:T(8,128)S(1)}, f32[4,3,32,128]{3,2,1,0:T(8,128)S(1)}, u32[]{:S(2)}, u32[]{:S(2)}) collective-permute-start(f32[4,3,32,128]{3,2,1,0:T(8,128)S(1)} %get-tuple-element.92), channel_id=1, source_target_pairs={{0,8},{1,9},{2,10},{3,11},{4,12},{5,13},{6,14},{7,15},{8,0},{9,1},... | collective-permute-start | bytes 589832 | tf_op jit(solution)/shard_map/ppermute | solution.py:164
  73.0 17.9 %collective-permute-start.19 = (f32[4,3,32,128]{3,2,1,0:T(8,128)S(1)}, f32[4,3,32,128]{3,2,1,0:T(8,128)S(1)}, u32[]{:S(2)}, u32[]{:S(2)}) collective-permute-start(f32[4,3,32,128]{3,2,1,0:T(8,128)S(1)} %get-tuple-element.93), channel_id=1, source_target_pairs={{0,12},{1,13},{2,14},{3,15},{4,8},{5,9},{6,10},{7,11},{8,4},{9,5},... | collective-permute-start | bytes 589832 | tf_op jit(solution)/shard_map/ppermute | solution.py:164
  90.9 40.6 %all-to-all-start = ((f32[16,6,32,128]{3,2,1,0:T(8,128)}), f32[16,6,32,128]{3,2,1,0:T(8,128)}, u32[]{:S(2)}, u32[]{:S(2)}) async-start(f32[16,6,32,128]{3,2,1,0:T(8,128)} %elastic.1), calls=%async_computation | async-start | bytes 3145728 | tf_op jit(solution)/shard_map/all_to_all | solution.py:235
  96.3 14.0 %collective-permute-start.22 = (f32[4,3,32,128]{3,2,1,0:T(8,128)}, f32[4,3,32,128]{3,2,1,0:T(8,128)S(1)}, u32[]{:S(2)}, u32[]{:S(2)}) collective-permute-start(f32[4,3,32,128]{3,2,1,0:T(8,128)} %pad_maximum_fusion.15), channel_id=1, source_target_pairs={{0,3},{1,2},{2,1},{3,0},{4,7},{5,6},{6,5},{7,4},{8,11},{9,10},{10,... | collective-permute-start | bytes 589832 | tf_op jit(solution)/shard_map/ppermute | solution.py:164
  97.4 18.3 %collective-permute-start.21 = (f32[4,3,32,128]{3,2,1,0:T(8,128)}, f32[4,3,32,128]{3,2,1,0:T(8,128)S(1)}, u32[]{:S(2)}, u32[]{:S(2)}) collective-permute-start(f32[4,3,32,128]{3,2,1,0:T(8,128)} %pad_maximum_fusion.14), channel_id=1, source_target_pairs={{0,2},{1,3},{2,0},{3,1},{4,6},{5,7},{6,4},{7,5},{8,10},{9,11},{10,... | collective-permute-start | bytes 589832 | tf_op jit(solution)/shard_map/ppermute | solution.py:164
  99.1 16.7 %collective-permute-start.20 = (f32[4,3,32,128]{3,2,1,0:T(8,128)}, f32[4,3,32,128]{3,2,1,0:T(8,128)}, u32[]{:S(2)}, u32[]{:S(2)}) collective-permute-start(f32[4,3,32,128]{3,2,1,0:T(8,128)} %pad_maximum_fusion.13), channel_id=1, source_target_pairs={{0,1},{1,0},{2,3},{3,2},{4,5},{5,4},{6,7},{7,6},{8,9},{9,8},{10,11... | collective-permute-start | bytes 589832 | tf_op jit(solution)/shard_map/ppermute | solution.py:164
  100.5 31.1 %copy-start.2 = (f32[6,32,2048]{2,1,0:T(8,128)S(1)}, f32[6,32,2048]{2,1,0:T(8,128)}, u32[]{:S(2)}) copy-start(f32[6,32,2048]{2,1,0:T(8,128)} %refs_5_.1) | copy-start | bytes 4718596
  115.8 1.1 copy-start.5

commit v7 on v6

--- a/solution.py
+++ b/solution.py
@@ -529,7 +529,7 @@
     planes = high_ref.shape[1]
     route.load(me_ref, psi_refs, coef_h, coef_l)
     transform(high_ref, low_ref, slice(0, planes), coef_h, coef_l, psi_out)
-    rows_step = 16
+    rows_step = 32
 
     def chunk(start):
         rows = pl.ds(start, rows_step)
@@ -585,7 +585,7 @@
     for member in range(6):
         psi_ref = first_ref if member < FIRST else second_ref
         grad_s[member] = dot3(split(psi_ref[member % FIRST]), gradient)
-    rows_step = 16
+    rows_step = 32
     inv_relax = 1.0 / RELAX_TIME
 
     def chunk(start):

time: 136 us -> 136 us (level)
  no operation moved by 1% of the time
where the time goes in v7:
time: 136 us; the launch traced here: 135 us
  waiting for transfers between devices  59.9 us (44%)
  Pallas kernels  40.5 us (30%)
  starting transfers between devices  28.7 us (21%)
  local copies, waits for them, and re-layouts  2.35 us (2%)
  other arithmetic  2.28 us (2%)
  between operations  1.69 us (1%)
    ppermute x21, waiting for transfers between devices, swap(): return lax.ppermute(block, 'mode', [(i, i ^ bits) for i in range(devices)])  43.2 us
    ppermute x21, starting transfers between devices, swap(): return lax.ppermute(block, 'mode', [(i, i ^ bits) for i in range(devices)])  21.5 us
    all_to_all x1, waiting for transfers between devices, in_one(): lax.all_to_all(arrays[0], 'mode', split_axis=0, concat_axis=0, tiled=True)  12 us
    pallas_call x1, Pallas kernels, body(): kernel_call(functools.partial(elastic_body, whole), (*psi_outs,), 14, scr...  9.16 us
    pallas_call x2, Pallas kernels, advance(): pl.pallas_call(functools.partial(advance_body, layers, step, route, len(r...  6.63 us
    pallas_call x1, Pallas kernels, body(): kernel_call(functools.partial(weights_body, layers), jax.ShapeDtypeStruct...  5.79 us
    pallas_call x1, Pallas kernels, body(): kernel_call(functools.partial(momentum_body, near_first, len(second_nodes...  5.61 us
    ppermute x1, waiting for transfers between devices, body(): above = lax.ppermute(to_down, 'mode', [(j, i) for i, j in up])  4.78 us
  transfers between devices with their start and end apart: 24, of which 13 were waited for; matrix products, arithmetic and copies ran while one was open for 2% of the time, Pallas kernels for 20%

profile of v7, /device:TPU:13, one launch (start us, length us, event | category | flops | bytes accessed | tf_op | source)
XLA Modules:
  0.0 135.4 jit_solution(18054591303333268703)
XLA Ops:
  0.7 3.5 %pack.1 = (f32[4,3,32,128]{3,2,1,0:T(8,128)}, f32[4,3,32,128]{3,2,1,0:T(8,128)}, f32[4,3,32,128]{3,2,1,0:T(8,128)}, f32[4,3,32,128]{3,2,1,0:T(8,128)}, f32[4,6,3...) custom-call(s32[1]{0:T(128)} %bitcast.me_ref.refs_0_, ...), custom_call_target="tpu_custom_call" | custom-call | tf_op jit(solution)/shard_map/pack/pallas_call | solution.py:260
  4.2 0.7 collective-permute-start
  5.0 0.2 collective-permute-start.4
  5.2 1.5 %collective-permute-start.5 = (f32[4,6,32,128]{3,2,1,0:T(8,128)}, f32[4,6,32,128]{3,2,1,0:T(8,128)S(1)}, u32[]{:S(2)}, u32[]{:S(2)}) collective-permute-start(f32[4,6,32,128]{3,2,1,0:T(8,128)} %get-tuple-element.62), channel_id=1, source_target_pairs={{0,3},{1,2},{2,1},{3,0},{4,7},{5,6},{6,5},{7,4},{8,11},{9,10},{10,... | collective-permute-start | bytes 1179656 | tf_op jit(solution)/shard_map/ppermute | solution.py:164
  6.7 2.3 %collective-permute-start.2 = (f32[4,3,32,128]{3,2,1,0:T(8,128)}, f32[4,3,32,128]{3,2,1,0:T(8,128)S(1)}, u32[]{:S(2)}, u32[]{:S(2)}) collective-permute-start(f32[4,3,32,128]{3,2,1,0:T(8,128)} %get-tuple-element.58), channel_id=1, source_target_pairs={{0,8},{1,9},{2,10},{3,11},{4,12},{5,13},{6,14},{7,15},{8,0},{9,1},... | collective-permute-start | bytes 589832 | tf_op jit(solution)/shard_map/ppermute | solution.py:164
  9.0 1.2 collective-permute-start.1
  10.2 0.9 copy-done.10
  11.1 5.8 %weights.1.refs_7_.refs_4_ = bf16[16,384,128]{2,1,0:T(8,128)(2,1)S(1)} custom-call(s32[32]{0:T(128)S(1)} %copy-done.12, bf16[3,128,128]{2,1,0:T(8,128)(2,1)S(1)} %copy-done.10), custom_call_target="tpu_custom_call" | custom-call | tf_op jit(solution)/shard_map/weights/pallas_call | solution.py:744
  17.0 1.7 %order.1 = (bf16[10,128,128]{2,1,0:T(8,128)(2,1)S(1)}, bf16[24,128,256]{2,1,0:T(8,128)(2,1)S(1)}, bf16[10,256,256]{2,1,0:T(8,128)(2,1)S(1)}, f32[8,128]{1,0:T(8,128)S(1)}) custom-call(s32[1]{0:T(128)} %bitcast.me_ref.refs_0_, s32[32]{0:T(128)S(1)} %copy-done.12, bf16[10,128,128]{2,1,0:T(8,128)(2,1)S(1)} %copy-done.8, bf16[24,128,256]{2,1,0:T(8,128)(2,1)S(1)} %copy-done.6, ...), custom_call_target="tpu_custom_call" | custom-call | tf_op jit(solution)/shard_map/order/pallas_call | solution.py:731
  18.7 3.6 %collective-permute-done.2 = f32[4,3,32,128]{3,2,1,0:T(8,128)S(1)} collective-permute-done((f32[4,3,32,128]{3,2,1,0:T(8,128)}, f32[4,3,32,128]{3,2,1,0:T(8,128)S(1)}, u32[]{:S(2)}, u32[]{:S(2)}) %collective-permute-start.2) | collective-permute-done | bytes 196640 | tf_op jit(solution)/shard_map/ppermute | solution.py:164
  22.3 4.2 %collective-permute-done.3 = f32[4,3,32,128]{3,2,1,0:T(8,128)S(1)} collective-permute-done((f32[4,3,32,128]{3,2,1,0:T(8,128)}, f32[4,3,32,128]{3,2,1,0:T(8,128)S(1)}, u32[]{:S(2)}, u32[]{:S(2)}) %collective-permute-start.3) | collective-permute-done | bytes 196640 | tf_op jit(solution)/shard_map/ppermute | solution.py:164
  26.7 2.2 %collective-permute-start.13 = (f32[4,3,32,128]{3,2,1,0:T(8,128)S(1)}, f32[4,3,32,128]{3,2,1,0:T(8,128)S(1)}, u32[]{:S(2)}, u32[]{:S(2)}) collective-permute-start(f32[4,3,32,128]{3,2,1,0:T(8,128)S(1)} %pad_maximum_fusion.11), channel_id=1, source_target_pairs={{0,12},{1,13},{2,14},{3,15},{4,8},{5,9},{6,10},{7,11},{8,4},{9,5},... | collective-permute-start | bytes 589832 | tf_op jit(solution)/shard_map/ppermute | solution.py:164
  29.1 0.9 collective-permute-start.8
  30.0 1.3 collective-permute-start.7
  31.6 5.0 %collective-permute-done.8.refs_3_ = f32[4,3,32,128]{3,2,1,0:T(8,128)S(1)} collective-permute-done((f32[4,3,32,128]{3,2,1,0:T(8,128)S(1)}, f32[4,3,32,128]{3,2,1,0:T(8,128)S(1)}, u32[]{:S(2)}, u32[]{:S(2)}) %collective-permute-start.8) | collective-permute-done | bytes 196640 | tf_op jit(solution)/shard_map/ppermute | solution.py:164
  36.6 1.2 collective-permute-start.11
  37.8 3.1 %collective-permute-done.7.refs_2_ = f32[4,3,32,128]{3,2,1,0:T(8,128)S(1)} collective-permute-done((f32[4,3,32,128]{3,2,1,0:T(8,128)S(1)}, f32[4,3,32,128]{3,2,1,0:T(8,128)S(1)}, u32[]{:S(2)}, u32[]{:S(2)}) %collective-permute-start.7) | collective-permute-done | bytes 196640 | tf_op jit(solution)/shard_map/ppermute | solution.py:164
  40.9 1.2 faces.1
  42.1 0.4 collective-permute-start.10
  42.5 2.3 %collective-permute-start.9 = (f32[384,128]{1,0:T(8,128)S(1)}, f32[384,128]{1,0:T(8,128)S(1)}, u32[]{:S(2)}, u32[]{:S(2)}) collective-permute-start(f32[384,128]{1,0:T(8,128)S(1)} %get-tuple-element.76), channel_id=1, source_target_pairs={{0,1},{1,2},{2,3},{3,4},{4,5},{5,6},{6,7},{7,8},{8,9},{9,10},{10,1... | collective-permute-start | bytes 589832 | tf_op jit(solution)/shard_map/ppermute | solution.py:778
  44.8 0.8 collective-permute-start.16
  45.7 3.5 %collective-permute-start.15 = (f32[4,3,32,128]{3,2,1,0:T(8,128)S(1)}, f32[4,3,32,128]{3,2,1,0:T(8,128)S(1)}, u32[]{:S(2)}, u32[]{:S(2)}) collective-permute-start(f32[4,3,32,128]{3,2,1,0:T(8,128)S(1)} %pad_maximum_fusion.2), channel_id=1, source_target_pairs={{0,8},{1,9},{2,10},{3,11},{4,12},{5,13},{6,14},{7,15},{8,0},{9,1},... | collective-permute-start | bytes 589832 | tf_op jit(solution)/shard_map/ppermute | solution.py:164
  49.2 3.9 %velocity.1 = (f32[3,512,128]{2,1,0:T(8,128)S(1)}, f32[15,512,128]{2,1,0:T(8,128)S(1)}, bf16[512,384]{1,0:T(8,128)(2,1)S(1)}, bf16[512,384]{1,0:T(8,128)(2,1)S(1)}, f32[3,512,128]{2,1,0:T(8,128)S(1)}) custom-call(s32[1]{0:T(128)} %bitcast.me_ref.refs_0_, f32[4,3,32,128]{3,2,1,0:T(8,128)S(1)} %pad_maximum_fusion.8.refs_0_, ...), custom_call_target="tpu_custom_call" | custom-call | tf_op jit(solution)/shard_map/velocity/pallas_call | solution.py:788
  53.1 4.8 %collective-permute-done.10.above_ref = f32[384,128]{1,0:T(8,128)S(1)} collective-permute-done((f32[384,128]{1,0:T(8,128)S(1)}, f32[384,128]{1,0:T(8,128)S(1)}, u32[]{:S(2)}, u32[]{:S(2)}) %collective-permute-start.10) | collective-permute-done | bytes 196640 | tf_op jit(solution)/shard_map/ppermute | solution.py:779
  58.0 2.9 %halo.1.refs_6_.refs_8_ = f32[12,512,128]{2,1,0:T(8,128)S(1)} custom-call(f32[384,128]{1,0:T(8,128)S(1)} %collective-permute-done.9.below_ref, f32[384,128]{1,0:T(8,128)S(1)} %collective-permute-done.10.above_ref, f32[3,512,128]{2,1,0:T(8,128)S(1)} %get-tuple-element.88.vel_ref, bf16[1024,512]{1,0:T(8,128)(2,1)S(1)} %copy-done, ...), custom_call_target="tpu_custom_call" | custom-call | tf_op jit(solution)/shard_map/halo/pallas_call | solution.py:804
  60.9 1.4 %collective-permute-done.16.refs_3_ = f32[4,3,32,128]{3,2,1,0:T(8,128)S(1)} collective-permute-done((f32[4,3,32,128]{3,2,1,0:T(8,128)S(1)}, f32[4,3,32,128]{3,2,1,0:T(8,128)S(1)}, u32[]{:S(2)}, u32[]{:S(2)}) %collective-permute-start.16) | collective-permute-done | bytes 196640 | tf_op jit(solution)/shard_map/ppermute | solution.py:164
  62.2 2.1 %collective-permute-done.15.refs_2_ = f32[4,3,32,128]{3,2,1,0:T(8,128)S(1)} collective-permute-done((f32[4,3,32,128]{3,2,1,0:T(8,128)S(1)}, f32[4,3,32,128]{3,2,1,0:T(8,128)S(1)}, u32[]{:S(2)}, u32[]{:S(2)}) %collective-permute-start.15) | collective-permute-done | bytes 196640 | tf_op jit(solution)/shard_map/ppermute | solution.py:164
  64.3 0.5 collective-permute-done.14.refs_1_
  64.8 5.6 %momentum.1 = (f32[4,3,32,128]{3,2,1,0:T(8,128)S(1)}, f32[4,3,32,128]{3,2,1,0:T(8,128)S(1)}, f32[4,3,32,128]{3,2,1,0:T(8,128)S(1)}, f32[4,3,32,128]{3,2,1,0:T(8,...) custom-call(s32[1]{0:T(128)} %bitcast.me_ref.refs_0_, ...), custom_call_target="tpu_custom_call" | custom-call | tf_op jit(solution)/shard_map/momentum/pallas_call | solution.py:817
  70.4 2.0 %collective-permute-start.17 = (f32[4,3,32,128]{3,2,1,0:T(8,128)S(1)}, f32[4,3,32,128]{3,2,1,0:T(8,128)S(1)}, u32[]{:S(2)}, u32[]{:S(2)}) collective-permute-start(f32[4,3,32,128]{3,2,1,0:T(8,128)S(1)} %get-tuple-element.91), channel_id=1, source_target_pairs={{0,4},{1,5},{2,6},{3,7},{4,0},{5,1},{6,2},{7,3},{8,12},{9,13},{10,... | collective-permute-start | bytes 589832 | tf_op jit(solution)/shard_map/ppermute | solution.py:164
  72.4 0.5 collective-permute-start.18
  72.9 0.7 collective-permute-start.19
  73.6 9.2 %elastic.1 = f32[16,6,32,128]{3,2,1,0:T(8,128)} custom-call(s32[1]{0:T(128)} %bitcast.me_ref.refs_0_, bf16[512,384]{1,0:T(8,128)(2,1)S(1)} %get-tuple-element.94.refs_0_, bf16[512,384]{1,0:T(8,128)(2,1)S(1)} %get-tuple-element.95.refs_1_, bf16[512,384]{1,0:T(8,128)(2,1)S(1)} %get-tuple-element.96.refs_2_, bf16[512,384]{1,0:T(8,128)(2,1)S(1)} %get-tuple-element.97.refs_3_, ...), custom_call_target="tpu_custom_call" | custom-call | tf_op jit(solution)/shard_map/elastic/pallas_call | solution.py:835
  82.8 3.2 %collective-permute-done.18 = f32[4,3,32,128]{3,2,1,0:T(8,128)S(1)} collective-permute-done((f32[4,3,32,128]{3,2,1,0:T(8,128)S(1)}, f32[4,3,32,128]{3,2,1,0:T(8,128)S(1)}, u32[]{:S(2)}, u32[]{:S(2)}) %collective-permute-start.18) | collective-permute-done | bytes 196640 | tf_op jit(solution)/shard_map/ppermute | solution.py:164
  86.1 4.8 %collective-permute-done.19 = f32[4,3,32,128]{3,2,1,0:T(8,128)S(1)} collective-permute-done((f32[4,3,32,128]{3,2,1,0:T(8,128)S(1)}, f32[4,3,32,128]{3,2,1,0:T(8,128)S(1)}, u32[]{:S(2)}, u32[]{:S(2)}) %collective-permute-start.19) | collective-permute-done | bytes 196640 | tf_op jit(solution)/shard_map/ppermute | solution.py:164
  90.8 4.5 %all-to-all-start = ((f32[16,6,32,128]{3,2,1,0:T(8,128)}), f32[16,6,32,128]{3,2,1,0:T(8,128)}, u32[]{:S(2)}, u32[]{:S(2)}) async-start(f32[16,6,32,128]{3,2,1,0:T(8,128)} %elastic.1), calls=%async_computation | async-start | bytes 3145728 | tf_op jit(solution)/shard_map/all_to_all | solution.py:235
  95.4 0.7 pad_maximum_fusion.15
  96.1 0.5 collective-permute-start.22
  96.6 0.7 pad_maximum_fusion.14
  97.3 1.0 collective-permute-start.21
  98.3 0.7 pad_maximum_fusion.13
  99.0 0.7 collective-permute-start.20
  100.4 9.8 %collective-permute-done.22.refs_6_ = f32[4,3,32,128]{3,2,1,0:T(8,128)S(1)} collective-permute-done((f32[4,3,32,128]{3,2,1,0:T(8,128)}, f32[4,3,32,128]{3,2,1,0:T(8,128)S(1)}, u32[]{:S(2)}, u32[]{:S(2)}) %collective-permute-start.22) | collective-permute-done | bytes 196640 | tf_op jit(solution)/shard_map/ppermute | solution.py:164
  110.2 5.5 %collective-permute-done.21.refs_5_ = f32[4,3,32,128]{3,2,1,0:T(8,128)S(1)} collective-permute-done((f32[4,3,32,128]{3,2,1,0:T(8,128)}, f32[4,3,32,128]{3,2,1,0:T(8,128)S(1)}, u32[]{:S(2)}, u32[]{:S(2)}) %collective-permute-start.21) | collective-permute-done | bytes 196640 | tf_op jit(solution)/shard_map/ppermute | solution.py:164
  115.7 1.1 copy-done.5
  116.8 2.7 %advance.2 = f32[3,32,2048]{2,1,0:T(8,128)} custom-call(s32[1]{0:T(128)} %bitcast.me_ref.refs_0_, s32[32]{0:T(128)S(1)} %copy-done.12, f32[1]{0:T(128)S(6)} %select_n.9.refs_2_, f32[4,3,32,128]{3,2,1,0:T(8,128)S(1)} %pad_maximum_fusion.12.refs_3_, f32[4,3,32,128]{3,2,1,0:T(8,128)} %collective-permute-done.20.refs_4_, ...), custom_call_target="tpu_custom_call" | custom-call | tf_op jit(solution)/shard_map/advance/pallas_call | solution.py:690
  119.5 12.0 %all-to-all-done.refs_3_ = f32[16,6,32,128]{3,2,1,0:T(8,128)} async-done(((f32[16,6,32,128]{3,2,1,0:T(8,128)}), f32[16,6,32,128]{3,2,1,0:T(8,128)}, u32[]{:S(2)}, u32[]{:S(2)}) %all-to-all-start) | async-done | bytes 1572896 | tf_op jit(solution)/shard_map/all_to_all | solution.py:235
  131.4 4.0 %advance.3 = f32[6,32,2048]{2,1,0:T(8,128)} custom-call(s32[1]{0:T(128)} %bitcast.me_ref.refs_0_, s32[32]{0:T(128)S(1)} %copy-done.12, f32[1]{0:T(128)S(6)} %select_n.9.refs_2_, f32[16,6,32,128]{3,2,1,0:T(8,128)} %all-to-all-done.refs_3_, bf16[16,384,128]{2,1,0:T(8,128)(2,1)S(1)} %weights.1.refs_7_.refs_4_, f32[6,32,2048]{2,1,0:T(8,128)S(1)} %copy-done.2), custom_call_target="tpu_custom_call" | custom-call | tf_op jit(solution)/shard_map/advance/pallas_call | solution.py:690
  (64 shorter events, 0.8 us)
Async XLA Ops:
  0.6 9.6 %copy-start.12 = (s32[32]{0:T(128)S(1)}, s32[32]{0:T(128)}, u32[]{:S(2)}) copy-start(s32[32]{0:T(128)} %refs_1_.5) | copy-start | bytes 388
  0.6 16.3 %copy-start.6 = (bf16[24,128,256]{2,1,0:T(8,128)(2,1)S(1)}, bf16[24,128,256]{2,1,0:T(8,128)(2,1)}, u32[]{:S(2)}) copy-start(bf16[24,128,256]{2,1,0:T(8,128)(2,1)} %constant.35.clone.faces_ref) | copy-start | bytes 4718596
  0.7 16.3 %copy-start.8 = (bf16[10,128,128]{2,1,0:T(8,128)(2,1)S(1)}, bf16[10,128,128]{2,1,0:T(8,128)(2,1)}, u32[]{:S(2)}) copy-start(bf16[10,128,128]{2,1,0:T(8,128)(2,1)} %constant.34.clone.both_ref) | copy-start | bytes 983044
  0.7 16.3 %copy-start.11 = (f32[128,128]{1,0:T(8,128)S(1)}, f32[128,128]{1,0:T(8,128)}, u32[]{:S(2)}) copy-start(f32[128,128]{1,0:T(8,128)} %constant.33.clone.inv_r_ref) | copy-start | bytes 196612
  4.2 12.7 %copy-start.7 = (bf16[18,256,128]{2,1,0:T(8,128)(2,1)S(1)}, bf16[18,256,128]{2,1,0:T(8,128)(2,1)}, u32[]{:S(2)}) copy-start(bf16[18,256,128]{2,1,0:T(8,128)(2,1)} %constant.36.clone.halos_ref) | copy-start | bytes 3538948
  4.2 4.8 %collective-permute-start = (f32[4,6,32,128]{3,2,1,0:T(8,128)}, f32[4,6,32,128]{3,2,1,0:T(8,128)S(1)}, u32[]{:S(2)}, u32[]{:S(2)}) collective-permute-start(f32[4,6,32,128]{3,2,1,0:T(8,128)} %get-tuple-element.56), channel_id=1, source_target_pairs={{0,1},{1,0},{2,3},{3,2},{4,5},{5,4},{6,7},{7,6},{8,9},{9,8},{10,11... | collective-permute-start | bytes 1179656 | tf_op jit(solution)/shard_map/ppermute | solution.py:164
  5.0 21.6 %collective-permute-start.4 = (f32[4,6,32,128]{3,2,1,0:T(8,128)}, f32[4,6,32,128]{3,2,1,0:T(8,128)S(1)}, u32[]{:S(2)}, u32[]{:S(2)}) collective-permute-start(f32[4,6,32,128]{3,2,1,0:T(8,128)} %get-tuple-element.61), channel_id=1, source_target_pairs={{0,2},{1,3},{2,0},{3,1},{4,6},{5,7},{6,4},{7,5},{8,10},{9,11},{10,... | collective-permute-start | bytes 1179656 | tf_op jit(solution)/shard_map/ppermute | solution.py:164
  5.2 21.3 %collective-permute-start.5 = (f32[4,6,32,128]{3,2,1,0:T(8,128)}, f32[4,6,32,128]{3,2,1,0:T(8,128)S(1)}, u32[]{:S(2)}, u32[]{:S(2)}) collective-permute-start(f32[4,6,32,128]{3,2,1,0:T(8,128)} %get-tuple-element.62), channel_id=1, source_target_pairs={{0,3},{1,2},{2,1},{3,0},{4,7},{5,6},{6,5},{7,4},{8,11},{9,10},{10,... | collective-permute-start | bytes 1179656 | tf_op jit(solution)/shard_map/ppermute | solution.py:164
  6.7 15.6 %collective-permute-start.2 = (f32[4,3,32,128]{3,2,1,0:T(8,128)}, f32[4,3,32,128]{3,2,1,0:T(8,128)S(1)}, u32[]{:S(2)}, u32[]{:S(2)}) collective-permute-start(f32[4,3,32,128]{3,2,1,0:T(8,128)} %get-tuple-element.58), channel_id=1, source_target_pairs={{0,8},{1,9},{2,10},{3,11},{4,12},{5,13},{6,14},{7,15},{8,0},{9,1},... | collective-permute-start | bytes 589832 | tf_op jit(solution)/shard_map/ppermute | solution.py:164
  9.0 17.5 %collective-permute-start.3 = (f32[4,3,32,128]{3,2,1,0:T(8,128)}, f32[4,3,32,128]{3,2,1,0:T(8,128)S(1)}, u32[]{:S(2)}, u32[]{:S(2)}) collective-permute-start(f32[4,3,32,128]{3,2,1,0:T(8,128)} %get-tuple-element.59), channel_id=1, source_target_pairs={{0,12},{1,13},{2,14},{3,15},{4,8},{5,9},{6,10},{7,11},{8,4},{9,5},... | collective-permute-start | bytes 589832 | tf_op jit(solution)/shard_map/ppermute | solution.py:164
  9.0 17.5 %collective-permute-start.1 = (f32[4,3,32,128]{3,2,1,0:T(8,128)}, f32[4,3,32,128]{3,2,1,0:T(8,128)S(1)}, u32[]{:S(2)}, u32[]{:S(2)}) collective-permute-start(f32[4,3,32,128]{3,2,1,0:T(8,128)} %get-tuple-element.57), channel_id=1, source_target_pairs={{0,4},{1,5},{2,6},{3,7},{4,0},{5,1},{6,2},{7,3},{8,12},{9,13},{10,... | collective-permute-start | bytes 589832 | tf_op jit(solution)/shard_map/ppermute | solution.py:164
  10.2 0.9 copy-start.10
  17.0 9.6 %copy-start.13 = (f32[4,6,32,128]{3,2,1,0:T(8,128)S(1)}, f32[4,6,32,128]{3,2,1,0:T(8,128)}, u32[]{:S(2)}) copy-start(f32[4,6,32,128]{3,2,1,0:T(8,128)} %get-tuple-element.67) | copy-start | bytes 1179652
  26.6 2.4 %copy-start.14 = (f32[4,3,32,128]{3,2,1,0:T(8,128)S(1)}, f32[4,3,32,128]{3,2,1,0:T(8,128)}, u32[]{:S(2)}) copy-start(f32[4,3,32,128]{3,2,1,0:T(8,128)} %get-tuple-element.71) | copy-start | bytes 589828
  26.7 18.1 %collective-permute-start.13 = (f32[4,3,32,128]{3,2,1,0:T(8,128)S(1)}, f32[4,3,32,128]{3,2,1,0:T(8,128)S(1)}, u32[]{:S(2)}, u32[]{:S(2)}) collective-permute-start(f32[4,3,32,128]{3,2,1,0:T(8,128)S(1)} %pad_maximum_fusion.11), channel_id=1, source_target_pairs={{0,12},{1,13},{2,14},{3,15},{4,8},{5,9},{6,10},{7,11},{8,4},{9,5},... | collective-permute-start | bytes 589832 | tf_op jit(solution)/shard_map/ppermute | solution.py:164
  28.9 16.8 %collective-permute-start.12 = (f32[4,3,32,128]{3,2,1,0:T(8,128)S(1)}, f32[4,3,32,128]{3,2,1,0:T(8,128)S(1)}, u32[]{:S(2)}, u32[]{:S(2)}) collective-permute-start(f32[4,3,32,128]{3,2,1,0:T(8,128)S(1)} %pad_maximum_fusion.10), channel_id=1, source_target_pairs={{0,8},{1,9},{2,10},{3,11},{4,12},{5,13},{6,14},{7,15},{8,0},{9,1},... | collective-permute-start | bytes 589832 | tf_op jit(solution)/shard_map/ppermute | solution.py:164
  29.1 7.5 %collective-permute-start.8 = (f32[4,3,32,128]{3,2,1,0:T(8,128)S(1)}, f32[4,3,32,128]{3,2,1,0:T(8,128)S(1)}, u32[]{:S(2)}, u32[]{:S(2)}) collective-permute-start(f32[4,3,32,128]{3,2,1,0:T(8,128)S(1)} %pad_maximum_fusion.7), channel_id=1, source_target_pairs={{0,3},{1,2},{2,1},{3,0},{4,7},{5,6},{6,5},{7,4},{8,11},{9,10},{10,... | collective-permute-start | bytes 589832 | tf_op jit(solution)/shard_map/ppermute | solution.py:164
  30.0 10.8 %collective-permute-start.7 = (f32[4,3,32,128]{3,2,1,0:T(8,128)S(1)}, f32[4,3,32,128]{3,2,1,0:T(8,128)S(1)}, u32[]{:S(2)}, u32[]{:S(2)}) collective-permute-start(f32[4,3,32,128]{3,2,1,0:T(8,128)S(1)} %pad_maximum_fusion.6), channel_id=1, source_target_pairs={{0,2},{1,3},{2,0},{3,1},{4,6},{5,7},{6,4},{7,5},{8,10},{9,11},{10,... | collective-permute-start | bytes 589832 | tf_op jit(solution)/shard_map/ppermute | solution.py:164
  31.4 9.5 %collective-permute-start.6 = (f32[4,3,32,128]{3,2,1,0:T(8,128)S(1)}, f32[4,3,32,128]{3,2,1,0:T(8,128)S(1)}, u32[]{:S(2)}, u32[]{:S(2)}) collective-permute-start(f32[4,3,32,128]{3,2,1,0:T(8,128)S(1)} %pad_maximum_fusion.5), channel_id=1, source_target_pairs={{0,1},{1,0},{2,3},{3,2},{4,5},{5,4},{6,7},{7,6},{8,9},{9,8},{10,11... | collective-permute-start | bytes 589832 | tf_op jit(solution)/shard_map/ppermute | solution.py:164
  31.6 17.5 %copy-start = (bf16[1024,512]{1,0:T(8,128)(2,1)S(1)}, bf16[1024,512]{1,0:T(8,128)(2,1)}, u32[]{:S(2)}) copy-start(bf16[1024,512]{1,0:T(8,128)(2,1)} %constant.29.clone.refs_6_.high_ref.refs_7_.refs_9_) | copy-start | bytes 3145732
  31.6 17.5 %copy-start.1 = (bf16[1024,512]{1,0:T(8,128)(2,1)S(1)}, bf16[1024,512]{1,0:T(8,128)(2,1)}, u32[]{:S(2)}) copy-start(bf16[1024,512]{1,0:T(8,128)(2,1)} %constant.30.clone.refs_7_.low_ref.refs_8_.refs_10_) | copy-start | bytes 3145732
  36.6 12.5 %collective-permute-start.11 = (f32[4,3,32,128]{3,2,1,0:T(8,128)S(1)}, f32[4,3,32,128]{3,2,1,0:T(8,128)S(1)}, u32[]{:S(2)}, u32[]{:S(2)}) collective-permute-start(f32[4,3,32,128]{3,2,1,0:T(8,128)S(1)} %pad_maximum_fusion.9), channel_id=1, source_target_pairs={{0,4},{1,5},{2,6},{3,7},{4,0},{5,1},{6,2},{7,3},{8,12},{9,13},{10,... | collective-permute-start | bytes 589832 | tf_op jit(solution)/shard_map/ppermute | solution.py:164
  42.1 15.8 %collective-permute-start.10 = (f32[384,128]{1,0:T(8,128)S(1)}, f32[384,128]{1,0:T(8,128)S(1)}, u32[]{:S(2)}, u32[]{:S(2)}) collective-permute-start(f32[384,128]{1,0:T(8,128)S(1)} %get-tuple-element.77), channel_id=1, source_target_pairs={{1,0},{2,1},{3,2},{4,3},{5,4},{6,5},{7,6},{8,7},{9,8},{10,9},{11,1... | collective-permute-start | bytes 589832 | tf_op jit(solution)/shard_map/ppermute | solution.py:779
  42.5 15.4 %collective-permute-start.9 = (f32[384,128]{1,0:T(8,128)S(1)}, f32[384,128]{1,0:T(8,128)S(1)}, u32[]{:S(2)}, u32[]{:S(2)}) collective-permute-start(f32[384,128]{1,0:T(8,128)S(1)} %get-tuple-element.76), channel_id=1, source_target_pairs={{0,1},{1,2},{2,3},{3,4},{4,5},{5,6},{6,7},{7,8},{8,9},{9,10},{10,1... | collective-permute-start | bytes 589832 | tf_op jit(solution)/shard_map/ppermute | solution.py:778
  44.8 17.4 %collective-permute-start.16 = (f32[4,3,32,128]{3,2,1,0:T(8,128)S(1)}, f32[4,3,32,128]{3,2,1,0:T(8,128)S(1)}, u32[]{:S(2)}, u32[]{:S(2)}) collective-permute-start(f32[4,3,32,128]{3,2,1,0:T(8,128)S(1)} %pad_maximum_fusion.3), channel_id=1, source_target_pairs={{0,12},{1,13},{2,14},{3,15},{4,8},{5,9},{6,10},{7,11},{8,4},{9,5},... | collective-permute-start | bytes 589832 | tf_op jit(solution)/shard_map/ppermute | solution.py:164
  45.7 18.6 %collective-permute-start.15 = (f32[4,3,32,128]{3,2,1,0:T(8,128)S(1)}, f32[4,3,32,128]{3,2,1,0:T(8,128)S(1)}, u32[]{:S(2)}, u32[]{:S(2)}) collective-permute-start(f32[4,3,32,128]{3,2,1,0:T(8,128)S(1)} %pad_maximum_fusion.2), channel_id=1, source_target_pairs={{0,8},{1,9},{2,10},{3,11},{4,12},{5,13},{6,14},{7,15},{8,0},{9,1},... | collective-permute-start | bytes 589832 | tf_op jit(solution)/shard_map/ppermute | solution.py:164
  49.1 8.8 %copy-start.9 = (bf16[3,128,128]{2,1,0:T(8,128)(2,1)S(1)}, bf16[3,128,128]{2,1,0:T(8,128)(2,1)}, u32[]{:S(2)}) copy-start(bf16[3,128,128]{2,1,0:T(8,128)(2,1)} %constant.38.clone.places_ref) | copy-start | bytes 294916
  57.9 6.9 %copy-start.3 = (bf16[512,1024]{1,0:T(8,128)(2,1)S(1)}, bf16[512,1024]{1,0:T(8,128)(2,1)}, u32[]{:S(2)}) copy-start(bf16[512,1024]{1,0:T(8,128)(2,1)} %constant.31.clone.refs_9_.refs_11_) | copy-start | bytes 3145732
  57.9 6.9 %copy-start.4 = (bf16[512,1024]{1,0:T(8,128)(2,1)S(1)}, bf16[512,1024]{1,0:T(8,128)(2,1)}, u32[]{:S(2)}) copy-start(bf16[512,1024]{1,0:T(8,128)(2,1)} %constant.32.clone.refs_10_.refs_12_) | copy-start | bytes 3145732
  57.9 6.9 %collective-permute-start.14 = (f32[4,3,32,128]{3,2,1,0:T(8,128)S(1)}, f32[4,3,32,128]{3,2,1,0:T(8,128)S(1)}, u32[]{:S(2)}, u32[]{:S(2)}) collective-permute-start(f32[4,3,32,128]{3,2,1,0:T(8,128)S(1)} %pad_maximum_fusion.1), channel_id=1, source_target_pairs={{0,4},{1,5},{2,6},{3,7},{4,0},{5,1},{6,2},{7,3},{8,12},{9,13},{10,... | collective-permute-start | bytes 589832 | tf_op jit(solution)/shard_map/ppermute | solution.py:164
  70.4 12.4 %collective-permute-start.17 = (f32[4,3,32,128]{3,2,1,0:T(8,128)S(1)}, f32[4,3,32,128]{3,2,1,0:T(8,128)S(1)}, u32[]{:S(2)}, u32[]{:S(2)}) collective-permute-start(f32[4,3,32,128]{3,2,1,0:T(8,128)S(1)} %get-tuple-element.91), channel_id=1, source_target_pairs={{0,4},{1,5},{2,6},{3,7},{4,0},{5,1},{6,2},{7,3},{8,12},{9,13},{10,... | collective-permute-start | bytes 589832 | tf_op jit(solution)/shard_map/ppermute | solution.py:164
  72.4 13.7 %collective-permute-start.18 = (f32[4,3,32,128]{3,2,1,0:T(8,128)S(1)}, f32[4,3,32,128]{3,2,1,0:T(8,128)S(1)}, u32[]{:S(2)}, u32[]{:S(2)}) collective-permute-start(f32[4,3,32,128]{3,2,1,0:T(8,128)S(1)} %get-tuple-element.92), channel_id=1, source_target_pairs={{0,8},{1,9},{2,10},{3,11},{4,12},{5,13},{6,14},{7,15},{8,0},{9,1},... | collective-permute-start | bytes 589832 | tf_op jit(solution)/shard_map/ppermute | solution.py:164
  72.9 17.9 %collective-permute-start.19 = (f32[4,3,32,128]{3,2,1,0:T(8,128)S(1)}, f32[4,3,32,128]{3,2,1,0:T(8,128)S(1)}, u32[]{:S(2)}, u32[]{:S(2)}) collective-permute-start(f32[4,3,32,128]{3,2,1,0:T(8,128)S(1)} %get-tuple-element.93), channel_id=1, source_target_pairs={{0,12},{1,13},{2,14},{3,15},{4,8},{5,9},{6,10},{7,11},{8,4},{9,5},... | collective-permute-start | bytes 589832 | tf_op jit(solution)/shard_map/ppermute | solution.py:164
  90.8 40.6 %all-to-all-start = ((f32[16,6,32,128]{3,2,1,0:T(8,128)}), f32[16,6,32,128]{3,2,1,0:T(8,128)}, u32[]{:S(2)}, u32[]{:S(2)}) async-start(f32[16,6,32,128]{3,2,1,0:T(8,128)} %elastic.1), calls=%async_computation | async-start | bytes 3145728 | tf_op jit(solution)/shard_map/all_to_all | solution.py:235
  96.1 14.0 %collective-permute-start.22 = (f32[4,3,32,128]{3,2,1,0:T(8,128)}, f32[4,3,32,128]{3,2,1,0:T(8,128)S(1)}, u32[]{:S(2)}, u32[]{:S(2)}) collective-permute-start(f32[4,3,32,128]{3,2,1,0:T(8,128)} %pad_maximum_fusion.15), channel_id=1, source_target_pairs={{0,3},{1,2},{2,1},{3,0},{4,7},{5,6},{6,5},{7,4},{8,11},{9,10},{10,... | collective-permute-start | bytes 589832 | tf_op jit(solution)/shard_map/ppermute | solution.py:164
  97.3 18.3 %collective-permute-start.21 = (f32[4,3,32,128]{3,2,1,0:T(8,128)}, f32[4,3,32,128]{3,2,1,0:T(8,128)S(1)}, u32[]{:S(2)}, u32[]{:S(2)}) collective-permute-start(f32[4,3,32,128]{3,2,1,0:T(8,128)} %pad_maximum_fusion.14), channel_id=1, source_target_pairs={{0,2},{1,3},{2,0},{3,1},{4,6},{5,7},{6,4},{7,5},{8,10},{9,11},{10,... | collective-permute-start | bytes 589832 | tf_op jit(solution)/shard_map/ppermute | solution.py:164
  99.0 16.7 %collective-permute-start.20 = (f32[4,3,32,128]{3,2,1,0:T(8,128)}, f32[4,3,32,128]{3,2,1,0:T(8,128)}, u32[]{:S(2)}, u32[]{:S(2)}) collective-permute-start(f32[4,3,32,128]{3,2,1,0:T(8,128)} %pad_maximum_fusion.13), channel_id=1, source_target_pairs={{0,1},{1,0},{2,3},{3,2},{4,5},{5,4},{6,7},{7,6},{8,9},{9,8},{10,11... | collective-permute-start | bytes 589832 | tf_op jit(solution)/shard_map/ppermute | solution.py:164
  100.4 31.1 %copy-start.2 = (f32[6,32,2048]{2,1,0:T(8,128)S(1)}, f32[6,32,2048]{2,1,0:T(8,128)}, u32[]{:S(2)}) copy-start(f32[6,32,2048]{2,1,0:T(8,128)} %refs_5_.1) | copy-start | bytes 4718596
  115.7 1.1 copy-start.5
